TPU v7x, 32 devices: a whole 2x2x4 slice. The times are simulated.
32 devices in a mesh: expert: 8 (over y, x, core), dp: 4 (over z).
Axes of the slice: x: 2, y: 2, z: 4, core: 2. Of those that a mesh axis runs over, the one named last changes fastest.
Arguments:
- tokens: bfloat16 [1024, 4096], P('expert'), may hold values from -6 to 6
- cotangent: bfloat16 [1024, 4096], P('expert'), may hold values from -3 to 3
- gate_weight: bfloat16 [8, 768, 4096], P('expert', 'dp'), may hold values from -0.09375 to 0.09375
- up_weight: bfloat16 [8, 768, 4096], P('expert', 'dp'), may hold values from -0.09375 to 0.09375
- down_weight: bfloat16 [8, 768, 4096], P('expert', 'dp'), may hold values from -0.21875 to 0.21875
- expert_ids: int32 [1024, 4], P('expert'), may hold values from 0 to 7, all different within a row; in each aligned block of 128 rows (0 to 127, 128 to 255, ...) at most 80 rows name the same one
- gates: bfloat16 [1024, 4], P('expert'), may hold values from 0.049804688 to 0.59765625
- swap_flags: int32 [4], replicated, may hold values 0 or 1
Outputs:
- input_grad: bfloat16 [1024, 4096], P('expert', 'dp')
- gate_grad: bfloat16 [1024, 4], P('expert')
- gate_weight_grad: bfloat16 [8, 768, 4096], P('expert', 'dp')
- up_weight_grad: bfloat16 [8, 768, 4096], P('expert', 'dp')
- down_weight_grad: bfloat16 [8, 768, 4096], P('expert', 'dp')
Inputs may be any that keep to these rules, and one draw needn't show every extreme that they name: `expert_ids`: each row names 4 different experts. Among the rows of one device no expert is named more than 80 times, and in every draw some expert is named exactly 80 times by the rows of some device.
All inputs are finite; a program needn't handle non-finite values.
Results may differ from a plain program's by a relative error of at most 0.011.
Values may be sent and summed in bfloat16 or wider, within the bound.
No kernel may reach another device: no remote copies, remote signals or barrier semaphores. Data moves between devices by JAX's collectives and lax.ppermute only.
A program may use at most 128 MiB of HBM per device.

v0:
```python
import jax
import jax.numpy as jnp
from jax import lax
from jax.sharding import PartitionSpec as P


def from_behind(value, axis, by):
    devices = lax.axis_size(axis)
    return lax.ppermute(value, axis, [(i, (i + by) % devices) for i in range(devices)])


def pair_lookup(experts, pair_flags, half_axis):
    match = experts[:, None] % half_axis == jnp.arange(half_axis, dtype=jnp.int32)[None, :]
    return jnp.sum(jnp.where(match, pair_flags[None, :], 0), axis=1)


def shards(tokens, cotangent, gate_weight, up_weight, down_weight, expert_ids, gates, swap_flags):
    expert_count = lax.axis_size("expert")
    half_axis = expert_count // 2
    my_slot = lax.axis_index("expert")
    row_count, model_width = tokens.shape
    routed = expert_ids.shape[1]
    capacity = row_count * routed * 5 // (4 * expert_count)
    groups = lax.axis_size("dp")
    quarter = model_width // groups
    own_flag = pair_lookup(jnp.reshape(my_slot, (1,)), swap_flags, half_axis)[0]
    flat_ids = expert_ids.reshape(-1)
    weights = (gate_weight, up_weight, down_weight)
    arrived = from_behind((gate_weight, up_weight, down_weight), "expert", half_axis)
    weights = tuple(
        (jnp.where(own_flag == 1, fresh, stay) for fresh, stay in zip(arrived, weights))
    )
    flipped = pair_lookup(flat_ids, swap_flags, half_axis)
    target = jnp.where(flipped == 1, (flat_ids + half_axis) % expert_count, flat_ids)
    copies = row_count * routed
    onehot = (target[:, None] == jnp.arange(expert_count, dtype=jnp.int32)[None, :]).astype(
        jnp.int32
    )
    earlier = jnp.cumsum(onehot, axis=0) - onehot
    position = jnp.sum(earlier * onehot, axis=1)
    buffer_index = target * capacity + position
    source = jnp.zeros((expert_count * capacity,), jnp.int32)
    source = source.at[buffer_index].set(jnp.arange(copies, dtype=jnp.int32) + 1)
    filled = source > 0
    copy_index = jnp.maximum(source - 1, 0)
    token_index = copy_index // routed
    x_buffer = jnp.where(filled[:, None], tokens[token_index], 0)
    dy_buffer = jnp.where(filled[:, None], cotangent[token_index], 0)
    gate_buffer = jnp.where(filled, gates.reshape(-1)[copy_index], 0)
    x_rows, dy_rows, gate_rows = (
        lax.all_to_all(x_buffer, "expert", split_axis=0, concat_axis=0, tiled=True),
        lax.all_to_all(dy_buffer, "expert", split_axis=0, concat_axis=0, tiled=True),
        lax.all_to_all(gate_buffer, "expert", split_axis=0, concat_axis=0, tiled=True),
    )
    w_gate = weights[0][0]
    w_up = weights[1][0]
    w_down = weights[2][0]
    contract_last = (((1,), (1,)), ((), ()))
    pre_gate = lax.dot_general(x_rows, w_gate, contract_last, preferred_element_type=jnp.float32)
    pre_up = lax.dot_general(x_rows, w_up, contract_last, preferred_element_type=jnp.float32)
    sigma = jax.nn.sigmoid(pre_gate)
    active = pre_gate * sigma
    hidden = (active * pre_up).astype(jnp.bfloat16)
    back = lax.dot_general(dy_rows, w_down, contract_last, preferred_element_type=jnp.float32)
    score_part = jnp.sum(hidden.astype(jnp.float32) * back, axis=1)
    grad_hidden = gate_rows.astype(jnp.float32)[:, None] * back
    slope = sigma * (1.0 + pre_gate * (1.0 - sigma))
    grad_gate = (grad_hidden * pre_up * slope).astype(jnp.bfloat16)
    grad_up = (grad_hidden * active).astype(jnp.bfloat16)
    input_part = jnp.dot(grad_gate, w_gate, preferred_element_type=jnp.float32)
    input_part = input_part + jnp.dot(grad_up, w_up, preferred_element_type=jnp.float32)
    scaled = gate_rows[:, None] * dy_rows
    contract_rows = (((0,), (0,)), ((), ()))
    grad_wgate = lax.dot_general(
        grad_gate, x_rows, contract_rows, preferred_element_type=jnp.float32
    )
    grad_wup = lax.dot_general(grad_up, x_rows, contract_rows, preferred_element_type=jnp.float32)
    grad_wdown = lax.dot_general(hidden, scaled, contract_rows, preferred_element_type=jnp.float32)
    scores = lax.psum(score_part, "dp")
    input_share = lax.psum_scatter(input_part, "dp", scatter_dimension=1, tiled=True).astype(
        jnp.bfloat16
    )
    back_rows, back_scores = (
        lax.all_to_all(input_share, "expert", split_axis=0, concat_axis=0, tiled=True),
        lax.all_to_all(
            scores.astype(jnp.bfloat16), "expert", split_axis=0, concat_axis=0, tiled=True
        ),
    )
    per_copy = back_rows[buffer_index].reshape(row_count, routed, quarter)
    input_grad = jnp.sum(per_copy.astype(jnp.float32), axis=1).astype(jnp.bfloat16)
    gate_grad = back_scores[buffer_index].reshape(row_count, routed)
    gradients = (
        grad_wgate.astype(jnp.bfloat16)[None],
        grad_wup.astype(jnp.bfloat16)[None],
        grad_wdown.astype(jnp.bfloat16)[None],
    )
    return (input_grad, gate_grad, gradients[0], gradients[1], gradients[2])


def solution(mesh):
    placed = (
        P("expert", None),
        P("expert", None),
        P("expert", "dp", None),
        P("expert", "dp", None),
        P("expert", "dp", None),
        P("expert", None),
        P("expert", None),
        P(),
    )
    return jax.shard_map(
        shards,
        mesh=mesh,
        in_specs=placed,
        out_specs=(
            P("expert", "dp"),
            P("expert", None),
            P("expert", "dp", None),
            P("expert", "dp", None),
            P("expert", "dp", None),
        ),
        check_vma=False,
    )
```

profile of v0, /device:TPU:0, one launch (start us, length us, event | category | flops | bytes accessed | tf_op | source)
XLA Modules:
  0.0 503.4 jit_solution(18278887214933519936)
XLA Ops:
  7.2 0.0 copy-start
  7.2 0.9 copy.25
  8.1 0.1 broadcast_in_dim_reshape.10
  8.2 0.1 broadcast_in_dim_reshape.12
  8.3 0.1 broadcast_in_dim_reshape.11
  8.4 0.7 select_reduce_fusion
  9.2 1.1 reduce-window.6
  10.3 0.2 slice_reduce_fusion
  10.6 0.1 fusion.24
  10.7 2.4 scatter_custom_fusion
  13.2 0.8 copy.28
  14.0 0.1 reshape.196
  14.1 4.3 gather_fusion
  18.5 0.7 all_to_all.49
  19.1 5.2 %all-to-all-start = ((bf16[8,80,1]{1,2,0:T(2,128)(2,1)}), bf16[8,80,1]{1,2,0:T(2,128)(2,1)S(1)}, u32[]{:S(2)}, u32[]{:S(2)}) async-start(bf16[8,80,1]{1,2,0:T(2,128)(2,1)} %all_to_all.49), calls=%async_computation | async-start | bytes 8192 | tf_op jit(solution)/shard_map/all_to_all | solution.py:53
  24.3 0.1 broadcast_in_dim.71
  24.4 0.0 copy-done
  24.4 0.0 copy-start.2
  24.4 5.3 %gather_fusion.2 = bf16[640,4096]{1,0:T(8,128)(2,1)} fusion(bf16[128,4096]{1,0:T(8,128)(2,1)S(1)} %copy-done, s32[1024]{0:T(1024)S(1)} %get-tuple-element.32), kind=kCustom, calls=%fused_computation.2 | custom fusion | bytes 10488320 | tf_op jit(solution)/shard_map/gather | solution.py:47
  29.7 0.0 copy-done.2
  29.7 5.3 %gather_fusion.1 = bf16[640,4096]{1,0:T(8,128)(2,1)} fusion(bf16[128,4096]{1,0:T(8,128)(2,1)S(1)} %copy-done.2, s32[1024]{0:T(1024)S(1)} %get-tuple-element.32), kind=kCustom, calls=%fused_computation.1 | custom fusion | bytes 10488320 | tf_op jit(solution)/shard_map/gather | solution.py:48
  35.1 8.7 %broadcast_select_fusion = (bf16[8,80,4096]{2,1,0:T(8,128)(2,1)}, bf16[8,80,4096]{2,1,0:T(8,128)(2,1)}) fusion(bf16[8,80,4096]{2,1,0:T(8,128)(2,1)} %bitcast.60, pred[8,80]{1,0:T(8,128)(4,1)S(1)} %broadcast_in_dim.71, bf16[8,80,4096]{2,1,0:T(8,128)(2,1)} %bitcast.61), kind=kLoop, calls=%fused_computation.9 | loop fusion | flops 5242880 | bytes 20972160 | tf_op jit(solution)/shard_map/jit(_where)/select_n | solution.py:47
  43.8 0.0 all-to-all-done
  43.8 64.9 %all_to_all.56 = bf16[8,80,4096]{2,1,0:T(8,128)(2,1)} all-to-all(bf16[8,80,4096]{2,1,0:T(8,128)(2,1)} %get-tuple-element.30), channel_id=1, replica_groups=mesh['expert'=8,'dp'=4] {'expert'}, dimensions={0} | all-to-all | bytes 10485760 | tf_op jit(solution)/shard_map/all_to_all | solution.py:51
  108.7 4.8 all-to-all-start.1
  113.4 0.2 reduce-scatter.2.cloned.1.call-start
  113.7 1.7 collective-permute-start.2
  115.4 0.4 collective-permute-start.1
  115.8 1.6 collective-permute-start
  117.4 0.0 copy-done.6
  117.4 0.6 fusion.35
  118.7 0.1 all_to_all.38
  118.8 88.2 %collective-permute-done.2 = bf16[1,192,4096]{2,1,0:T(8,128)(2,1)} collective-permute-done((bf16[1,192,4096]{2,1,0:T(8,128)(2,1)}, bf16[1,192,4096]{2,1,0:T(8,128)(2,1)}, u32[]{:S(2)}, u32[]{:S(2)}) %collective-permute-start.2) | collective-permute-done | bytes 1572896 | tf_op jit(solution)/shard_map/ppermute | solution.py:9
  207.0 5.0 fusion.12
  212.0 28.7 %collective-permute-done.1 = bf16[1,192,4096]{2,1,0:T(8,128)(2,1)} collective-permute-done((bf16[1,192,4096]{2,1,0:T(8,128)(2,1)}, bf16[1,192,4096]{2,1,0:T(8,128)(2,1)}, u32[]{:S(2)}, u32[]{:S(2)}) %collective-permute-start.1) | collective-permute-done | bytes 1572896 | tf_op jit(solution)/shard_map/ppermute | solution.py:9
  240.7 3.3 fusion.16
  244.1 29.9 %collective-permute-done = bf16[1,192,4096]{2,1,0:T(8,128)(2,1)} collective-permute-done((bf16[1,192,4096]{2,1,0:T(8,128)(2,1)}, bf16[1,192,4096]{2,1,0:T(8,128)(2,1)}, u32[]{:S(2)}, u32[]{:S(2)}) %collective-permute-start) | collective-permute-done | bytes 1572896 | tf_op jit(solution)/shard_map/ppermute | solution.py:9
  274.0 0.0 all-to-all-done.1
  274.0 5.1 %multiply_reduce_fusion = (f32[640]{0:T(1024)S(1)}, bf16[640,192]{0,1:T(8,128)(2,1)S(1)}, bf16[640,192]{0,1:T(8,128)(2,1)S(1)}, bf16[640,192]{0,1:T(8,128)(2,1)S(1)}) fusion(f32[640,192]{0,1:T(8,128)S(1)} %fusion.16, f32[640,192]{0,1:T(8,128)S(1)} %fusion.12, f32[640]{0:T(1024)S(1)} %convert_element_type.50, bf16[640,4096]{1,0:T(8,128)(2,1)} %bitcast.6, ...), kind=kOutput, calls=%fused_computation.31 | convolution fusion | flops 1009753472 | bytes 10114049 | tf_op jit(solution)/shard_map/dot_general | solution.py:64
  279.1 0.0 copy-start.3
  279.1 3.1 fusion.14
  282.2 7.1 %convolution_add_fusion = f32[640,4096]{1,0:T(8,128)} fusion(f32[640,4096]{1,0:T(8,128)S(1)} %fusion.14, bf16[640,192]{0,1:T(8,128)(2,1)S(1)} %get-tuple-element.26, bf16[1,192,4096]{2,1,0:T(8,128)(2,1)} %collective-permute-done.2, bf16[1,192,4096]{2,1,0:T(8,128)(2,1)S(1)} %copy-done.3, pred[]{:T(512)S(6)} %eq.91), kind=kOutput, calls=%fused_computation.6 | convolution fusion | flops 1010040832 | bytes 24363008 | tf_op jit(solution)/shard_map/dot_general | solution.py:70
  289.3 0.0 reduce-scatter.2.cloned.1.call-update
  289.3 12.3 %psum.7 = bf16[640]{0:T(1024)(128)(2,1)S(1)} all-reduce(f32[640]{0:T(1024)S(1)} %get-tuple-element.20), channel_id=1, replica_groups=mesh['expert'=8,'dp'=4] {'dp'}, use_global_device_ids=true, to_apply=%region_9.10 | all-reduce | flops 640 | bytes 3840 | tf_op jit(solution)/shard_map/psum | solution.py:79
  301.6 0.7 all_to_all.50
  302.3 3.3 all-to-all-start.4
  305.6 161.3 %reduce-scatter.2.cloned.1.call-done = f32[640,1024]{1,0:T(8,128)} async-done(((f32[640,4096]{1,0:T(8,128)}), f32[640,1024]{1,0:T(8,128)}) %reduce-scatter.2.cloned.1.call-update) | async-done | bytes 2621456 | tf_op jit(solution)/shard_map/reduce_scatter | solution.py:80
  466.9 3.0 convert_element_type.53
  469.9 0.0 all-to-all-done.4
  469.9 3.9 all-to-all-start.3
  473.9 0.0 slice-start.3
  473.9 5.2 %fusion.5 = bf16[1,192,4096]{2,1,0:T(8,128)(2,1)} fusion(bf16[640,192]{0,1:T(8,128)(2,1)S(1)} %get-tuple-element.26, bf16[640,4096]{1,0:T(8,128)(2,1)} %bitcast.52), kind=kOutput, calls=%fused_computation.14 | convolution fusion | flops 1007419392 | bytes 7061504 | tf_op jit(solution)/shard_map/dot_general | solution.py:74
  479.1 0.0 slice-done.3
  479.1 2.5 fusion.6
  481.6 5.2 %fusion.7 = bf16[1,192,4096]{2,1,0:T(8,128)(2,1)} fusion(bf16[640,192]{0,1:T(8,128)(2,1)S(1)} %get-tuple-element.21, bf16[640,4096]{1,0:T(8,128)(2,1)} %bitcast.6, bf16[640]{0:T(1024)(128)(2,1)S(1)} %all_to_all.38), kind=kOutput, calls=%fused_computation.16 | convolution fusion | flops 1010040832 | bytes 7062784 | tf_op jit(solution)/shard_map/dot_general | solution.py:78
  486.8 0.1 all_to_all.48
  486.9 3.5 gather_fusion.4
  490.4 0.1 reshape.198
  490.5 0.7 copy.31
  491.2 0.7 all-to-all-done.3
  491.9 2.0 gather_fusion.3
  494.0 0.4 reshape.197
  494.4 2.1 reduce_sum.54
  496.5 0.0 copy-done.1
  (30 shorter events, 0.2 us)
Async XLA Ops:
  7.2 17.2 %copy-start = (bf16[128,4096]{1,0:T(8,128)(2,1)S(1)}, bf16[128,4096]{1,0:T(8,128)(2,1)}, u32[]{:S(2)}) copy-start(bf16[128,4096]{1,0:T(8,128)(2,1)} %param.8) | copy-start | bytes 3145732
  19.1 24.7 %all-to-all-start = ((bf16[8,80,1]{1,2,0:T(2,128)(2,1)}), bf16[8,80,1]{1,2,0:T(2,128)(2,1)S(1)}, u32[]{:S(2)}, u32[]{:S(2)}) async-start(bf16[8,80,1]{1,2,0:T(2,128)(2,1)} %all_to_all.49), calls=%async_computation | async-start | bytes 8192 | tf_op jit(solution)/shard_map/all_to_all | solution.py:53
  24.4 5.3 %copy-start.2 = (bf16[128,4096]{1,0:T(8,128)(2,1)S(1)}, bf16[128,4096]{1,0:T(8,128)(2,1)}, u32[]{:S(2)}) copy-start(bf16[128,4096]{1,0:T(8,128)(2,1)} %param.9) | copy-start | bytes 3145732
  108.7 8.7 %copy-start.6 = (s32[4]{0:T(128)S(1)}, s32[4]{0:T(128)}, u32[]{:S(2)}) copy-start(s32[4]{0:T(128)} %param.15) | copy-start | bytes 52
  108.7 132.1 %slice-start = ((s8[5242880]{0:T(1024)(128)(4,1)}), s8[1048576]{0:T(1024)(128)(4,1)S(1)}, s32[]{:S(2)}) async-start(s8[5242880]{0:T(1024)(128)(4,1)} %bitcast.53), calls=%async_computation.7 | async-start | bytes 2097152
  108.7 165.3 %all-to-all-start.1 = ((bf16[8,80,4096]{2,1,0:T(8,128)(2,1)}), bf16[8,80,4096]{2,1,0:T(8,128)(2,1)}, u32[]{:S(2)}, u32[]{:S(2)}) async-start(bf16[8,80,4096]{2,1,0:T(8,128)(2,1)} %get-tuple-element.31), calls=%async_computation.1 | async-start | bytes 10485760 | tf_op jit(solution)/shard_map/all_to_all | solution.py:52
  113.4 353.5 %reduce-scatter.2.cloned.1.call-start = ((), (), s32[]{:S(2)}) async-start(), calls=%async_computation.6 | async-start | bytes 13107200 | tf_op jit(solution)/shard_map/reduce_scatter | solution.py:80
  113.7 93.4 %collective-permute-start.2 = (bf16[1,192,4096]{2,1,0:T(8,128)(2,1)}, bf16[1,192,4096]{2,1,0:T(8,128)(2,1)}, u32[]{:S(2)}, u32[]{:S(2)}) collective-permute-start(bf16[1,192,4096]{2,1,0:T(8,128)(2,1)} %param.10), channel_id=1, source_target_pairs={{0,16},{4,20},{8,24},{12,28},{16,0},{20,4},{24,8},{28,12},{1,17},{... | collective-permute-start | bytes 4718600 | tf_op jit(solution)/shard_map/ppermute | solution.py:9
  115.4 125.4 %collective-permute-start.1 = (bf16[1,192,4096]{2,1,0:T(8,128)(2,1)}, bf16[1,192,4096]{2,1,0:T(8,128)(2,1)}, u32[]{:S(2)}, u32[]{:S(2)}) collective-permute-start(bf16[1,192,4096]{2,1,0:T(8,128)(2,1)} %param.11), channel_id=1, source_target_pairs={{0,16},{4,20},{8,24},{12,28},{16,0},{20,4},{24,8},{28,12},{1,17},{... | collective-permute-start | bytes 4718600 | tf_op jit(solution)/shard_map/ppermute | solution.py:9
  115.8 158.2 %collective-permute-start = (bf16[1,192,4096]{2,1,0:T(8,128)(2,1)}, bf16[1,192,4096]{2,1,0:T(8,128)(2,1)}, u32[]{:S(2)}, u32[]{:S(2)}) collective-permute-start(bf16[1,192,4096]{2,1,0:T(8,128)(2,1)} %param.12), channel_id=1, source_target_pairs={{0,16},{4,20},{8,24},{12,28},{16,0},{20,4},{24,8},{28,12},{1,17},{... | collective-permute-start | bytes 4718600 | tf_op jit(solution)/shard_map/ppermute | solution.py:9
  207.0 33.7 %slice-start.1 = ((s8[5242880]{0:T(1024)(128)(4,1)}), s8[4194304]{0:T(1024)(128)(4,1)S(1)}, s32[]{:S(2)}) async-start(s8[5242880]{0:T(1024)(128)(4,1)} %bitcast.53), calls=%async_computation.8 | async-start | bytes 8388608
  207.0 33.7 %copy-start.4 = (bf16[1,192,4096]{2,1,0:T(8,128)(2,1)S(1)}, bf16[1,192,4096]{2,1,0:T(8,128)(2,1)}, u32[]{:S(2)}) copy-start(bf16[1,192,4096]{2,1,0:T(8,128)(2,1)} %param.11) | copy-start | bytes 4718596
  274.0 5.1 %copy-start.5 = (bf16[1,192,4096]{2,1,0:T(8,128)(2,1)S(1)}, bf16[1,192,4096]{2,1,0:T(8,128)(2,1)}, u32[]{:S(2)}) copy-start(bf16[1,192,4096]{2,1,0:T(8,128)(2,1)} %param.11) | copy-start | bytes 4718596
  279.1 3.1 copy-start.3
  302.3 167.7 %all-to-all-start.4 = ((bf16[8,80,1]{1,2,0:T(2,128)(2,1)}), bf16[8,80,1]{1,2,0:T(2,128)(2,1)S(1)}, u32[]{:S(2)}, u32[]{:S(2)}) async-start(bf16[8,80,1]{1,2,0:T(2,128)(2,1)} %all_to_all.50), calls=%async_computation.5 | async-start | bytes 8192 | tf_op jit(solution)/shard_map/all_to_all | solution.py:85
  469.9 9.1 %slice-start.2 = ((s8[5242880]{0:T(1024)(128)(4,1)}), s8[1048576]{0:T(1024)(128)(4,1)S(1)}, s32[]{:S(2)}) async-start(s8[5242880]{0:T(1024)(128)(4,1)} %bitcast.56), calls=%async_computation.9 | async-start | bytes 2097152
  469.9 22.0 %all-to-all-start.3 = ((bf16[8,80,1024]{2,1,0:T(8,128)(2,1)}), bf16[8,80,1024]{2,1,0:T(8,128)(2,1)S(1)}, u32[]{:S(2)}, u32[]{:S(2)}) async-start(bf16[8,80,1024]{2,1,0:T(8,128)(2,1)} %bitcast.62), calls=%async_computation.4 | async-start | bytes 2621440 | tf_op jit(solution)/shard_map/all_to_all | solution.py:84
  473.9 5.2 %slice-start.3 = ((s8[5242880]{0:T(1024)(128)(4,1)}), s8[4194304]{0:T(1024)(128)(4,1)S(1)}, s32[]{:S(2)}) async-start(s8[5242880]{0:T(1024)(128)(4,1)} %bitcast.56), calls=%async_computation.10 | async-start | bytes 8388608
  491.9 4.6 copy-start.1
Sparse Core Ops, SparseCore 0:
  289.4 177.4 reduce-scatter.1
where the time goes:
time: 504 us; the launch traced here: 503 us
  waiting for transfers between devices  309 us (61%)
  blocking collectives  77.1 us (15%)
  matrix products  36.4 us (7%)
  local copies, waits for them, and re-layouts  28.2 us (6%)
  starting transfers between devices  21.1 us (4%)
  other arithmetic  16.6 us (3%)
  between operations  14.9 us (3%)
    reduce_scatter x1, waiting for transfers between devices, shards(): lax.psum_scatter(input_part, 'dp', scatter_dimension=1, tiled=True)  161 us
    ppermute x3, waiting for transfers between devices, from_behind(): lax.ppermute(value, axis, [(i, (i + by) % devices) for i in range(devices)])  147 us
    all_to_all x1, blocking collectives, shards(): lax.all_to_all(x_buffer, 'expert', split_axis=0, concat_axis=0, tiled=True)  64.9 us
    psum x1, blocking collectives, shards(): scores = lax.psum(score_part, 'dp')  12.3 us
  transfers between devices with their start and end apart: 8, of which 5 were waited for; matrix products, arithmetic and copies ran while one was open for 10% of the time, Pallas kernels for 0%

commit v1 on v0

--- a/solution.py
+++ b/solution.py
@@ -14,7 +14,70 @@
     return jnp.sum(jnp.where(match, pair_flags[None, :], 0), axis=1)
 
 
-def shards(tokens, cotangent, gate_weight, up_weight, down_weight, expert_ids, gates, swap_flags):
+CONTRACT_LAST = (((1,), (1,)), ((), ()))
+CONTRACT_ROWS = (((0,), (0,)), ((), ()))
+
+
+def whole_shards(tokens, cotangent, gate_weight, up_weight, down_weight, expert_ids, gates, swap_flags):
+    expert_count = lax.axis_size("expert")
+    half_axis = expert_count // 2
+    me = lax.axis_index("expert")
+    row_count, model_width = tokens.shape
+    f32, bf16 = jnp.float32, jnp.bfloat16
+    own_flag = pair_lookup(jnp.reshape(me, (1,)), swap_flags, half_axis)[0]
+
+    named = expert_ids[:, :, None] == jnp.arange(expert_count, dtype=jnp.int32)[None, None, :]
+    table = jnp.sum(jnp.where(named, gates[:, :, None].astype(f32), 0), axis=1)
+    all_gates = lax.all_gather(table, "expert", tiled=True)
+    x = lax.all_gather(tokens, "expert", tiled=True)
+    dy = lax.all_gather(cotangent, "expert", tiled=True)
+    mine = jnp.arange(expert_count, dtype=jnp.int32)[None, :] == me
+    g = jnp.sum(jnp.where(mine, all_gates, 0), axis=1)[:, None]
+
+    w_gate, w_up, w_down = gate_weight[0], up_weight[0], down_weight[0]
+    pre_gate = lax.dot_general(x, w_gate, CONTRACT_LAST, preferred_element_type=f32)
+    pre_up = lax.dot_general(x, w_up, CONTRACT_LAST, preferred_element_type=f32)
+    back = lax.dot_general(dy, w_down, CONTRACT_LAST, preferred_element_type=f32)
+    sigma = jax.nn.sigmoid(pre_gate)
+    active = pre_gate * sigma
+    hidden = active * pre_up
+    score_part = jnp.sum(hidden * back, axis=1)
+    grad_hidden = g * back
+    slope = sigma * (1.0 + pre_gate * (1.0 - sigma))
+    grad_gate = (grad_hidden * pre_up * slope).astype(bf16)
+    grad_up = (grad_hidden * active).astype(bf16)
+    weighted = (g * hidden).astype(bf16)
+
+    acts = jnp.concatenate([grad_gate, grad_up, weighted], axis=1)
+    arrived = from_behind(acts, "expert", half_axis)
+    acts = jnp.where(own_flag == 1, arrived, acts)
+    width = grad_gate.shape[1]
+
+    part = jnp.dot(grad_gate, w_gate, preferred_element_type=f32)
+    part = part + jnp.dot(grad_up, w_up, preferred_element_type=f32)
+    share = lax.psum_scatter(part.astype(bf16), "expert", scatter_dimension=0, tiled=True)
+    input_grad = lax.psum_scatter(share, "dp", scatter_dimension=1, tiled=True)
+
+    scores = lax.psum(score_part, "dp")
+    scores = lax.all_to_all(
+        scores.astype(bf16).reshape(expert_count, row_count), "expert", split_axis=0, concat_axis=0, tiled=True
+    )
+    picked = jnp.where(named, scores.T[:, None, :].astype(f32), 0)
+    gate_grad = jnp.sum(picked, axis=2).astype(bf16)
+
+    grad_wboth = lax.dot_general(acts[:, : 2 * width], x, CONTRACT_ROWS, preferred_element_type=f32)
+    grad_wdown = lax.dot_general(acts[:, 2 * width :], dy, CONTRACT_ROWS, preferred_element_type=f32)
+    grad_wboth = grad_wboth.astype(bf16)
+    return (
+        input_grad.astype(bf16),
+        gate_grad,
+        grad_wboth[None, :width],
+        grad_wboth[None, width:],
+        grad_wdown.astype(bf16)[None],
+    )
+
+
+def packed_shards(tokens, cotangent, gate_weight, up_weight, down_weight, expert_ids, gates, swap_flags):
     expert_count = lax.axis_size("expert")
     half_axis = expert_count // 2
     my_slot = lax.axis_index("expert")
@@ -97,6 +160,12 @@
     return (input_grad, gate_grad, gradients[0], gradients[1], gradients[2])
 
 
+def chosen(tokens, cotangent, gate_weight, up_weight, down_weight, expert_ids, gates, swap_flags):
+    capacity = tokens.shape[0] * expert_ids.shape[1] * 5 // (4 * lax.axis_size("expert"))
+    body = whole_shards if 2 * capacity >= tokens.shape[0] else packed_shards
+    return body(tokens, cotangent, gate_weight, up_weight, down_weight, expert_ids, gates, swap_flags)
+
+
 def solution(mesh):
     placed = (
         P("expert", None),
@@ -109,7 +178,7 @@
         P(),
     )
     return jax.shard_map(
-        shards,
+        chosen,
         mesh=mesh,
         in_specs=placed,
         out_specs=(

time: 504 us -> 290 us (0.58)
  waiting for transfers between devices: 309 us -> 188 us
  blocking collectives: 77.1 us -> 19.9 us
  local copies, waits for them, and re-layouts: 28.2 us -> 2.66 us
  starting transfers between devices: 21.1 us -> 4.94 us
  matrix products: 36.4 us -> 52.4 us
  other arithmetic: 16.6 us -> 7.13 us
    ppermute x3 -> x1, waiting for transfers between devices: 147 us -> 31.4 us  [from_behind(): lax.ppermute(value, axis, [(i, (i + by) % devices) for i in range(devices)])]
    reduce_scatter x1 -> x2, waiting for transfers between devices: 161 us -> 46.9 us  [the longest x1 32.8 us: whole_shards(): lax.psum_scatter(part.astype(bf16), 'expert', scatter_dimension=0, tiled=...]
    all_gather x0 -> x2, waiting for transfers between devices: none -> 104 us  [the longest x1 58.3 us: whole_shards(): x = lax.all_gather(tokens, 'expert', tiled=True)]
    all_to_all x1 -> x0, blocking collectives: 64.9 us -> none  [shards(): lax.all_to_all(x_buffer, 'expert', split_axis=0, concat_axis=0, tiled=True)]
    gather x5 -> x0, local copies, waits for them, and re-layouts: 20.5 us -> none  [the longest x1 5.33 us: shards(): dy_buffer = jnp.where(filled[:, None], cotangent[token_index], 0)]
    dot_general x8 -> x7, matrix products: 36.4 us -> 52.4 us  [the longest x1 11.4 us: whole_shards(): part = part + jnp.dot(grad_up, w_up, preferred_element_type=f32)]
    all_to_all x4 -> x1, starting transfers between devices: 17.2 us -> 3.31 us  [whole_shards(): lax.all_to_all(scores.astype(bf16).reshape(expert_count, row_count), 'exp...]
    all_gather x0 -> x1, blocking collectives: none -> 8.28 us  [whole_shards(): all_gates = lax.all_gather(table, 'expert', tiled=True)]
  transfers between devices with their start and end apart: 8 -> 6, of which waited for: 5 -> 6; matrix products, arithmetic and copies ran while one was open for 10% -> 11% of each run, Pallas kernels for 0% -> 0%
where the time goes in v1:
time: 290 us; the launch traced here: 289 us
  waiting for transfers between devices  188 us (65%)
  matrix products  52.4 us (18%)
  blocking collectives  19.9 us (7%)
  between operations  14.5 us (5%)
  other arithmetic  7.13 us (2%)
  starting transfers between devices  4.94 us (2%)
    all_gather x1, waiting for transfers between devices, whole_shards(): x = lax.all_gather(tokens, 'expert', tiled=True)  58.3 us
    all_gather x1, waiting for transfers between devices, whole_shards(): dy = lax.all_gather(cotangent, 'expert', tiled=True)  45.2 us
    reduce_scatter x1, waiting for transfers between devices, whole_shards(): lax.psum_scatter(part.astype(bf16), 'expert', scatter_dimension=0, tiled=...  32.8 us
    ppermute x1, waiting for transfers between devices, from_behind(): lax.ppermute(value, axis, [(i, (i + by) % devices) for i in range(devices)])  31.4 us
    reduce_scatter x1, waiting for transfers between devices, whole_shards(): input_grad = lax.psum_scatter(share, 'dp', scatter_dimension=1, tiled=True)  14.1 us
    psum x1, blocking collectives, whole_shards(): scores = lax.psum(score_part, 'dp')  11.7 us
    dot_general x1, matrix products, whole_shards(): part = part + jnp.dot(grad_up, w_up, preferred_element_type=f32)  11.4 us
    all_gather x1, blocking collectives, whole_shards(): all_gates = lax.all_gather(table, 'expert', tiled=True)  8.28 us
  transfers between devices with their start and end apart: 6, of which 6 were waited for; matrix products, arithmetic and copies ran while one was open for 11% of the time, Pallas kernels for 0%

profile of v1, /device:TPU:0, one launch (start us, length us, event | category | flops | bytes accessed | tf_op | source)
XLA Modules:
  0.0 289.3 jit_solution(8157889017531547858)
XLA Ops:
  7.2 0.0 copy-start
  7.2 0.0 all-gather.5.cloned.1.call-start
  7.2 0.7 all-gather.5.cloned.1.call-update
  7.9 0.0 all-gather.3.cloned.1.call-start
  8.0 0.7 all-gather.3.cloned.1.call-update
  8.7 0.0 copy-start.1
  8.7 58.3 %all-gather.5.cloned.1.call-done = bf16[1024,4096]{1,0:T(8,128)(2,1)} async-done(((bf16[128,4096]{1,0:T(8,128)(2,1)}), bf16[1024,4096]{1,0:T(8,128)(2,1)}) %all-gather.5.cloned.1.call-update) | async-done | bytes 8388624 | tf_op jit(solution)/shard_map/all_gather | solution.py:32
  67.0 0.0 copy-done
  67.0 0.0 copy-start.7
  67.0 7.3 %fusion.3 = f32[1024,192]{0,1:T(8,128)} fusion(bf16[1024,4096]{1,0:T(8,128)(2,1)} %all-gather.5.cloned.1.call-done, bf16[1,192,4096]{2,1,0:T(8,128)(2,1)S(1)} %copy-done), kind=kOutput, calls=%fused_computation.8 | convolution fusion | flops 1610612736 | bytes 10747904 | tf_op jit(solution)/shard_map/dot_general | solution.py:38
  74.3 0.0 copy-done.1
  74.3 0.0 copy-done.7
  74.3 3.8 %fusion.6 = f32[1024,192]{0,1:T(8,128)} fusion(bf16[1024,4096]{1,0:T(8,128)(2,1)S(1)} %copy-done.7, bf16[1,192,4096]{2,1,0:T(8,128)(2,1)S(1)} %copy-done.1), kind=kOutput, calls=%fused_computation.11 | convolution fusion | flops 1610612736 | bytes 10747904 | tf_op jit(solution)/shard_map/dot_general | solution.py:39
  78.1 0.0 copy-start.6
  78.1 0.0 copy-start.5
  78.2 0.0 copy-start.4
  78.2 45.2 %all-gather.3.cloned.1.call-done = bf16[1024,4096]{1,0:T(8,128)(2,1)} async-done(((bf16[128,4096]{1,0:T(8,128)(2,1)}), bf16[1024,4096]{1,0:T(8,128)(2,1)}) %all-gather.3.cloned.1.call-update) | async-done | bytes 8388624 | tf_op jit(solution)/shard_map/all_gather | solution.py:33
  123.3 8.0 %multiply_reduce_fusion = (f32[1024]{0:T(1024)S(1)}, f32[1024,192]{0,1:T(8,128)}) fusion(f32[1024,192]{0,1:T(8,128)} %fusion.6, f32[1024,192]{0,1:T(8,128)} %fusion.3, bf16[1024,4096]{1,0:T(8,128)(2,1)} %all-gather.3.cloned.1.call-done, bf16[1,192,4096]{2,1,0:T(8,128)(2,1)} %param.12), kind=kOutput, calls=%fused_computation.19 | convolution fusion | flops 1611987968 | bytes 12324864 | tf_op jit(solution)/shard_map/dot_general | solution.py:40
  131.4 11.7 %psum.7 = bf16[1024]{0:T(1024)(128)(2,1)S(1)} all-reduce(f32[1024]{0:T(1024)S(1)} %get-tuple-element.12), channel_id=1, replica_groups=mesh['expert'=8,'dp'=4] {'dp'}, use_global_device_ids=true, to_apply=%region_5.6 | all-reduce | flops 1024 | bytes 6144 | tf_op jit(solution)/shard_map/psum | solution.py:61
  143.0 0.6 copy.22
  143.6 3.3 %all-to-all-start = ((bf16[8,1,128]{2,1,0:T(2,128)(2,1)}), bf16[8,1,128]{2,1,0:T(2,128)(2,1)S(1)}, u32[]{:S(2)}, u32[]{:S(2)}) async-start(bf16[8,1,128]{2,1,0:T(2,128)(2,1)} %copy.22), calls=%async_computation.2 | async-start | bytes 8192 | tf_op jit(solution)/shard_map/all_to_all | solution.py:62
  147.0 0.0 reduce-scatter.3.cloned.1.call-start
  147.0 0.0 copy-done.6
  147.0 4.4 %all-to-all-done = bf16[8,1,128]{2,1,0:T(2,128)(2,1)S(1)} async-done(((bf16[8,1,128]{2,1,0:T(2,128)(2,1)}), bf16[8,1,128]{2,1,0:T(2,128)(2,1)S(1)}, u32[]{:S(2)}, u32[]{:S(2)}) %all-to-all-start) | async-done | bytes 2080 | tf_op jit(solution)/shard_map/all_to_all | solution.py:62
  151.5 0.0 copy-done.5
  151.5 0.6 select_reduce_fusion.1
  152.1 8.3 %all_gather.9 = f32[1024,8]{0,1:T(8,128)S(1)} all-gather(f32[128,8]{0,1:T(8,128)S(1)} %get-tuple-element.6), channel_id=1, replica_groups=mesh['expert'=8,'dp'=4] {'expert'}, dimensions={0}, use_global_device_ids=true | all-gather | bytes 36864 | tf_op jit(solution)/shard_map/all_gather | solution.py:31
  160.4 0.1 select_reduce_fusion
  160.4 0.0 copy-done.4
  160.4 1.9 multiply_convert_fusion
  162.4 0.0 copy-start.2
  162.4 8.1 %fusion.1 = f32[1024,4096]{1,0:T(8,128)} fusion(bf16[1024,192]{0,1:T(8,128)(2,1)S(1)} %get-tuple-element.10, bf16[1,192,4096]{2,1,0:T(8,128)(2,1)S(1)} %copy-done), kind=kOutput, calls=%fused_computation.6 | convolution fusion | flops 1610612736 | bytes 18743296 | tf_op jit(solution)/shard_map/dot_general | solution.py:56
  170.5 0.0 copy-done.2
  170.5 11.4 %add_convert_fusion = bf16[1024,4096]{1,0:T(8,128)(2,1)} fusion(f32[1024,4096]{1,0:T(8,128)} %fusion.1, bf16[1024,192]{0,1:T(8,128)(2,1)S(1)} %get-tuple-element.11, bf16[1,192,4096]{2,1,0:T(8,128)(2,1)S(1)} %copy-done.2), kind=kOutput, calls=%fused_computation | convolution fusion | flops 1619001344 | bytes 27131904 | tf_op jit(solution)/shard_map/dot_general | solution.py:57
  181.9 0.0 reduce-scatter.3.cloned.1.call-update
  181.9 0.0 copy-start.8
  181.9 0.0 reduce-scatter.5.cloned.1.call-start
  182.0 1.1 pad_maximum_fusion
  183.1 1.5 collective-permute-start
  184.5 0.0 copy-done.8
  184.5 0.6 fusion.13
  185.8 31.4 %collective-permute-done = bf16[1024,576]{0,1:T(8,128)(2,1)} collective-permute-done((bf16[1024,576]{0,1:T(8,128)(2,1)}, bf16[1024,576]{0,1:T(8,128)(2,1)}, u32[]{:S(2)}, u32[]{:S(2)}) %collective-permute-start) | collective-permute-done | bytes 1179680 | tf_op jit(solution)/shard_map/ppermute | solution.py:9
  217.2 2.8 broadcast_select_fusion
  220.0 32.8 %reduce-scatter.3.cloned.1.call-done = bf16[128,4096]{1,0:T(8,128)(2,1)} async-done(((bf16[1024,4096]{1,0:T(8,128)(2,1)}), bf16[128,4096]{1,0:T(8,128)(2,1)}) %reduce-scatter.3.cloned.1.call-update) | async-done | bytes 1048592 | tf_op jit(solution)/shard_map/reduce_scatter | solution.py:58
  252.7 0.0 reduce-scatter.5.cloned.1.call-update
  252.8 0.0 copy-start.3
  252.8 6.5 %fusion = bf16[1,192,4096]{2,1,0:T(8,128)(2,1)} fusion(bf16[1024,4096]{1,0:T(8,128)(2,1)} %all-gather.3.cloned.1.call-done, bf16[1024,576]{0,1:T(8,128)(2,1)} %broadcast_select_fusion), kind=kOutput, calls=%fused_computation.3 | convolution fusion | flops 1611399168 | bytes 10354688 | tf_op jit(solution)/shard_map/dot_general | solution.py:69
  259.3 0.0 copy-done.3
  259.3 7.3 %convolution_convert_fusion = bf16[384,4096]{1,0:T(8,128)(2,1)S(1)} fusion(bf16[1024,4096]{1,0:T(8,128)(2,1)} %all-gather.5.cloned.1.call-done, bf16[1024,576]{0,1:T(8,128)(2,1)S(1)} %copy-done.3), kind=kOutput, calls=%fused_computation.1 | convolution fusion | flops 3222798336 | bytes 12320768 | tf_op jit(solution)/shard_map/dot_general | solution.py:68
  266.6 2.0 slice_bitcast_fusion
  268.6 14.1 %reduce-scatter.5.cloned.1.call-done = bf16[128,1024]{1,0:T(8,128)(2,1)} async-done(((bf16[128,4096]{1,0:T(8,128)(2,1)}), bf16[128,1024]{1,0:T(8,128)(2,1)}) %reduce-scatter.5.cloned.1.call-update) | async-done | bytes 262160 | tf_op jit(solution)/shard_map/reduce_scatter | solution.py:59
  (3 shorter events, 0.0 us)
Async XLA Ops:
  7.2 59.9 %copy-start = (bf16[1,192,4096]{2,1,0:T(8,128)(2,1)S(1)}, bf16[1,192,4096]{2,1,0:T(8,128)(2,1)}, u32[]{:S(2)}) copy-start(bf16[1,192,4096]{2,1,0:T(8,128)(2,1)} %param.10) | copy-start | bytes 4718596
  7.2 59.8 %all-gather.5.cloned.1.call-start = ((), (), s32[]{:S(2)}) async-start(), calls=%async_computation.4 | async-start | bytes 9437184 | tf_op jit(solution)/shard_map/all_gather | solution.py:32
  7.9 115.4 %all-gather.3.cloned.1.call-start = ((), (), s32[]{:S(2)}) async-start(), calls=%async_computation.3 | async-start | bytes 9437184 | tf_op jit(solution)/shard_map/all_gather | solution.py:33
  8.7 65.7 %copy-start.1 = (bf16[1,192,4096]{2,1,0:T(8,128)(2,1)S(1)}, bf16[1,192,4096]{2,1,0:T(8,128)(2,1)}, u32[]{:S(2)}) copy-start(bf16[1,192,4096]{2,1,0:T(8,128)(2,1)} %param.11) | copy-start | bytes 4718596
  67.0 7.3 %copy-start.7 = (bf16[1024,4096]{1,0:T(8,128)(2,1)S(1)}, bf16[1024,4096]{1,0:T(8,128)(2,1)}, u32[]{:S(2)}) copy-start(bf16[1024,4096]{1,0:T(8,128)(2,1)} %all-gather.5.cloned.1.call-done) | copy-start | bytes 25165828
  78.1 68.9 %copy-start.6 = (bf16[128,4]{0,1:T(4,128)(2,1)S(1)}, bf16[128,4]{0,1:T(4,128)(2,1)}, u32[]{:S(2)}) copy-start(bf16[128,4]{0,1:T(4,128)(2,1)} %param.14) | copy-start | bytes 3076
  78.1 73.3 %copy-start.5 = (s32[128,4]{0,1:T(4,128)S(1)}, s32[128,4]{0,1:T(4,128)}, u32[]{:S(2)}) copy-start(s32[128,4]{0,1:T(4,128)} %param.13) | copy-start | bytes 6148
  78.2 82.3 %copy-start.4 = (f32[1024,192]{0,1:T(8,128)S(1)}, f32[1024,192]{0,1:T(8,128)}, u32[]{:S(2)}) copy-start(f32[1024,192]{0,1:T(8,128)} %fusion.3) | copy-start | bytes 2359300
  143.6 7.8 %all-to-all-start = ((bf16[8,1,128]{2,1,0:T(2,128)(2,1)}), bf16[8,1,128]{2,1,0:T(2,128)(2,1)S(1)}, u32[]{:S(2)}, u32[]{:S(2)}) async-start(bf16[8,1,128]{2,1,0:T(2,128)(2,1)} %copy.22), calls=%async_computation.2 | async-start | bytes 8192 | tf_op jit(solution)/shard_map/all_to_all | solution.py:62
  147.0 105.8 %reduce-scatter.3.cloned.1.call-start = ((), (), s32[]{:S(2)}) async-start(), calls=%async_computation.5 | async-start | bytes 9437184 | tf_op jit(solution)/shard_map/reduce_scatter | solution.py:58
  162.4 8.1 %copy-start.2 = (bf16[1,192,4096]{2,1,0:T(8,128)(2,1)S(1)}, bf16[1,192,4096]{2,1,0:T(8,128)(2,1)}, u32[]{:S(2)}) copy-start(bf16[1,192,4096]{2,1,0:T(8,128)(2,1)} %param.11) | copy-start | bytes 4718596
  181.9 2.6 copy-start.8
  181.9 100.8 %reduce-scatter.5.cloned.1.call-start = ((), (), s32[]{:S(2)}) async-start(), calls=%async_computation.6 | async-start | bytes 1310720 | tf_op jit(solution)/shard_map/reduce_scatter | solution.py:59
  183.1 34.1 %collective-permute-start = (bf16[1024,576]{0,1:T(8,128)(2,1)}, bf16[1024,576]{0,1:T(8,128)(2,1)}, u32[]{:S(2)}, u32[]{:S(2)}) collective-permute-start(bf16[1024,576]{0,1:T(8,128)(2,1)} %pad_maximum_fusion), channel_id=1, source_target_pairs={{0,16},{4,20},{8,24},{12,28},{16,0},{20,4},{24,8},{28,12},{1,17},{... | collective-permute-start | bytes 3538952 | tf_op jit(solution)/shard_map/ppermute | solution.py:9
  252.8 6.6 %copy-start.3 = (bf16[1024,576]{0,1:T(8,128)(2,1)S(1)}, bf16[1024,576]{0,1:T(8,128)(2,1)}, u32[]{:S(2)}) copy-start(bf16[1024,576]{0,1:T(8,128)(2,1)} %broadcast_select_fusion) | copy-start | bytes 3538948
Sparse Core Ops, SparseCore 0:
  9.9 57.0 all-gather.4
  68.9 54.3 all-gather.2
  182.0 70.6 reduce-scatter.2
  255.6 27.1 reduce-scatter.4

commit v2 on v0

--- a/solution.py
+++ b/solution.py
@@ -1,7 +1,16 @@
+import functools
+
 import jax
 import jax.numpy as jnp
 from jax import lax
+from jax.experimental import pallas as pl
+from jax.experimental.pallas import tpu as pltpu
 from jax.sharding import PartitionSpec as P
+
+
+CONTRACT_LAST = (((1,), (1,)), ((), ()))
+CONTRACT_ROWS = (((0,), (0,)), ((), ()))
+VMEM = 56 * 1024 * 1024
 
 
 def from_behind(value, axis, by):
@@ -9,12 +18,222 @@
     return lax.ppermute(value, axis, [(i, (i + by) % devices) for i in range(devices)])
 
 
+def swap(value, axis, by):
+    return lax.ppermute(value, axis, [(i, i ^ by) for i in range(lax.axis_size(axis))])
+
+
 def pair_lookup(experts, pair_flags, half_axis):
     match = experts[:, None] % half_axis == jnp.arange(half_axis, dtype=jnp.int32)[None, :]
     return jnp.sum(jnp.where(match, pair_flags[None, :], 0), axis=1)
 
 
-def shards(tokens, cotangent, gate_weight, up_weight, down_weight, expert_ids, gates, swap_flags):
+def activations_kernel(blocks, parts, where_ref, gates_ref, *refs):
+    count = len(blocks)
+    x_refs, dy_refs = refs[:count], refs[count : 2 * count]
+    gate_ref, up_ref, down_ref = refs[2 * count : 2 * count + 3]
+    acts_ref, score_ref, keep_ref, give_ref = refs[2 * count + 3 : 2 * count + 7]
+    x_all, dy_all, in_all, down_all, sems = refs[2 * count + 7 :]
+    rows, width = x_refs[0].shape
+    units = gate_ref.shape[0]
+    chunk = width // parts
+    copies = []
+    for part in range(parts):
+        columns = pl.ds(part * chunk, chunk)
+        moves = [(gate_ref, in_all, 0, units), (up_ref, in_all, units, units), (down_ref, down_all, 0, units)]
+        moves += [(ref, x_all, i * rows, rows) for i, ref in enumerate(x_refs)]
+        moves += [(ref, dy_all, i * rows, rows) for i, ref in enumerate(dy_refs)]
+        copies.append(
+            [
+                pltpu.make_async_copy(
+                    ref.at[:, columns], target.at[pl.ds(start, size), columns], sems.at[part, i]
+                )
+                for i, (ref, target, start, size) in enumerate(moves)
+            ]
+        )
+        for copy in copies[-1]:
+            copy.start()
+    me, group = where_ref[0], where_ref[1]
+    pre, back = None, None
+    for part in range(parts):
+        for copy in copies[part]:
+            copy.wait()
+        columns = pl.ds(part * chunk, chunk)
+        one = lax.dot_general(
+            in_all[:, columns], x_all[:, columns], CONTRACT_LAST, preferred_element_type=jnp.float32
+        )
+        two = lax.dot_general(
+            down_all[:, columns], dy_all[:, columns], CONTRACT_LAST, preferred_element_type=jnp.float32
+        )
+        pre = one if pre is None else pre + one
+        back = two if back is None else back + two
+    pre_gate, pre_up = pre[:units], pre[units:]
+    g = jnp.concatenate([gates_ref[pl.ds(me ^ block, 1), :] for block in blocks], axis=1)
+    sigma = jax.nn.sigmoid(pre_gate)
+    active = pre_gate * sigma
+    hidden = active * pre_up
+    score_ref[...] = jnp.sum(hidden * back, axis=0, keepdims=True)
+    grad_hidden = g * back
+    slope = sigma * (1.0 + pre_gate * (1.0 - sigma))
+    acts_ref[pl.ds(0, units), :] = (grad_hidden * pre_up * slope).astype(jnp.bfloat16)
+    acts_ref[pl.ds(units, units), :] = (grad_hidden * active).astype(jnp.bfloat16)
+    acts_ref[pl.ds(2 * units, units), :] = (g * hidden).astype(jnp.bfloat16)
+    both = acts_ref[pl.ds(0, 2 * units), :]
+    for part in range(parts):
+        columns = pl.ds(pl.multiple_of((group ^ part) * chunk, chunk), chunk)
+        share = lax.dot_general(both, in_all[:, columns], CONTRACT_ROWS, preferred_element_type=jnp.float32)
+        share = share.astype(jnp.bfloat16)
+        for pair in range(count // 2):
+            keep_ref[part, pl.ds(pair * rows, rows), :] = share[2 * pair * rows : (2 * pair + 1) * rows]
+            give_ref[part, pl.ds(pair * rows, rows), :] = share[(2 * pair + 1) * rows : (2 * pair + 2) * rows]
+
+
+def activations(blocks, parts, where, gates, x_blocks, dy_blocks, w_gate, w_up, w_down):
+    count = len(blocks)
+    rows, width = x_blocks[0].shape
+    units = w_gate.shape[0]
+    bf16 = jnp.bfloat16
+    share = jax.ShapeDtypeStruct((parts, count // 2 * rows, width // parts), bf16)
+    return pl.pallas_call(
+        functools.partial(activations_kernel, blocks, parts),
+        out_shape=(
+            jax.ShapeDtypeStruct((3 * units, count * rows), bf16),
+            jax.ShapeDtypeStruct((1, count * rows), jnp.float32),
+            share,
+            share,
+        ),
+        in_specs=[pl.BlockSpec(memory_space=pltpu.SMEM), pl.BlockSpec(memory_space=pltpu.VMEM)]
+        + [pl.BlockSpec(memory_space=pl.ANY)] * (2 * count + 3),
+        out_specs=[pl.BlockSpec(memory_space=pltpu.VMEM)] * 4,
+        scratch_shapes=[
+            pltpu.VMEM((count * rows, width), bf16),
+            pltpu.VMEM((count * rows, width), bf16),
+            pltpu.VMEM((2 * units, width), bf16),
+            pltpu.VMEM((units, width), bf16),
+            pltpu.SemaphoreType.DMA((parts, 2 * count + 3)),
+        ],
+        compiler_params=pltpu.CompilerParams(vmem_limit_bytes=VMEM),
+        name="activations",
+    )(where, gates, *x_blocks, *dy_blocks, w_gate, w_up, w_down)
+
+
+def weight_grads_kernel(order, parts, flag_ref, *refs):
+    count = len(order)
+    x_refs, dy_refs = refs[:count], refs[count : 2 * count]
+    own_ref, other_ref = refs[2 * count : 2 * count + 2]
+    outs = refs[2 * count + 2 : 2 * count + 5]
+    x_all, dy_all, acts, sems = refs[2 * count + 5 :]
+    rows, width = x_refs[0].shape
+    units = outs[0].shape[1]
+    chunk = width // parts
+    copies = []
+    for part in range(parts):
+        columns = pl.ds(part * chunk, chunk)
+        moves = [(ref, x_all, i * rows) for i, ref in enumerate(x_refs)]
+        moves += [(ref, dy_all, i * rows) for i, ref in enumerate(dy_refs)]
+        copies.append(
+            [
+                pltpu.make_async_copy(ref.at[:, columns], target.at[pl.ds(start, rows), columns], sems.at[part, i])
+                for i, (ref, target, start) in enumerate(moves)
+            ]
+        )
+        for copy in copies[-1]:
+            copy.start()
+    half = count // 2
+    for place, block in enumerate(order):
+        theirs = order.index(block ^ half)
+        arrived = other_ref[:, pl.ds(theirs * rows, rows)]
+        stay = own_ref[:, pl.ds(place * rows, rows)]
+        acts[:, pl.ds(place * rows, rows)] = jnp.where(flag_ref[0] == 1, arrived, stay)
+    for part in range(parts):
+        for copy in copies[part]:
+            copy.wait()
+        columns = pl.ds(part * chunk, chunk)
+        both = jnp.dot(acts[pl.ds(0, 2 * units), :], x_all[:, columns], preferred_element_type=jnp.float32)
+        down = jnp.dot(acts[pl.ds(2 * units, units), :], dy_all[:, columns], preferred_element_type=jnp.float32)
+        outs[0][0, :, columns] = both[:units].astype(jnp.bfloat16)
+        outs[1][0, :, columns] = both[units:].astype(jnp.bfloat16)
+        outs[2][0, :, columns] = down.astype(jnp.bfloat16)
+
+
+def weight_grads(order, flag, x_blocks, dy_blocks, own, other):
+    count, parts = len(order), 8
+    rows, width = x_blocks[0].shape
+    units = own.shape[0] // 3
+    bf16 = jnp.bfloat16
+    return pl.pallas_call(
+        functools.partial(weight_grads_kernel, order, parts),
+        out_shape=(jax.ShapeDtypeStruct((1, units, width), bf16),) * 3,
+        in_specs=[pl.BlockSpec(memory_space=pltpu.SMEM)]
+        + [pl.BlockSpec(memory_space=pl.ANY)] * (2 * count)
+        + [pl.BlockSpec(memory_space=pltpu.VMEM)] * 2,
+        out_specs=[pl.BlockSpec(memory_space=pltpu.VMEM)] * 3,
+        scratch_shapes=[
+            pltpu.VMEM((count * rows, width), bf16),
+            pltpu.VMEM((count * rows, width), bf16),
+            pltpu.VMEM((3 * units, count * rows), bf16),
+            pltpu.SemaphoreType.DMA((parts, 2 * count)),
+        ],
+        compiler_params=pltpu.CompilerParams(vmem_limit_bytes=VMEM),
+        name="weight_grads",
+    )(flag, *x_blocks, *dy_blocks, own, other)
+
+
+CORE, ACROSS_X, ACROSS_Y = 1, 2, 4
+
+
+def whole_shards(tokens, cotangent, gate_weight, up_weight, down_weight, expert_ids, gates, swap_flags):
+    expert_count = lax.axis_size("expert")
+    half_axis = expert_count // 2
+    me, group = lax.axis_index("expert"), lax.axis_index("dp")
+    row_count = tokens.shape[0]
+    parts = lax.axis_size("dp")
+    f32, bf16 = jnp.float32, jnp.bfloat16
+    own_flag = pair_lookup(jnp.reshape(me, (1,)), swap_flags, half_axis)
+    where = jnp.stack([me, group]).astype(jnp.int32)
+
+    x, dy = {0: tokens}, {0: cotangent}
+    x[2], dy[4] = swap(tokens, "expert", ACROSS_X), swap(cotangent, "expert", ACROSS_Y)
+    x[1], dy[1] = swap(tokens, "expert", CORE), swap(cotangent, "expert", CORE)
+    x[4], dy[2] = swap(tokens, "expert", ACROSS_Y), swap(cotangent, "expert", ACROSS_X)
+    x[6], dy[6] = swap(x[2], "expert", ACROSS_Y), swap(dy[4], "expert", ACROSS_X)
+    for block in (2, 4, 6):
+        x[block + 1], dy[block + 1] = swap(x[block], "expert", CORE), swap(dy[block], "expert", CORE)
+
+    named = expert_ids[:, :, None] == jnp.arange(expert_count, dtype=jnp.int32)[None, None, :]
+    table = jnp.sum(jnp.where(named, gates[:, :, None].astype(f32), 0), axis=1)
+    gate_rows = lax.all_to_all(table.T, "expert", split_axis=0, concat_axis=0, tiled=True)
+
+    weights = (gate_weight[0], up_weight[0], down_weight[0])
+    groups = ((0, 1), (2, 3, 4, 5), (6, 7))
+    order = sum(groups, ())
+    acts, scores, totals = [], [], {}
+    for blocks in groups:
+        act, score, keep, give = activations(
+            blocks, parts, where, gate_rows, [x[b] for b in blocks], [dy[b] for b in blocks], *weights
+        )
+        acts.append(act)
+        scores.append(score)
+        both = keep + swap(give, "expert", CORE)
+        total = both[0].astype(f32)
+        for part in range(1, parts):
+            total = total + swap(both[part], "dp", part).astype(f32)
+        for pair in range(len(blocks) // 2):
+            totals[blocks[2 * pair]] = total[pair * row_count : (pair + 1) * row_count]
+    input_grad = totals[0]
+    for block in (ACROSS_X, ACROSS_Y, ACROSS_X | ACROSS_Y):
+        input_grad = input_grad + swap(totals[block].astype(bf16), "expert", block).astype(f32)
+
+    acts = jnp.concatenate(acts, axis=1)
+    grads = weight_grads(order, own_flag, [x[b] for b in order], [dy[b] for b in order], acts, swap(acts, "expert", half_axis))
+
+    score_rows = lax.psum(jnp.concatenate(scores, axis=1).reshape(expert_count, row_count), "dp").astype(bf16)
+    score_rows = jnp.take(score_rows, jnp.arange(expert_count, dtype=jnp.int32) ^ me, axis=0)
+    score_rows = lax.all_to_all(score_rows, "expert", split_axis=0, concat_axis=0, tiled=True)
+    gate_grad = jnp.sum(jnp.where(named, score_rows.T[:, None, :].astype(f32), 0), axis=2)
+    return (input_grad.astype(bf16), gate_grad.astype(bf16), *grads)
+
+
+def packed_shards(tokens, cotangent, gate_weight, up_weight, down_weight, expert_ids, gates, swap_flags):
     expert_count = lax.axis_size("expert")
     half_axis = expert_count // 2
     my_slot = lax.axis_index("expert")
@@ -97,6 +316,12 @@
     return (input_grad, gate_grad, gradients[0], gradients[1], gradients[2])
 
 
+def chosen(tokens, cotangent, gate_weight, up_weight, down_weight, expert_ids, gates, swap_flags):
+    capacity = tokens.shape[0] * expert_ids.shape[1] * 5 // (4 * lax.axis_size("expert"))
+    body = whole_shards if 2 * capacity >= tokens.shape[0] else packed_shards
+    return body(tokens, cotangent, gate_weight, up_weight, down_weight, expert_ids, gates, swap_flags)
+
+
 def solution(mesh):
     placed = (
         P("expert", None),
@@ -109,7 +334,7 @@
         P(),
     )
     return jax.shard_map(
-        shards,
+        chosen,
         mesh=mesh,
         in_specs=placed,
         out_specs=(

time: 504 us -> 241 us (0.48)
  waiting for transfers between devices: 309 us -> 99.3 us
  blocking collectives: 77.1 us -> 27.1 us
  Pallas kernels: 0 us -> 41.2 us
  matrix products: 36.4 us -> 0 us
  starting transfers between devices: 21.1 us -> 46.3 us
  local copies, waits for them, and re-layouts: 28.2 us -> 10.3 us
  between operations: 14.9 us -> 0.98 us
  other arithmetic: 16.6 us -> 11 us
    reduce_scatter x1 -> x0, waiting for transfers between devices: 161 us -> none  [shards(): lax.psum_scatter(input_part, 'dp', scatter_dimension=1, tiled=True)]
    all_to_all x1 -> x0, blocking collectives: 64.9 us -> none  [shards(): lax.all_to_all(x_buffer, 'expert', split_axis=0, concat_axis=0, tiled=True)]
    ppermute x3 -> x30, waiting for transfers between devices: 147 us -> 91.5 us  [swap(): lax.ppermute(value, axis, [(i, i ^ by) for i in range(lax.axis_size(axis))])]
    pallas_call x0 -> x4, Pallas kernels: none -> 41.2 us  [the longest x3 27.9 us: activations(): pl.pallas_call(functools.partial(activations_kernel, blocks, parts), out_...]
    dot_general x8 -> x0, matrix products: 36.4 us -> none  [the longest x1 7.07 us: shards(): input_part = jnp.dot(grad_gate, w_gate, preferred_element_type=jnp.float32)]
    ppermute x3 -> x30, starting transfers between devices: 3.72 us -> 39.6 us  [swap(): lax.ppermute(value, axis, [(i, i ^ by) for i in range(lax.axis_size(axis))])]
    gather x5 -> x1, local copies, waits for them, and re-layouts: 20.5 us -> 0.56 us  [whole_shards(): jnp.take(score_rows, jnp.arange(expert_count, dtype=jnp.int32) ^ me, axis=0)]
    psum x1, blocking collectives: 12.3 us -> 27.1 us  [whole_shards(): lax.psum(jnp.concatenate(scores, axis=1).reshape(expert_count, row_count)...]
  transfers between devices with their start and end apart: 8 -> 32, of which waited for: 5 -> 8; matrix products, arithmetic and copies ran while one was open for 10% -> 7% of each run, Pallas kernels for 0% -> 17%
where the time goes in v2:
time: 241 us; the launch traced here: 236 us
  waiting for transfers between devices  99.3 us (41%)
  starting transfers between devices  46.3 us (19%)
  Pallas kernels  41.2 us (17%)
  blocking collectives  27.1 us (11%)
  other arithmetic  11 us (5%)
  local copies, waits for them, and re-layouts  10.3 us (4%)
    ppermute x30, waiting for transfers between devices, swap(): lax.ppermute(value, axis, [(i, i ^ by) for i in range(lax.axis_size(axis))])  91.5 us
    ppermute x30, starting transfers between devices, swap(): lax.ppermute(value, axis, [(i, i ^ by) for i in range(lax.axis_size(axis))])  39.6 us
    pallas_call x3, Pallas kernels, activations(): pl.pallas_call(functools.partial(activations_kernel, blocks, parts), out_...  27.9 us
    psum x1, blocking collectives, whole_shards(): lax.psum(jnp.concatenate(scores, axis=1).reshape(expert_count, row_count)...  27.1 us
    pallas_call x1, Pallas kernels, weight_grads(): pl.pallas_call(functools.partial(weight_grads_kernel, order, parts), out_...  13.3 us
    unnamed x52, local copies, waits for them, and re-layouts  5.38 us
  transfers between devices with their start and end apart: 32, of which 8 were waited for; matrix products, arithmetic and copies ran while one was open for 7% of the time, Pallas kernels for 17%

profile of v2, /device:TPU:0, one launch (start us, length us, event | category | flops | bytes accessed | tf_op | source)
XLA Modules:
  0.0 236.1 jit_solution(16897171427652627380)
XLA Ops:
  0.6 3.0 %collective-permute-start.6 = (bf16[128,4096]{1,0:T(8,128)(2,1)}, bf16[128,4096]{1,0:T(8,128)(2,1)S(1)}, u32[]{:S(2)}, u32[]{:S(2)}) collective-permute-start(bf16[128,4096]{1,0:T(8,128)(2,1)} %refs_0_.3), channel_id=1, source_target_pairs={{0,8},{4,12},{8,0},{12,4},{16,24},{20,28},{24,16},{28,20},{1,9},{5... | collective-permute-start | bytes 3145736 | tf_op jit(solution)/shard_map/ppermute | solution.py:22
  3.6 1.5 collective-permute-start.12
  5.2 0.5 collective-permute-start.8
  5.7 0.1 collective-permute-start.10
  5.7 22.1 %collective-permute-done.6.refs_0_.refs_2_ = bf16[128,4096]{1,0:T(8,128)(2,1)S(1)} collective-permute-done((bf16[128,4096]{1,0:T(8,128)(2,1)}, bf16[128,4096]{1,0:T(8,128)(2,1)S(1)}, u32[]{:S(2)}, u32[]{:S(2)}) %collective-permute-start.6) | collective-permute-done | bytes 1048608 | tf_op jit(solution)/shard_map/ppermute | solution.py:22
  27.8 2.1 collective-permute-start.20
  29.9 1.5 collective-permute-start.22
  31.4 21.0 %collective-permute-done.8.refs_2_.refs_4_ = bf16[128,4096]{1,0:T(8,128)(2,1)S(1)} collective-permute-done((bf16[128,4096]{1,0:T(8,128)(2,1)}, bf16[128,4096]{1,0:T(8,128)(2,1)S(1)}, u32[]{:S(2)}, u32[]{:S(2)}) %collective-permute-start.8) | collective-permute-done | bytes 1048608 | tf_op jit(solution)/shard_map/ppermute | solution.py:22
  52.4 0.5 collective-permute-start.11
  52.9 20.6 %collective-permute-done.20.refs_0_.refs_6_ = bf16[128,4096]{1,0:T(8,128)(2,1)} collective-permute-done((bf16[128,4096]{1,0:T(8,128)(2,1)S(1)}, bf16[128,4096]{1,0:T(8,128)(2,1)}, u32[]{:S(2)}, u32[]{:S(2)}) %collective-permute-start.20) | collective-permute-done | bytes 1048608 | tf_op jit(solution)/shard_map/ppermute | solution.py:22
  73.5 0.5 collective-permute-start
  74.0 0.1 collective-permute-start.1
  74.1 0.5 collective-permute-start.21
  74.6 0.4 copy-done.4
  75.0 0.4 copy-done.5
  75.4 1.0 copy-done.6
  76.4 0.2 collective-permute-start.23
  76.5 0.7 convert_element_type.86
  77.2 1.3 select_reduce_fusion.1
  78.5 3.3 %all-to-all-start = ((f32[8,1,128]{2,1,0:T(1,128)}), f32[8,1,128]{2,1,0:T(1,128)S(1)}, u32[]{:S(2)}, u32[]{:S(2)}) async-start(f32[8,1,128]{2,1,0:T(1,128)} %bitcast.4), calls=%async_computation | async-start | bytes 8192 | tf_op jit(solution)/shard_map/all_to_all | solution.py:204
  81.8 0.6 pad_add_fusion.where_ref
  82.4 3.9 %all-to-all-done = f32[8,1,128]{2,1,0:T(1,128)S(1)} async-done(((f32[8,1,128]{2,1,0:T(1,128)}), f32[8,1,128]{2,1,0:T(1,128)S(1)}, u32[]{:S(2)}, u32[]{:S(2)}) %all-to-all-start) | async-done | bytes 4128 | tf_op jit(solution)/shard_map/all_to_all | solution.py:204
  86.4 0.6 copy-done.19
  86.9 11.8 %activations.4 = (bf16[576,512]{1,0:T(8,128)(2,1)}, f32[1,512]{1,0:T(1,128)}, bf16[4,256,1024]{2,1,0:T(8,128)(2,1)}, bf16[4,256,1024]{2,1,0:T(8,128)(2,1)}) custom-call(s32[2]{0:T(128)} %pad_add_fusion.where_ref, f32[8,128]{1,0:T(8,128)} %bitcast.64, bf16[128,4096]{1,0:T(8,128)(2,1)} %copy-done, bf16[128,4096]{1,0:T(8,128)(2,1)} %copy-done.4, ...), custom_call_target="tpu_custom_call" | custom-call | tf_op jit(solution)/shard_map/activations/pallas_call | solution.py:96
  98.9 8.0 %activations.3 = (bf16[576,256]{1,0:T(8,128)(2,1)}, f32[1,256]{1,0:T(1,128)}, bf16[4,128,1024]{2,1,0:T(8,128)(2,1)}, bf16[4,128,1024]{2,1,0:T(8,128)(2,1)}) custom-call(s32[2]{0:T(128)} %pad_add_fusion.where_ref, f32[8,128]{1,0:T(8,128)} %bitcast.65, bf16[128,4096]{1,0:T(8,128)(2,1)} %refs_0_.3, bf16[128,4096]{1,0:T(8,128)(2,1)} %collective-permute-done.refs_1_, ...), custom_call_target="tpu_custom_call" | custom-call | tf_op jit(solution)/shard_map/activations/pallas_call | solution.py:96
  106.9 0.5 collective-permute-start.2
  107.5 8.0 %activations.5 = (bf16[576,256]{1,0:T(8,128)(2,1)}, f32[1,256]{1,0:T(1,128)}, bf16[4,128,1024]{2,1,0:T(8,128)(2,1)}, bf16[4,128,1024]{2,1,0:T(8,128)(2,1)}) custom-call(s32[2]{0:T(128)} %pad_add_fusion.where_ref, f32[8,128]{1,0:T(8,128)} %bitcast.66, bf16[128,4096]{1,0:T(8,128)(2,1)} %collective-permute-done.20.refs_0_.refs_6_, ...), custom_call_target="tpu_custom_call" | custom-call | tf_op jit(solution)/shard_map/activations/pallas_call | solution.py:96
  115.5 0.2 collective-permute-start.24
  115.7 0.8 constant_dynamic-update-slice_fusion.2
  116.5 0.4 add.68
  116.9 0.6 copy-done.11
  117.6 0.9 constant_dynamic-update-slice_fusion.1
  118.5 0.8 constant_dynamic-update-slice_fusion.refs_16_
  119.3 0.6 collective-permute-start.29
  119.9 0.4 add.78
  120.3 0.8 slice_bitcast_fusion.6
  121.0 3.6 %collective-permute-start.27 = (bf16[128,1024]{1,0:T(8,128)(2,1)S(1)}, bf16[128,1024]{1,0:T(8,128)(2,1)S(1)}, u32[]{:S(2)}, u32[]{:S(2)}) collective-permute-start(bf16[128,1024]{1,0:T(8,128)(2,1)S(1)} %get-tuple-element.42), channel_id=1, source_target_pairs={{0,3},{1,2},{2,1},{3,0},{4,7},{5,6},{6,5},{7,4},{8,11},{9,10},{10,... | collective-permute-start | bytes 786440 | tf_op jit(solution)/shard_map/ppermute | solution.py:22
  124.6 0.8 collective-permute-start.25
  125.4 1.1 add.72
  126.6 1.2 slice_bitcast_fusion.2
  127.8 3.6 %collective-permute-start.17 = (bf16[256,1024]{1,0:T(8,128)(2,1)}, bf16[256,1024]{1,0:T(8,128)(2,1)}, u32[]{:S(2)}, u32[]{:S(2)}) collective-permute-start(bf16[256,1024]{1,0:T(8,128)(2,1)} %get-tuple-element.36), channel_id=1, source_target_pairs={{0,3},{1,2},{2,1},{3,0},{4,7},{5,6},{6,5},{7,4},{8,11},{9,10},{10,... | collective-permute-start | bytes 1572872 | tf_op jit(solution)/shard_map/ppermute | solution.py:22
  131.3 0.8 collective-permute-done.27
  132.1 11.9 %collective-permute-start.16 = (bf16[256,1024]{1,0:T(8,128)(2,1)}, bf16[256,1024]{1,0:T(8,128)(2,1)}, u32[]{:S(2)}, u32[]{:S(2)}) collective-permute-start(bf16[256,1024]{1,0:T(8,128)(2,1)} %get-tuple-element.37), channel_id=1, source_target_pairs={{0,2},{1,3},{2,0},{3,1},{4,6},{5,7},{6,4},{7,5},{8,10},{9,11},{10,... | collective-permute-start | bytes 1572872 | tf_op jit(solution)/shard_map/ppermute | solution.py:22
  144.0 26.5 %collective-permute-done.26 = bf16[128,1024]{1,0:T(8,128)(2,1)S(1)} collective-permute-done((bf16[128,1024]{1,0:T(8,128)(2,1)S(1)}, bf16[128,1024]{1,0:T(8,128)(2,1)S(1)}, u32[]{:S(2)}, u32[]{:S(2)}) %collective-permute-start.26) | collective-permute-done | bytes 262176 | tf_op jit(solution)/shard_map/ppermute | solution.py:22
  170.5 1.0 slice_bitcast_fusion.10
  171.5 27.1 %psum.7 = bf16[8,128]{1,0:T(8,128)(2,1)S(1)} all-reduce(f32[8,128]{1,0:T(8,128)S(1)} %bitcast.68), channel_id=1, replica_groups=mesh['expert'=8,'dp'=4] {'dp'}, use_global_device_ids=true, to_apply=%region_1.2 | all-reduce | flops 1024 | bytes 6144 | tf_op jit(solution)/shard_map/psum | solution.py:229
  198.6 0.6 gather_fusion
  199.2 0.7 copy-done.16
  199.9 1.3 fusion.5
  201.2 1.0 collective-permute-start.4
  202.2 3.5 %collective-permute-start.3 = (bf16[128,1024]{1,0:T(8,128)(2,1)}, bf16[128,1024]{1,0:T(8,128)(2,1)}, u32[]{:S(2)}, u32[]{:S(2)}) collective-permute-start(bf16[128,1024]{1,0:T(8,128)(2,1)} %get-tuple-element.38), channel_id=1, source_target_pairs={{0,1},{1,0},{2,3},{3,2},{4,5},{5,4},{6,7},{7,6},{8,9},{9,8},{10,11... | collective-permute-start | bytes 786440 | tf_op jit(solution)/shard_map/ppermute | solution.py:22
  205.7 1.5 collective-permute-start.28
  207.1 1.7 fusion.2
  208.9 0.5 collective-permute-done.5
  209.4 1.5 collective-permute-start.19
  210.9 0.6 collective-permute-start.18
  211.4 0.1 bitcast_select_fusion
  211.5 0.6 copy.21
  212.1 3.3 %all-to-all-start.1 = ((bf16[8,1,128]{2,1,0:T(2,128)(2,1)}), bf16[8,1,128]{2,1,0:T(2,128)(2,1)S(1)}, u32[]{:S(2)}, u32[]{:S(2)}) async-start(bf16[8,1,128]{2,1,0:T(2,128)(2,1)} %copy.21), calls=%async_computation.1 | async-start | bytes 8192 | tf_op jit(solution)/shard_map/all_to_all | solution.py:231
  215.4 0.6 fusion.12
  216.1 3.9 %all-to-all-done.1 = bf16[8,1,128]{2,1,0:T(2,128)(2,1)S(1)} async-done(((bf16[8,1,128]{2,1,0:T(2,128)(2,1)}), bf16[8,1,128]{2,1,0:T(2,128)(2,1)S(1)}, u32[]{:S(2)}, u32[]{:S(2)}) %all-to-all-start.1) | async-done | bytes 2080 | tf_op jit(solution)/shard_map/all_to_all | solution.py:231
  219.9 0.6 select_reduce_fusion
  220.5 13.3 %weight_grads.1 = (bf16[1,192,4096]{2,1,0:T(8,128)(2,1)}, bf16[1,192,4096]{2,1,0:T(8,128)(2,1)}, bf16[1,192,4096]{2,1,0:T(8,128)(2,1)}) custom-call(s32[1]{0:T(128)} %bitcast.28.flag_ref, bf16[128,4096]{1,0:T(8,128)(2,1)} %refs_0_.3, bf16[128,4096]{1,0:T(8,128)(2,1)} %collective-permute-done.refs_1_, bf16[128,4096]{1,0:T(8,128)(2,1)} %copy-done, ...), custom_call_target="tpu_custom_call" | custom-call | tf_op jit(solution)/shard_map/weight_grads/pallas_call | solution.py:163
  233.9 2.2 fusion.11
  (81 shorter events, 0.3 us)
Async XLA Ops:
  0.6 27.2 %collective-permute-start.6 = (bf16[128,4096]{1,0:T(8,128)(2,1)}, bf16[128,4096]{1,0:T(8,128)(2,1)S(1)}, u32[]{:S(2)}, u32[]{:S(2)}) collective-permute-start(bf16[128,4096]{1,0:T(8,128)(2,1)} %refs_0_.3), channel_id=1, source_target_pairs={{0,8},{4,12},{8,0},{12,4},{16,24},{20,28},{24,16},{28,20},{1,9},{5... | collective-permute-start | bytes 3145736 | tf_op jit(solution)/shard_map/ppermute | solution.py:22
  3.6 26.3 %collective-permute-start.12 = (bf16[128,4096]{1,0:T(8,128)(2,1)}, bf16[128,4096]{1,0:T(8,128)(2,1)S(1)}, u32[]{:S(2)}, u32[]{:S(2)}) collective-permute-start(bf16[128,4096]{1,0:T(8,128)(2,1)} %refs_8_.1), channel_id=1, source_target_pairs={{0,16},{4,20},{8,24},{12,28},{16,0},{20,4},{24,8},{28,12},{1,17},{... | collective-permute-start | bytes 3145736 | tf_op jit(solution)/shard_map/ppermute | solution.py:22
  5.2 47.2 %collective-permute-start.8 = (bf16[128,4096]{1,0:T(8,128)(2,1)}, bf16[128,4096]{1,0:T(8,128)(2,1)S(1)}, u32[]{:S(2)}, u32[]{:S(2)}) collective-permute-start(bf16[128,4096]{1,0:T(8,128)(2,1)} %refs_0_.3), channel_id=1, source_target_pairs={{0,16},{4,20},{8,24},{12,28},{16,0},{20,4},{24,8},{28,12},{1,17},{... | collective-permute-start | bytes 3145736 | tf_op jit(solution)/shard_map/ppermute | solution.py:22
  5.7 46.7 %collective-permute-start.10 = (bf16[128,4096]{1,0:T(8,128)(2,1)}, bf16[128,4096]{1,0:T(8,128)(2,1)S(1)}, u32[]{:S(2)}, u32[]{:S(2)}) collective-permute-start(bf16[128,4096]{1,0:T(8,128)(2,1)} %refs_8_.1), channel_id=1, source_target_pairs={{0,8},{4,12},{8,0},{12,4},{16,24},{20,28},{24,16},{28,20},{1,9},{5... | collective-permute-start | bytes 3145736 | tf_op jit(solution)/shard_map/ppermute | solution.py:22
  27.8 58.5 %copy-start = (bf16[128,4096]{1,0:T(8,128)(2,1)}, bf16[128,4096]{1,0:T(8,128)(2,1)S(1)}, u32[]{:S(2)}) copy-start(bf16[128,4096]{1,0:T(8,128)(2,1)S(1)} %collective-permute-done.6.refs_0_.refs_2_) | copy-start | bytes 3145732
  27.8 45.7 %collective-permute-start.20 = (bf16[128,4096]{1,0:T(8,128)(2,1)S(1)}, bf16[128,4096]{1,0:T(8,128)(2,1)}, u32[]{:S(2)}, u32[]{:S(2)}) collective-permute-start(bf16[128,4096]{1,0:T(8,128)(2,1)S(1)} %collective-permute-done.6.refs_0_.refs_2_), channel_id=1, source_target_pairs={{0,16},{4,20},{8,24},{12,28},{16,0},{20,4},{24,8},{28,12},{1,17},{... | collective-permute-start | bytes 3145736 | tf_op jit(solution)/shard_map/ppermute | solution.py:22
  29.9 56.4 %copy-start.1 = (bf16[128,4096]{1,0:T(8,128)(2,1)}, bf16[128,4096]{1,0:T(8,128)(2,1)S(1)}, u32[]{:S(2)}) copy-start(bf16[128,4096]{1,0:T(8,128)(2,1)S(1)} %collective-permute-done.12.refs_6_.refs_12_) | copy-start | bytes 3145732
  29.9 43.6 %collective-permute-start.22 = (bf16[128,4096]{1,0:T(8,128)(2,1)S(1)}, bf16[128,4096]{1,0:T(8,128)(2,1)}, u32[]{:S(2)}, u32[]{:S(2)}) collective-permute-start(bf16[128,4096]{1,0:T(8,128)(2,1)S(1)} %collective-permute-done.12.refs_6_.refs_12_), channel_id=1, source_target_pairs={{0,8},{4,12},{8,0},{12,4},{16,24},{20,28},{24,16},{28,20},{1,9},{5... | collective-permute-start | bytes 3145736 | tf_op jit(solution)/shard_map/ppermute | solution.py:22
  31.4 42.6 %collective-permute-start.7 = (bf16[128,4096]{1,0:T(8,128)(2,1)S(1)}, bf16[128,4096]{1,0:T(8,128)(2,1)S(1)}, u32[]{:S(2)}, u32[]{:S(2)}) collective-permute-start(bf16[128,4096]{1,0:T(8,128)(2,1)S(1)} %collective-permute-done.6.refs_0_.refs_2_), channel_id=1, source_target_pairs={{0,4},{4,0},{8,12},{12,8},{16,20},{20,16},{24,28},{28,24},{1,5},{5... | collective-permute-start | bytes 3145736 | tf_op jit(solution)/shard_map/ppermute | solution.py:22
  52.4 34.0 %copy-start.2 = (bf16[128,4096]{1,0:T(8,128)(2,1)}, bf16[128,4096]{1,0:T(8,128)(2,1)S(1)}, u32[]{:S(2)}) copy-start(bf16[128,4096]{1,0:T(8,128)(2,1)S(1)} %collective-permute-done.8.refs_2_.refs_4_) | copy-start | bytes 3145732
  52.4 21.7 %collective-permute-start.9 = (bf16[128,4096]{1,0:T(8,128)(2,1)S(1)}, bf16[128,4096]{1,0:T(8,128)(2,1)S(1)}, u32[]{:S(2)}, u32[]{:S(2)}) collective-permute-start(bf16[128,4096]{1,0:T(8,128)(2,1)S(1)} %collective-permute-done.8.refs_2_.refs_4_), channel_id=1, source_target_pairs={{0,4},{4,0},{8,12},{12,8},{16,20},{20,16},{24,28},{28,24},{1,5},{5... | collective-permute-start | bytes 3145736 | tf_op jit(solution)/shard_map/ppermute | solution.py:22
  52.4 21.7 %copy-start.3 = (bf16[128,4096]{1,0:T(8,128)(2,1)}, bf16[128,4096]{1,0:T(8,128)(2,1)S(1)}, u32[]{:S(2)}) copy-start(bf16[128,4096]{1,0:T(8,128)(2,1)S(1)} %collective-permute-done.10.refs_4_.refs_10_) | copy-start | bytes 3145732
  52.4 22.2 %collective-permute-start.11 = (bf16[128,4096]{1,0:T(8,128)(2,1)S(1)}, bf16[128,4096]{1,0:T(8,128)(2,1)S(1)}, u32[]{:S(2)}, u32[]{:S(2)}) collective-permute-start(bf16[128,4096]{1,0:T(8,128)(2,1)S(1)} %collective-permute-done.10.refs_4_.refs_10_), channel_id=1, source_target_pairs={{0,4},{4,0},{8,12},{12,8},{16,20},{20,16},{24,28},{28,24},{1,5},{5... | collective-permute-start | bytes 3145736 | tf_op jit(solution)/shard_map/ppermute | solution.py:22
  73.5 12.8 %collective-permute-start.13 = (bf16[128,4096]{1,0:T(8,128)(2,1)S(1)}, bf16[128,4096]{1,0:T(8,128)(2,1)}, u32[]{:S(2)}, u32[]{:S(2)}) collective-permute-start(bf16[128,4096]{1,0:T(8,128)(2,1)S(1)} %collective-permute-done.12.refs_6_.refs_12_), channel_id=1, source_target_pairs={{0,4},{4,0},{8,12},{12,8},{16,20},{20,16},{24,28},{28,24},{1,5},{5... | collective-permute-start | bytes 3145736 | tf_op jit(solution)/shard_map/ppermute | solution.py:22
  73.5 25.3 %collective-permute-start = (bf16[128,4096]{1,0:T(8,128)(2,1)}, bf16[128,4096]{1,0:T(8,128)(2,1)}, u32[]{:S(2)}, u32[]{:S(2)}) collective-permute-start(bf16[128,4096]{1,0:T(8,128)(2,1)} %refs_0_.3), channel_id=1, source_target_pairs={{0,4},{4,0},{8,12},{12,8},{16,20},{20,16},{24,28},{28,24},{1,5},{5... | collective-permute-start | bytes 3145736 | tf_op jit(solution)/shard_map/ppermute | solution.py:22
  74.0 1.0 copy-start.4
  74.0 24.8 %collective-permute-start.1 = (bf16[128,4096]{1,0:T(8,128)(2,1)}, bf16[128,4096]{1,0:T(8,128)(2,1)}, u32[]{:S(2)}, u32[]{:S(2)}) collective-permute-start(bf16[128,4096]{1,0:T(8,128)(2,1)} %refs_8_.1), channel_id=1, source_target_pairs={{0,4},{4,0},{8,12},{12,8},{16,20},{20,16},{24,28},{28,24},{1,5},{5... | collective-permute-start | bytes 3145736 | tf_op jit(solution)/shard_map/ppermute | solution.py:22
  74.1 1.3 copy-start.5
  74.1 33.3 %collective-permute-start.21 = (bf16[128,4096]{1,0:T(8,128)(2,1)}, bf16[128,4096]{1,0:T(8,128)(2,1)}, u32[]{:S(2)}, u32[]{:S(2)}) collective-permute-start(bf16[128,4096]{1,0:T(8,128)(2,1)} %collective-permute-done.20.refs_0_.refs_6_), channel_id=1, source_target_pairs={{0,4},{4,0},{8,12},{12,8},{16,20},{20,16},{24,28},{28,24},{1,5},{5... | collective-permute-start | bytes 3145736 | tf_op jit(solution)/shard_map/ppermute | solution.py:22
  75.4 1.0 copy-start.6
  76.4 31.1 %collective-permute-start.23 = (bf16[128,4096]{1,0:T(8,128)(2,1)}, bf16[128,4096]{1,0:T(8,128)(2,1)}, u32[]{:S(2)}, u32[]{:S(2)}) collective-permute-start(bf16[128,4096]{1,0:T(8,128)(2,1)} %collective-permute-done.22.refs_2_.refs_14_), channel_id=1, source_target_pairs={{0,4},{4,0},{8,12},{12,8},{16,20},{20,16},{24,28},{28,24},{1,5},{5... | collective-permute-start | bytes 3145736 | tf_op jit(solution)/shard_map/ppermute | solution.py:22
  78.5 7.8 %all-to-all-start = ((f32[8,1,128]{2,1,0:T(1,128)}), f32[8,1,128]{2,1,0:T(1,128)S(1)}, u32[]{:S(2)}, u32[]{:S(2)}) async-start(f32[8,1,128]{2,1,0:T(1,128)} %bitcast.4), calls=%async_computation | async-start | bytes 8192 | tf_op jit(solution)/shard_map/all_to_all | solution.py:204
  86.3 0.6 copy-start.19
  98.8 26.7 %collective-permute-start.14 = (bf16[4,256,1024]{2,1,0:T(8,128)(2,1)}, bf16[4,256,1024]{2,1,0:T(8,128)(2,1)S(1)}, u32[]{:S(2)}, u32[]{:S(2)}) collective-permute-start(bf16[4,256,1024]{2,1,0:T(8,128)(2,1)} %get-tuple-element.23), channel_id=1, source_target_pairs={{0,4},{4,0},{8,12},{12,8},{16,20},{20,16},{24,28},{28,24},{1,5},{5... | collective-permute-start | bytes 6291464 | tf_op jit(solution)/shard_map/ppermute | solution.py:22
  106.9 8.8 %copy-start.12 = (bf16[576,256]{1,0:T(8,128)(2,1)S(1)}, bf16[576,256]{1,0:T(8,128)(2,1)}, u32[]{:S(2)}) copy-start(bf16[576,256]{1,0:T(8,128)(2,1)} %get-tuple-element.29) | copy-start | bytes 884740
  106.9 9.6 %copy-start.10 = (bf16[4,128,1024]{2,1,0:T(8,128)(2,1)S(1)}, bf16[4,128,1024]{2,1,0:T(8,128)(2,1)}, u32[]{:S(2)}) copy-start(bf16[4,128,1024]{2,1,0:T(8,128)(2,1)} %get-tuple-element.20) | copy-start | bytes 3145732
  106.9 9.6 %collective-permute-start.2 = (bf16[4,128,1024]{2,1,0:T(8,128)(2,1)}, bf16[4,128,1024]{2,1,0:T(8,128)(2,1)S(1)}, u32[]{:S(2)}, u32[]{:S(2)}) collective-permute-start(bf16[4,128,1024]{2,1,0:T(8,128)(2,1)} %get-tuple-element.21), channel_id=1, source_target_pairs={{0,4},{4,0},{8,12},{12,8},{16,20},{20,16},{24,28},{28,24},{1,5},{5... | collective-permute-start | bytes 3145736 | tf_op jit(solution)/shard_map/ppermute | solution.py:22
  115.5 4.4 %collective-permute-start.24 = (bf16[4,128,1024]{2,1,0:T(8,128)(2,1)}, bf16[4,128,1024]{2,1,0:T(8,128)(2,1)S(1)}, u32[]{:S(2)}, u32[]{:S(2)}) collective-permute-start(bf16[4,128,1024]{2,1,0:T(8,128)(2,1)} %get-tuple-element.25), channel_id=1, source_target_pairs={{0,4},{4,0},{8,12},{12,8},{16,20},{20,16},{24,28},{28,24},{1,5},{5... | collective-permute-start | bytes 3145736 | tf_op jit(solution)/shard_map/ppermute | solution.py:22
  116.5 1.1 copy-start.11
  116.5 2.0 copy-start.13
  116.9 53.6 %copy-start.7 = (bf16[4,128,1024]{2,1,0:T(8,128)(2,1)}, bf16[4,128,1024]{2,1,0:T(8,128)(2,1)S(1)}, u32[]{:S(2)}) copy-start(bf16[4,128,1024]{2,1,0:T(8,128)(2,1)S(1)} %add.68) | copy-start | bytes 3145732
  116.9 2.9 %copy-start.9 = (bf16[4,128,1024]{2,1,0:T(8,128)(2,1)S(1)}, bf16[4,128,1024]{2,1,0:T(8,128)(2,1)}, u32[]{:S(2)}) copy-start(bf16[4,128,1024]{2,1,0:T(8,128)(2,1)} %get-tuple-element.24) | copy-start | bytes 3145732
  119.3 91.6 %collective-permute-start.29 = (bf16[576,1024]{1,0:T(8,128)(2,1)}, bf16[576,1024]{1,0:T(8,128)(2,1)}, u32[]{:S(2)}, u32[]{:S(2)}) collective-permute-start(bf16[576,1024]{1,0:T(8,128)(2,1)} %constant_dynamic-update-slice_fusion.refs_16_), channel_id=1, source_target_pairs={{0,16},{4,20},{8,24},{12,28},{16,0},{20,4},{24,8},{28,12},{1,17},{... | collective-permute-start | bytes 3538952 | tf_op jit(solution)/shard_map/ppermute | solution.py:22
  119.9 5.6 %copy-start.8 = (bf16[4,256,1024]{2,1,0:T(8,128)(2,1)S(1)}, bf16[4,256,1024]{2,1,0:T(8,128)(2,1)}, u32[]{:S(2)}) copy-start(bf16[4,256,1024]{2,1,0:T(8,128)(2,1)} %get-tuple-element.22) | copy-start | bytes 6291460
  121.0 11.1 %collective-permute-start.27 = (bf16[128,1024]{1,0:T(8,128)(2,1)S(1)}, bf16[128,1024]{1,0:T(8,128)(2,1)S(1)}, u32[]{:S(2)}, u32[]{:S(2)}) collective-permute-start(bf16[128,1024]{1,0:T(8,128)(2,1)S(1)} %get-tuple-element.42), channel_id=1, source_target_pairs={{0,3},{1,2},{2,1},{3,0},{4,7},{5,6},{6,5},{7,4},{8,11},{9,10},{10,... | collective-permute-start | bytes 786440 | tf_op jit(solution)/shard_map/ppermute | solution.py:22
  124.6 45.9 %collective-permute-start.26 = (bf16[128,1024]{1,0:T(8,128)(2,1)S(1)}, bf16[128,1024]{1,0:T(8,128)(2,1)S(1)}, u32[]{:S(2)}, u32[]{:S(2)}) collective-permute-start(bf16[128,1024]{1,0:T(8,128)(2,1)S(1)} %get-tuple-element.43), channel_id=1, source_target_pairs={{0,2},{1,3},{2,0},{3,1},{4,6},{5,7},{6,4},{7,5},{8,10},{9,11},{10,... | collective-permute-start | bytes 786440 | tf_op jit(solution)/shard_map/ppermute | solution.py:22
  124.6 74.6 %collective-permute-start.25 = (bf16[128,1024]{1,0:T(8,128)(2,1)}, bf16[128,1024]{1,0:T(8,128)(2,1)S(1)}, u32[]{:S(2)}, u32[]{:S(2)}) collective-permute-start(bf16[128,1024]{1,0:T(8,128)(2,1)} %get-tuple-element.41), channel_id=1, source_target_pairs={{0,1},{1,0},{2,3},{3,2},{4,5},{5,4},{6,7},{7,6},{8,9},{9,8},{10,11... | collective-permute-start | bytes 786440 | tf_op jit(solution)/shard_map/ppermute | solution.py:22
  127.7 43.8 %copy-start.21 = (f32[1,512]{1,0:T(1,128)S(1)}, f32[1,512]{1,0:T(1,128)}, u32[]{:S(2)}) copy-start(f32[1,512]{1,0:T(1,128)} %get-tuple-element.27) | copy-start | bytes 6148
  127.7 43.8 %copy-start.22 = (f32[1,256]{1,0:T(1,128)S(1)}, f32[1,256]{1,0:T(1,128)}, u32[]{:S(2)}) copy-start(f32[1,256]{1,0:T(1,128)} %get-tuple-element.26) | copy-start | bytes 3076
  127.7 43.8 %copy-start.23 = (f32[1,256]{1,0:T(1,128)S(1)}, f32[1,256]{1,0:T(1,128)}, u32[]{:S(2)}) copy-start(f32[1,256]{1,0:T(1,128)} %get-tuple-element.28) | copy-start | bytes 3076
  127.8 73.4 %collective-permute-start.17 = (bf16[256,1024]{1,0:T(8,128)(2,1)}, bf16[256,1024]{1,0:T(8,128)(2,1)}, u32[]{:S(2)}, u32[]{:S(2)}) collective-permute-start(bf16[256,1024]{1,0:T(8,128)(2,1)} %get-tuple-element.36), channel_id=1, source_target_pairs={{0,3},{1,2},{2,1},{3,0},{4,7},{5,6},{6,5},{7,4},{8,11},{9,10},{10,... | collective-permute-start | bytes 1572872 | tf_op jit(solution)/shard_map/ppermute | solution.py:22
  132.1 39.4 %copy-start.14 = (bf16[128,1024]{1,0:T(8,128)(2,1)}, bf16[128,1024]{1,0:T(8,128)(2,1)S(1)}, u32[]{:S(2)}) copy-start(bf16[128,1024]{1,0:T(8,128)(2,1)S(1)} %collective-permute-done.27) | copy-start | bytes 786436
  132.1 70.1 %collective-permute-start.16 = (bf16[256,1024]{1,0:T(8,128)(2,1)}, bf16[256,1024]{1,0:T(8,128)(2,1)}, u32[]{:S(2)}, u32[]{:S(2)}) collective-permute-start(bf16[256,1024]{1,0:T(8,128)(2,1)} %get-tuple-element.37), channel_id=1, source_target_pairs={{0,2},{1,3},{2,0},{3,1},{4,6},{5,7},{6,4},{7,5},{8,10},{9,11},{10,... | collective-permute-start | bytes 1572872 | tf_op jit(solution)/shard_map/ppermute | solution.py:22
  170.5 1.0 copy-start.15
  170.5 35.2 %collective-permute-start.15 = (bf16[256,1024]{1,0:T(8,128)(2,1)}, bf16[256,1024]{1,0:T(8,128)(2,1)}, u32[]{:S(2)}, u32[]{:S(2)}) collective-permute-start(bf16[256,1024]{1,0:T(8,128)(2,1)} %get-tuple-element.35), channel_id=1, source_target_pairs={{0,1},{1,0},{2,3},{3,2},{4,5},{5,4},{6,7},{7,6},{8,9},{9,8},{10,11... | collective-permute-start | bytes 1572872 | tf_op jit(solution)/shard_map/ppermute | solution.py:22
  199.2 0.7 copy-start.16
  199.9 9.5 %collective-permute-start.5 = (bf16[128,1024]{1,0:T(8,128)(2,1)}, bf16[128,1024]{1,0:T(8,128)(2,1)S(1)}, u32[]{:S(2)}, u32[]{:S(2)}) collective-permute-start(bf16[128,1024]{1,0:T(8,128)(2,1)} %get-tuple-element.39), channel_id=1, source_target_pairs={{0,3},{1,2},{2,1},{3,0},{4,7},{5,6},{6,5},{7,4},{8,11},{9,10},{10,... | collective-permute-start | bytes 786440 | tf_op jit(solution)/shard_map/ppermute | solution.py:22
  201.2 32.6 %collective-permute-start.4 = (bf16[128,1024]{1,0:T(8,128)(2,1)}, bf16[128,1024]{1,0:T(8,128)(2,1)}, u32[]{:S(2)}, u32[]{:S(2)}) collective-permute-start(bf16[128,1024]{1,0:T(8,128)(2,1)} %get-tuple-element.40), channel_id=1, source_target_pairs={{0,2},{1,3},{2,0},{3,1},{4,6},{5,7},{6,4},{7,5},{8,10},{9,11},{10,... | collective-permute-start | bytes 786440 | tf_op jit(solution)/shard_map/ppermute | solution.py:22
  202.2 13.2 %copy-start.24 = (s32[4]{0:T(128)S(1)}, s32[4]{0:T(128)}, u32[]{:S(2)}) copy-start(s32[4]{0:T(128)} %param.15) | copy-start | bytes 52
  202.2 17.7 %copy-start.20 = (s32[128,4]{0,1:T(4,128)S(1)}, s32[128,4]{0,1:T(4,128)}, u32[]{:S(2)}) copy-start(s32[128,4]{0,1:T(4,128)} %param.13) | copy-start | bytes 6148
  202.2 31.7 %collective-permute-start.3 = (bf16[128,1024]{1,0:T(8,128)(2,1)}, bf16[128,1024]{1,0:T(8,128)(2,1)}, u32[]{:S(2)}, u32[]{:S(2)}) collective-permute-start(bf16[128,1024]{1,0:T(8,128)(2,1)} %get-tuple-element.38), channel_id=1, source_target_pairs={{0,1},{1,0},{2,3},{3,2},{4,5},{5,4},{6,7},{7,6},{8,9},{9,8},{10,11... | collective-permute-start | bytes 786440 | tf_op jit(solution)/shard_map/ppermute | solution.py:22
  205.7 28.2 %collective-permute-start.28 = (bf16[128,1024]{1,0:T(8,128)(2,1)S(1)}, bf16[128,1024]{1,0:T(8,128)(2,1)}, u32[]{:S(2)}, u32[]{:S(2)}) collective-permute-start(bf16[128,1024]{1,0:T(8,128)(2,1)S(1)} %fusion.5), channel_id=1, source_target_pairs={{0,24},{4,28},{8,16},{12,20},{16,8},{20,12},{24,0},{28,4},{1,25},{... | collective-permute-start | bytes 786440 | tf_op jit(solution)/shard_map/ppermute | solution.py:22
  209.4 2.0 copy-start.17
  209.4 24.5 %collective-permute-start.19 = (bf16[128,1024]{1,0:T(8,128)(2,1)S(1)}, bf16[128,1024]{1,0:T(8,128)(2,1)S(1)}, u32[]{:S(2)}, u32[]{:S(2)}) collective-permute-start(bf16[128,1024]{1,0:T(8,128)(2,1)S(1)} %get-tuple-element.45), channel_id=1, source_target_pairs={{0,16},{4,20},{8,24},{12,28},{16,0},{20,4},{24,8},{28,12},{1,17},{... | collective-permute-start | bytes 786440 | tf_op jit(solution)/shard_map/ppermute | solution.py:22
  210.9 23.0 %collective-permute-start.18 = (bf16[128,1024]{1,0:T(8,128)(2,1)S(1)}, bf16[128,1024]{1,0:T(8,128)(2,1)S(1)}, u32[]{:S(2)}, u32[]{:S(2)}) collective-permute-start(bf16[128,1024]{1,0:T(8,128)(2,1)S(1)} %get-tuple-element.44), channel_id=1, source_target_pairs={{0,8},{4,12},{8,0},{12,4},{16,24},{20,28},{24,16},{28,20},{1,9},{5... | collective-permute-start | bytes 786440 | tf_op jit(solution)/shard_map/ppermute | solution.py:22
  212.1 7.8 %all-to-all-start.1 = ((bf16[8,1,128]{2,1,0:T(2,128)(2,1)}), bf16[8,1,128]{2,1,0:T(2,128)(2,1)S(1)}, u32[]{:S(2)}, u32[]{:S(2)}) async-start(bf16[8,1,128]{2,1,0:T(2,128)(2,1)} %copy.21), calls=%async_computation.1 | async-start | bytes 8192 | tf_op jit(solution)/shard_map/all_to_all | solution.py:231
  220.5 13.4 %copy-start.18 = (bf16[128,1024]{1,0:T(8,128)(2,1)S(1)}, bf16[128,1024]{1,0:T(8,128)(2,1)}, u32[]{:S(2)}) copy-start(bf16[128,1024]{1,0:T(8,128)(2,1)} %copy-done.17) | copy-start | bytes 786436

commit v3 on v2

--- a/solution.py
+++ b/solution.py
@@ -27,27 +27,34 @@
     return jnp.sum(jnp.where(match, pair_flags[None, :], 0), axis=1)
 
 
-def activations_kernel(blocks, parts, where_ref, gates_ref, *refs):
-    count = len(blocks)
-    x_refs, dy_refs = refs[:count], refs[count : 2 * count]
-    gate_ref, up_ref, down_ref = refs[2 * count : 2 * count + 3]
-    acts_ref, score_ref, keep_ref, give_ref = refs[2 * count + 3 : 2 * count + 7]
-    x_all, dy_all, in_all, down_all, sems = refs[2 * count + 7 :]
-    rows, width = x_refs[0].shape
+def part_order(parts):
+    return (*range(0, parts, 2), *range(1, parts, 2))
+
+
+def activations_kernel(sources, parts, where_ref, gates_ref, *refs):
+    messages = refs[:4]
+    gate_ref, up_ref, down_ref = refs[4:7]
+    acts_ref, score_ref, keep_ref, give_ref = refs[8:12]
+    x_all, dy_all, in_all, down_all, sems = refs[12:]
+    rows, width = messages[0].shape
+    half = rows // 2
     units = gate_ref.shape[0]
     chunk = width // parts
     copies = []
     for part in range(parts):
         columns = pl.ds(part * chunk, chunk)
-        moves = [(gate_ref, in_all, 0, units), (up_ref, in_all, units, units), (down_ref, down_all, 0, units)]
-        moves += [(ref, x_all, i * rows, rows) for i, ref in enumerate(x_refs)]
-        moves += [(ref, dy_all, i * rows, rows) for i, ref in enumerate(dy_refs)]
+        everything = pl.ds(0, units)
+        moves = [(gate_ref, everything, in_all, 0, units), (up_ref, everything, in_all, units, units)]
+        moves.append((down_ref, everything, down_all, 0, units))
+        for i, ref in enumerate(messages):
+            moves.append((ref, pl.ds(0, half), x_all, i * half, half))
+            moves.append((ref, pl.ds(half, half), dy_all, i * half, half))
         copies.append(
             [
                 pltpu.make_async_copy(
-                    ref.at[:, columns], target.at[pl.ds(start, size), columns], sems.at[part, i]
+                    ref.at[place, columns], target.at[pl.ds(start, size), columns], sems.at[part, i]
                 )
-                for i, (ref, target, start, size) in enumerate(moves)
+                for i, (ref, place, target, start, size) in enumerate(moves)
             ]
         )
         for copy in copies[-1]:
@@ -67,7 +74,14 @@
         pre = one if pre is None else pre + one
         back = two if back is None else back + two
     pre_gate, pre_up = pre[:units], pre[units:]
-    g = jnp.concatenate([gates_ref[pl.ds(me ^ block, 1), :] for block in blocks], axis=1)
+    first = lax.broadcasted_iota(jnp.int32, (1, rows), 1) < half
+    g = jnp.concatenate(
+        [
+            jnp.where(first, gates_ref[pl.ds(me ^ one, 1), :], gates_ref[pl.ds(me ^ two, 1), :])
+            for one, two in (sources, (sources[0] ^ CORE, sources[1] ^ CORE))
+        ],
+        axis=1,
+    )
     sigma = jax.nn.sigmoid(pre_gate)
     active = pre_gate * sigma
     hidden = active * pre_up
@@ -78,70 +92,76 @@
     acts_ref[pl.ds(units, units), :] = (grad_hidden * active).astype(jnp.bfloat16)
     acts_ref[pl.ds(2 * units, units), :] = (g * hidden).astype(jnp.bfloat16)
     both = acts_ref[pl.ds(0, 2 * units), :]
-    for part in range(parts):
+    for place, part in enumerate(part_order(parts)):
         columns = pl.ds(pl.multiple_of((group ^ part) * chunk, chunk), chunk)
         share = lax.dot_general(both, in_all[:, columns], CONTRACT_ROWS, preferred_element_type=jnp.float32)
         share = share.astype(jnp.bfloat16)
-        for pair in range(count // 2):
-            keep_ref[part, pl.ds(pair * rows, rows), :] = share[2 * pair * rows : (2 * pair + 1) * rows]
-            give_ref[part, pl.ds(pair * rows, rows), :] = share[(2 * pair + 1) * rows : (2 * pair + 2) * rows]
-
-
-def activations(blocks, parts, where, gates, x_blocks, dy_blocks, w_gate, w_up, w_down):
-    count = len(blocks)
-    rows, width = x_blocks[0].shape
-    units = w_gate.shape[0]
+        keep_ref[place] = share[:rows]
+        give_ref[place] = share[rows:]
+
+
+def activations(sources, parts, where, gates, messages, weights, before):
+    rows, width = messages[0].shape
+    units = weights[0].shape[0]
     bf16 = jnp.bfloat16
-    share = jax.ShapeDtypeStruct((parts, count // 2 * rows, width // parts), bf16)
+    share = jax.ShapeDtypeStruct((parts, rows, width // parts), bf16)
     return pl.pallas_call(
-        functools.partial(activations_kernel, blocks, parts),
+        functools.partial(activations_kernel, sources, parts),
         out_shape=(
-            jax.ShapeDtypeStruct((3 * units, count * rows), bf16),
-            jax.ShapeDtypeStruct((1, count * rows), jnp.float32),
+            jax.ShapeDtypeStruct((3 * units, 2 * rows), bf16),
+            jax.ShapeDtypeStruct((1, 2 * rows), jnp.float32),
             share,
             share,
         ),
         in_specs=[pl.BlockSpec(memory_space=pltpu.SMEM), pl.BlockSpec(memory_space=pltpu.VMEM)]
-        + [pl.BlockSpec(memory_space=pl.ANY)] * (2 * count + 3),
+        + [pl.BlockSpec(memory_space=pl.ANY)] * 8,
         out_specs=[pl.BlockSpec(memory_space=pltpu.VMEM)] * 4,
         scratch_shapes=[
-            pltpu.VMEM((count * rows, width), bf16),
-            pltpu.VMEM((count * rows, width), bf16),
+            pltpu.VMEM((2 * rows, width), bf16),
+            pltpu.VMEM((2 * rows, width), bf16),
             pltpu.VMEM((2 * units, width), bf16),
             pltpu.VMEM((units, width), bf16),
-            pltpu.SemaphoreType.DMA((parts, 2 * count + 3)),
+            pltpu.SemaphoreType.DMA((parts, 11)),
         ],
         compiler_params=pltpu.CompilerParams(vmem_limit_bytes=VMEM),
+        cost_estimate=pl.CostEstimate(flops=1, bytes_accessed=1, transcendentals=0),
         name="activations",
-    )(where, gates, *x_blocks, *dy_blocks, w_gate, w_up, w_down)
-
-
-def weight_grads_kernel(order, parts, flag_ref, *refs):
-    count = len(order)
-    x_refs, dy_refs = refs[:count], refs[count : 2 * count]
-    own_ref, other_ref = refs[2 * count : 2 * count + 2]
-    outs = refs[2 * count + 2 : 2 * count + 5]
-    x_all, dy_all, acts, sems = refs[2 * count + 5 :]
-    rows, width = x_refs[0].shape
+    )(where, gates, *messages, *weights, before)
+
+
+def weight_grads_kernel(sources, parts, flag_ref, *refs):
+    count = 4 * len(sources)
+    messages = refs[:count]
+    own_ref, other_ref = refs[count : count + 2]
+    outs = refs[count + 2 : count + 5]
+    x_all, dy_all, acts, sems = refs[count + 5 :]
+    rows, width = messages[0].shape
+    half = rows // 2
     units = outs[0].shape[1]
     chunk = width // parts
     copies = []
     for part in range(parts):
         columns = pl.ds(part * chunk, chunk)
-        moves = [(ref, x_all, i * rows) for i, ref in enumerate(x_refs)]
-        moves += [(ref, dy_all, i * rows) for i, ref in enumerate(dy_refs)]
-        copies.append(
-            [
-                pltpu.make_async_copy(ref.at[:, columns], target.at[pl.ds(start, rows), columns], sems.at[part, i])
-                for i, (ref, target, start) in enumerate(moves)
-            ]
-        )
+        copies.append([])
+        for i, ref in enumerate(messages):
+            for start, target in ((0, x_all), (half, dy_all)):
+                copies[-1].append(
+                    pltpu.make_async_copy(
+                        ref.at[pl.ds(start, half), columns],
+                        target.at[pl.ds(i * half, half), columns],
+                        sems.at[part, len(copies[-1])],
+                    )
+                )
         for copy in copies[-1]:
             copy.start()
-    half = count // 2
-    for place, block in enumerate(order):
-        theirs = order.index(block ^ half)
-        arrived = other_ref[:, pl.ds(theirs * rows, rows)]
+    tiles = [(one ^ core, two ^ core) for one, two in sources for core in (0, CORE)]
+    first = lax.broadcasted_iota(jnp.int32, (1, rows), 1) < half
+    for place, (one, two) in enumerate(tiles):
+        from_one = [tile[0] for tile in tiles].index(one ^ ACROSS_Y)
+        from_two = [tile[1] for tile in tiles].index(two ^ ACROSS_Y)
+        arrived = jnp.where(
+            first, other_ref[:, pl.ds(from_one * rows, rows)], other_ref[:, pl.ds(from_two * rows, rows)]
+        )
         stay = own_ref[:, pl.ds(place * rows, rows)]
         acts[:, pl.ds(place * rows, rows)] = jnp.where(flag_ref[0] == 1, arrived, stay)
     for part in range(parts):
@@ -155,27 +175,29 @@
         outs[2][0, :, columns] = down.astype(jnp.bfloat16)
 
 
-def weight_grads(order, flag, x_blocks, dy_blocks, own, other):
-    count, parts = len(order), 8
-    rows, width = x_blocks[0].shape
+def weight_grads(sources, flag, messages, own, other):
+    parts = 8
+    rows, width = messages[0].shape
     units = own.shape[0] // 3
+    total = len(messages) * rows // 2
     bf16 = jnp.bfloat16
     return pl.pallas_call(
-        functools.partial(weight_grads_kernel, order, parts),
+        functools.partial(weight_grads_kernel, sources, parts),
         out_shape=(jax.ShapeDtypeStruct((1, units, width), bf16),) * 3,
         in_specs=[pl.BlockSpec(memory_space=pltpu.SMEM)]
-        + [pl.BlockSpec(memory_space=pl.ANY)] * (2 * count)
+        + [pl.BlockSpec(memory_space=pl.ANY)] * len(messages)
         + [pl.BlockSpec(memory_space=pltpu.VMEM)] * 2,
         out_specs=[pl.BlockSpec(memory_space=pltpu.VMEM)] * 3,
         scratch_shapes=[
-            pltpu.VMEM((count * rows, width), bf16),
-            pltpu.VMEM((count * rows, width), bf16),
-            pltpu.VMEM((3 * units, count * rows), bf16),
-            pltpu.SemaphoreType.DMA((parts, 2 * count)),
+            pltpu.VMEM((total, width), bf16),
+            pltpu.VMEM((total, width), bf16),
+            pltpu.VMEM((3 * units, total), bf16),
+            pltpu.SemaphoreType.DMA((parts, 2 * len(messages))),
         ],
         compiler_params=pltpu.CompilerParams(vmem_limit_bytes=VMEM),
+        cost_estimate=pl.CostEstimate(flops=1, bytes_accessed=1, transcendentals=0),
         name="weight_grads",
-    )(flag, *x_blocks, *dy_blocks, own, other)
+    )(flag, *messages, own, other)
 
 
 CORE, ACROSS_X, ACROSS_Y = 1, 2, 4
@@ -185,49 +207,82 @@
     expert_count = lax.axis_size("expert")
     half_axis = expert_count // 2
     me, group = lax.axis_index("expert"), lax.axis_index("dp")
-    row_count = tokens.shape[0]
+    half = tokens.shape[0] // 2
     parts = lax.axis_size("dp")
     f32, bf16 = jnp.float32, jnp.bfloat16
     own_flag = pair_lookup(jnp.reshape(me, (1,)), swap_flags, half_axis)
     where = jnp.stack([me, group]).astype(jnp.int32)
-
-    x, dy = {0: tokens}, {0: cotangent}
-    x[2], dy[4] = swap(tokens, "expert", ACROSS_X), swap(cotangent, "expert", ACROSS_Y)
-    x[1], dy[1] = swap(tokens, "expert", CORE), swap(cotangent, "expert", CORE)
-    x[4], dy[2] = swap(tokens, "expert", ACROSS_Y), swap(cotangent, "expert", ACROSS_X)
-    x[6], dy[6] = swap(x[2], "expert", ACROSS_Y), swap(dy[4], "expert", ACROSS_X)
-    for block in (2, 4, 6):
-        x[block + 1], dy[block + 1] = swap(x[block], "expert", CORE), swap(dy[block], "expert", CORE)
+    weights = (gate_weight[0], up_weight[0], down_weight[0])
+
+    def expert_swap(value, by):
+        return swap(value, "expert", by)
+
+    a = {0: jnp.concatenate([tokens[:half], cotangent[:half]])}
+    b = {0: jnp.concatenate([tokens[half:], cotangent[half:]])}
+    a[2], b[4] = expert_swap(a[0], ACROSS_X), expert_swap(b[0], ACROSS_Y)
+    a[4], b[2] = expert_swap(a[0], ACROSS_Y), expert_swap(b[0], ACROSS_X)
+    a[1], b[1] = expert_swap(a[0], CORE), expert_swap(b[0], CORE)
 
     named = expert_ids[:, :, None] == jnp.arange(expert_count, dtype=jnp.int32)[None, None, :]
     table = jnp.sum(jnp.where(named, gates[:, :, None].astype(f32), 0), axis=1)
     gate_rows = lax.all_to_all(table.T, "expert", split_axis=0, concat_axis=0, tiled=True)
 
-    weights = (gate_weight[0], up_weight[0], down_weight[0])
-    groups = ((0, 1), (2, 3, 4, 5), (6, 7))
-    order = sum(groups, ())
-    acts, scores, totals = [], [], {}
-    for blocks in groups:
-        act, score, keep, give = activations(
-            blocks, parts, where, gate_rows, [x[b] for b in blocks], [dy[b] for b in blocks], *weights
-        )
+    acts, scores, messages = [], [], []
+
+    def work(one, two, before):
+        held = [a[one], b[two], a[one ^ CORE], b[two ^ CORE]]
+        act, score, keep, give = activations((one, two), parts, where, gate_rows, held, weights, before)
         acts.append(act)
         scores.append(score)
-        both = keep + swap(give, "expert", CORE)
-        total = both[0].astype(f32)
-        for part in range(1, parts):
-            total = total + swap(both[part], "dp", part).astype(f32)
-        for pair in range(len(blocks) // 2):
-            totals[blocks[2 * pair]] = total[pair * row_count : (pair + 1) * row_count]
-    input_grad = totals[0]
-    for block in (ACROSS_X, ACROSS_Y, ACROSS_X | ACROSS_Y):
-        input_grad = input_grad + swap(totals[block].astype(bf16), "expert", block).astype(f32)
-
-    acts = jnp.concatenate(acts, axis=1)
-    grads = weight_grads(order, own_flag, [x[b] for b in order], [dy[b] for b in order], acts, swap(acts, "expert", half_axis))
-
-    score_rows = lax.psum(jnp.concatenate(scores, axis=1).reshape(expert_count, row_count), "dp").astype(bf16)
-    score_rows = jnp.take(score_rows, jnp.arange(expert_count, dtype=jnp.int32) ^ me, axis=0)
+        messages.extend(held)
+        return score, keep, expert_swap(give, CORE)
+
+    def near_sum(keep, given):
+        far = keep[parts // 2 :] + given[parts // 2 :]
+        near = keep[: parts // 2] + given[: parts // 2]
+        return near + swap(far, "dp", 1)
+
+    def far_sum(near):
+        return near[0].astype(f32) + swap(near[1], "dp", 2).astype(f32)
+
+    done_a, *share_a = work(0, 0, where)
+    a[2], b[4], done_a = lax.optimization_barrier((a[2], b[4], done_a))
+    a[6], b[6] = expert_swap(a[2], ACROSS_Y), expert_swap(b[4], ACROSS_X)
+    a[3], b[5] = expert_swap(a[2], CORE), expert_swap(b[4], CORE)
+    done_b, *share_b = work(2, 4, done_a)
+    near_a = near_sum(*share_a)
+    a[4], b[2], done_b, near_a = lax.optimization_barrier((a[4], b[2], done_b, near_a))
+    a[5], b[3] = expert_swap(a[4], CORE), expert_swap(b[2], CORE)
+    done_c, *share_c = work(4, 2, done_b)
+    total_a, near_b = far_sum(near_a), near_sum(*share_b)
+    a[6], b[6], done_c, total_a, near_b = lax.optimization_barrier((a[6], b[6], done_c, total_a, near_b))
+    a[7], b[7] = expert_swap(a[6], CORE), expert_swap(b[6], CORE)
+    total_b, near_c = far_sum(near_b), near_sum(*share_c)
+    _, *share_d = work(6, 6, done_c)
+    total_c, total_d = far_sum(near_c), far_sum(near_sum(*share_d))
+    totals = (total_a, total_b, total_c, total_d)
+
+    to_x = jnp.concatenate([totals[1][:half], totals[2][half:]]).astype(bf16)
+    to_y = jnp.concatenate([totals[2][:half], totals[1][half:]]).astype(bf16)
+    input_grad = totals[0] + expert_swap(to_x, ACROSS_X).astype(f32) + expert_swap(to_y, ACROSS_Y).astype(f32)
+    input_grad = input_grad + expert_swap(totals[3].astype(bf16), ACROSS_X | ACROSS_Y).astype(f32)
+
+    sources = ((0, 0), (2, 4), (4, 2), (6, 6))
+    own = jnp.concatenate(acts, axis=1)
+    grads = weight_grads(sources, own_flag, messages, own, expert_swap(own, half_axis))
+
+    tiles = jnp.concatenate(scores, axis=1).reshape(expert_count, 2 * half)
+    score_rows = jnp.concatenate(
+        [
+            tiles[:2],
+            jnp.concatenate([tiles[2:6, :half], tiles[jnp.array([4, 5, 2, 3]), half:]], axis=1),
+            tiles[6:],
+        ]
+    )
+    summed = score_rows
+    for part in range(1, parts):
+        summed = summed + swap(score_rows, "dp", part)
+    score_rows = jnp.take(summed.astype(bf16), jnp.arange(expert_count, dtype=jnp.int32) ^ me, axis=0)
     score_rows = lax.all_to_all(score_rows, "expert", split_axis=0, concat_axis=0, tiled=True)
     gate_grad = jnp.sum(jnp.where(named, score_rows.T[:, None, :].astype(f32), 0), axis=2)
     return (input_grad.astype(bf16), gate_grad.astype(bf16), *grads)

time: 241 us -> 218 us (0.905); the launches traced: 236 us -> 217 us
  blocking collectives: 27.1 us -> 0 us
  local copies, waits for them, and re-layouts: 10.3 us -> 18.1 us
  waiting for transfers between devices: 99.3 us -> 91.8 us
  Pallas kernels: 41.2 us -> 47.7 us
  other arithmetic: 11 us -> 17.1 us
  starting transfers between devices: 46.3 us -> 41.1 us
    psum x1 -> x0, blocking collectives: 27.1 us -> none  [whole_shards(): lax.psum(jnp.concatenate(scores, axis=1).reshape(expert_count, row_count)...]
    ppermute x30 -> x33, waiting for transfers between devices: 91.5 us -> 69 us  [swap(): lax.ppermute(value, axis, [(i, i ^ by) for i in range(lax.axis_size(axis))])]
    all_to_all x1, waiting for transfers between devices: 3.92 us -> 19 us  [whole_shards(): lax.all_to_all(table.T, 'expert', split_axis=0, concat_axis=0, tiled=True)]
    gather x1 -> x17, local copies, waits for them, and re-layouts: 0.56 us -> 8.53 us  [whole_shards(): jnp.take(score_rows, jnp.arange(expert_count, dtype=jnp.int32) ^ me, axis=0)]
    add x3 -> x9, other arithmetic: 1.96 us -> 8.82 us  [the longest x4 4.07 us: near_sum(): return near + swap(far, 'dp', 1)]
    pallas_call x4 -> x5, Pallas kernels: 41.2 us -> 47.7 us  [the longest x4 33.1 us: activations(): pl.pallas_call(functools.partial(activations_kernel, sources, parts), out...]
    ppermute x30 -> x33, starting transfers between devices: 39.6 us -> 34.5 us  [swap(): lax.ppermute(value, axis, [(i, i ^ by) for i in range(lax.axis_size(axis))])]
    unnamed x52 -> x77, local copies, waits for them, and re-layouts: 5.38 us -> 5.85 us
  transfers between devices with their start and end apart: 32 -> 35, of which waited for: 8 -> 11; matrix products, arithmetic and copies ran while one was open for 7% -> 12% of each run, Pallas kernels for 17% -> 22%
where the time goes in v3:
time: 218 us; the launch traced here: 217 us
  waiting for transfers between devices  91.8 us (42%)
  Pallas kernels  47.7 us (22%)
  starting transfers between devices  41.1 us (19%)
  local copies, waits for them, and re-layouts  18.1 us (8%)
  other arithmetic  17.1 us (8%)
    ppermute x33, waiting for transfers between devices, swap(): lax.ppermute(value, axis, [(i, i ^ by) for i in range(lax.axis_size(axis))])  69 us
    ppermute x33, starting transfers between devices, swap(): lax.ppermute(value, axis, [(i, i ^ by) for i in range(lax.axis_size(axis))])  34.5 us
    pallas_call x4, Pallas kernels, activations(): pl.pallas_call(functools.partial(activations_kernel, sources, parts), out...  33.1 us
    all_to_all x1, waiting for transfers between devices, whole_shards(): lax.all_to_all(table.T, 'expert', split_axis=0, concat_axis=0, tiled=True)  19 us
    pallas_call x1, Pallas kernels, weight_grads(): pl.pallas_call(functools.partial(weight_grads_kernel, sources, parts), ou...  14.7 us
    gather x16, local copies, waits for them, and re-layouts  7.97 us
    unnamed x77, local copies, waits for them, and re-layouts  5.85 us
  transfers between devices with their start and end apart: 35, of which 11 were waited for; matrix products, arithmetic and copies ran while one was open for 12% of the time, Pallas kernels for 22%

profile of v3, /device:TPU:0, one launch (start us, length us, event | category | flops | bytes accessed | tf_op | source)
XLA Modules:
  0.0 217.2 jit_solution(16710034187884704121)
XLA Ops:
  0.6 1.7 fusion.10
  3.2 2.9 %collective-permute-start = (bf16[128,4096]{1,0:T(8,128)(2,1)S(1)}, bf16[128,4096]{1,0:T(8,128)(2,1)}, u32[]{:S(2)}, u32[]{:S(2)}) collective-permute-start(bf16[128,4096]{1,0:T(8,128)(2,1)S(1)} %pad_maximum_fusion.refs_0_), channel_id=1, source_target_pairs={{0,8},{4,12},{8,0},{12,4},{16,24},{20,28},{24,16},{28,20},{1,9},{5... | collective-permute-start | bytes 3145736 | tf_op jit(solution)/shard_map/ppermute | solution.py:22
  6.1 1.5 collective-permute-start.1
  7.6 0.6 select_reduce_fusion.1
  8.2 3.3 %all-to-all-start = ((f32[8,1,128]{2,1,0:T(1,128)}), f32[8,1,128]{2,1,0:T(1,128)S(1)}, u32[]{:S(2)}, u32[]{:S(2)}) async-start(f32[8,1,128]{2,1,0:T(1,128)} %bitcast.4), calls=%async_computation | async-start | bytes 8192 | tf_op jit(solution)/shard_map/all_to_all | solution.py:228
  11.6 0.6 pad_add_fusion.where_ref.refs_7_
  12.1 19.0 %all-to-all-done = f32[8,1,128]{2,1,0:T(1,128)S(1)} async-done(((f32[8,1,128]{2,1,0:T(1,128)}), f32[8,1,128]{2,1,0:T(1,128)S(1)}, u32[]{:S(2)}, u32[]{:S(2)}) %all-to-all-start) | async-done | bytes 4128 | tf_op jit(solution)/shard_map/all_to_all | solution.py:228
  32.1 8.1 %activations.4 = (bf16[576,256]{1,0:T(8,128)(2,1)}, f32[1,256]{1,0:T(1,128)}, bf16[4,128,1024]{2,1,0:T(8,128)(2,1)}, bf16[4,128,1024]{2,1,0:T(8,128)(2,1)}) custom-call(s32[2]{0:T(128)} %pad_add_fusion.where_ref.refs_7_, f32[8,128]{1,0:T(8,128)} %bitcast.66, bf16[128,4096]{1,0:T(8,128)(2,1)} %copy-done, bf16[128,4096]{1,0:T(8,128)(2,1)} %copy-done.1, ...), custom_call_target="tpu_custom_call" | custom-call | flops 1 | bytes 1 | tf_op jit(solution)/shard_map/activations/pallas_call | solution.py:108
  41.0 1.5 collective-permute-start.6
  43.2 1.5 collective-permute-done.9.refs_3_.refs_7_
  44.7 0.9 copy-done.4
  45.7 8.2 %activations.5 = (bf16[576,256]{1,0:T(8,128)(2,1)}, f32[1,256]{1,0:T(1,128)}, bf16[4,128,1024]{2,1,0:T(8,128)(2,1)}, bf16[4,128,1024]{2,1,0:T(8,128)(2,1)}) custom-call(s32[2]{0:T(128)} %pad_add_fusion.where_ref.refs_7_, f32[8,128]{1,0:T(8,128)} %bitcast.67, bf16[128,4096]{1,0:T(8,128)(2,1)} %collective-permute-done.refs_0_.refs_4_, ...), custom_call_target="tpu_custom_call" | custom-call | flops 1 | bytes 1 | tf_op jit(solution)/shard_map/activations/pallas_call | solution.py:108
  54.2 1.7 collective-permute-start.11
  55.9 1.5 collective-permute-start.4
  57.4 11.1 %collective-permute-done.11 = bf16[2,128,1024]{2,1,0:T(8,128)(2,1)S(1)} collective-permute-done((bf16[2,128,1024]{2,1,0:T(8,128)(2,1)S(1)}, bf16[2,128,1024]{2,1,0:T(8,128)(2,1)S(1)}, u32[]{:S(2)}, u32[]{:S(2)}) %collective-permute-start.11) | collective-permute-done | bytes 524320 | tf_op jit(solution)/shard_map/ppermute | solution.py:22
  68.5 1.1 collective-permute-start.5
  69.7 0.7 copy-done.11
  70.4 2.6 %collective-permute-start.14 = (bf16[128,1024]{1,0:T(8,128)(2,1)S(1)}, bf16[128,1024]{1,0:T(8,128)(2,1)S(1)}, u32[]{:S(2)}, u32[]{:S(2)}) collective-permute-start(bf16[128,1024]{1,0:T(8,128)(2,1)S(1)} %slice_bitcast_fusion.5), channel_id=1, source_target_pairs={{0,2},{1,3},{2,0},{3,1},{4,6},{5,7},{6,4},{7,5},{8,10},{9,11},{10,... | collective-permute-start | bytes 786440 | tf_op jit(solution)/shard_map/ppermute | solution.py:22
  73.6 0.8 slice_add_fusion.4
  74.4 10.0 %collective-permute-done.14 = bf16[128,1024]{1,0:T(8,128)(2,1)S(1)} collective-permute-done((bf16[128,1024]{1,0:T(8,128)(2,1)S(1)}, bf16[128,1024]{1,0:T(8,128)(2,1)S(1)}, u32[]{:S(2)}, u32[]{:S(2)}) %collective-permute-start.14) | collective-permute-done | bytes 262176 | tf_op jit(solution)/shard_map/ppermute | solution.py:22
  84.4 0.7 collective-permute-start.16
  85.7 1.8 convert_add_fusion.3
  87.5 10.0 %collective-permute-done.16 = bf16[2,128,1024]{2,1,0:T(8,128)(2,1)} collective-permute-done((bf16[2,128,1024]{2,1,0:T(8,128)(2,1)}, bf16[2,128,1024]{2,1,0:T(8,128)(2,1)}, u32[]{:S(2)}, u32[]{:S(2)}) %collective-permute-start.16) | collective-permute-done | bytes 524320 | tf_op jit(solution)/shard_map/ppermute | solution.py:22
  97.5 1.3 fusion.2
  98.9 8.3 %activations.6 = (bf16[576,256]{1,0:T(8,128)(2,1)}, f32[1,256]{1,0:T(1,128)}, bf16[4,128,1024]{2,1,0:T(8,128)(2,1)}, bf16[4,128,1024]{2,1,0:T(8,128)(2,1)}) custom-call(s32[2]{0:T(128)} %pad_add_fusion.where_ref.refs_7_, f32[8,128]{1,0:T(8,128)} %bitcast.68, bf16[128,4096]{1,0:T(8,128)(2,1)} %copy-done.5, ...), custom_call_target="tpu_custom_call" | custom-call | flops 1 | bytes 1 | tf_op jit(solution)/shard_map/activations/pallas_call | solution.py:108
  107.3 3.4 %collective-permute-start.17 = (bf16[128,1024]{1,0:T(8,128)(2,1)S(1)}, bf16[128,1024]{1,0:T(8,128)(2,1)S(1)}, u32[]{:S(2)}, u32[]{:S(2)}) collective-permute-start(bf16[128,1024]{1,0:T(8,128)(2,1)S(1)} %slice_bitcast_fusion.4), channel_id=1, source_target_pairs={{0,2},{1,3},{2,0},{3,1},{4,6},{5,7},{6,4},{7,5},{8,10},{9,11},{10,... | collective-permute-start | bytes 786440 | tf_op jit(solution)/shard_map/ppermute | solution.py:22
  111.4 11.9 %collective-permute-done.17 = bf16[128,1024]{1,0:T(8,128)(2,1)S(1)} collective-permute-done((bf16[128,1024]{1,0:T(8,128)(2,1)S(1)}, bf16[128,1024]{1,0:T(8,128)(2,1)S(1)}, u32[]{:S(2)}, u32[]{:S(2)}) %collective-permute-start.17) | collective-permute-done | bytes 262176 | tf_op jit(solution)/shard_map/ppermute | solution.py:22
  123.4 0.7 fusion.12
  124.1 0.9 slice_add_fusion.2
  125.0 0.8 collective-permute-start.19
  125.9 1.0 copy-done.8
  126.8 1.0 copy-done.9
  127.8 8.4 %activations.7 = (bf16[576,256]{1,0:T(8,128)(2,1)}, f32[1,256]{1,0:T(1,128)}, bf16[4,128,1024]{2,1,0:T(8,128)(2,1)}, bf16[4,128,1024]{2,1,0:T(8,128)(2,1)}) custom-call(s32[2]{0:T(128)} %pad_add_fusion.where_ref.refs_7_, f32[8,128]{1,0:T(8,128)} %bitcast.69, bf16[128,4096]{1,0:T(8,128)(2,1)} %copy-done.6, bf16[128,4096]{1,0:T(8,128)(2,1)} %copy-done.7, ...), custom_call_target="tpu_custom_call" | custom-call | flops 1 | bytes 1 | tf_op jit(solution)/shard_map/activations/pallas_call | solution.py:108
  136.3 0.7 pad_maximum_fusion.4
  137.0 8.0 %while.1 = (s32[]{:T(128)}, f32[8,128]{1,0:T(8,128)S(1)}, s32[4,2]{0,1:T(2,128)S(1)}, f32[4,64]{1,0:T(4,128)S(1)}, s32[]{:T(128)}, /*index=5*/s32[]{:T(128)}) while((s32[]{:T(128)}, f32[8,128]{1,0:T(8,128)S(1)}, s32[4,2]{0,1:T(2,128)S(1)}, f32[4,64]{1,0:T(4,128)S(1)}, s32[]{:T(128)}, /*index=5*/s32[]{:T(128)}) %tuple.40), condition=%wide.while_cond, body=%wide.while_body.sunk | while | flops 2 | bytes 1145 | solution.py:278
  137.6 1.4 dynamic-slice.7
  139.6 1.4 dynamic-slice.7
  141.6 1.4 dynamic-slice.7
  143.6 1.4 dynamic-slice.7
  145.0 0.7 pad_maximum_fusion.5
  145.7 3.0 %collective-permute-start.31 = (f32[8,128]{1,0:T(8,128)S(1)}, f32[8,128]{1,0:T(8,128)S(1)}, u32[]{:S(2)}, u32[]{:S(2)}) collective-permute-start(f32[8,128]{1,0:T(8,128)S(1)} %pad_maximum_fusion.5), channel_id=1, source_target_pairs={{0,3},{1,2},{2,1},{3,0},{4,7},{5,6},{6,5},{7,4},{8,11},{9,10},{10,... | collective-permute-start | bytes 12296 | tf_op jit(solution)/shard_map/ppermute | solution.py:22
  149.2 1.0 collective-permute-start.29
  150.1 1.3 fusion.1
  151.4 0.7 slice_bitcast_fusion.2
  152.1 2.5 %collective-permute-start.20 = (bf16[128,1024]{1,0:T(8,128)(2,1)}, bf16[128,1024]{1,0:T(8,128)(2,1)}, u32[]{:S(2)}, u32[]{:S(2)}) collective-permute-start(bf16[128,1024]{1,0:T(8,128)(2,1)} %slice_bitcast_fusion.2), channel_id=1, source_target_pairs={{0,2},{1,3},{2,0},{3,1},{4,6},{5,7},{6,4},{7,5},{8,10},{9,11},{10,... | collective-permute-start | bytes 786440 | tf_op jit(solution)/shard_map/ppermute | solution.py:22
  154.6 1.1 slice_add_fusion
  155.7 1.1 collective-permute-start.26
  156.9 1.0 collective-permute-start.32
  158.5 8.5 %collective-permute-done.20 = bf16[128,1024]{1,0:T(8,128)(2,1)} collective-permute-done((bf16[128,1024]{1,0:T(8,128)(2,1)}, bf16[128,1024]{1,0:T(8,128)(2,1)}, u32[]{:S(2)}, u32[]{:S(2)}) %collective-permute-start.20) | collective-permute-done | bytes 262176 | tf_op jit(solution)/shard_map/ppermute | solution.py:22
  166.9 1.0 fusion.5
  168.0 5.8 %collective-permute-done.26 = bf16[2,128,1024]{2,1,0:T(8,128)(2,1)} collective-permute-done((bf16[2,128,1024]{2,1,0:T(8,128)(2,1)S(1)}, bf16[2,128,1024]{2,1,0:T(8,128)(2,1)}, u32[]{:S(2)}, u32[]{:S(2)}) %collective-permute-start.26) | collective-permute-done | bytes 524320 | tf_op jit(solution)/shard_map/ppermute | solution.py:22
  173.8 1.4 fusion
  175.5 1.0 collective-permute-start.22
  176.5 0.7 pad_maximum_fusion.2
  177.2 1.5 collective-permute-start.21
  178.7 9.8 %collective-permute-done.27 = bf16[128,1024]{1,0:T(8,128)(2,1)S(1)} collective-permute-done((bf16[128,1024]{1,0:T(8,128)(2,1)S(1)}, bf16[128,1024]{1,0:T(8,128)(2,1)S(1)}, u32[]{:S(2)}, u32[]{:S(2)}) %collective-permute-start.27) | collective-permute-done | bytes 262176 | tf_op jit(solution)/shard_map/ppermute | solution.py:22
  188.6 1.9 collective-permute-start.28
  190.6 0.6 copy.22
  191.2 3.3 %all-to-all-start.1 = ((bf16[8,1,128]{2,1,0:T(2,128)(2,1)}), bf16[8,1,128]{2,1,0:T(2,128)(2,1)S(1)}, u32[]{:S(2)}, u32[]{:S(2)}) async-start(bf16[8,1,128]{2,1,0:T(2,128)(2,1)} %copy.22), calls=%async_computation.1 | async-start | bytes 8192 | tf_op jit(solution)/shard_map/all_to_all | solution.py:286
  194.5 0.6 fusion.7
  195.2 3.9 %all-to-all-done.1 = bf16[8,1,128]{2,1,0:T(2,128)(2,1)S(1)} async-done(((bf16[8,1,128]{2,1,0:T(2,128)(2,1)}), bf16[8,1,128]{2,1,0:T(2,128)(2,1)S(1)}, u32[]{:S(2)}, u32[]{:S(2)}) %all-to-all-start.1) | async-done | bytes 2080 | tf_op jit(solution)/shard_map/all_to_all | solution.py:286
  199.6 1.0 copy-done.13
  200.6 14.7 %weight_grads.1 = (bf16[1,192,4096]{2,1,0:T(8,128)(2,1)}, bf16[1,192,4096]{2,1,0:T(8,128)(2,1)}, bf16[1,192,4096]{2,1,0:T(8,128)(2,1)}) custom-call(s32[1]{0:T(128)} %bitcast.26.flag_ref, bf16[128,4096]{1,0:T(8,128)(2,1)} %copy-done, bf16[128,4096]{1,0:T(8,128)(2,1)} %copy-done.1, bf16[128,4096]{1,0:T(8,128)(2,1)} %copy-done.2, ...), custom_call_target="tpu_custom_call" | custom-call | flops 1 | bytes 1 | tf_op jit(solution)/shard_map/weight_grads/pallas_call | solution.py:184
  215.4 1.8 add_convert_fusion
  (147 shorter events, 10.0 us)
Async XLA Ops:
  2.4 28.7 %copy-start = (bf16[128,4096]{1,0:T(8,128)(2,1)}, bf16[128,4096]{1,0:T(8,128)(2,1)S(1)}, u32[]{:S(2)}) copy-start(bf16[128,4096]{1,0:T(8,128)(2,1)S(1)} %pad_maximum_fusion.refs_0_) | copy-start | bytes 3145732
  2.4 5.2 %copy-start.34 = (bf16[128,4]{0,1:T(4,128)(2,1)S(1)}, bf16[128,4]{0,1:T(4,128)(2,1)}, u32[]{:S(2)}) copy-start(bf16[128,4]{0,1:T(4,128)(2,1)} %param.15) | copy-start | bytes 3076
  2.4 5.2 %copy-start.30 = (s32[128,4]{0,1:T(4,128)S(1)}, s32[128,4]{0,1:T(4,128)}, u32[]{:S(2)}) copy-start(s32[128,4]{0,1:T(4,128)} %param.14) | copy-start | bytes 6148
  2.4 28.7 %collective-permute-start.2 = (bf16[128,4096]{1,0:T(8,128)(2,1)S(1)}, bf16[128,4096]{1,0:T(8,128)(2,1)S(1)}, u32[]{:S(2)}, u32[]{:S(2)}) collective-permute-start(bf16[128,4096]{1,0:T(8,128)(2,1)S(1)} %pad_maximum_fusion.refs_0_), channel_id=1, source_target_pairs={{0,4},{4,0},{8,12},{12,8},{16,20},{20,16},{24,28},{28,24},{1,5},{5... | collective-permute-start | bytes 3145736 | tf_op jit(solution)/shard_map/ppermute | solution.py:22
  3.0 28.1 %copy-start.1 = (bf16[128,4096]{1,0:T(8,128)(2,1)}, bf16[128,4096]{1,0:T(8,128)(2,1)S(1)}, u32[]{:S(2)}) copy-start(bf16[128,4096]{1,0:T(8,128)(2,1)S(1)} %pad_maximum_fusion.1.refs_1_) | copy-start | bytes 3145732
  3.0 28.1 %collective-permute-start.3 = (bf16[128,4096]{1,0:T(8,128)(2,1)S(1)}, bf16[128,4096]{1,0:T(8,128)(2,1)}, u32[]{:S(2)}, u32[]{:S(2)}) collective-permute-start(bf16[128,4096]{1,0:T(8,128)(2,1)S(1)} %pad_maximum_fusion.1.refs_1_), channel_id=1, source_target_pairs={{0,4},{4,0},{8,12},{12,8},{16,20},{20,16},{24,28},{28,24},{1,5},{5... | collective-permute-start | bytes 3145736 | tf_op jit(solution)/shard_map/ppermute | solution.py:22
  3.2 37.1 %collective-permute-start = (bf16[128,4096]{1,0:T(8,128)(2,1)S(1)}, bf16[128,4096]{1,0:T(8,128)(2,1)}, u32[]{:S(2)}, u32[]{:S(2)}) collective-permute-start(bf16[128,4096]{1,0:T(8,128)(2,1)S(1)} %pad_maximum_fusion.refs_0_), channel_id=1, source_target_pairs={{0,8},{4,12},{8,0},{12,4},{16,24},{20,28},{24,16},{28,20},{1,9},{5... | collective-permute-start | bytes 3145736 | tf_op jit(solution)/shard_map/ppermute | solution.py:22
  6.1 34.2 %collective-permute-start.1 = (bf16[128,4096]{1,0:T(8,128)(2,1)S(1)}, bf16[128,4096]{1,0:T(8,128)(2,1)}, u32[]{:S(2)}, u32[]{:S(2)}) collective-permute-start(bf16[128,4096]{1,0:T(8,128)(2,1)S(1)} %pad_maximum_fusion.1.refs_1_), channel_id=1, source_target_pairs={{0,16},{4,20},{8,24},{12,28},{16,0},{20,4},{24,8},{28,12},{1,17},{... | collective-permute-start | bytes 3145736 | tf_op jit(solution)/shard_map/ppermute | solution.py:22
  8.2 22.9 %all-to-all-start = ((f32[8,1,128]{2,1,0:T(1,128)}), f32[8,1,128]{2,1,0:T(1,128)S(1)}, u32[]{:S(2)}, u32[]{:S(2)}) async-start(f32[8,1,128]{2,1,0:T(1,128)} %bitcast.4), calls=%async_computation | async-start | bytes 8192 | tf_op jit(solution)/shard_map/all_to_all | solution.py:228
  40.3 2.9 %collective-permute-start.8 = (bf16[128,4096]{1,0:T(8,128)(2,1)}, bf16[128,4096]{1,0:T(8,128)(2,1)S(1)}, u32[]{:S(2)}, u32[]{:S(2)}) collective-permute-start(bf16[128,4096]{1,0:T(8,128)(2,1)} %collective-permute-done.refs_0_.refs_4_), channel_id=1, source_target_pairs={{0,4},{4,0},{8,12},{12,8},{16,20},{20,16},{24,28},{28,24},{1,5},{5... | collective-permute-start | bytes 3145736 | tf_op jit(solution)/shard_map/ppermute | solution.py:22
  40.4 4.3 %collective-permute-start.9 = (bf16[128,4096]{1,0:T(8,128)(2,1)}, bf16[128,4096]{1,0:T(8,128)(2,1)S(1)}, u32[]{:S(2)}, u32[]{:S(2)}) collective-permute-start(bf16[128,4096]{1,0:T(8,128)(2,1)} %collective-permute-done.1.refs_1_.refs_5_), channel_id=1, source_target_pairs={{0,4},{4,0},{8,12},{12,8},{16,20},{20,16},{24,28},{28,24},{1,5},{5... | collective-permute-start | bytes 3145736 | tf_op jit(solution)/shard_map/ppermute | solution.py:22
  40.9 13.3 %copy-start.21 = (bf16[4,128,1024]{2,1,0:T(8,128)(2,1)S(1)}, bf16[4,128,1024]{2,1,0:T(8,128)(2,1)}, u32[]{:S(2)}) copy-start(bf16[4,128,1024]{2,1,0:T(8,128)(2,1)} %get-tuple-element.41) | copy-start | bytes 3145732
  40.9 13.3 %collective-permute-start.10 = (bf16[4,128,1024]{2,1,0:T(8,128)(2,1)}, bf16[4,128,1024]{2,1,0:T(8,128)(2,1)S(1)}, u32[]{:S(2)}, u32[]{:S(2)}) collective-permute-start(bf16[4,128,1024]{2,1,0:T(8,128)(2,1)} %get-tuple-element.42), channel_id=1, source_target_pairs={{0,4},{4,0},{8,12},{12,8},{16,20},{20,16},{24,28},{28,24},{1,5},{5... | collective-permute-start | bytes 3145736 | tf_op jit(solution)/shard_map/ppermute | solution.py:22
  41.0 28.7 %collective-permute-start.6 = (bf16[128,4096]{1,0:T(8,128)(2,1)}, bf16[128,4096]{1,0:T(8,128)(2,1)S(1)}, u32[]{:S(2)}, u32[]{:S(2)}) collective-permute-start(bf16[128,4096]{1,0:T(8,128)(2,1)} %copy-done), channel_id=1, source_target_pairs={{0,16},{4,20},{8,24},{12,28},{16,0},{20,4},{24,8},{28,12},{1,17},{... | collective-permute-start | bytes 3145736 | tf_op jit(solution)/shard_map/ppermute | solution.py:22
  42.5 27.2 %collective-permute-start.7 = (bf16[128,4096]{1,0:T(8,128)(2,1)}, bf16[128,4096]{1,0:T(8,128)(2,1)}, u32[]{:S(2)}, u32[]{:S(2)}) collective-permute-start(bf16[128,4096]{1,0:T(8,128)(2,1)} %copy-done.1), channel_id=1, source_target_pairs={{0,8},{4,12},{8,0},{12,4},{16,24},{20,28},{24,16},{28,20},{1,9},{5... | collective-permute-start | bytes 3145736 | tf_op jit(solution)/shard_map/ppermute | solution.py:22
  43.2 1.5 copy-start.3
  53.9 19.1 %collective-permute-start.15 = (bf16[4,128,1024]{2,1,0:T(8,128)(2,1)}, bf16[4,128,1024]{2,1,0:T(8,128)(2,1)S(1)}, u32[]{:S(2)}, u32[]{:S(2)}) collective-permute-start(bf16[4,128,1024]{2,1,0:T(8,128)(2,1)} %get-tuple-element.49), channel_id=1, source_target_pairs={{0,4},{4,0},{8,12},{12,8},{16,20},{20,16},{24,28},{28,24},{1,5},{5... | collective-permute-start | bytes 3145736 | tf_op jit(solution)/shard_map/ppermute | solution.py:22
  54.2 19.4 %copy-start.18 = (bf16[4,128,1024]{2,1,0:T(8,128)(2,1)S(1)}, bf16[4,128,1024]{2,1,0:T(8,128)(2,1)}, u32[]{:S(2)}) copy-start(bf16[4,128,1024]{2,1,0:T(8,128)(2,1)} %get-tuple-element.48) | copy-start | bytes 3145732
  54.2 14.3 %collective-permute-start.11 = (bf16[2,128,1024]{2,1,0:T(8,128)(2,1)S(1)}, bf16[2,128,1024]{2,1,0:T(8,128)(2,1)S(1)}, u32[]{:S(2)}, u32[]{:S(2)}) collective-permute-start(bf16[2,128,1024]{2,1,0:T(8,128)(2,1)S(1)} %slice_add_fusion.6), channel_id=1, source_target_pairs={{0,1},{1,0},{2,3},{3,2},{4,5},{5,4},{6,7},{7,6},{8,9},{9,8},{10,11... | collective-permute-start | bytes 1572872 | tf_op jit(solution)/shard_map/ppermute | solution.py:22
  55.9 51.3 %collective-permute-start.4 = (bf16[128,4096]{1,0:T(8,128)(2,1)}, bf16[128,4096]{1,0:T(8,128)(2,1)S(1)}, u32[]{:S(2)}, u32[]{:S(2)}) collective-permute-start(bf16[128,4096]{1,0:T(8,128)(2,1)} %collective-permute-done.refs_0_.refs_4_), channel_id=1, source_target_pairs={{0,16},{4,20},{8,24},{12,28},{16,0},{20,4},{24,8},{28,12},{1,17},{... | collective-permute-start | bytes 3145736 | tf_op jit(solution)/shard_map/ppermute | solution.py:22
  68.5 38.7 %collective-permute-start.5 = (bf16[128,4096]{1,0:T(8,128)(2,1)}, bf16[128,4096]{1,0:T(8,128)(2,1)S(1)}, u32[]{:S(2)}, u32[]{:S(2)}) collective-permute-start(bf16[128,4096]{1,0:T(8,128)(2,1)} %collective-permute-done.1.refs_1_.refs_5_), channel_id=1, source_target_pairs={{0,8},{4,12},{8,0},{12,4},{16,24},{20,28},{24,16},{28,20},{1,9},{5... | collective-permute-start | bytes 3145736 | tf_op jit(solution)/shard_map/ppermute | solution.py:22
  69.7 17.8 %copy-start.5 = (bf16[128,4096]{1,0:T(8,128)(2,1)}, bf16[128,4096]{1,0:T(8,128)(2,1)S(1)}, u32[]{:S(2)}) copy-start(bf16[128,4096]{1,0:T(8,128)(2,1)S(1)} %collective-permute-done.6.refs_0_.refs_8_) | copy-start | bytes 3145732
  70.4 14.0 %collective-permute-start.14 = (bf16[128,1024]{1,0:T(8,128)(2,1)S(1)}, bf16[128,1024]{1,0:T(8,128)(2,1)S(1)}, u32[]{:S(2)}, u32[]{:S(2)}) collective-permute-start(bf16[128,1024]{1,0:T(8,128)(2,1)S(1)} %slice_bitcast_fusion.5), channel_id=1, source_target_pairs={{0,2},{1,3},{2,0},{3,1},{4,6},{5,7},{6,4},{7,5},{8,10},{9,11},{10,... | collective-permute-start | bytes 786440 | tf_op jit(solution)/shard_map/ppermute | solution.py:22
  73.0 25.8 %collective-permute-start.12 = (bf16[128,4096]{1,0:T(8,128)(2,1)S(1)}, bf16[128,4096]{1,0:T(8,128)(2,1)}, u32[]{:S(2)}, u32[]{:S(2)}) collective-permute-start(bf16[128,4096]{1,0:T(8,128)(2,1)S(1)} %collective-permute-done.6.refs_0_.refs_8_), channel_id=1, source_target_pairs={{0,4},{4,0},{8,12},{12,8},{16,20},{20,16},{24,28},{28,24},{1,5},{5... | collective-permute-start | bytes 3145736 | tf_op jit(solution)/shard_map/ppermute | solution.py:22
  73.0 25.8 %collective-permute-start.13 = (bf16[128,4096]{1,0:T(8,128)(2,1)}, bf16[128,4096]{1,0:T(8,128)(2,1)}, u32[]{:S(2)}, u32[]{:S(2)}) collective-permute-start(bf16[128,4096]{1,0:T(8,128)(2,1)} %collective-permute-done.7.refs_1_.refs_9_), channel_id=1, source_target_pairs={{0,4},{4,0},{8,12},{12,8},{16,20},{20,16},{24,28},{28,24},{1,5},{5... | collective-permute-start | bytes 3145736 | tf_op jit(solution)/shard_map/ppermute | solution.py:22
  84.4 13.1 %collective-permute-start.16 = (bf16[2,128,1024]{2,1,0:T(8,128)(2,1)}, bf16[2,128,1024]{2,1,0:T(8,128)(2,1)}, u32[]{:S(2)}, u32[]{:S(2)}) collective-permute-start(bf16[2,128,1024]{2,1,0:T(8,128)(2,1)} %slice_add_fusion.4), channel_id=1, source_target_pairs={{0,1},{1,0},{2,3},{3,2},{4,5},{5,4},{6,7},{7,6},{8,9},{9,8},{10,11... | collective-permute-start | bytes 1572872 | tf_op jit(solution)/shard_map/ppermute | solution.py:22
  85.1 12.4 %copy-start.19 = (bf16[4,128,1024]{2,1,0:T(8,128)(2,1)S(1)}, bf16[4,128,1024]{2,1,0:T(8,128)(2,1)}, u32[]{:S(2)}) copy-start(bf16[4,128,1024]{2,1,0:T(8,128)(2,1)} %get-tuple-element.48) | copy-start | bytes 3145732
  98.8 12.4 %copy-start.23 = (bf16[576,256]{1,0:T(8,128)(2,1)S(1)}, bf16[576,256]{1,0:T(8,128)(2,1)}, u32[]{:S(2)}) copy-start(bf16[576,256]{1,0:T(8,128)(2,1)} %get-tuple-element.60) | copy-start | bytes 884740
  107.1 4.2 %copy-start.24 = (bf16[576,256]{1,0:T(8,128)(2,1)S(1)}, bf16[576,256]{1,0:T(8,128)(2,1)}, u32[]{:S(2)}) copy-start(bf16[576,256]{1,0:T(8,128)(2,1)} %get-tuple-element.61) | copy-start | bytes 884740
  107.1 4.2 %copy-start.26 = (bf16[576,256]{1,0:T(8,128)(2,1)S(1)}, bf16[576,256]{1,0:T(8,128)(2,1)}, u32[]{:S(2)}) copy-start(bf16[576,256]{1,0:T(8,128)(2,1)} %get-tuple-element.62) | copy-start | bytes 884740
  107.2 16.2 %copy-start.6 = (bf16[128,4096]{1,0:T(8,128)(2,1)}, bf16[128,4096]{1,0:T(8,128)(2,1)S(1)}, u32[]{:S(2)}) copy-start(bf16[128,4096]{1,0:T(8,128)(2,1)S(1)} %collective-permute-done.4.refs_0_.refs_12_) | copy-start | bytes 3145732
  107.2 16.2 %copy-start.7 = (bf16[128,4096]{1,0:T(8,128)(2,1)}, bf16[128,4096]{1,0:T(8,128)(2,1)S(1)}, u32[]{:S(2)}) copy-start(bf16[128,4096]{1,0:T(8,128)(2,1)S(1)} %collective-permute-done.5.refs_1_.refs_13_) | copy-start | bytes 3145732
  107.2 16.9 %collective-permute-start.18 = (bf16[4,128,1024]{2,1,0:T(8,128)(2,1)}, bf16[4,128,1024]{2,1,0:T(8,128)(2,1)S(1)}, u32[]{:S(2)}, u32[]{:S(2)}) collective-permute-start(bf16[4,128,1024]{2,1,0:T(8,128)(2,1)} %get-tuple-element.53), channel_id=1, source_target_pairs={{0,4},{4,0},{8,12},{12,8},{16,20},{20,16},{24,28},{28,24},{1,5},{5... | collective-permute-start | bytes 3145736 | tf_op jit(solution)/shard_map/ppermute | solution.py:22
  107.3 16.0 %collective-permute-start.17 = (bf16[128,1024]{1,0:T(8,128)(2,1)S(1)}, bf16[128,1024]{1,0:T(8,128)(2,1)S(1)}, u32[]{:S(2)}, u32[]{:S(2)}) collective-permute-start(bf16[128,1024]{1,0:T(8,128)(2,1)S(1)} %slice_bitcast_fusion.4), channel_id=1, source_target_pairs={{0,2},{1,3},{2,0},{3,1},{4,6},{5,7},{6,4},{7,5},{8,10},{9,11},{10,... | collective-permute-start | bytes 786440 | tf_op jit(solution)/shard_map/ppermute | solution.py:22
  110.7 15.1 %collective-permute-start.23 = (bf16[128,4096]{1,0:T(8,128)(2,1)S(1)}, bf16[128,4096]{1,0:T(8,128)(2,1)S(1)}, u32[]{:S(2)}, u32[]{:S(2)}) collective-permute-start(bf16[128,4096]{1,0:T(8,128)(2,1)S(1)} %collective-permute-done.4.refs_0_.refs_12_), channel_id=1, source_target_pairs={{0,4},{4,0},{8,12},{12,8},{16,20},{20,16},{24,28},{28,24},{1,5},{5... | collective-permute-start | bytes 3145736 | tf_op jit(solution)/shard_map/ppermute | solution.py:22
  111.0 14.9 %collective-permute-start.24 = (bf16[128,4096]{1,0:T(8,128)(2,1)S(1)}, bf16[128,4096]{1,0:T(8,128)(2,1)S(1)}, u32[]{:S(2)}, u32[]{:S(2)}) collective-permute-start(bf16[128,4096]{1,0:T(8,128)(2,1)S(1)} %collective-permute-done.5.refs_1_.refs_13_), channel_id=1, source_target_pairs={{0,4},{4,0},{8,12},{12,8},{16,20},{20,16},{24,28},{28,24},{1,5},{5... | collective-permute-start | bytes 3145736 | tf_op jit(solution)/shard_map/ppermute | solution.py:22
  111.3 12.8 %copy-start.14 = (bf16[4,128,1024]{2,1,0:T(8,128)(2,1)S(1)}, bf16[4,128,1024]{2,1,0:T(8,128)(2,1)}, u32[]{:S(2)}) copy-start(bf16[4,128,1024]{2,1,0:T(8,128)(2,1)} %get-tuple-element.52) | copy-start | bytes 3145732
  124.1 1.8 copy-start.15
  125.0 11.3 %copy-start.29 = (f32[1,256]{1,0:T(1,128)S(1)}, f32[1,256]{1,0:T(1,128)}, u32[]{:S(2)}) copy-start(f32[1,256]{1,0:T(1,128)} %get-tuple-element.39.refs_7_) | copy-start | bytes 3076
  125.0 11.3 %copy-start.31 = (f32[1,256]{1,0:T(1,128)S(1)}, f32[1,256]{1,0:T(1,128)}, u32[]{:S(2)}) copy-start(f32[1,256]{1,0:T(1,128)} %get-tuple-element.45.refs_7_) | copy-start | bytes 3076
  125.0 11.3 %copy-start.32 = (f32[1,256]{1,0:T(1,128)S(1)}, f32[1,256]{1,0:T(1,128)}, u32[]{:S(2)}) copy-start(f32[1,256]{1,0:T(1,128)} %get-tuple-element.56.refs_7_) | copy-start | bytes 3076
  125.0 12.0 %copy-start.28 = (s32[4,2]{0,1:T(2,128)S(1)}, s32[4,2]{0,1:T(2,128)}, u32[]{:S(2)}) copy-start(s32[4,2]{0,1:T(2,128)} %constant.78) | copy-start | bytes 100
  125.0 12.0 %copy-start.33 = (f32[4,64]{1,0:T(4,128)S(1)}, f32[4,64]{1,0:T(4,128)}, u32[]{:S(2)}) copy-start(f32[4,64]{1,0:T(4,128)} %custom-call.3) | copy-start | bytes 3076
  125.0 25.1 %collective-permute-start.19 = (bf16[2,128,1024]{2,1,0:T(8,128)(2,1)}, bf16[2,128,1024]{2,1,0:T(8,128)(2,1)}, u32[]{:S(2)}, u32[]{:S(2)}) collective-permute-start(bf16[2,128,1024]{2,1,0:T(8,128)(2,1)} %slice_add_fusion.2), channel_id=1, source_target_pairs={{0,1},{1,0},{2,3},{3,2},{4,5},{5,4},{6,7},{7,6},{8,9},{9,8},{10,11... | collective-permute-start | bytes 1572872 | tf_op jit(solution)/shard_map/ppermute | solution.py:22
  127.8 22.3 %copy-start.16 = (bf16[4,128,1024]{2,1,0:T(8,128)(2,1)S(1)}, bf16[4,128,1024]{2,1,0:T(8,128)(2,1)}, u32[]{:S(2)}) copy-start(bf16[4,128,1024]{2,1,0:T(8,128)(2,1)} %copy-done.15) | copy-start | bytes 3145732
  137.0 17.6 %collective-permute-start.25 = (bf16[4,128,1024]{2,1,0:T(8,128)(2,1)}, bf16[4,128,1024]{2,1,0:T(8,128)(2,1)}, u32[]{:S(2)}, u32[]{:S(2)}) collective-permute-start(bf16[4,128,1024]{2,1,0:T(8,128)(2,1)} %get-tuple-element.58), channel_id=1, source_target_pairs={{0,4},{4,0},{8,12},{12,8},{16,20},{20,16},{24,28},{28,24},{1,5},{5... | collective-permute-start | bytes 3145736 | tf_op jit(solution)/shard_map/ppermute | solution.py:22
  145.7 8.9 %copy-start.17 = (bf16[4,128,1024]{2,1,0:T(8,128)(2,1)S(1)}, bf16[4,128,1024]{2,1,0:T(8,128)(2,1)}, u32[]{:S(2)}) copy-start(bf16[4,128,1024]{2,1,0:T(8,128)(2,1)} %get-tuple-element.57) | copy-start | bytes 3145732
  145.7 11.2 %collective-permute-start.31 = (f32[8,128]{1,0:T(8,128)S(1)}, f32[8,128]{1,0:T(8,128)S(1)}, u32[]{:S(2)}, u32[]{:S(2)}) collective-permute-start(f32[8,128]{1,0:T(8,128)S(1)} %pad_maximum_fusion.5), channel_id=1, source_target_pairs={{0,3},{1,2},{2,1},{3,0},{4,7},{5,6},{6,5},{7,4},{8,11},{9,10},{10,... | collective-permute-start | bytes 12296 | tf_op jit(solution)/shard_map/ppermute | solution.py:22
  148.7 9.2 %collective-permute-start.30 = (f32[8,128]{1,0:T(8,128)S(1)}, f32[8,128]{1,0:T(8,128)S(1)}, u32[]{:S(2)}, u32[]{:S(2)}) collective-permute-start(f32[8,128]{1,0:T(8,128)S(1)} %pad_maximum_fusion.5), channel_id=1, source_target_pairs={{0,2},{1,3},{2,0},{3,1},{4,6},{5,7},{6,4},{7,5},{8,10},{9,11},{10,... | collective-permute-start | bytes 12296 | tf_op jit(solution)/shard_map/ppermute | solution.py:22
  149.2 8.7 %collective-permute-start.29 = (f32[8,128]{1,0:T(8,128)S(1)}, f32[8,128]{1,0:T(8,128)S(1)}, u32[]{:S(2)}, u32[]{:S(2)}) collective-permute-start(f32[8,128]{1,0:T(8,128)S(1)} %pad_maximum_fusion.5), channel_id=1, source_target_pairs={{0,1},{1,0},{2,3},{3,2},{4,5},{5,4},{6,7},{7,6},{8,9},{9,8},{10,11... | collective-permute-start | bytes 12296 | tf_op jit(solution)/shard_map/ppermute | solution.py:22
  151.4 5.4 %copy-start.25 = (bf16[576,256]{1,0:T(8,128)(2,1)S(1)}, bf16[576,256]{1,0:T(8,128)(2,1)}, u32[]{:S(2)}) copy-start(bf16[576,256]{1,0:T(8,128)(2,1)} %get-tuple-element.63) | copy-start | bytes 884740
  152.1 14.8 %collective-permute-start.20 = (bf16[128,1024]{1,0:T(8,128)(2,1)}, bf16[128,1024]{1,0:T(8,128)(2,1)}, u32[]{:S(2)}, u32[]{:S(2)}) collective-permute-start(bf16[128,1024]{1,0:T(8,128)(2,1)} %slice_bitcast_fusion.2), channel_id=1, source_target_pairs={{0,2},{1,3},{2,0},{3,1},{4,6},{5,7},{6,4},{7,5},{8,10},{9,11},{10,... | collective-permute-start | bytes 786440 | tf_op jit(solution)/shard_map/ppermute | solution.py:22
  155.7 18.1 %collective-permute-start.26 = (bf16[2,128,1024]{2,1,0:T(8,128)(2,1)S(1)}, bf16[2,128,1024]{2,1,0:T(8,128)(2,1)}, u32[]{:S(2)}, u32[]{:S(2)}) collective-permute-start(bf16[2,128,1024]{2,1,0:T(8,128)(2,1)S(1)} %slice_add_fusion), channel_id=1, source_target_pairs={{0,1},{1,0},{2,3},{3,2},{4,5},{5,4},{6,7},{7,6},{8,9},{9,8},{10,11... | collective-permute-start | bytes 1572872 | tf_op jit(solution)/shard_map/ppermute | solution.py:22
  156.9 18.4 %copy-start.12 = (bf16[576,1024]{1,0:T(8,128)(2,1)}, bf16[576,1024]{1,0:T(8,128)(2,1)S(1)}, u32[]{:S(2)}) copy-start(bf16[576,1024]{1,0:T(8,128)(2,1)S(1)} %constant_dynamic-update-slice_fusion.refs_16_) | copy-start | bytes 3538948
  156.9 42.7 %collective-permute-start.32 = (bf16[576,1024]{1,0:T(8,128)(2,1)S(1)}, bf16[576,1024]{1,0:T(8,128)(2,1)S(1)}, u32[]{:S(2)}, u32[]{:S(2)}) collective-permute-start(bf16[576,1024]{1,0:T(8,128)(2,1)S(1)} %constant_dynamic-update-slice_fusion.refs_16_), channel_id=1, source_target_pairs={{0,16},{4,20},{8,24},{12,28},{16,0},{20,4},{24,8},{28,12},{1,17},{... | collective-permute-start | bytes 3538952 | tf_op jit(solution)/shard_map/ppermute | solution.py:22
  167.9 7.5 %copy-start.22 = (bf16[64,1024]{1,0:T(8,128)(2,1)S(1)}, bf16[64,1024]{1,0:T(8,128)(2,1)}, u32[]{:S(2)}) copy-start(bf16[64,1024]{1,0:T(8,128)(2,1)} %get-tuple-element.90) | copy-start | bytes 393220
  175.3 15.3 %copy-start.35 = (pred[8]{0:T(512)(128)(4,1)S(1)}, pred[8]{0:T(512)(128)(4,1)}, u32[]{:S(2)}) copy-start(pred[8]{0:T(512)(128)(4,1)} %compare_and_fusion) | copy-start | bytes 28
  175.3 19.2 %copy-start.36 = (s32[4]{0:T(128)S(1)}, s32[4]{0:T(128)}, u32[]{:S(2)}) copy-start(s32[4]{0:T(128)} %param.16) | copy-start | bytes 52
  175.3 13.2 %collective-permute-start.27 = (bf16[128,1024]{1,0:T(8,128)(2,1)S(1)}, bf16[128,1024]{1,0:T(8,128)(2,1)S(1)}, u32[]{:S(2)}, u32[]{:S(2)}) collective-permute-start(bf16[128,1024]{1,0:T(8,128)(2,1)S(1)} %slice_bitcast_fusion), channel_id=1, source_target_pairs={{0,2},{1,3},{2,0},{3,1},{4,6},{5,7},{6,4},{7,5},{8,10},{9,11},{10,... | collective-permute-start | bytes 786440 | tf_op jit(solution)/shard_map/ppermute | solution.py:22
  175.5 39.9 %collective-permute-start.22 = (bf16[128,1024]{1,0:T(8,128)(2,1)S(1)}, bf16[128,1024]{1,0:T(8,128)(2,1)}, u32[]{:S(2)}, u32[]{:S(2)}) collective-permute-start(bf16[128,1024]{1,0:T(8,128)(2,1)S(1)} %pad_maximum_fusion.3), channel_id=1, source_target_pairs={{0,16},{4,20},{8,24},{12,28},{16,0},{20,4},{24,8},{28,12},{1,17},{... | collective-permute-start | bytes 786440 | tf_op jit(solution)/shard_map/ppermute | solution.py:22
  177.2 38.2 %collective-permute-start.21 = (bf16[128,1024]{1,0:T(8,128)(2,1)}, bf16[128,1024]{1,0:T(8,128)(2,1)S(1)}, u32[]{:S(2)}, u32[]{:S(2)}) collective-permute-start(bf16[128,1024]{1,0:T(8,128)(2,1)} %pad_maximum_fusion.2), channel_id=1, source_target_pairs={{0,8},{4,12},{8,0},{12,4},{16,24},{20,28},{24,16},{28,20},{1,9},{5... | collective-permute-start | bytes 786440 | tf_op jit(solution)/shard_map/ppermute | solution.py:22
  188.6 26.8 %collective-permute-start.28 = (bf16[128,1024]{1,0:T(8,128)(2,1)S(1)}, bf16[128,1024]{1,0:T(8,128)(2,1)S(1)}, u32[]{:S(2)}, u32[]{:S(2)}) collective-permute-start(bf16[128,1024]{1,0:T(8,128)(2,1)S(1)} %fusion.4), channel_id=1, source_target_pairs={{0,24},{4,28},{8,16},{12,20},{16,8},{20,12},{24,0},{28,4},{1,25},{... | collective-permute-start | bytes 786440 | tf_op jit(solution)/shard_map/ppermute | solution.py:22
  191.2 7.8 %all-to-all-start.1 = ((bf16[8,1,128]{2,1,0:T(2,128)(2,1)}), bf16[8,1,128]{2,1,0:T(2,128)(2,1)S(1)}, u32[]{:S(2)}, u32[]{:S(2)}) async-start(bf16[8,1,128]{2,1,0:T(2,128)(2,1)} %copy.22), calls=%async_computation.1 | async-start | bytes 8192 | tf_op jit(solution)/shard_map/all_to_all | solution.py:286
  200.6 14.7 %copy-start.10 = (f32[128,1024]{1,0:T(8,128)S(1)}, f32[128,1024]{1,0:T(8,128)}, u32[]{:S(2)}) copy-start(f32[128,1024]{1,0:T(8,128)} %convert_add_fusion.3) | copy-start | bytes 1572868
  (8 other events, 7.7 us)

commit v4 on v3

--- a/solution.py
+++ b/solution.py
@@ -31,11 +31,11 @@
     return (*range(0, parts, 2), *range(1, parts, 2))
 
 
-def activations_kernel(sources, parts, where_ref, gates_ref, *refs):
+def activations_kernel(parts, where_ref, one_ref, two_ref, *refs):
     messages = refs[:4]
     gate_ref, up_ref, down_ref = refs[4:7]
     acts_ref, score_ref, keep_ref, give_ref = refs[8:12]
-    x_all, dy_all, in_all, down_all, sems = refs[12:]
+    held, in_all, down_all, both, shares, sems, out_sems = refs[12:]
     rows, width = messages[0].shape
     half = rows // 2
     units = gate_ref.shape[0]
@@ -43,90 +43,96 @@
     copies = []
     for part in range(parts):
         columns = pl.ds(part * chunk, chunk)
-        everything = pl.ds(0, units)
-        moves = [(gate_ref, everything, in_all, 0, units), (up_ref, everything, in_all, units, units)]
-        moves.append((down_ref, everything, down_all, 0, units))
-        for i, ref in enumerate(messages):
-            moves.append((ref, pl.ds(0, half), x_all, i * half, half))
-            moves.append((ref, pl.ds(half, half), dy_all, i * half, half))
+        moves = [(ref, held.at[i, :, columns]) for i, ref in enumerate(messages)]
+        moves.append((gate_ref, in_all.at[pl.ds(0, units), columns]))
+        moves.append((up_ref, in_all.at[pl.ds(units, units), columns]))
+        moves.append((down_ref, down_all.at[:, columns]))
         copies.append(
             [
-                pltpu.make_async_copy(
-                    ref.at[place, columns], target.at[pl.ds(start, size), columns], sems.at[part, i]
-                )
-                for i, (ref, place, target, start, size) in enumerate(moves)
+                pltpu.make_async_copy(ref.at[:, columns], target, sems.at[part, i])
+                for i, (ref, target) in enumerate(moves)
             ]
         )
         for copy in copies[-1]:
             copy.start()
     me, group = where_ref[0], where_ref[1]
+    first = lax.broadcasted_iota(jnp.int32, (1, rows), 1) < half
+    experts = one_ref.shape[0] // 2
+    g = jnp.concatenate(
+        [
+            jnp.where(first, one_ref[pl.ds(me + core, 1), :], two_ref[pl.ds(me + core, 1), :])
+            for core in (0, experts)
+        ],
+        axis=1,
+    )
     pre, back = None, None
     for part in range(parts):
         for copy in copies[part]:
             copy.wait()
         columns = pl.ds(part * chunk, chunk)
-        one = lax.dot_general(
-            in_all[:, columns], x_all[:, columns], CONTRACT_LAST, preferred_element_type=jnp.float32
-        )
-        two = lax.dot_general(
-            down_all[:, columns], dy_all[:, columns], CONTRACT_LAST, preferred_element_type=jnp.float32
-        )
+        x = held[:, pl.ds(0, half), columns].reshape(2 * rows, chunk)
+        dy = held[:, pl.ds(half, half), columns].reshape(2 * rows, chunk)
+        one = lax.dot_general(in_all[:, columns], x, CONTRACT_LAST, preferred_element_type=jnp.float32)
+        two = lax.dot_general(down_all[:, columns], dy, CONTRACT_LAST, preferred_element_type=jnp.float32)
         pre = one if pre is None else pre + one
         back = two if back is None else back + two
     pre_gate, pre_up = pre[:units], pre[units:]
-    first = lax.broadcasted_iota(jnp.int32, (1, rows), 1) < half
-    g = jnp.concatenate(
-        [
-            jnp.where(first, gates_ref[pl.ds(me ^ one, 1), :], gates_ref[pl.ds(me ^ two, 1), :])
-            for one, two in (sources, (sources[0] ^ CORE, sources[1] ^ CORE))
-        ],
-        axis=1,
-    )
     sigma = jax.nn.sigmoid(pre_gate)
     active = pre_gate * sigma
     hidden = active * pre_up
     score_ref[...] = jnp.sum(hidden * back, axis=0, keepdims=True)
     grad_hidden = g * back
     slope = sigma * (1.0 + pre_gate * (1.0 - sigma))
-    acts_ref[pl.ds(0, units), :] = (grad_hidden * pre_up * slope).astype(jnp.bfloat16)
-    acts_ref[pl.ds(units, units), :] = (grad_hidden * active).astype(jnp.bfloat16)
+    grads = jnp.concatenate([grad_hidden * pre_up * slope, grad_hidden * active], axis=0)
+    acts_ref[pl.ds(0, 2 * units), :] = grads.astype(jnp.bfloat16)
     acts_ref[pl.ds(2 * units, units), :] = (g * hidden).astype(jnp.bfloat16)
-    both = acts_ref[pl.ds(0, 2 * units), :]
+    both[...] = grads.T.astype(jnp.bfloat16)
+    copies = []
     for place, part in enumerate(part_order(parts)):
         columns = pl.ds(pl.multiple_of((group ^ part) * chunk, chunk), chunk)
-        share = lax.dot_general(both, in_all[:, columns], CONTRACT_ROWS, preferred_element_type=jnp.float32)
-        share = share.astype(jnp.bfloat16)
-        keep_ref[place] = share[:rows]
-        give_ref[place] = share[rows:]
-
-
-def activations(sources, parts, where, gates, messages, weights, before):
+        share = jnp.dot(both[...], in_all[:, columns], preferred_element_type=jnp.float32)
+        shares[place] = share.astype(jnp.bfloat16)
+        for i, ref in enumerate((keep_ref, give_ref)):
+            copies.append(
+                pltpu.make_async_copy(
+                    shares.at[place, pl.ds(i * rows, rows), :], ref.at[place], out_sems.at[place, i]
+                )
+            )
+            copies[-1].start()
+    for copy in copies:
+        copy.wait()
+
+
+def activations(parts, where, tables, messages, weights, before):
     rows, width = messages[0].shape
     units = weights[0].shape[0]
     bf16 = jnp.bfloat16
     share = jax.ShapeDtypeStruct((parts, rows, width // parts), bf16)
     return pl.pallas_call(
-        functools.partial(activations_kernel, sources, parts),
+        functools.partial(activations_kernel, parts),
         out_shape=(
             jax.ShapeDtypeStruct((3 * units, 2 * rows), bf16),
             jax.ShapeDtypeStruct((1, 2 * rows), jnp.float32),
             share,
             share,
         ),
-        in_specs=[pl.BlockSpec(memory_space=pltpu.SMEM), pl.BlockSpec(memory_space=pltpu.VMEM)]
+        in_specs=[pl.BlockSpec(memory_space=pltpu.SMEM)]
+        + [pl.BlockSpec(memory_space=pltpu.VMEM)] * 2
         + [pl.BlockSpec(memory_space=pl.ANY)] * 8,
-        out_specs=[pl.BlockSpec(memory_space=pltpu.VMEM)] * 4,
+        out_specs=[pl.BlockSpec(memory_space=pltpu.VMEM)] * 2 + [pl.BlockSpec(memory_space=pl.ANY)] * 2,
         scratch_shapes=[
-            pltpu.VMEM((2 * rows, width), bf16),
-            pltpu.VMEM((2 * rows, width), bf16),
+            pltpu.VMEM((4, rows, width), bf16),
             pltpu.VMEM((2 * units, width), bf16),
             pltpu.VMEM((units, width), bf16),
-            pltpu.SemaphoreType.DMA((parts, 11)),
+            pltpu.VMEM((2 * rows, 2 * units), bf16),
+            pltpu.VMEM((parts, 2 * rows, width // parts), bf16),
+            pltpu.SemaphoreType.DMA((parts, 7)),
+            pltpu.SemaphoreType.DMA((parts, 2)),
         ],
         compiler_params=pltpu.CompilerParams(vmem_limit_bytes=VMEM),
         cost_estimate=pl.CostEstimate(flops=1, bytes_accessed=1, transcendentals=0),
         name="activations",
-    )(where, gates, *messages, *weights, before)
+    )(where, *tables, *messages, *weights, before)
 
 
 def weight_grads_kernel(sources, parts, flag_ref, *refs):
@@ -134,7 +140,7 @@
     messages = refs[:count]
     own_ref, other_ref = refs[count : count + 2]
     outs = refs[count + 2 : count + 5]
-    x_all, dy_all, acts, sems = refs[count + 5 :]
+    held, acts, results, sems, out_sems = refs[count + 5 :]
     rows, width = messages[0].shape
     half = rows // 2
     units = outs[0].shape[1]
@@ -142,16 +148,12 @@
     copies = []
     for part in range(parts):
         columns = pl.ds(part * chunk, chunk)
-        copies.append([])
-        for i, ref in enumerate(messages):
-            for start, target in ((0, x_all), (half, dy_all)):
-                copies[-1].append(
-                    pltpu.make_async_copy(
-                        ref.at[pl.ds(start, half), columns],
-                        target.at[pl.ds(i * half, half), columns],
-                        sems.at[part, len(copies[-1])],
-                    )
-                )
+        copies.append(
+            [
+                pltpu.make_async_copy(ref.at[:, columns], held.at[i, :, columns], sems.at[part, i])
+                for i, ref in enumerate(messages)
+            ]
+        )
         for copy in copies[-1]:
             copy.start()
     tiles = [(one ^ core, two ^ core) for one, two in sources for core in (0, CORE)]
@@ -164,19 +166,30 @@
         )
         stay = own_ref[:, pl.ds(place * rows, rows)]
         acts[:, pl.ds(place * rows, rows)] = jnp.where(flag_ref[0] == 1, arrived, stay)
+    sent = []
     for part in range(parts):
         for copy in copies[part]:
             copy.wait()
         columns = pl.ds(part * chunk, chunk)
-        both = jnp.dot(acts[pl.ds(0, 2 * units), :], x_all[:, columns], preferred_element_type=jnp.float32)
-        down = jnp.dot(acts[pl.ds(2 * units, units), :], dy_all[:, columns], preferred_element_type=jnp.float32)
-        outs[0][0, :, columns] = both[:units].astype(jnp.bfloat16)
-        outs[1][0, :, columns] = both[units:].astype(jnp.bfloat16)
-        outs[2][0, :, columns] = down.astype(jnp.bfloat16)
+        x = held[:, pl.ds(0, half), columns].reshape(count * half, chunk)
+        dy = held[:, pl.ds(half, half), columns].reshape(count * half, chunk)
+        both = jnp.dot(acts[pl.ds(0, 2 * units), :], x, preferred_element_type=jnp.float32)
+        results[part, pl.ds(0, 2 * units), :] = both.astype(jnp.bfloat16)
+        down = jnp.dot(acts[pl.ds(2 * units, units), :], dy, preferred_element_type=jnp.float32)
+        results[part, pl.ds(2 * units, units), :] = down.astype(jnp.bfloat16)
+        for i, out in enumerate(outs):
+            sent.append(
+                pltpu.make_async_copy(
+                    results.at[part, pl.ds(i * units, units), :], out.at[0, :, columns], out_sems.at[part, i]
+                )
+            )
+            sent[-1].start()
+    for copy in sent:
+        copy.wait()
 
 
 def weight_grads(sources, flag, messages, own, other):
-    parts = 8
+    parts = 4
     rows, width = messages[0].shape
     units = own.shape[0] // 3
     total = len(messages) * rows // 2
@@ -187,12 +200,13 @@
         in_specs=[pl.BlockSpec(memory_space=pltpu.SMEM)]
         + [pl.BlockSpec(memory_space=pl.ANY)] * len(messages)
         + [pl.BlockSpec(memory_space=pltpu.VMEM)] * 2,
-        out_specs=[pl.BlockSpec(memory_space=pltpu.VMEM)] * 3,
+        out_specs=[pl.BlockSpec(memory_space=pl.ANY)] * 3,
         scratch_shapes=[
-            pltpu.VMEM((total, width), bf16),
-            pltpu.VMEM((total, width), bf16),
+            pltpu.VMEM((len(messages), rows, width), bf16),
             pltpu.VMEM((3 * units, total), bf16),
-            pltpu.SemaphoreType.DMA((parts, 2 * len(messages))),
+            pltpu.VMEM((parts, 3 * units, width // parts), bf16),
+            pltpu.SemaphoreType.DMA((parts, len(messages))),
+            pltpu.SemaphoreType.DMA((parts, 3)),
         ],
         compiler_params=pltpu.CompilerParams(vmem_limit_bytes=VMEM),
         cost_estimate=pl.CostEstimate(flops=1, bytes_accessed=1, transcendentals=0),
@@ -225,65 +239,75 @@
 
     named = expert_ids[:, :, None] == jnp.arange(expert_count, dtype=jnp.int32)[None, None, :]
     table = jnp.sum(jnp.where(named, gates[:, :, None].astype(f32), 0), axis=1)
-    gate_rows = lax.all_to_all(table.T, "expert", split_axis=0, concat_axis=0, tiled=True)
+    tables = {0: jnp.concatenate([table.T, expert_swap(table.T, CORE)])}
+    tables[2], tables[4] = expert_swap(tables[0], ACROSS_X), expert_swap(tables[0], ACROSS_Y)
 
     acts, scores, messages = [], [], []
 
     def work(one, two, before):
         held = [a[one], b[two], a[one ^ CORE], b[two ^ CORE]]
-        act, score, keep, give = activations((one, two), parts, where, gate_rows, held, weights, before)
+        act, score, keep, give = activations(
+            parts, where, (tables[one], tables[two]), held, weights, before
+        )
         acts.append(act)
         scores.append(score)
         messages.extend(held)
         return score, keep, expert_swap(give, CORE)
 
-    def near_sum(keep, given):
+    def to_neighbour(keep, given):
         far = keep[parts // 2 :] + given[parts // 2 :]
-        near = keep[: parts // 2] + given[: parts // 2]
-        return near + swap(far, "dp", 1)
-
-    def far_sum(near):
-        return near[0].astype(f32) + swap(near[1], "dp", 2).astype(f32)
+        return keep[: parts // 2] + given[: parts // 2], swap(far, "dp", 1)
+
+    def to_far(near, arrived):
+        near = near + arrived
+        return near[0].astype(f32), swap(near[1], "dp", 2)
+
+    barrier = lax.optimization_barrier
 
     done_a, *share_a = work(0, 0, where)
-    a[2], b[4], done_a = lax.optimization_barrier((a[2], b[4], done_a))
+    a[2], b[4], tables[2], tables[4], done_a = barrier((a[2], b[4], tables[2], tables[4], done_a))
     a[6], b[6] = expert_swap(a[2], ACROSS_Y), expert_swap(b[4], ACROSS_X)
+    tables[6] = expert_swap(tables[2], ACROSS_Y)
     a[3], b[5] = expert_swap(a[2], CORE), expert_swap(b[4], CORE)
     done_b, *share_b = work(2, 4, done_a)
-    near_a = near_sum(*share_a)
-    a[4], b[2], done_b, near_a = lax.optimization_barrier((a[4], b[2], done_b, near_a))
+    near_a, near_in_a = to_neighbour(*share_a)
+    a[4], b[2], done_b, near_in_a = barrier((a[4], b[2], done_b, near_in_a))
     a[5], b[3] = expert_swap(a[4], CORE), expert_swap(b[2], CORE)
     done_c, *share_c = work(4, 2, done_b)
-    total_a, near_b = far_sum(near_a), near_sum(*share_b)
-    a[6], b[6], done_c, total_a, near_b = lax.optimization_barrier((a[6], b[6], done_c, total_a, near_b))
+    total_a, far_in_a = to_far(near_a, near_in_a)
+    near_b, near_in_b = to_neighbour(*share_b)
+    a[6], b[6], done_c, far_in_a, near_in_b = barrier((a[6], b[6], done_c, far_in_a, near_in_b))
     a[7], b[7] = expert_swap(a[6], CORE), expert_swap(b[6], CORE)
-    total_b, near_c = far_sum(near_b), near_sum(*share_c)
-    _, *share_d = work(6, 6, done_c)
-    total_c, total_d = far_sum(near_c), far_sum(near_sum(*share_d))
-    totals = (total_a, total_b, total_c, total_d)
-
-    to_x = jnp.concatenate([totals[1][:half], totals[2][half:]]).astype(bf16)
-    to_y = jnp.concatenate([totals[2][:half], totals[1][half:]]).astype(bf16)
-    input_grad = totals[0] + expert_swap(to_x, ACROSS_X).astype(f32) + expert_swap(to_y, ACROSS_Y).astype(f32)
-    input_grad = input_grad + expert_swap(totals[3].astype(bf16), ACROSS_X | ACROSS_Y).astype(f32)
+    done_d, *share_d = work(6, 6, done_c)
+    total_b, far_in_b = to_far(near_b, near_in_b)
+    near_c, near_in_c = to_neighbour(*share_c)
+    done_d, far_in_b, near_in_c = barrier((done_d, far_in_b, near_in_c))
+    scores[-1] = done_d
+    total_c, far_in_c = to_far(near_c, near_in_c)
+    near_d, near_in_d = to_neighbour(*share_d)
 
     sources = ((0, 0), (2, 4), (4, 2), (6, 6))
     own = jnp.concatenate(acts, axis=1)
-    grads = weight_grads(sources, own_flag, messages, own, expert_swap(own, half_axis))
+    other = expert_swap(own, half_axis)
 
     tiles = jnp.concatenate(scores, axis=1).reshape(expert_count, 2 * half)
-    score_rows = jnp.concatenate(
-        [
-            tiles[:2],
-            jnp.concatenate([tiles[2:6, :half], tiles[jnp.array([4, 5, 2, 3]), half:]], axis=1),
-            tiles[6:],
-        ]
-    )
-    summed = score_rows
-    for part in range(1, parts):
-        summed = summed + swap(score_rows, "dp", part)
+    second = jnp.concatenate([tiles[:2, half:], tiles[4:6, half:], tiles[2:4, half:], tiles[6:, half:]])
+    score_rows = jnp.concatenate([tiles[:, :half], second], axis=1)
+    summed = score_rows + swap(score_rows, "dp", 1)
+    summed, near_in_d, far_in_c = barrier((summed, near_in_d, far_in_c))
+    summed = summed + swap(summed, "dp", 2)
     score_rows = jnp.take(summed.astype(bf16), jnp.arange(expert_count, dtype=jnp.int32) ^ me, axis=0)
     score_rows = lax.all_to_all(score_rows, "expert", split_axis=0, concat_axis=0, tiled=True)
+    total_d, far_in_d = to_far(near_d, near_in_d)
+    score_rows, far_in_d, own_flag = barrier((score_rows, far_in_d, own_flag))
+    total_a, total_b = total_a + far_in_a.astype(f32), total_b + far_in_b.astype(f32)
+    total_c, total_d = total_c + far_in_c.astype(f32), (total_d + far_in_d.astype(f32)).astype(bf16)
+    grads = weight_grads(sources, own_flag, messages, own, other)
+
+    to_x = jnp.concatenate([total_b[:half], total_c[half:]]).astype(bf16)
+    to_y = jnp.concatenate([total_c[:half], total_b[half:]]).astype(bf16)
+    input_grad = total_a + expert_swap(to_x, ACROSS_X).astype(f32) + expert_swap(to_y, ACROSS_Y).astype(f32)
+    input_grad = input_grad + expert_swap(total_d, ACROSS_X | ACROSS_Y).astype(f32)
     gate_grad = jnp.sum(jnp.where(named, score_rows.T[:, None, :].astype(f32), 0), axis=2)
     return (input_grad.astype(bf16), gate_grad.astype(bf16), *grads)
 

time: 218 us -> 168 us (0.77)
  waiting for transfers between devices: 91.8 us -> 55.2 us
  starting transfers between devices: 41.1 us -> 36.3 us
  other arithmetic: 17.1 us -> 13.6 us
  local copies, waits for them, and re-layouts: 18.1 us -> 14.8 us
    all_to_all x1 -> x0, waiting for transfers between devices: 19 us -> none  [whole_shards(): lax.all_to_all(table.T, 'expert', split_axis=0, concat_axis=0, tiled=True)]
    ppermute x33 -> x36, waiting for transfers between devices: 69 us -> 53.4 us  [swap(): lax.ppermute(value, axis, [(i, i ^ by) for i in range(lax.axis_size(axis))])]
    gather x16 -> x0, local copies, waits for them, and re-layouts: 7.97 us -> none
    unnamed x77 -> x86, local copies, waits for them, and re-layouts: 5.85 us -> 9.29 us
    all_to_all x1 -> x0, starting transfers between devices: 3.31 us -> none  [whole_shards(): lax.all_to_all(table.T, 'expert', split_axis=0, concat_axis=0, tiled=True)]
    pallas_call x1, Pallas kernels: 14.7 us -> 11.9 us  [weight_grads(): pl.pallas_call(functools.partial(weight_grads_kernel, sources, parts), ou...]
    add x9, other arithmetic: 8.82 us -> 6.36 us  [the longest x4 3.85 us: to_far(): near = near + arrived]
    ppermute x33 -> x36, starting transfers between devices: 34.5 us -> 32.8 us  [swap(): lax.ppermute(value, axis, [(i, i ^ by) for i in range(lax.axis_size(axis))])]
  transfers between devices with their start and end apart: 35 -> 37, of which waited for: 11 -> 11; matrix products, arithmetic and copies ran while one was open for 12% -> 10% of each run, Pallas kernels for 22% -> 28%
where the time goes in v4:
time: 168 us; the launch traced here: 167 us
  waiting for transfers between devices  55.2 us (33%)
  Pallas kernels  46 us (27%)
  starting transfers between devices  36.3 us (22%)
  local copies, waits for them, and re-layouts  14.8 us (9%)
  other arithmetic  13.6 us (8%)
    ppermute x36, waiting for transfers between devices, swap(): lax.ppermute(value, axis, [(i, i ^ by) for i in range(lax.axis_size(axis))])  53.4 us
    pallas_call x4, Pallas kernels, activations(): pl.pallas_call(functools.partial(activations_kernel, parts), out_shape=(j...  34.1 us
    ppermute x36, starting transfers between devices, swap(): lax.ppermute(value, axis, [(i, i ^ by) for i in range(lax.axis_size(axis))])  32.8 us
    pallas_call x1, Pallas kernels, weight_grads(): pl.pallas_call(functools.partial(weight_grads_kernel, sources, parts), ou...  11.9 us
    unnamed x86, local copies, waits for them, and re-layouts  9.29 us
    add x4, other arithmetic, to_far(): near = near + arrived  3.85 us
    all_to_all x1, starting transfers between devices, whole_shards(): lax.all_to_all(score_rows, 'expert', split_axis=0, concat_axis=0, tiled=T...  3.54 us
  transfers between devices with their start and end apart: 37, of which 11 were waited for; matrix products, arithmetic and copies ran while one was open for 10% of the time, Pallas kernels for 28%

profile of v4, /device:TPU:0, one launch (start us, length us, event | category | flops | bytes accessed | tf_op | source)
XLA Modules:
  0.0 167.2 jit_solution(13788119143747032552)
XLA Ops:
  0.6 1.7 fusion.13
  2.4 0.5 collective-permute-start.1
  3.2 2.9 %collective-permute-start.6 = (bf16[128,4096]{1,0:T(8,128)(2,1)S(1)}, bf16[128,4096]{1,0:T(8,128)(2,1)}, u32[]{:S(2)}, u32[]{:S(2)}) collective-permute-start(bf16[128,4096]{1,0:T(8,128)(2,1)S(1)} %pad_maximum_fusion.refs_0_), channel_id=1, source_target_pairs={{0,8},{4,12},{8,0},{12,4},{16,24},{20,28},{24,16},{28,20},{1,9},{5... | collective-permute-start | bytes 3145736 | tf_op jit(solution)/shard_map/ppermute | solution.py:22
  6.1 1.5 collective-permute-start.7
  7.7 0.6 pad_add_fusion.where_ref.refs_7_
  8.3 0.6 collective-permute-done
  8.9 0.6 pad_maximum_fusion.4.one_ref.two_ref
  9.5 1.0 copy-done.2
  10.5 8.6 %activations.4 = (bf16[576,256]{1,0:T(8,128)(2,1)}, f32[1,256]{1,0:T(1,128)}, bf16[4,128,1024]{2,1,0:T(8,128)(2,1)}, bf16[4,128,1024]{2,1,0:T(8,128)(2,1)}) custom-call(s32[2]{0:T(128)} %pad_add_fusion.where_ref.refs_7_, f32[16,128]{1,0:T(8,128)} %pad_maximum_fusion.4.one_ref.two_ref, f32[16,128]{1,0:T(8,128)} %pad_maximum_fusion.4.one_ref.two_ref, ...), custom_call_target="tpu_custom_call" | custom-call | flops 1 | bytes 1 | tf_op jit(solution)/shard_map/activations/pallas_call | solution.py:111
  19.4 0.7 collective-permute-start.9
  20.1 11.1 %collective-permute-done.9.two_ref.one_ref = f32[16,128]{1,0:T(8,128)S(1)} collective-permute-done((f32[16,128]{1,0:T(8,128)S(1)}, f32[16,128]{1,0:T(8,128)S(1)}, u32[]{:S(2)}, u32[]{:S(2)}) %collective-permute-start.9) | collective-permute-done | bytes 8224 | tf_op jit(solution)/shard_map/ppermute | solution.py:22
  31.8 1.5 collective-permute-start.4
  33.3 0.5 collective-permute-start.5
  33.8 1.5 slice_add_fusion.6
  35.3 1.6 collective-permute-start.12
  37.0 1.0 copy-done.3
  37.9 1.0 copy-done.4
  38.9 8.5 %activations.5 = (bf16[576,256]{1,0:T(8,128)(2,1)}, f32[1,256]{1,0:T(1,128)}, bf16[4,128,1024]{2,1,0:T(8,128)(2,1)}, bf16[4,128,1024]{2,1,0:T(8,128)(2,1)}) custom-call(s32[2]{0:T(128)} %pad_add_fusion.where_ref.refs_7_, f32[16,128]{1,0:T(8,128)} %copy-done.30, f32[16,128]{1,0:T(8,128)} %copy-done.32, ...), custom_call_target="tpu_custom_call" | custom-call | flops 1 | bytes 1 | tf_op jit(solution)/shard_map/activations/pallas_call | solution.py:111
  47.5 9.6 %collective-permute-done.4.refs_0_.refs_8_ = bf16[128,4096]{1,0:T(8,128)(2,1)S(1)} collective-permute-done((bf16[128,4096]{1,0:T(8,128)(2,1)}, bf16[128,4096]{1,0:T(8,128)(2,1)S(1)}, u32[]{:S(2)}, u32[]{:S(2)}) %collective-permute-start.4) | collective-permute-done | bytes 1048608 | tf_op jit(solution)/shard_map/ppermute | solution.py:22
  57.1 1.2 collective-permute-done.5.refs_1_.refs_9_
  58.9 0.5 collective-permute-start.13
  59.8 1.4 fusion.3
  61.2 0.9 slice_add_fusion.5
  62.2 1.8 %collective-permute-start.19 = (bf16[2,128,1024]{2,1,0:T(8,128)(2,1)}, bf16[2,128,1024]{2,1,0:T(8,128)(2,1)S(1)}, u32[]{:S(2)}, u32[]{:S(2)}) collective-permute-start(bf16[2,128,1024]{2,1,0:T(8,128)(2,1)} %slice_add_fusion.5), channel_id=1, source_target_pairs={{0,1},{1,0},{2,3},{3,2},{4,5},{5,4},{6,7},{7,6},{8,9},{9,8},{10,11... | collective-permute-start | bytes 1572872 | tf_op jit(solution)/shard_map/ppermute | solution.py:22
  64.0 1.0 copy-done.7
  65.0 1.0 copy-done.8
  66.0 8.5 %activations.6 = (bf16[576,256]{1,0:T(8,128)(2,1)}, f32[1,256]{1,0:T(1,128)}, bf16[4,128,1024]{2,1,0:T(8,128)(2,1)}, bf16[4,128,1024]{2,1,0:T(8,128)(2,1)}) custom-call(s32[2]{0:T(128)} %pad_add_fusion.where_ref.refs_7_, f32[16,128]{1,0:T(8,128)} %copy-done.32, f32[16,128]{1,0:T(8,128)} %copy-done.30, bf16[128,4096]{1,0:T(8,128)(2,1)} %copy-done.5, ...), custom_call_target="tpu_custom_call" | custom-call | flops 1 | bytes 1 | tf_op jit(solution)/shard_map/activations/pallas_call | solution.py:111
  74.6 2.7 %collective-permute-start.17 = (bf16[128,1024]{1,0:T(8,128)(2,1)S(1)}, bf16[128,1024]{1,0:T(8,128)(2,1)S(1)}, u32[]{:S(2)}, u32[]{:S(2)}) collective-permute-start(bf16[128,1024]{1,0:T(8,128)(2,1)S(1)} %slice_bitcast_fusion.6), channel_id=1, source_target_pairs={{0,2},{1,3},{2,0},{3,1},{4,6},{5,7},{6,4},{7,5},{8,10},{9,11},{10,... | collective-permute-start | bytes 786440 | tf_op jit(solution)/shard_map/ppermute | solution.py:22
  77.3 0.6 fusion.11
  77.9 6.3 %collective-permute-done.13.refs_0_.refs_12_ = bf16[128,4096]{1,0:T(8,128)(2,1)S(1)} collective-permute-done((bf16[128,4096]{1,0:T(8,128)(2,1)}, bf16[128,4096]{1,0:T(8,128)(2,1)S(1)}, u32[]{:S(2)}, u32[]{:S(2)}) %collective-permute-start.13) | collective-permute-done | bytes 1048608 | tf_op jit(solution)/shard_map/ppermute | solution.py:22
  84.4 5.3 %collective-permute-done.17 = bf16[128,1024]{1,0:T(8,128)(2,1)S(1)} collective-permute-done((bf16[128,1024]{1,0:T(8,128)(2,1)S(1)}, bf16[128,1024]{1,0:T(8,128)(2,1)S(1)}, u32[]{:S(2)}, u32[]{:S(2)}) %collective-permute-start.17) | collective-permute-done | bytes 262176 | tf_op jit(solution)/shard_map/ppermute | solution.py:22
  90.3 1.6 collective-permute-start.20
  92.0 1.2 fusion.2
  93.5 0.8 slice_bitcast_fusion.4
  94.3 3.0 %collective-permute-start.23 = (bf16[128,1024]{1,0:T(8,128)(2,1)}, bf16[128,1024]{1,0:T(8,128)(2,1)S(1)}, u32[]{:S(2)}, u32[]{:S(2)}) collective-permute-start(bf16[128,1024]{1,0:T(8,128)(2,1)} %slice_bitcast_fusion.4), channel_id=1, source_target_pairs={{0,2},{1,3},{2,0},{3,1},{4,6},{5,7},{6,4},{7,5},{8,10},{9,11},{10,... | collective-permute-start | bytes 786440 | tf_op jit(solution)/shard_map/ppermute | solution.py:22
  97.4 0.6 copy-done.33
  98.4 1.0 copy-done.12
  99.4 8.6 %activations.7 = (bf16[576,256]{1,0:T(8,128)(2,1)}, f32[1,256]{1,0:T(1,128)}, bf16[4,128,1024]{2,1,0:T(8,128)(2,1)}, bf16[4,128,1024]{2,1,0:T(8,128)(2,1)}) custom-call(s32[2]{0:T(128)} %pad_add_fusion.where_ref.refs_7_, f32[16,128]{1,0:T(8,128)} %copy-done.33, f32[16,128]{1,0:T(8,128)} %copy-done.33, bf16[128,4096]{1,0:T(8,128)(2,1)} %copy-done.9, ...), custom_call_target="tpu_custom_call" | custom-call | flops 1 | bytes 1 | tf_op jit(solution)/shard_map/activations/pallas_call | solution.py:111
  108.0 1.1 constant_dynamic-update-slice_fusion.1
  109.1 1.0 constant_dynamic-update-slice_fusion.refs_16_
  110.1 0.6 collective-permute-start.35
  110.7 2.1 %collective-permute-done.25 = bf16[2,128,1024]{2,1,0:T(8,128)(2,1)} collective-permute-done((bf16[2,128,1024]{2,1,0:T(8,128)(2,1)S(1)}, bf16[2,128,1024]{2,1,0:T(8,128)(2,1)}, u32[]{:S(2)}, u32[]{:S(2)}) %collective-permute-start.25) | collective-permute-done | bytes 524320 | tf_op jit(solution)/shard_map/ppermute | solution.py:22
  112.8 1.1 fusion.1
  114.0 1.2 collective-permute-start.29
  115.3 2.1 %collective-permute-start.28 = (bf16[2,128,1024]{2,1,0:T(8,128)(2,1)S(1)}, bf16[2,128,1024]{2,1,0:T(8,128)(2,1)S(1)}, u32[]{:S(2)}, u32[]{:S(2)}) collective-permute-start(bf16[2,128,1024]{2,1,0:T(8,128)(2,1)S(1)} %slice_add_fusion.1), channel_id=1, source_target_pairs={{0,1},{1,0},{2,3},{3,2},{4,5},{5,4},{6,7},{7,6},{8,9},{9,8},{10,11... | collective-permute-start | bytes 1572872 | tf_op jit(solution)/shard_map/ppermute | solution.py:22
  117.7 15.7 %collective-permute-done.26 = f32[8,128]{1,0:T(8,128)S(1)} collective-permute-done((f32[8,128]{1,0:T(8,128)S(1)}, f32[8,128]{1,0:T(8,128)S(1)}, u32[]{:S(2)}, u32[]{:S(2)}) %collective-permute-start.26) | collective-permute-done | bytes 4128 | tf_op jit(solution)/shard_map/ppermute | solution.py:22
  133.5 1.7 %collective-permute-start.32 = (f32[8,128]{1,0:T(8,128)S(1)}, f32[8,128]{1,0:T(8,128)S(1)}, u32[]{:S(2)}, u32[]{:S(2)}) collective-permute-start(f32[8,128]{1,0:T(8,128)S(1)} %add.95), channel_id=1, source_target_pairs={{0,2},{1,3},{2,0},{3,1},{4,6},{5,7},{6,4},{7,5},{8,10},{9,11},{10,... | collective-permute-start | bytes 12296 | tf_op jit(solution)/shard_map/ppermute | solution.py:22
  135.3 0.7 slice_bitcast_fusion
  136.0 1.2 collective-permute-start.33
  137.3 0.7 pad_maximum_fusion.3
  138.0 0.7 collective-permute-start.31
  138.7 0.6 gather_fusion
  139.4 0.6 copy.24
  140.0 3.5 %all-to-all-start = ((bf16[8,1,128]{2,1,0:T(2,128)(2,1)}), bf16[8,1,128]{2,1,0:T(2,128)(2,1)S(1)}, u32[]{:S(2)}, u32[]{:S(2)}) async-start(bf16[8,1,128]{2,1,0:T(2,128)(2,1)} %copy.24), calls=%async_computation | async-start | bytes 8192 | tf_op jit(solution)/shard_map/all_to_all | solution.py:300
  143.5 0.7 pad_maximum_fusion.2
  144.2 2.0 %collective-permute-start.30 = (bf16[128,1024]{1,0:T(8,128)(2,1)}, bf16[128,1024]{1,0:T(8,128)(2,1)S(1)}, u32[]{:S(2)}, u32[]{:S(2)}) collective-permute-start(bf16[128,1024]{1,0:T(8,128)(2,1)} %pad_maximum_fusion.2), channel_id=1, source_target_pairs={{0,8},{4,12},{8,0},{12,4},{16,24},{20,28},{24,16},{28,20},{1,9},{5... | collective-permute-start | bytes 786440 | tf_op jit(solution)/shard_map/ppermute | solution.py:22
  146.3 1.8 %all-to-all-done = bf16[8,1,128]{2,1,0:T(2,128)(2,1)S(1)} async-done(((bf16[8,1,128]{2,1,0:T(2,128)(2,1)}), bf16[8,1,128]{2,1,0:T(2,128)(2,1)S(1)}, u32[]{:S(2)}, u32[]{:S(2)}) %all-to-all-start) | async-done | bytes 2080 | tf_op jit(solution)/shard_map/all_to_all | solution.py:300
  148.1 1.1 collective-permute-done.33
  149.2 1.0 fusion.4
  150.3 1.5 collective-permute-start.34
  151.8 1.0 copy-done.16
  152.8 11.9 %weight_grads.1 = (bf16[1,192,4096]{2,1,0:T(8,128)(2,1)}, bf16[1,192,4096]{2,1,0:T(8,128)(2,1)}, bf16[1,192,4096]{2,1,0:T(8,128)(2,1)}) custom-call(s32[1]{0:T(128)} %bitcast.19.flag_ref, bf16[128,4096]{1,0:T(8,128)(2,1)} %copy-done, bf16[128,4096]{1,0:T(8,128)(2,1)} %copy-done.1, bf16[128,4096]{1,0:T(8,128)(2,1)} %copy-done.2, ...), custom_call_target="tpu_custom_call" | custom-call | flops 1 | bytes 1 | tf_op jit(solution)/shard_map/weight_grads/pallas_call | solution.py:197
  164.8 0.6 select_reduce_fusion
  165.4 1.9 %fusion.10 = bf16[128,1024]{1,0:T(8,128)(2,1)} fusion(bf16[128,1024]{1,0:T(8,128)(2,1)S(1)} %collective-permute-done.34, bf16[128,1024]{1,0:T(8,128)(2,1)} %collective-permute-done.31, bf16[128,1024]{1,0:T(8,128)(2,1)S(1)} %collective-permute-done.30, bf16[128,1024]{1,0:T(8,128)(2,1)S(1)} %copy-done.28, bf16[2,128,1024]{2,1,0:T(8,128)(2,1)S(1)} %copy-done.14), kind=kLoop, calls=%fused_computation.25 | loop fusion | flops 1310720 | bytes 1572864 | tf_op jit(solution)/shard_map/convert_element_type | solution.py:312
  (143 shorter events, 4.5 us)
Async XLA Ops:
  2.4 7.1 %copy-start = (bf16[128,4096]{1,0:T(8,128)(2,1)}, bf16[128,4096]{1,0:T(8,128)(2,1)S(1)}, u32[]{:S(2)}) copy-start(bf16[128,4096]{1,0:T(8,128)(2,1)S(1)} %pad_maximum_fusion.refs_0_) | copy-start | bytes 3145732
  2.4 5.2 %copy-start.38 = (bf16[128,4]{0,1:T(4,128)(2,1)S(1)}, bf16[128,4]{0,1:T(4,128)(2,1)}, u32[]{:S(2)}) copy-start(bf16[128,4]{0,1:T(4,128)(2,1)} %param.14) | copy-start | bytes 3076
  2.4 5.2 %copy-start.34 = (s32[128,4]{0,1:T(4,128)S(1)}, s32[128,4]{0,1:T(4,128)}, u32[]{:S(2)}) copy-start(s32[128,4]{0,1:T(4,128)} %param.13) | copy-start | bytes 6148
  2.4 7.1 %collective-permute-start.1 = (bf16[128,4096]{1,0:T(8,128)(2,1)S(1)}, bf16[128,4096]{1,0:T(8,128)(2,1)S(1)}, u32[]{:S(2)}, u32[]{:S(2)}) collective-permute-start(bf16[128,4096]{1,0:T(8,128)(2,1)S(1)} %pad_maximum_fusion.refs_0_), channel_id=1, source_target_pairs={{0,4},{4,0},{8,12},{12,8},{16,20},{20,16},{24,28},{28,24},{1,5},{5... | collective-permute-start | bytes 3145736 | tf_op jit(solution)/shard_map/ppermute | solution.py:22
  3.0 6.5 %copy-start.1 = (bf16[128,4096]{1,0:T(8,128)(2,1)}, bf16[128,4096]{1,0:T(8,128)(2,1)S(1)}, u32[]{:S(2)}) copy-start(bf16[128,4096]{1,0:T(8,128)(2,1)S(1)} %pad_maximum_fusion.1.refs_1_) | copy-start | bytes 3145732
  3.0 6.4 %collective-permute-start.2 = (bf16[128,4096]{1,0:T(8,128)(2,1)S(1)}, bf16[128,4096]{1,0:T(8,128)(2,1)}, u32[]{:S(2)}, u32[]{:S(2)}) collective-permute-start(bf16[128,4096]{1,0:T(8,128)(2,1)S(1)} %pad_maximum_fusion.1.refs_1_), channel_id=1, source_target_pairs={{0,4},{4,0},{8,12},{12,8},{16,20},{20,16},{24,28},{28,24},{1,5},{5... | collective-permute-start | bytes 3145736 | tf_op jit(solution)/shard_map/ppermute | solution.py:22
  3.2 28.0 %collective-permute-start.6 = (bf16[128,4096]{1,0:T(8,128)(2,1)S(1)}, bf16[128,4096]{1,0:T(8,128)(2,1)}, u32[]{:S(2)}, u32[]{:S(2)}) collective-permute-start(bf16[128,4096]{1,0:T(8,128)(2,1)S(1)} %pad_maximum_fusion.refs_0_), channel_id=1, source_target_pairs={{0,8},{4,12},{8,0},{12,4},{16,24},{20,28},{24,16},{28,20},{1,9},{5... | collective-permute-start | bytes 3145736 | tf_op jit(solution)/shard_map/ppermute | solution.py:22
  6.1 25.1 %collective-permute-start.7 = (bf16[128,4096]{1,0:T(8,128)(2,1)S(1)}, bf16[128,4096]{1,0:T(8,128)(2,1)}, u32[]{:S(2)}, u32[]{:S(2)}) collective-permute-start(bf16[128,4096]{1,0:T(8,128)(2,1)S(1)} %pad_maximum_fusion.1.refs_1_), channel_id=1, source_target_pairs={{0,16},{4,20},{8,24},{12,28},{16,0},{20,4},{24,8},{28,12},{1,17},{... | collective-permute-start | bytes 3145736 | tf_op jit(solution)/shard_map/ppermute | solution.py:22
  7.6 1.2 collective-permute-start
  10.5 8.8 %copy-start.29 = (f32[16,128]{1,0:T(8,128)S(1)}, f32[16,128]{1,0:T(8,128)}, u32[]{:S(2)}) copy-start(f32[16,128]{1,0:T(8,128)} %pad_maximum_fusion.4.one_ref.two_ref) | copy-start | bytes 24580
  19.1 14.7 %collective-permute-start.3 = (bf16[4,128,1024]{2,1,0:T(8,128)(2,1)}, bf16[4,128,1024]{2,1,0:T(8,128)(2,1)S(1)}, u32[]{:S(2)}, u32[]{:S(2)}) collective-permute-start(bf16[4,128,1024]{2,1,0:T(8,128)(2,1)} %get-tuple-element.48), channel_id=1, source_target_pairs={{0,4},{4,0},{8,12},{12,8},{16,20},{20,16},{24,28},{28,24},{1,5},{5... | collective-permute-start | bytes 3145736 | tf_op jit(solution)/shard_map/ppermute | solution.py:22
  19.4 11.8 %collective-permute-start.9 = (f32[16,128]{1,0:T(8,128)S(1)}, f32[16,128]{1,0:T(8,128)S(1)}, u32[]{:S(2)}, u32[]{:S(2)}) collective-permute-start(f32[16,128]{1,0:T(8,128)S(1)} %copy-done.29), channel_id=1, source_target_pairs={{0,16},{4,20},{8,24},{12,28},{16,0},{20,4},{24,8},{28,12},{1,17},{... | collective-permute-start | bytes 24584 | tf_op jit(solution)/shard_map/ppermute | solution.py:22
  20.1 11.1 %collective-permute-start.8 = (f32[16,128]{1,0:T(8,128)S(1)}, f32[16,128]{1,0:T(8,128)S(1)}, u32[]{:S(2)}, u32[]{:S(2)}) collective-permute-start(f32[16,128]{1,0:T(8,128)S(1)} %copy-done.29), channel_id=1, source_target_pairs={{0,8},{4,12},{8,0},{12,4},{16,24},{20,28},{24,16},{28,20},{1,9},{5... | collective-permute-start | bytes 24584 | tf_op jit(solution)/shard_map/ppermute | solution.py:22
  31.2 5.8 %copy-start.32 = (f32[16,128]{1,0:T(8,128)}, f32[16,128]{1,0:T(8,128)S(1)}, u32[]{:S(2)}) copy-start(f32[16,128]{1,0:T(8,128)S(1)} %collective-permute-done.9.two_ref.one_ref) | copy-start | bytes 24580
  31.2 5.8 %copy-start.30 = (f32[16,128]{1,0:T(8,128)}, f32[16,128]{1,0:T(8,128)S(1)}, u32[]{:S(2)}) copy-start(f32[16,128]{1,0:T(8,128)S(1)} %collective-permute-done.8.one_ref.two_ref) | copy-start | bytes 24580
  31.2 5.7 %collective-permute-start.10 = (bf16[128,4096]{1,0:T(8,128)(2,1)}, bf16[128,4096]{1,0:T(8,128)(2,1)S(1)}, u32[]{:S(2)}, u32[]{:S(2)}) collective-permute-start(bf16[128,4096]{1,0:T(8,128)(2,1)} %collective-permute-done.6.refs_0_.refs_4_), channel_id=1, source_target_pairs={{0,4},{4,0},{8,12},{12,8},{16,20},{20,16},{24,28},{28,24},{1,5},{5... | collective-permute-start | bytes 3145736 | tf_op jit(solution)/shard_map/ppermute | solution.py:22
  31.3 5.7 %collective-permute-start.11 = (bf16[128,4096]{1,0:T(8,128)(2,1)}, bf16[128,4096]{1,0:T(8,128)(2,1)S(1)}, u32[]{:S(2)}, u32[]{:S(2)}) collective-permute-start(bf16[128,4096]{1,0:T(8,128)(2,1)} %collective-permute-done.7.refs_1_.refs_5_), channel_id=1, source_target_pairs={{0,4},{4,0},{8,12},{12,8},{16,20},{20,16},{24,28},{28,24},{1,5},{5... | collective-permute-start | bytes 3145736 | tf_op jit(solution)/shard_map/ppermute | solution.py:22
  31.8 25.4 %collective-permute-start.4 = (bf16[128,4096]{1,0:T(8,128)(2,1)}, bf16[128,4096]{1,0:T(8,128)(2,1)S(1)}, u32[]{:S(2)}, u32[]{:S(2)}) collective-permute-start(bf16[128,4096]{1,0:T(8,128)(2,1)} %copy-done), channel_id=1, source_target_pairs={{0,16},{4,20},{8,24},{12,28},{16,0},{20,4},{24,8},{28,12},{1,17},{... | collective-permute-start | bytes 3145736 | tf_op jit(solution)/shard_map/ppermute | solution.py:22
  33.3 25.1 %collective-permute-start.5 = (bf16[128,4096]{1,0:T(8,128)(2,1)}, bf16[128,4096]{1,0:T(8,128)(2,1)S(1)}, u32[]{:S(2)}, u32[]{:S(2)}) collective-permute-start(bf16[128,4096]{1,0:T(8,128)(2,1)} %copy-done.1), channel_id=1, source_target_pairs={{0,8},{4,12},{8,0},{12,4},{16,24},{20,28},{24,16},{28,20},{1,9},{5... | collective-permute-start | bytes 3145736 | tf_op jit(solution)/shard_map/ppermute | solution.py:22
  33.8 13.6 %copy-start.24 = (bf16[4,128,1024]{2,1,0:T(8,128)(2,1)}, bf16[4,128,1024]{2,1,0:T(8,128)(2,1)S(1)}, u32[]{:S(2)}) copy-start(bf16[4,128,1024]{2,1,0:T(8,128)(2,1)S(1)} %collective-permute-done.3) | copy-start | bytes 3145732
  35.3 23.1 %collective-permute-start.12 = (bf16[2,128,1024]{2,1,0:T(8,128)(2,1)S(1)}, bf16[2,128,1024]{2,1,0:T(8,128)(2,1)}, u32[]{:S(2)}, u32[]{:S(2)}) collective-permute-start(bf16[2,128,1024]{2,1,0:T(8,128)(2,1)S(1)} %slice_add_fusion.6), channel_id=1, source_target_pairs={{0,1},{1,0},{2,3},{3,2},{4,5},{5,4},{6,7},{7,6},{8,9},{9,8},{10,11... | collective-permute-start | bytes 1572872 | tf_op jit(solution)/shard_map/ppermute | solution.py:22
  47.4 13.8 %copy-start.20 = (bf16[4,128,1024]{2,1,0:T(8,128)(2,1)S(1)}, bf16[4,128,1024]{2,1,0:T(8,128)(2,1)}, u32[]{:S(2)}) copy-start(bf16[4,128,1024]{2,1,0:T(8,128)(2,1)} %get-tuple-element.61) | copy-start | bytes 3145732
  47.4 13.8 %collective-permute-start.18 = (bf16[4,128,1024]{2,1,0:T(8,128)(2,1)}, bf16[4,128,1024]{2,1,0:T(8,128)(2,1)S(1)}, u32[]{:S(2)}, u32[]{:S(2)}) collective-permute-start(bf16[4,128,1024]{2,1,0:T(8,128)(2,1)} %get-tuple-element.62), channel_id=1, source_target_pairs={{0,4},{4,0},{8,12},{12,8},{16,20},{20,16},{24,28},{28,24},{1,5},{5... | collective-permute-start | bytes 3145736 | tf_op jit(solution)/shard_map/ppermute | solution.py:22
  57.1 5.1 %copy-start.5 = (bf16[128,4096]{1,0:T(8,128)(2,1)}, bf16[128,4096]{1,0:T(8,128)(2,1)S(1)}, u32[]{:S(2)}) copy-start(bf16[128,4096]{1,0:T(8,128)(2,1)S(1)} %collective-permute-done.4.refs_0_.refs_8_) | copy-start | bytes 3145732
  58.4 3.8 %copy-start.6 = (bf16[128,4096]{1,0:T(8,128)(2,1)}, bf16[128,4096]{1,0:T(8,128)(2,1)S(1)}, u32[]{:S(2)}) copy-start(bf16[128,4096]{1,0:T(8,128)(2,1)S(1)} %collective-permute-done.5.refs_1_.refs_9_) | copy-start | bytes 3145732
  58.4 5.6 %collective-permute-start.15 = (bf16[128,4096]{1,0:T(8,128)(2,1)S(1)}, bf16[128,4096]{1,0:T(8,128)(2,1)S(1)}, u32[]{:S(2)}, u32[]{:S(2)}) collective-permute-start(bf16[128,4096]{1,0:T(8,128)(2,1)S(1)} %collective-permute-done.4.refs_0_.refs_8_), channel_id=1, source_target_pairs={{0,4},{4,0},{8,12},{12,8},{16,20},{20,16},{24,28},{28,24},{1,5},{5... | collective-permute-start | bytes 3145736 | tf_op jit(solution)/shard_map/ppermute | solution.py:22
  58.4 5.7 %collective-permute-start.16 = (bf16[128,4096]{1,0:T(8,128)(2,1)S(1)}, bf16[128,4096]{1,0:T(8,128)(2,1)S(1)}, u32[]{:S(2)}, u32[]{:S(2)}) collective-permute-start(bf16[128,4096]{1,0:T(8,128)(2,1)S(1)} %collective-permute-done.5.refs_1_.refs_9_), channel_id=1, source_target_pairs={{0,4},{4,0},{8,12},{12,8},{16,20},{20,16},{24,28},{28,24},{1,5},{5... | collective-permute-start | bytes 3145736 | tf_op jit(solution)/shard_map/ppermute | solution.py:22
  58.9 25.3 %collective-permute-start.13 = (bf16[128,4096]{1,0:T(8,128)(2,1)}, bf16[128,4096]{1,0:T(8,128)(2,1)S(1)}, u32[]{:S(2)}, u32[]{:S(2)}) collective-permute-start(bf16[128,4096]{1,0:T(8,128)(2,1)} %collective-permute-done.6.refs_0_.refs_4_), channel_id=1, source_target_pairs={{0,16},{4,20},{8,24},{12,28},{16,0},{20,4},{24,8},{28,12},{1,17},{... | collective-permute-start | bytes 3145736 | tf_op jit(solution)/shard_map/ppermute | solution.py:22
  59.4 25.1 %collective-permute-start.14 = (bf16[128,4096]{1,0:T(8,128)(2,1)}, bf16[128,4096]{1,0:T(8,128)(2,1)S(1)}, u32[]{:S(2)}, u32[]{:S(2)}) collective-permute-start(bf16[128,4096]{1,0:T(8,128)(2,1)} %collective-permute-done.7.refs_1_.refs_5_), channel_id=1, source_target_pairs={{0,8},{4,12},{8,0},{12,4},{16,24},{20,28},{24,16},{28,20},{1,9},{5... | collective-permute-start | bytes 3145736 | tf_op jit(solution)/shard_map/ppermute | solution.py:22
  61.2 13.4 %copy-start.13 = (bf16[2,128,1024]{2,1,0:T(8,128)(2,1)}, bf16[2,128,1024]{2,1,0:T(8,128)(2,1)S(1)}, u32[]{:S(2)}) copy-start(bf16[2,128,1024]{2,1,0:T(8,128)(2,1)S(1)} %fusion.3) | copy-start | bytes 1572868
  61.2 2.8 %copy-start.22 = (bf16[4,128,1024]{2,1,0:T(8,128)(2,1)}, bf16[4,128,1024]{2,1,0:T(8,128)(2,1)S(1)}, u32[]{:S(2)}) copy-start(bf16[4,128,1024]{2,1,0:T(8,128)(2,1)S(1)} %collective-permute-done.18) | copy-start | bytes 3145732
  62.2 15.1 %copy-start.40 = (s32[4]{0:T(128)S(1)}, s32[4]{0:T(128)}, u32[]{:S(2)}) copy-start(s32[4]{0:T(128)} %param.15) | copy-start | bytes 52
  62.2 28.1 %copy-start.31 = (f32[16,128]{1,0:T(8,128)S(1)}, f32[16,128]{1,0:T(8,128)}, u32[]{:S(2)}) copy-start(f32[16,128]{1,0:T(8,128)} %copy-done.30) | copy-start | bytes 24580
  62.2 29.7 %copy-start.25 = (bf16[576,256]{1,0:T(8,128)(2,1)S(1)}, bf16[576,256]{1,0:T(8,128)(2,1)}, u32[]{:S(2)}) copy-start(bf16[576,256]{1,0:T(8,128)(2,1)} %get-tuple-element.82) | copy-start | bytes 884740
  62.2 27.5 %collective-permute-start.19 = (bf16[2,128,1024]{2,1,0:T(8,128)(2,1)}, bf16[2,128,1024]{2,1,0:T(8,128)(2,1)S(1)}, u32[]{:S(2)}, u32[]{:S(2)}) collective-permute-start(bf16[2,128,1024]{2,1,0:T(8,128)(2,1)} %slice_add_fusion.5), channel_id=1, source_target_pairs={{0,1},{1,0},{2,3},{3,2},{4,5},{5,4},{6,7},{7,6},{8,9},{9,8},{10,11... | collective-permute-start | bytes 1572872 | tf_op jit(solution)/shard_map/ppermute | solution.py:22
  74.5 17.4 %copy-start.21 = (bf16[4,128,1024]{2,1,0:T(8,128)(2,1)S(1)}, bf16[4,128,1024]{2,1,0:T(8,128)(2,1)}, u32[]{:S(2)}) copy-start(bf16[4,128,1024]{2,1,0:T(8,128)(2,1)} %get-tuple-element.61) | copy-start | bytes 3145732
  74.5 18.7 %collective-permute-start.24 = (bf16[4,128,1024]{2,1,0:T(8,128)(2,1)}, bf16[4,128,1024]{2,1,0:T(8,128)(2,1)S(1)}, u32[]{:S(2)}, u32[]{:S(2)}) collective-permute-start(bf16[4,128,1024]{2,1,0:T(8,128)(2,1)} %get-tuple-element.70), channel_id=1, source_target_pairs={{0,4},{4,0},{8,12},{12,8},{16,20},{20,16},{24,28},{28,24},{1,5},{5... | collective-permute-start | bytes 3145736 | tf_op jit(solution)/shard_map/ppermute | solution.py:22
  74.6 15.1 %collective-permute-start.17 = (bf16[128,1024]{1,0:T(8,128)(2,1)S(1)}, bf16[128,1024]{1,0:T(8,128)(2,1)S(1)}, u32[]{:S(2)}, u32[]{:S(2)}) collective-permute-start(bf16[128,1024]{1,0:T(8,128)(2,1)S(1)} %slice_bitcast_fusion.6), channel_id=1, source_target_pairs={{0,2},{1,3},{2,0},{3,1},{4,6},{5,7},{6,4},{7,5},{8,10},{9,11},{10,... | collective-permute-start | bytes 786440 | tf_op jit(solution)/shard_map/ppermute | solution.py:22
  84.2 8.9 %copy-start.9 = (bf16[128,4096]{1,0:T(8,128)(2,1)}, bf16[128,4096]{1,0:T(8,128)(2,1)S(1)}, u32[]{:S(2)}) copy-start(bf16[128,4096]{1,0:T(8,128)(2,1)S(1)} %collective-permute-done.13.refs_0_.refs_12_) | copy-start | bytes 3145732
  84.4 8.7 %copy-start.10 = (bf16[128,4096]{1,0:T(8,128)(2,1)}, bf16[128,4096]{1,0:T(8,128)(2,1)S(1)}, u32[]{:S(2)}) copy-start(bf16[128,4096]{1,0:T(8,128)(2,1)S(1)} %collective-permute-done.14.refs_1_.refs_13_) | copy-start | bytes 3145732
  89.7 7.7 %collective-permute-start.21 = (bf16[128,4096]{1,0:T(8,128)(2,1)S(1)}, bf16[128,4096]{1,0:T(8,128)(2,1)S(1)}, u32[]{:S(2)}, u32[]{:S(2)}) collective-permute-start(bf16[128,4096]{1,0:T(8,128)(2,1)S(1)} %collective-permute-done.13.refs_0_.refs_12_), channel_id=1, source_target_pairs={{0,4},{4,0},{8,12},{12,8},{16,20},{20,16},{24,28},{28,24},{1,5},{5... | collective-permute-start | bytes 3145736 | tf_op jit(solution)/shard_map/ppermute | solution.py:22
  89.8 7.6 %collective-permute-start.22 = (bf16[128,4096]{1,0:T(8,128)(2,1)S(1)}, bf16[128,4096]{1,0:T(8,128)(2,1)S(1)}, u32[]{:S(2)}, u32[]{:S(2)}) collective-permute-start(bf16[128,4096]{1,0:T(8,128)(2,1)S(1)} %collective-permute-done.14.refs_1_.refs_13_), channel_id=1, source_target_pairs={{0,4},{4,0},{8,12},{12,8},{16,20},{20,16},{24,28},{28,24},{1,5},{5... | collective-permute-start | bytes 3145736 | tf_op jit(solution)/shard_map/ppermute | solution.py:22
  90.3 7.1 %collective-permute-start.20 = (f32[16,128]{1,0:T(8,128)S(1)}, f32[16,128]{1,0:T(8,128)S(1)}, u32[]{:S(2)}, u32[]{:S(2)}) collective-permute-start(f32[16,128]{1,0:T(8,128)S(1)} %copy-done.31), channel_id=1, source_target_pairs={{0,16},{4,20},{8,24},{12,28},{16,0},{20,4},{24,8},{28,12},{1,17},{... | collective-permute-start | bytes 24584 | tf_op jit(solution)/shard_map/ppermute | solution.py:22
  93.2 4.1 %copy-start.26 = (bf16[576,256]{1,0:T(8,128)(2,1)S(1)}, bf16[576,256]{1,0:T(8,128)(2,1)}, u32[]{:S(2)}) copy-start(bf16[576,256]{1,0:T(8,128)(2,1)} %get-tuple-element.83) | copy-start | bytes 884740
  93.2 4.2 %copy-start.18 = (bf16[4,128,1024]{2,1,0:T(8,128)(2,1)}, bf16[4,128,1024]{2,1,0:T(8,128)(2,1)S(1)}, u32[]{:S(2)}) copy-start(bf16[4,128,1024]{2,1,0:T(8,128)(2,1)S(1)} %collective-permute-done.24) | copy-start | bytes 3145732
  93.4 19.4 %collective-permute-start.25 = (bf16[2,128,1024]{2,1,0:T(8,128)(2,1)S(1)}, bf16[2,128,1024]{2,1,0:T(8,128)(2,1)}, u32[]{:S(2)}, u32[]{:S(2)}) collective-permute-start(bf16[2,128,1024]{2,1,0:T(8,128)(2,1)S(1)} %slice_add_fusion.3), channel_id=1, source_target_pairs={{0,1},{1,0},{2,3},{3,2},{4,5},{5,4},{6,7},{7,6},{8,9},{9,8},{10,11... | collective-permute-start | bytes 1572872 | tf_op jit(solution)/shard_map/ppermute | solution.py:22
  94.3 16.4 %collective-permute-start.23 = (bf16[128,1024]{1,0:T(8,128)(2,1)}, bf16[128,1024]{1,0:T(8,128)(2,1)S(1)}, u32[]{:S(2)}, u32[]{:S(2)}) collective-permute-start(bf16[128,1024]{1,0:T(8,128)(2,1)} %slice_bitcast_fusion.4), channel_id=1, source_target_pairs={{0,2},{1,3},{2,0},{3,1},{4,6},{5,7},{6,4},{7,5},{8,10},{9,11},{10,... | collective-permute-start | bytes 786440 | tf_op jit(solution)/shard_map/ppermute | solution.py:22
  107.9 4.9 %copy-start.19 = (bf16[4,128,1024]{2,1,0:T(8,128)(2,1)S(1)}, bf16[4,128,1024]{2,1,0:T(8,128)(2,1)}, u32[]{:S(2)}) copy-start(bf16[4,128,1024]{2,1,0:T(8,128)(2,1)} %copy-done.18) | copy-start | bytes 3145732
  107.9 7.3 %collective-permute-start.27 = (bf16[4,128,1024]{2,1,0:T(8,128)(2,1)}, bf16[4,128,1024]{2,1,0:T(8,128)(2,1)S(1)}, u32[]{:S(2)}, u32[]{:S(2)}) collective-permute-start(bf16[4,128,1024]{2,1,0:T(8,128)(2,1)} %get-tuple-element.75), channel_id=1, source_target_pairs={{0,4},{4,0},{8,12},{12,8},{16,20},{20,16},{24,28},{28,24},{1,5},{5... | collective-permute-start | bytes 3145736 | tf_op jit(solution)/shard_map/ppermute | solution.py:22
  110.1 3.9 %copy-start.15 = (bf16[576,1024]{1,0:T(8,128)(2,1)}, bf16[576,1024]{1,0:T(8,128)(2,1)S(1)}, u32[]{:S(2)}) copy-start(bf16[576,1024]{1,0:T(8,128)(2,1)S(1)} %constant_dynamic-update-slice_fusion.refs_16_) | copy-start | bytes 3538948
  110.1 41.7 %collective-permute-start.35 = (bf16[576,1024]{1,0:T(8,128)(2,1)S(1)}, bf16[576,1024]{1,0:T(8,128)(2,1)S(1)}, u32[]{:S(2)}, u32[]{:S(2)}) collective-permute-start(bf16[576,1024]{1,0:T(8,128)(2,1)S(1)} %constant_dynamic-update-slice_fusion.refs_16_), channel_id=1, source_target_pairs={{0,16},{4,20},{8,24},{12,28},{16,0},{20,4},{24,8},{28,12},{1,17},{... | collective-permute-start | bytes 3538952 | tf_op jit(solution)/shard_map/ppermute | solution.py:22
  112.8 2.4 %copy-start.36 = (f32[1,256]{1,0:T(1,128)S(1)}, f32[1,256]{1,0:T(1,128)}, u32[]{:S(2)}) copy-start(f32[1,256]{1,0:T(1,128)} %get-tuple-element.59.refs_7_) | copy-start | bytes 3076
  112.8 2.4 %copy-start.37 = (f32[1,256]{1,0:T(1,128)S(1)}, f32[1,256]{1,0:T(1,128)}, u32[]{:S(2)}) copy-start(f32[1,256]{1,0:T(1,128)} %get-tuple-element.67.refs_7_) | copy-start | bytes 3076
  114.0 19.4 %collective-permute-start.29 = (bf16[128,1024]{1,0:T(8,128)(2,1)S(1)}, bf16[128,1024]{1,0:T(8,128)(2,1)S(1)}, u32[]{:S(2)}, u32[]{:S(2)}) collective-permute-start(bf16[128,1024]{1,0:T(8,128)(2,1)S(1)} %slice_bitcast_fusion.2), channel_id=1, source_target_pairs={{0,2},{1,3},{2,0},{3,1},{4,6},{5,7},{6,4},{7,5},{8,10},{9,11},{10,... | collective-permute-start | bytes 786440 | tf_op jit(solution)/shard_map/ppermute | solution.py:22
  115.3 18.1 %collective-permute-start.28 = (bf16[2,128,1024]{2,1,0:T(8,128)(2,1)S(1)}, bf16[2,128,1024]{2,1,0:T(8,128)(2,1)S(1)}, u32[]{:S(2)}, u32[]{:S(2)}) collective-permute-start(bf16[2,128,1024]{2,1,0:T(8,128)(2,1)S(1)} %slice_add_fusion.1), channel_id=1, source_target_pairs={{0,1},{1,0},{2,3},{3,2},{4,5},{5,4},{6,7},{7,6},{8,9},{9,8},{10,11... | collective-permute-start | bytes 1572872 | tf_op jit(solution)/shard_map/ppermute | solution.py:22
  117.6 15.8 %collective-permute-start.26 = (f32[8,128]{1,0:T(8,128)S(1)}, f32[8,128]{1,0:T(8,128)S(1)}, u32[]{:S(2)}, u32[]{:S(2)}) collective-permute-start(f32[8,128]{1,0:T(8,128)S(1)} %maximum_maximum_fusion), channel_id=1, source_target_pairs={{0,1},{1,0},{2,3},{3,2},{4,5},{5,4},{6,7},{7,6},{8,9},{9,8},{10,11... | collective-permute-start | bytes 12296 | tf_op jit(solution)/shard_map/ppermute | solution.py:22
  133.5 5.2 %collective-permute-start.32 = (f32[8,128]{1,0:T(8,128)S(1)}, f32[8,128]{1,0:T(8,128)S(1)}, u32[]{:S(2)}, u32[]{:S(2)}) collective-permute-start(f32[8,128]{1,0:T(8,128)S(1)} %add.95), channel_id=1, source_target_pairs={{0,2},{1,3},{2,0},{3,1},{4,6},{5,7},{6,4},{7,5},{8,10},{9,11},{10,... | collective-permute-start | bytes 12296 | tf_op jit(solution)/shard_map/ppermute | solution.py:22
  136.0 13.2 %collective-permute-start.33 = (bf16[128,1024]{1,0:T(8,128)(2,1)}, bf16[128,1024]{1,0:T(8,128)(2,1)}, u32[]{:S(2)}, u32[]{:S(2)}) collective-permute-start(bf16[128,1024]{1,0:T(8,128)(2,1)} %slice_bitcast_fusion), channel_id=1, source_target_pairs={{0,2},{1,3},{2,0},{3,1},{4,6},{5,7},{6,4},{7,5},{8,10},{9,11},{10,... | collective-permute-start | bytes 786440 | tf_op jit(solution)/shard_map/ppermute | solution.py:22
  138.0 27.3 %collective-permute-start.31 = (bf16[128,1024]{1,0:T(8,128)(2,1)}, bf16[128,1024]{1,0:T(8,128)(2,1)}, u32[]{:S(2)}, u32[]{:S(2)}) collective-permute-start(bf16[128,1024]{1,0:T(8,128)(2,1)} %pad_maximum_fusion.3), channel_id=1, source_target_pairs={{0,16},{4,20},{8,24},{12,28},{16,0},{20,4},{24,8},{28,12},{1,17},{... | collective-permute-start | bytes 786440 | tf_op jit(solution)/shard_map/ppermute | solution.py:22
  140.0 8.1 %all-to-all-start = ((bf16[8,1,128]{2,1,0:T(2,128)(2,1)}), bf16[8,1,128]{2,1,0:T(2,128)(2,1)S(1)}, u32[]{:S(2)}, u32[]{:S(2)}) async-start(bf16[8,1,128]{2,1,0:T(2,128)(2,1)} %copy.24), calls=%async_computation | async-start | bytes 8192 | tf_op jit(solution)/shard_map/all_to_all | solution.py:300
  144.2 21.1 %collective-permute-start.30 = (bf16[128,1024]{1,0:T(8,128)(2,1)}, bf16[128,1024]{1,0:T(8,128)(2,1)S(1)}, u32[]{:S(2)}, u32[]{:S(2)}) collective-permute-start(bf16[128,1024]{1,0:T(8,128)(2,1)} %pad_maximum_fusion.2), channel_id=1, source_target_pairs={{0,8},{4,12},{8,0},{12,4},{16,24},{20,28},{24,16},{28,20},{1,9},{5... | collective-permute-start | bytes 786440 | tf_op jit(solution)/shard_map/ppermute | solution.py:22
  150.3 15.1 %copy-start.14 = (bf16[2,128,1024]{2,1,0:T(8,128)(2,1)S(1)}, bf16[2,128,1024]{2,1,0:T(8,128)(2,1)}, u32[]{:S(2)}) copy-start(bf16[2,128,1024]{2,1,0:T(8,128)(2,1)} %copy-done.13) | copy-start | bytes 1572868
  150.3 15.1 %copy-start.28 = (bf16[128,1024]{1,0:T(8,128)(2,1)S(1)}, bf16[128,1024]{1,0:T(8,128)(2,1)}, u32[]{:S(2)}) copy-start(bf16[128,1024]{1,0:T(8,128)(2,1)} %copy-done.27) | copy-start | bytes 786436
  150.3 15.1 %collective-permute-start.34 = (bf16[128,1024]{1,0:T(8,128)(2,1)S(1)}, bf16[128,1024]{1,0:T(8,128)(2,1)S(1)}, u32[]{:S(2)}, u32[]{:S(2)}) collective-permute-start(bf16[128,1024]{1,0:T(8,128)(2,1)S(1)} %fusion.4), channel_id=1, source_target_pairs={{0,24},{4,28},{8,16},{12,20},{16,8},{20,12},{24,0},{28,4},{1,25},{... | collective-permute-start | bytes 786440 | tf_op jit(solution)/shard_map/ppermute | solution.py:22
  (14 other events, 18.2 us)

commit v5 on v4

--- a/solution.py
+++ b/solution.py
@@ -10,7 +10,7 @@
 
 CONTRACT_LAST = (((1,), (1,)), ((), ()))
 CONTRACT_ROWS = (((0,), (0,)), ((), ()))
-VMEM = 56 * 1024 * 1024
+VMEM = 20 * 1024 * 1024
 
 
 def from_behind(value, axis, by):
@@ -27,34 +27,22 @@
     return jnp.sum(jnp.where(match, pair_flags[None, :], 0), axis=1)
 
 
-def part_order(parts):
-    return (*range(0, parts, 2), *range(1, parts, 2))
+def in_vmem(*values):
+    return [pltpu.with_memory_space_constraint(value, pltpu.VMEM) for value in values]
+
+
+def rows_of(messages, start, size, columns):
+    return jnp.concatenate([ref[pl.ds(start, size), columns] for ref in messages], axis=0)
 
 
 def activations_kernel(parts, where_ref, one_ref, two_ref, *refs):
     messages = refs[:4]
-    gate_ref, up_ref, down_ref = refs[4:7]
-    acts_ref, score_ref, keep_ref, give_ref = refs[8:12]
-    held, in_all, down_all, both, shares, sems, out_sems = refs[12:]
+    in_ref, down_ref = refs[4:6]
+    acts_ref, score_ref, keep_near, keep_far, give_near, give_far, both = refs[7:]
     rows, width = messages[0].shape
     half = rows // 2
-    units = gate_ref.shape[0]
+    units = down_ref.shape[0]
     chunk = width // parts
-    copies = []
-    for part in range(parts):
-        columns = pl.ds(part * chunk, chunk)
-        moves = [(ref, held.at[i, :, columns]) for i, ref in enumerate(messages)]
-        moves.append((gate_ref, in_all.at[pl.ds(0, units), columns]))
-        moves.append((up_ref, in_all.at[pl.ds(units, units), columns]))
-        moves.append((down_ref, down_all.at[:, columns]))
-        copies.append(
-            [
-                pltpu.make_async_copy(ref.at[:, columns], target, sems.at[part, i])
-                for i, (ref, target) in enumerate(moves)
-            ]
-        )
-        for copy in copies[-1]:
-            copy.start()
     me, group = where_ref[0], where_ref[1]
     first = lax.broadcasted_iota(jnp.int32, (1, rows), 1) < half
     experts = one_ref.shape[0] // 2
@@ -67,13 +55,10 @@
     )
     pre, back = None, None
     for part in range(parts):
-        for copy in copies[part]:
-            copy.wait()
         columns = pl.ds(part * chunk, chunk)
-        x = held[:, pl.ds(0, half), columns].reshape(2 * rows, chunk)
-        dy = held[:, pl.ds(half, half), columns].reshape(2 * rows, chunk)
-        one = lax.dot_general(in_all[:, columns], x, CONTRACT_LAST, preferred_element_type=jnp.float32)
-        two = lax.dot_general(down_all[:, columns], dy, CONTRACT_LAST, preferred_element_type=jnp.float32)
+        x, dy = rows_of(messages, 0, half, columns), rows_of(messages, half, half, columns)
+        one = lax.dot_general(in_ref[:, columns], x, CONTRACT_LAST, preferred_element_type=jnp.float32)
+        two = lax.dot_general(down_ref[:, columns], dy, CONTRACT_LAST, preferred_element_type=jnp.float32)
         pre = one if pre is None else pre + one
         back = two if back is None else back + two
     pre_gate, pre_up = pre[:units], pre[units:]
@@ -87,92 +72,66 @@
     acts_ref[pl.ds(0, 2 * units), :] = grads.astype(jnp.bfloat16)
     acts_ref[pl.ds(2 * units, units), :] = (g * hidden).astype(jnp.bfloat16)
     both[...] = grads.T.astype(jnp.bfloat16)
-    copies = []
-    for place, part in enumerate(part_order(parts)):
+    for part in range(parts):
         columns = pl.ds(pl.multiple_of((group ^ part) * chunk, chunk), chunk)
-        share = jnp.dot(both[...], in_all[:, columns], preferred_element_type=jnp.float32)
-        shares[place] = share.astype(jnp.bfloat16)
-        for i, ref in enumerate((keep_ref, give_ref)):
-            copies.append(
-                pltpu.make_async_copy(
-                    shares.at[place, pl.ds(i * rows, rows), :], ref.at[place], out_sems.at[place, i]
-                )
-            )
-            copies[-1].start()
-    for copy in copies:
-        copy.wait()
+        share = jnp.dot(both[...], in_ref[:, columns], preferred_element_type=jnp.float32)
+        share = share.astype(jnp.bfloat16)
+        keep, give = (keep_far, give_far) if part % 2 else (keep_near, give_near)
+        keep[part // 2] = share[:rows]
+        give[part // 2] = share[rows:]
 
 
 def activations(parts, where, tables, messages, weights, before):
     rows, width = messages[0].shape
-    units = weights[0].shape[0]
+    units = weights[1].shape[0]
     bf16 = jnp.bfloat16
-    share = jax.ShapeDtypeStruct((parts, rows, width // parts), bf16)
+    share = pltpu.VMEM((parts // 2, rows, width // parts), bf16)
     return pl.pallas_call(
         functools.partial(activations_kernel, parts),
         out_shape=(
-            jax.ShapeDtypeStruct((3 * units, 2 * rows), bf16),
-            jax.ShapeDtypeStruct((1, 2 * rows), jnp.float32),
+            pltpu.VMEM((3 * units, 2 * rows), bf16),
+            pltpu.VMEM((1, 2 * rows), jnp.float32),
+            share,
+            share,
             share,
             share,
         ),
         in_specs=[pl.BlockSpec(memory_space=pltpu.SMEM)]
-        + [pl.BlockSpec(memory_space=pltpu.VMEM)] * 2
-        + [pl.BlockSpec(memory_space=pl.ANY)] * 8,
-        out_specs=[pl.BlockSpec(memory_space=pltpu.VMEM)] * 2 + [pl.BlockSpec(memory_space=pl.ANY)] * 2,
-        scratch_shapes=[
-            pltpu.VMEM((4, rows, width), bf16),
-            pltpu.VMEM((2 * units, width), bf16),
-            pltpu.VMEM((units, width), bf16),
-            pltpu.VMEM((2 * rows, 2 * units), bf16),
-            pltpu.VMEM((parts, 2 * rows, width // parts), bf16),
-            pltpu.SemaphoreType.DMA((parts, 7)),
-            pltpu.SemaphoreType.DMA((parts, 2)),
-        ],
+        + [pl.BlockSpec(memory_space=pltpu.VMEM)] * 8
+        + [pl.BlockSpec(memory_space=pl.ANY)],
+        out_specs=[pl.BlockSpec(memory_space=pltpu.VMEM)] * 6,
+        scratch_shapes=[pltpu.VMEM((2 * rows, 2 * units), bf16)],
         compiler_params=pltpu.CompilerParams(vmem_limit_bytes=VMEM),
         cost_estimate=pl.CostEstimate(flops=1, bytes_accessed=1, transcendentals=0),
         name="activations",
-    )(where, *tables, *messages, *weights, before)
+    )(where, *in_vmem(*tables, *messages, *weights), before)
 
 
 def weight_grads_kernel(sources, parts, flag_ref, *refs):
-    count = 4 * len(sources)
-    messages = refs[:count]
-    own_ref, other_ref = refs[count : count + 2]
-    outs = refs[count + 2 : count + 5]
-    held, acts, results, sems, out_sems = refs[count + 5 :]
+    groups = len(sources)
+    messages, refs = refs[: 4 * groups], refs[4 * groups :]
+    own, other, refs = refs[:groups], refs[groups : 2 * groups], refs[2 * groups :]
+    outs = refs[:3]
+    acts, results, out_sems = refs[3:]
     rows, width = messages[0].shape
     half = rows // 2
     units = outs[0].shape[1]
     chunk = width // parts
-    copies = []
-    for part in range(parts):
-        columns = pl.ds(part * chunk, chunk)
-        copies.append(
-            [
-                pltpu.make_async_copy(ref.at[:, columns], held.at[i, :, columns], sems.at[part, i])
-                for i, ref in enumerate(messages)
-            ]
-        )
-        for copy in copies[-1]:
-            copy.start()
     tiles = [(one ^ core, two ^ core) for one, two in sources for core in (0, CORE)]
     first = lax.broadcasted_iota(jnp.int32, (1, rows), 1) < half
+
+    def tile_of(groups_of, place):
+        return groups_of[place // 2][:, pl.ds(place % 2 * rows, rows)]
+
     for place, (one, two) in enumerate(tiles):
         from_one = [tile[0] for tile in tiles].index(one ^ ACROSS_Y)
         from_two = [tile[1] for tile in tiles].index(two ^ ACROSS_Y)
-        arrived = jnp.where(
-            first, other_ref[:, pl.ds(from_one * rows, rows)], other_ref[:, pl.ds(from_two * rows, rows)]
-        )
-        stay = own_ref[:, pl.ds(place * rows, rows)]
-        acts[:, pl.ds(place * rows, rows)] = jnp.where(flag_ref[0] == 1, arrived, stay)
+        arrived = jnp.where(first, tile_of(other, from_one), tile_of(other, from_two))
+        acts[:, pl.ds(place * rows, rows)] = jnp.where(flag_ref[0] == 1, arrived, tile_of(own, place))
     sent = []
     for part in range(parts):
-        for copy in copies[part]:
-            copy.wait()
         columns = pl.ds(part * chunk, chunk)
-        x = held[:, pl.ds(0, half), columns].reshape(count * half, chunk)
-        dy = held[:, pl.ds(half, half), columns].reshape(count * half, chunk)
+        x, dy = rows_of(messages, 0, half, columns), rows_of(messages, half, half, columns)
         both = jnp.dot(acts[pl.ds(0, 2 * units), :], x, preferred_element_type=jnp.float32)
         results[part, pl.ds(0, 2 * units), :] = both.astype(jnp.bfloat16)
         down = jnp.dot(acts[pl.ds(2 * units, units), :], dy, preferred_element_type=jnp.float32)
@@ -189,29 +148,26 @@
 
 
 def weight_grads(sources, flag, messages, own, other):
-    parts = 4
+    parts = 8
     rows, width = messages[0].shape
-    units = own.shape[0] // 3
+    units = own[0].shape[0] // 3
     total = len(messages) * rows // 2
     bf16 = jnp.bfloat16
+    operands = in_vmem(*messages, *own, *other)
     return pl.pallas_call(
         functools.partial(weight_grads_kernel, sources, parts),
         out_shape=(jax.ShapeDtypeStruct((1, units, width), bf16),) * 3,
-        in_specs=[pl.BlockSpec(memory_space=pltpu.SMEM)]
-        + [pl.BlockSpec(memory_space=pl.ANY)] * len(messages)
-        + [pl.BlockSpec(memory_space=pltpu.VMEM)] * 2,
+        in_specs=[pl.BlockSpec(memory_space=pltpu.SMEM)] + [pl.BlockSpec(memory_space=pltpu.VMEM)] * len(operands),
         out_specs=[pl.BlockSpec(memory_space=pl.ANY)] * 3,
         scratch_shapes=[
-            pltpu.VMEM((len(messages), rows, width), bf16),
             pltpu.VMEM((3 * units, total), bf16),
             pltpu.VMEM((parts, 3 * units, width // parts), bf16),
-            pltpu.SemaphoreType.DMA((parts, len(messages))),
             pltpu.SemaphoreType.DMA((parts, 3)),
         ],
         compiler_params=pltpu.CompilerParams(vmem_limit_bytes=VMEM),
         cost_estimate=pl.CostEstimate(flops=1, bytes_accessed=1, transcendentals=0),
         name="weight_grads",
-    )(flag, *messages, own, other)
+    )(flag, *operands)
 
 
 CORE, ACROSS_X, ACROSS_Y = 1, 2, 4
@@ -226,7 +182,7 @@
     f32, bf16 = jnp.float32, jnp.bfloat16
     own_flag = pair_lookup(jnp.reshape(me, (1,)), swap_flags, half_axis)
     where = jnp.stack([me, group]).astype(jnp.int32)
-    weights = (gate_weight[0], up_weight[0], down_weight[0])
+    weights = (jnp.concatenate([gate_weight[0], up_weight[0]]), down_weight[0])
 
     def expert_swap(value, by):
         return swap(value, "expert", by)
@@ -243,26 +199,24 @@
     tables[2], tables[4] = expert_swap(tables[0], ACROSS_X), expert_swap(tables[0], ACROSS_Y)
 
     acts, scores, messages = [], [], []
+    barrier = lax.optimization_barrier
 
     def work(one, two, before):
         held = [a[one], b[two], a[one ^ CORE], b[two ^ CORE]]
-        act, score, keep, give = activations(
+        act, score, keep_near, keep_far, give_near, give_far = activations(
             parts, where, (tables[one], tables[two]), held, weights, before
         )
         acts.append(act)
         scores.append(score)
         messages.extend(held)
-        return score, keep, expert_swap(give, CORE)
-
-    def to_neighbour(keep, given):
-        far = keep[parts // 2 :] + given[parts // 2 :]
-        return keep[: parts // 2] + given[: parts // 2], swap(far, "dp", 1)
+        return score, keep_near, keep_far, expert_swap(give_near, CORE), expert_swap(give_far, CORE)
+
+    def to_neighbour(keep_near, keep_far, near, far):
+        return keep_near + near, swap(keep_far + far, "dp", 1)
 
     def to_far(near, arrived):
         near = near + arrived
         return near[0].astype(f32), swap(near[1], "dp", 2)
-
-    barrier = lax.optimization_barrier
 
     done_a, *share_a = work(0, 0, where)
     a[2], b[4], tables[2], tables[4], done_a = barrier((a[2], b[4], tables[2], tables[4], done_a))
@@ -278,32 +232,31 @@
     near_b, near_in_b = to_neighbour(*share_b)
     a[6], b[6], done_c, far_in_a, near_in_b = barrier((a[6], b[6], done_c, far_in_a, near_in_b))
     a[7], b[7] = expert_swap(a[6], CORE), expert_swap(b[6], CORE)
+    other = [expert_swap(act, half_axis) for act in acts[:2]]
     done_d, *share_d = work(6, 6, done_c)
     total_b, far_in_b = to_far(near_b, near_in_b)
     near_c, near_in_c = to_neighbour(*share_c)
-    done_d, far_in_b, near_in_c = barrier((done_d, far_in_b, near_in_c))
-    scores[-1] = done_d
-    total_c, far_in_c = to_far(near_c, near_in_c)
-    near_d, near_in_d = to_neighbour(*share_d)
-
-    sources = ((0, 0), (2, 4), (4, 2), (6, 6))
-    own = jnp.concatenate(acts, axis=1)
-    other = expert_swap(own, half_axis)
-
-    tiles = jnp.concatenate(scores, axis=1).reshape(expert_count, 2 * half)
+    done_d, far_in_b, near_in_c, *other = barrier((done_d, far_in_b, near_in_c, *other))
+    other += [expert_swap(act, half_axis) for act in acts[2:]]
+    tiles = jnp.concatenate(scores[:3] + [done_d], axis=1).reshape(expert_count, 2 * half)
     second = jnp.concatenate([tiles[:2, half:], tiles[4:6, half:], tiles[2:4, half:], tiles[6:, half:]])
     score_rows = jnp.concatenate([tiles[:, :half], second], axis=1)
-    summed = score_rows + swap(score_rows, "dp", 1)
-    summed, near_in_d, far_in_c = barrier((summed, near_in_d, far_in_c))
-    summed = summed + swap(summed, "dp", 2)
-    score_rows = jnp.take(summed.astype(bf16), jnp.arange(expert_count, dtype=jnp.int32) ^ me, axis=0)
+    score_in = swap(score_rows, "dp", 1)
+    keep_near, keep_far, near, far = share_d
+    far, score_in = barrier((far, score_in))
+    near_d, near_in_d = to_neighbour(keep_near, keep_far, near, far)
+    score_rows = score_rows + score_in
+    score_rows = score_rows + swap(score_rows, "dp", 2)
+    score_rows = jnp.take(score_rows.astype(bf16), jnp.arange(expert_count, dtype=jnp.int32) ^ me, axis=0)
     score_rows = lax.all_to_all(score_rows, "expert", split_axis=0, concat_axis=0, tiled=True)
+    total_c, far_in_c = to_far(near_c, near_in_c)
+    score_rows, near_in_d, far_in_c, own_flag = barrier((score_rows, near_in_d, far_in_c, own_flag))
     total_d, far_in_d = to_far(near_d, near_in_d)
-    score_rows, far_in_d, own_flag = barrier((score_rows, far_in_d, own_flag))
+    grads = weight_grads(((0, 0), (2, 4), (4, 2), (6, 6)), own_flag, messages, acts, other)
+    far_in_d, grads = barrier((far_in_d, grads))
+
     total_a, total_b = total_a + far_in_a.astype(f32), total_b + far_in_b.astype(f32)
     total_c, total_d = total_c + far_in_c.astype(f32), (total_d + far_in_d.astype(f32)).astype(bf16)
-    grads = weight_grads(sources, own_flag, messages, own, other)
-
     to_x = jnp.concatenate([total_b[:half], total_c[half:]]).astype(bf16)
     to_y = jnp.concatenate([total_c[:half], total_b[half:]]).astype(bf16)
     input_grad = total_a + expert_swap(to_x, ACROSS_X).astype(f32) + expert_swap(to_y, ACROSS_Y).astype(f32)

time: 168 us -> 176 us (1.048)
  waiting for transfers between devices: 55.2 us -> 74.8 us
  Pallas kernels: 46 us -> 30 us
  starting transfers between devices: 36.3 us -> 44.2 us
  other arithmetic: 13.6 us -> 10.2 us
    ppermute x36 -> x43, waiting for transfers between devices: 53.4 us -> 74 us  [swap(): lax.ppermute(value, axis, [(i, i ^ by) for i in range(lax.axis_size(axis))])]
    pallas_call x4, Pallas kernels: 34.1 us -> 20.1 us  [activations(): pl.pallas_call(functools.partial(activations_kernel, parts), out_shape=(p...]
    ppermute x36 -> x43, starting transfers between devices: 32.8 us -> 40.8 us  [swap(): lax.ppermute(value, axis, [(i, i ^ by) for i in range(lax.axis_size(axis))])]
    pallas_call x1, Pallas kernels: 11.9 us -> 9.85 us  [weight_grads(): pl.pallas_call(functools.partial(weight_grads_kernel, sources, parts), ou...]
    add x4, other arithmetic: 3.85 us -> 1.83 us  [to_far(): near = near + arrived]
    slice x2, local copies, waits for them, and re-layouts: 0.04 us -> 1.82 us  [whole_shards(): to_x = jnp.concatenate([total_b[:half], total_c[half:]]).astype(bf16)]
    another operation x2, other arithmetic: 0.13 us -> 1.9 us
    unnamed x86 -> x87, local copies, waits for them, and re-layouts: 9.29 us -> 9.08 us
  transfers between devices with their start and end apart: 37 -> 44, of which waited for: 11 -> 18; matrix products, arithmetic and copies ran while one was open for 10% -> 7% of each run, Pallas kernels for 28% -> 17%
where the time goes in v5:
time: 176 us; the launch traced here: 175 us
  waiting for transfers between devices  74.8 us (42%)
  starting transfers between devices  44.2 us (25%)
  Pallas kernels  30 us (17%)
  local copies, waits for them, and re-layouts  14.6 us (8%)
  other arithmetic  10.2 us (6%)
    ppermute x43, waiting for transfers between devices, swap(): lax.ppermute(value, axis, [(i, i ^ by) for i in range(lax.axis_size(axis))])  74 us
    ppermute x43, starting transfers between devices, swap(): lax.ppermute(value, axis, [(i, i ^ by) for i in range(lax.axis_size(axis))])  40.8 us
    pallas_call x4, Pallas kernels, activations(): pl.pallas_call(functools.partial(activations_kernel, parts), out_shape=(p...  20.1 us
    pallas_call x1, Pallas kernels, weight_grads(): pl.pallas_call(functools.partial(weight_grads_kernel, sources, parts), ou...  9.85 us
    unnamed x87, local copies, waits for them, and re-layouts  9.08 us
  transfers between devices with their start and end apart: 44, of which 18 were waited for; matrix products, arithmetic and copies ran while one was open for 7% of the time, Pallas kernels for 17%

profile of v5, /device:TPU:0, one launch (start us, length us, event | category | flops | bytes accessed | tf_op | source)
XLA Modules:
  0.0 175.0 jit_solution(2649253476614047640)
XLA Ops:
  0.6 1.7 fusion.9
  2.3 1.0 pad_maximum_fusion.2.refs_1_
  3.8 1.0 pad_maximum_fusion.1.refs_0_
  4.9 3.0 %collective-permute-start.7 = (bf16[128,4096]{1,0:T(8,128)(2,1)}, bf16[128,4096]{1,0:T(8,128)(2,1)}, u32[]{:S(2)}, u32[]{:S(2)}) collective-permute-start(bf16[128,4096]{1,0:T(8,128)(2,1)} %pad_maximum_fusion.2.refs_1_), channel_id=1, source_target_pairs={{0,16},{4,20},{8,24},{12,28},{16,0},{20,4},{24,8},{28,12},{1,17},{... | collective-permute-start | bytes 3145736 | tf_op jit(solution)/shard_map/ppermute | solution.py:22
  7.9 1.5 collective-permute-start.6
  9.7 0.9 collective-permute-done
  11.2 0.8 collective-permute-start.9
  12.1 1.4 copy-done
  13.5 5.6 %activations.4 = (bf16[576,256]{1,0:T(8,128)(2,1)S(1)}, f32[1,256]{1,0:T(1,128)S(1)}, bf16[2,128,1024]{2,1,0:T(8,128)(2,1)S(1)}, bf16[2,128,1024]{2,1,0:T(8,128)...) custom-call(s32[2]{0:T(128)S(1)} %pad_add_fusion.where_ref.refs_6_, ...), custom_call_target="tpu_custom_call" | custom-call | flops 1 | bytes 1 | tf_op jit(solution)/shard_map/activations/pallas_call | solution.py:89
  19.2 13.9 %collective-permute-done.8.one_ref.two_ref = f32[16,128]{1,0:T(8,128)S(1)} collective-permute-done((f32[16,128]{1,0:T(8,128)S(1)}, f32[16,128]{1,0:T(8,128)S(1)}, u32[]{:S(2)}, u32[]{:S(2)}) %collective-permute-start.8) | collective-permute-done | bytes 8224 | tf_op jit(solution)/shard_map/ppermute | solution.py:22
  33.8 1.5 collective-permute-start.5
  35.8 1.6 collective-permute-done.12
  37.5 1.6 collective-permute-start.13
  39.2 5.8 %activations.5 = (bf16[576,256]{1,0:T(8,128)(2,1)S(1)}, f32[1,256]{1,0:T(1,128)S(1)}, bf16[2,128,1024]{2,1,0:T(8,128)(2,1)S(1)}, bf16[2,128,1024]{2,1,0:T(8,128)...) custom-call(s32[2]{0:T(128)S(1)} %pad_add_fusion.where_ref.refs_6_, ...), custom_call_target="tpu_custom_call" | custom-call | flops 1 | bytes 1 | tf_op jit(solution)/shard_map/activations/pallas_call | solution.py:89
  45.1 14.4 %collective-permute-done.5.refs_1_.refs_9_ = bf16[128,4096]{1,0:T(8,128)(2,1)S(1)} collective-permute-done((bf16[128,4096]{1,0:T(8,128)(2,1)}, bf16[128,4096]{1,0:T(8,128)(2,1)S(1)}, u32[]{:S(2)}, u32[]{:S(2)}) %collective-permute-start.5) | collective-permute-done | bytes 1048608 | tf_op jit(solution)/shard_map/ppermute | solution.py:22
  59.5 1.2 collective-permute-done.4.refs_0_.refs_8_
  62.4 1.8 %collective-permute-done.3 = bf16[2,128,1024]{2,1,0:T(8,128)(2,1)S(1)} collective-permute-done((bf16[2,128,1024]{2,1,0:T(8,128)(2,1)S(1)}, bf16[2,128,1024]{2,1,0:T(8,128)(2,1)S(1)}, u32[]{:S(2)}, u32[]{:S(2)}) %collective-permute-start.3) | collective-permute-done | bytes 524320 | tf_op jit(solution)/shard_map/ppermute | solution.py:22
  64.1 1.6 collective-permute-start.20
  65.8 2.7 %collective-permute-start.18 = (bf16[128,1024]{1,0:T(8,128)(2,1)S(1)}, bf16[128,1024]{1,0:T(8,128)(2,1)S(1)}, u32[]{:S(2)}, u32[]{:S(2)}) collective-permute-start(bf16[128,1024]{1,0:T(8,128)(2,1)S(1)} %slice_bitcast_fusion.6), channel_id=1, source_target_pairs={{0,2},{1,3},{2,0},{3,1},{4,6},{5,7},{6,4},{7,5},{8,10},{9,11},{10,... | collective-permute-start | bytes 786440 | tf_op jit(solution)/shard_map/ppermute | solution.py:22
  68.5 4.0 %activations.6 = (bf16[576,256]{1,0:T(8,128)(2,1)}, f32[1,256]{1,0:T(1,128)S(1)}, bf16[2,128,1024]{2,1,0:T(8,128)(2,1)S(1)}, bf16[2,128,1024]{2,1,0:T(8,128)(2,1...) custom-call(s32[2]{0:T(128)S(1)} %pad_add_fusion.where_ref.refs_6_, ...), custom_call_target="tpu_custom_call" | custom-call | flops 1 | bytes 1 | tf_op jit(solution)/shard_map/activations/pallas_call | solution.py:89
  72.5 14.5 %collective-permute-done.14.refs_0_.refs_12_ = bf16[128,4096]{1,0:T(8,128)(2,1)S(1)} collective-permute-done((bf16[128,4096]{1,0:T(8,128)(2,1)}, bf16[128,4096]{1,0:T(8,128)(2,1)S(1)}, u32[]{:S(2)}, u32[]{:S(2)}) %collective-permute-start.14) | collective-permute-done | bytes 1048608 | tf_op jit(solution)/shard_map/ppermute | solution.py:22
  88.3 1.5 collective-permute-start.22
  89.9 0.9 collective-permute-done.21
  90.7 1.5 collective-permute-start.28
  92.3 0.6 collective-permute-done.26
  93.2 1.6 collective-permute-start.27
  94.9 1.6 collective-permute-start.29
  96.5 2.6 %collective-permute-start.25 = (bf16[128,1024]{1,0:T(8,128)(2,1)S(1)}, bf16[128,1024]{1,0:T(8,128)(2,1)S(1)}, u32[]{:S(2)}, u32[]{:S(2)}) collective-permute-start(bf16[128,1024]{1,0:T(8,128)(2,1)S(1)} %slice_bitcast_fusion.4), channel_id=1, source_target_pairs={{0,2},{1,3},{2,0},{3,1},{4,6},{5,7},{6,4},{7,5},{8,10},{9,11},{10,... | collective-permute-start | bytes 786440 | tf_op jit(solution)/shard_map/ppermute | solution.py:22
  99.1 0.7 fusion.7
  99.8 4.7 %activations.7 = (bf16[576,256]{1,0:T(8,128)(2,1)S(1)}, f32[1,256]{1,0:T(1,128)S(1)}, bf16[2,128,1024]{2,1,0:T(8,128)(2,1)S(1)}, bf16[2,128,1024]{2,1,0:T(8,128)...) custom-call(s32[2]{0:T(128)S(1)} %pad_add_fusion.where_ref.refs_6_, ...), custom_call_target="tpu_custom_call" | custom-call | flops 1 | bytes 1 | tf_op jit(solution)/shard_map/activations/pallas_call | solution.py:89
  105.2 0.9 collective-permute-done.29.refs_21_
  106.1 5.8 %collective-permute-done.25 = bf16[128,1024]{1,0:T(8,128)(2,1)S(1)} collective-permute-done((bf16[128,1024]{1,0:T(8,128)(2,1)S(1)}, bf16[128,1024]{1,0:T(8,128)(2,1)S(1)}, u32[]{:S(2)}, u32[]{:S(2)}) %collective-permute-start.25) | collective-permute-done | bytes 262176 | tf_op jit(solution)/shard_map/ppermute | solution.py:22
  111.9 0.9 collective-permute-done.27
  113.0 2.6 %collective-permute-start.32 = (f32[8,128]{1,0:T(8,128)S(1)}, f32[8,128]{1,0:T(8,128)S(1)}, u32[]{:S(2)}, u32[]{:S(2)}) collective-permute-start(f32[8,128]{1,0:T(8,128)S(1)} %maximum_maximum_fusion), channel_id=1, source_target_pairs={{0,1},{1,0},{2,3},{3,2},{4,5},{5,4},{6,7},{7,6},{8,9},{9,8},{10,11... | collective-permute-start | bytes 12296 | tf_op jit(solution)/shard_map/ppermute | solution.py:22
  115.7 0.8 slice_bitcast_fusion.2
  116.5 1.6 collective-permute-start.35
  118.1 1.4 collective-permute-start.33
  119.5 0.8 fusion.2
  120.3 1.0 add.99
  121.3 1.4 collective-permute-start.34
  122.6 9.1 %collective-permute-done.33 = f32[8,128]{1,0:T(8,128)S(1)} collective-permute-done((f32[8,128]{1,0:T(8,128)S(1)}, f32[8,128]{1,0:T(8,128)S(1)}, u32[]{:S(2)}, u32[]{:S(2)}) %collective-permute-start.33) | collective-permute-done | bytes 4128 | tf_op jit(solution)/shard_map/ppermute | solution.py:22
  132.4 0.6 copy.24
  133.0 3.3 %all-to-all-start = ((bf16[8,1,128]{2,1,0:T(2,128)(2,1)}), bf16[8,1,128]{2,1,0:T(2,128)(2,1)S(1)}, u32[]{:S(2)}, u32[]{:S(2)}) async-start(bf16[8,1,128]{2,1,0:T(2,128)(2,1)} %copy.24), calls=%async_computation | async-start | bytes 8192 | tf_op jit(solution)/shard_map/all_to_all | solution.py:251
  136.3 1.8 %fusion.11 = (bf16[64,1024]{1,0:T(8,128)(2,1)}, bf16[64,1024]{1,0:T(8,128)(2,1)}) fusion(bf16[128,1024]{1,0:T(8,128)(2,1)} %fusion.2), kind=kLoop, calls=%fused_computation.49 | loop fusion | bytes 524288 | tf_op jit(solution)/shard_map/slice | solution.py:260
  138.1 1.9 %collective-permute-start.41 = (bf16[576,256]{1,0:T(8,128)(2,1)}, bf16[576,256]{1,0:T(8,128)(2,1)}, u32[]{:S(2)}, u32[]{:S(2)}) collective-permute-start(bf16[576,256]{1,0:T(8,128)(2,1)} %copy-done.29), channel_id=1, source_target_pairs={{0,16},{4,20},{8,24},{12,28},{16,0},{20,4},{24,8},{28,12},{1,17},{... | collective-permute-start | bytes 884744 | tf_op jit(solution)/shard_map/ppermute | solution.py:22
  140.0 0.8 all-to-all-done
  140.9 0.7 collective-permute-done.34
  141.6 1.1 fusion.1
  142.8 1.6 add_add_fusion
  144.5 0.6 collective-permute-start.36
  145.2 1.6 collective-permute-start.37
  146.8 1.3 collective-permute-done.41.refs_23_
  148.1 1.2 copy-done.17
  149.3 1.2 copy-done.19
  150.6 1.2 copy-done.21
  151.8 1.0 copy-done.24
  152.7 1.0 copy-done.26
  153.7 1.0 copy-done.28
  154.7 1.0 copy-done.30
  155.6 9.9 %weight_grads.1 = (bf16[1,192,4096]{2,1,0:T(8,128)(2,1)}, bf16[1,192,4096]{2,1,0:T(8,128)(2,1)}, bf16[1,192,4096]{2,1,0:T(8,128)(2,1)}) custom-call(s32[1]{0:T(128)} %bitcast.17.flag_ref, bf16[128,4096]{1,0:T(8,128)(2,1)} %pad_maximum_fusion.1.refs_0_, bf16[128,4096]{1,0:T(8,128)(2,1)} %pad_maximum_fusion.2.refs_1_, ...), custom_call_target="tpu_custom_call" | custom-call | flops 1 | bytes 1 | tf_op jit(solution)/shard_map/weight_grads/pallas_call | solution.py:157
  165.6 2.8 %collective-permute-start.42 = (bf16[128,1024]{1,0:T(8,128)(2,1)S(1)}, bf16[128,1024]{1,0:T(8,128)(2,1)S(1)}, u32[]{:S(2)}, u32[]{:S(2)}) collective-permute-start(bf16[128,1024]{1,0:T(8,128)(2,1)S(1)} %fusion), channel_id=1, source_target_pairs={{0,24},{4,28},{8,16},{12,20},{16,8},{20,12},{24,0},{28,4},{1,25},{... | collective-permute-start | bytes 786440 | tf_op jit(solution)/shard_map/ppermute | solution.py:22
  168.3 0.6 select_reduce_fusion
  168.9 5.2 %collective-permute-done.42 = bf16[128,1024]{1,0:T(8,128)(2,1)S(1)} collective-permute-done((bf16[128,1024]{1,0:T(8,128)(2,1)S(1)}, bf16[128,1024]{1,0:T(8,128)(2,1)S(1)}, u32[]{:S(2)}, u32[]{:S(2)}) %collective-permute-start.42) | collective-permute-done | bytes 262176 | tf_op jit(solution)/shard_map/ppermute | solution.py:22
  174.1 0.9 fusion.6
  (158 shorter events, 8.1 us)
Async XLA Ops:
  2.3 7.1 %copy-start.41 = (bf16[128,4]{0,1:T(4,128)(2,1)S(1)}, bf16[128,4]{0,1:T(4,128)(2,1)}, u32[]{:S(2)}) copy-start(bf16[128,4]{0,1:T(4,128)(2,1)} %param.14) | copy-start | bytes 3076
  2.3 7.2 %copy-start.34 = (bf16[1,192,4096]{2,1,0:T(8,128)(2,1)S(1)}, bf16[1,192,4096]{2,1,0:T(8,128)(2,1)}, u32[]{:S(2)}) copy-start(bf16[1,192,4096]{2,1,0:T(8,128)(2,1)} %param.11) | copy-start | bytes 4718596
  2.3 7.2 %copy-start.35 = (bf16[1,192,4096]{2,1,0:T(8,128)(2,1)S(1)}, bf16[1,192,4096]{2,1,0:T(8,128)(2,1)}, u32[]{:S(2)}) copy-start(bf16[1,192,4096]{2,1,0:T(8,128)(2,1)} %param.10) | copy-start | bytes 4718596
  3.4 7.8 %collective-permute-start.2 = (bf16[128,4096]{1,0:T(8,128)(2,1)}, bf16[128,4096]{1,0:T(8,128)(2,1)}, u32[]{:S(2)}, u32[]{:S(2)}) collective-permute-start(bf16[128,4096]{1,0:T(8,128)(2,1)} %pad_maximum_fusion.2.refs_1_), channel_id=1, source_target_pairs={{0,4},{4,0},{8,12},{12,8},{16,20},{20,16},{24,28},{28,24},{1,5},{5... | collective-permute-start | bytes 3145736 | tf_op jit(solution)/shard_map/ppermute | solution.py:22
  4.9 7.2 %collective-permute-start.1 = (bf16[128,4096]{1,0:T(8,128)(2,1)}, bf16[128,4096]{1,0:T(8,128)(2,1)}, u32[]{:S(2)}, u32[]{:S(2)}) collective-permute-start(bf16[128,4096]{1,0:T(8,128)(2,1)} %pad_maximum_fusion.1.refs_0_), channel_id=1, source_target_pairs={{0,4},{4,0},{8,12},{12,8},{16,20},{20,16},{24,28},{28,24},{1,5},{5... | collective-permute-start | bytes 3145736 | tf_op jit(solution)/shard_map/ppermute | solution.py:22
  4.9 28.2 %collective-permute-start.7 = (bf16[128,4096]{1,0:T(8,128)(2,1)}, bf16[128,4096]{1,0:T(8,128)(2,1)}, u32[]{:S(2)}, u32[]{:S(2)}) collective-permute-start(bf16[128,4096]{1,0:T(8,128)(2,1)} %pad_maximum_fusion.2.refs_1_), channel_id=1, source_target_pairs={{0,16},{4,20},{8,24},{12,28},{16,0},{20,4},{24,8},{28,12},{1,17},{... | collective-permute-start | bytes 3145736 | tf_op jit(solution)/shard_map/ppermute | solution.py:22
  7.9 25.2 %collective-permute-start.6 = (bf16[128,4096]{1,0:T(8,128)(2,1)}, bf16[128,4096]{1,0:T(8,128)(2,1)}, u32[]{:S(2)}, u32[]{:S(2)}) collective-permute-start(bf16[128,4096]{1,0:T(8,128)(2,1)} %pad_maximum_fusion.1.refs_0_), channel_id=1, source_target_pairs={{0,8},{4,12},{8,0},{12,4},{16,24},{20,28},{24,16},{28,20},{1,9},{5... | collective-permute-start | bytes 3145736 | tf_op jit(solution)/shard_map/ppermute | solution.py:22
  9.4 1.2 collective-permute-start
  10.7 22.4 %collective-permute-start.8 = (f32[16,128]{1,0:T(8,128)S(1)}, f32[16,128]{1,0:T(8,128)S(1)}, u32[]{:S(2)}, u32[]{:S(2)}) collective-permute-start(f32[16,128]{1,0:T(8,128)S(1)} %pad_maximum_fusion.5.one_ref.two_ref), channel_id=1, source_target_pairs={{0,8},{4,12},{8,0},{12,4},{16,24},{20,28},{24,16},{28,20},{1,9},{5... | collective-permute-start | bytes 24584 | tf_op jit(solution)/shard_map/ppermute | solution.py:22
  11.2 21.9 %collective-permute-start.9 = (f32[16,128]{1,0:T(8,128)S(1)}, f32[16,128]{1,0:T(8,128)S(1)}, u32[]{:S(2)}, u32[]{:S(2)}) collective-permute-start(f32[16,128]{1,0:T(8,128)S(1)} %pad_maximum_fusion.5.one_ref.two_ref), channel_id=1, source_target_pairs={{0,16},{4,20},{8,24},{12,28},{16,0},{20,4},{24,8},{28,12},{1,17},{... | collective-permute-start | bytes 24584 | tf_op jit(solution)/shard_map/ppermute | solution.py:22
  19.2 20.0 %copy-start.1 = (bf16[1,192,4096]{2,1,0:T(8,128)(2,1)S(1)}, bf16[1,192,4096]{2,1,0:T(8,128)(2,1)}, u32[]{:S(2)}) copy-start(bf16[1,192,4096]{2,1,0:T(8,128)(2,1)} %param.12) | copy-start | bytes 4718596
  33.1 6.1 %collective-permute-start.10 = (bf16[128,4096]{1,0:T(8,128)(2,1)}, bf16[128,4096]{1,0:T(8,128)(2,1)S(1)}, u32[]{:S(2)}, u32[]{:S(2)}) collective-permute-start(bf16[128,4096]{1,0:T(8,128)(2,1)} %collective-permute-done.6.refs_0_.refs_4_), channel_id=1, source_target_pairs={{0,4},{4,0},{8,12},{12,8},{16,20},{20,16},{24,28},{28,24},{1,5},{5... | collective-permute-start | bytes 3145736 | tf_op jit(solution)/shard_map/ppermute | solution.py:22
  33.2 6.0 %collective-permute-start.11 = (bf16[128,4096]{1,0:T(8,128)(2,1)}, bf16[128,4096]{1,0:T(8,128)(2,1)S(1)}, u32[]{:S(2)}, u32[]{:S(2)}) collective-permute-start(bf16[128,4096]{1,0:T(8,128)(2,1)} %collective-permute-done.7.refs_1_.refs_5_), channel_id=1, source_target_pairs={{0,4},{4,0},{8,12},{12,8},{16,20},{20,16},{24,28},{28,24},{1,5},{5... | collective-permute-start | bytes 3145736 | tf_op jit(solution)/shard_map/ppermute | solution.py:22
  33.7 3.6 %collective-permute-start.12 = (bf16[2,128,1024]{2,1,0:T(8,128)(2,1)S(1)}, bf16[2,128,1024]{2,1,0:T(8,128)(2,1)S(1)}, u32[]{:S(2)}, u32[]{:S(2)}) collective-permute-start(bf16[2,128,1024]{2,1,0:T(8,128)(2,1)S(1)} %get-tuple-element.71), channel_id=1, source_target_pairs={{0,4},{4,0},{8,12},{12,8},{16,20},{20,16},{24,28},{28,24},{1,5},{5... | collective-permute-start | bytes 1572872 | tf_op jit(solution)/shard_map/ppermute | solution.py:22
  33.8 25.7 %collective-permute-start.5 = (bf16[128,4096]{1,0:T(8,128)(2,1)}, bf16[128,4096]{1,0:T(8,128)(2,1)S(1)}, u32[]{:S(2)}, u32[]{:S(2)}) collective-permute-start(bf16[128,4096]{1,0:T(8,128)(2,1)} %pad_maximum_fusion.2.refs_1_), channel_id=1, source_target_pairs={{0,8},{4,12},{8,0},{12,4},{16,24},{20,28},{24,16},{28,20},{1,9},{5... | collective-permute-start | bytes 3145736 | tf_op jit(solution)/shard_map/ppermute | solution.py:22
  35.3 25.4 %collective-permute-start.4 = (bf16[128,4096]{1,0:T(8,128)(2,1)}, bf16[128,4096]{1,0:T(8,128)(2,1)S(1)}, u32[]{:S(2)}, u32[]{:S(2)}) collective-permute-start(bf16[128,4096]{1,0:T(8,128)(2,1)} %pad_maximum_fusion.1.refs_0_), channel_id=1, source_target_pairs={{0,16},{4,20},{8,24},{12,28},{16,0},{20,4},{24,8},{28,12},{1,17},{... | collective-permute-start | bytes 3145736 | tf_op jit(solution)/shard_map/ppermute | solution.py:22
  37.5 23.2 %collective-permute-start.13 = (bf16[2,128,1024]{2,1,0:T(8,128)(2,1)S(1)}, bf16[2,128,1024]{2,1,0:T(8,128)(2,1)S(1)}, u32[]{:S(2)}, u32[]{:S(2)}) collective-permute-start(bf16[2,128,1024]{2,1,0:T(8,128)(2,1)S(1)} %add.85), channel_id=1, source_target_pairs={{0,1},{1,0},{2,3},{3,2},{4,5},{5,4},{6,7},{7,6},{8,9},{9,8},{10,11... | collective-permute-start | bytes 1572872 | tf_op jit(solution)/shard_map/ppermute | solution.py:22
  45.0 49.9 %copy-start.23 = (bf16[576,256]{1,0:T(8,128)(2,1)}, bf16[576,256]{1,0:T(8,128)(2,1)S(1)}, u32[]{:S(2)}) copy-start(bf16[576,256]{1,0:T(8,128)(2,1)S(1)} %get-tuple-element.90.refs_17_) | copy-start | bytes 884740
  45.0 16.8 %collective-permute-start.19 = (bf16[2,128,1024]{2,1,0:T(8,128)(2,1)S(1)}, bf16[2,128,1024]{2,1,0:T(8,128)(2,1)S(1)}, u32[]{:S(2)}, u32[]{:S(2)}) collective-permute-start(bf16[2,128,1024]{2,1,0:T(8,128)(2,1)S(1)} %get-tuple-element.78), channel_id=1, source_target_pairs={{0,4},{4,0},{8,12},{12,8},{16,20},{20,16},{24,28},{28,24},{1,5},{5... | collective-permute-start | bytes 1572872 | tf_op jit(solution)/shard_map/ppermute | solution.py:22
  59.5 9.0 %copy-start.6 = (bf16[128,4096]{1,0:T(8,128)(2,1)}, bf16[128,4096]{1,0:T(8,128)(2,1)S(1)}, u32[]{:S(2)}) copy-start(bf16[128,4096]{1,0:T(8,128)(2,1)S(1)} %collective-permute-done.5.refs_1_.refs_9_) | copy-start | bytes 3145732
  60.7 7.8 %copy-start.8 = (bf16[128,4096]{1,0:T(8,128)(2,1)}, bf16[128,4096]{1,0:T(8,128)(2,1)S(1)}, u32[]{:S(2)}) copy-start(bf16[128,4096]{1,0:T(8,128)(2,1)S(1)} %collective-permute-done.4.refs_0_.refs_8_) | copy-start | bytes 3145732
  60.7 5.1 %collective-permute-start.16 = (bf16[128,4096]{1,0:T(8,128)(2,1)S(1)}, bf16[128,4096]{1,0:T(8,128)(2,1)S(1)}, u32[]{:S(2)}, u32[]{:S(2)}) collective-permute-start(bf16[128,4096]{1,0:T(8,128)(2,1)S(1)} %collective-permute-done.4.refs_0_.refs_8_), channel_id=1, source_target_pairs={{0,4},{4,0},{8,12},{12,8},{16,20},{20,16},{24,28},{28,24},{1,5},{5... | collective-permute-start | bytes 3145736 | tf_op jit(solution)/shard_map/ppermute | solution.py:22
  60.7 3.4 %collective-permute-start.3 = (bf16[2,128,1024]{2,1,0:T(8,128)(2,1)S(1)}, bf16[2,128,1024]{2,1,0:T(8,128)(2,1)S(1)}, u32[]{:S(2)}, u32[]{:S(2)}) collective-permute-start(bf16[2,128,1024]{2,1,0:T(8,128)(2,1)S(1)} %get-tuple-element.62), channel_id=1, source_target_pairs={{0,4},{4,0},{8,12},{12,8},{16,20},{20,16},{24,28},{28,24},{1,5},{5... | collective-permute-start | bytes 1572872 | tf_op jit(solution)/shard_map/ppermute | solution.py:22
  61.2 7.3 %collective-permute-start.17 = (bf16[128,4096]{1,0:T(8,128)(2,1)S(1)}, bf16[128,4096]{1,0:T(8,128)(2,1)S(1)}, u32[]{:S(2)}, u32[]{:S(2)}) collective-permute-start(bf16[128,4096]{1,0:T(8,128)(2,1)S(1)} %collective-permute-done.5.refs_1_.refs_9_), channel_id=1, source_target_pairs={{0,4},{4,0},{8,12},{12,8},{16,20},{20,16},{24,28},{28,24},{1,5},{5... | collective-permute-start | bytes 3145736 | tf_op jit(solution)/shard_map/ppermute | solution.py:22
  61.3 25.7 %collective-permute-start.14 = (bf16[128,4096]{1,0:T(8,128)(2,1)}, bf16[128,4096]{1,0:T(8,128)(2,1)S(1)}, u32[]{:S(2)}, u32[]{:S(2)}) collective-permute-start(bf16[128,4096]{1,0:T(8,128)(2,1)} %collective-permute-done.6.refs_0_.refs_4_), channel_id=1, source_target_pairs={{0,16},{4,20},{8,24},{12,28},{16,0},{20,4},{24,8},{28,12},{1,17},{... | collective-permute-start | bytes 3145736 | tf_op jit(solution)/shard_map/ppermute | solution.py:22
  61.8 25.4 %collective-permute-start.15 = (bf16[128,4096]{1,0:T(8,128)(2,1)}, bf16[128,4096]{1,0:T(8,128)(2,1)S(1)}, u32[]{:S(2)}, u32[]{:S(2)}) collective-permute-start(bf16[128,4096]{1,0:T(8,128)(2,1)} %collective-permute-done.7.refs_1_.refs_5_), channel_id=1, source_target_pairs={{0,8},{4,12},{8,0},{12,4},{16,24},{20,28},{24,16},{28,20},{1,9},{5... | collective-permute-start | bytes 3145736 | tf_op jit(solution)/shard_map/ppermute | solution.py:22
  64.1 23.1 %collective-permute-start.20 = (bf16[2,128,1024]{2,1,0:T(8,128)(2,1)S(1)}, bf16[2,128,1024]{2,1,0:T(8,128)(2,1)S(1)}, u32[]{:S(2)}, u32[]{:S(2)}) collective-permute-start(bf16[2,128,1024]{2,1,0:T(8,128)(2,1)S(1)} %add.87), channel_id=1, source_target_pairs={{0,1},{1,0},{2,3},{3,2},{4,5},{5,4},{6,7},{7,6},{8,9},{9,8},{10,11... | collective-permute-start | bytes 1572872 | tf_op jit(solution)/shard_map/ppermute | solution.py:22
  65.8 21.4 %collective-permute-start.18 = (bf16[128,1024]{1,0:T(8,128)(2,1)S(1)}, bf16[128,1024]{1,0:T(8,128)(2,1)S(1)}, u32[]{:S(2)}, u32[]{:S(2)}) collective-permute-start(bf16[128,1024]{1,0:T(8,128)(2,1)S(1)} %slice_bitcast_fusion.6), channel_id=1, source_target_pairs={{0,2},{1,3},{2,0},{3,1},{4,6},{5,7},{6,4},{7,5},{8,10},{9,11},{10,... | collective-permute-start | bytes 786440 | tf_op jit(solution)/shard_map/ppermute | solution.py:22
  87.0 12.8 %copy-start.14 = (bf16[128,4096]{1,0:T(8,128)(2,1)}, bf16[128,4096]{1,0:T(8,128)(2,1)S(1)}, u32[]{:S(2)}) copy-start(bf16[128,4096]{1,0:T(8,128)(2,1)S(1)} %collective-permute-done.14.refs_0_.refs_12_) | copy-start | bytes 3145732
  87.2 12.6 %copy-start.16 = (bf16[128,4096]{1,0:T(8,128)(2,1)}, bf16[128,4096]{1,0:T(8,128)(2,1)S(1)}, u32[]{:S(2)}) copy-start(bf16[128,4096]{1,0:T(8,128)(2,1)S(1)} %collective-permute-done.15.refs_1_.refs_13_) | copy-start | bytes 3145732
  87.2 7.6 %copy-start.38 = (bf16[128,1024]{1,0:T(8,128)(2,1)}, bf16[128,1024]{1,0:T(8,128)(2,1)S(1)}, u32[]{:S(2)}) copy-start(bf16[128,1024]{1,0:T(8,128)(2,1)S(1)} %collective-permute-done.18) | copy-start | bytes 786436
  87.2 9.2 %collective-permute-start.23 = (bf16[128,4096]{1,0:T(8,128)(2,1)S(1)}, bf16[128,4096]{1,0:T(8,128)(2,1)S(1)}, u32[]{:S(2)}, u32[]{:S(2)}) collective-permute-start(bf16[128,4096]{1,0:T(8,128)(2,1)S(1)} %collective-permute-done.14.refs_0_.refs_12_), channel_id=1, source_target_pairs={{0,4},{4,0},{8,12},{12,8},{16,20},{20,16},{24,28},{28,24},{1,5},{5... | collective-permute-start | bytes 3145736 | tf_op jit(solution)/shard_map/ppermute | solution.py:22
  87.3 3.4 %collective-permute-start.21 = (bf16[2,128,1024]{2,1,0:T(8,128)(2,1)S(1)}, bf16[2,128,1024]{2,1,0:T(8,128)(2,1)S(1)}, u32[]{:S(2)}, u32[]{:S(2)}) collective-permute-start(bf16[2,128,1024]{2,1,0:T(8,128)(2,1)S(1)} %get-tuple-element.81), channel_id=1, source_target_pairs={{0,4},{4,0},{8,12},{12,8},{16,20},{20,16},{24,28},{28,24},{1,5},{5... | collective-permute-start | bytes 1572872 | tf_op jit(solution)/shard_map/ppermute | solution.py:22
  87.8 11.9 %collective-permute-start.24 = (bf16[128,4096]{1,0:T(8,128)(2,1)S(1)}, bf16[128,4096]{1,0:T(8,128)(2,1)S(1)}, u32[]{:S(2)}, u32[]{:S(2)}) collective-permute-start(bf16[128,4096]{1,0:T(8,128)(2,1)S(1)} %collective-permute-done.15.refs_1_.refs_13_), channel_id=1, source_target_pairs={{0,4},{4,0},{8,12},{12,8},{16,20},{20,16},{24,28},{28,24},{1,5},{5... | collective-permute-start | bytes 3145736 | tf_op jit(solution)/shard_map/ppermute | solution.py:22
  87.9 5.1 %collective-permute-start.26 = (bf16[2,128,1024]{2,1,0:T(8,128)(2,1)S(1)}, bf16[2,128,1024]{2,1,0:T(8,128)(2,1)S(1)}, u32[]{:S(2)}, u32[]{:S(2)}) collective-permute-start(bf16[2,128,1024]{2,1,0:T(8,128)(2,1)S(1)} %get-tuple-element.88), channel_id=1, source_target_pairs={{0,4},{4,0},{8,12},{12,8},{16,20},{20,16},{24,28},{28,24},{1,5},{5... | collective-permute-start | bytes 1572872 | tf_op jit(solution)/shard_map/ppermute | solution.py:22
  88.3 6.5 %collective-permute-start.22 = (f32[16,128]{1,0:T(8,128)S(1)}, f32[16,128]{1,0:T(8,128)S(1)}, u32[]{:S(2)}, u32[]{:S(2)}) collective-permute-start(f32[16,128]{1,0:T(8,128)S(1)} %collective-permute-done.8.one_ref.two_ref), channel_id=1, source_target_pairs={{0,16},{4,20},{8,24},{12,28},{16,0},{20,4},{24,8},{28,12},{1,17},{... | collective-permute-start | bytes 24584 | tf_op jit(solution)/shard_map/ppermute | solution.py:22
  90.7 13.8 %collective-permute-start.28 = (bf16[576,256]{1,0:T(8,128)(2,1)S(1)}, bf16[576,256]{1,0:T(8,128)(2,1)S(1)}, u32[]{:S(2)}, u32[]{:S(2)}) collective-permute-start(bf16[576,256]{1,0:T(8,128)(2,1)S(1)} %get-tuple-element.89.refs_16_), channel_id=1, source_target_pairs={{0,16},{4,20},{8,24},{12,28},{16,0},{20,4},{24,8},{28,12},{1,17},{... | collective-permute-start | bytes 884744 | tf_op jit(solution)/shard_map/ppermute | solution.py:22
  93.2 19.6 %collective-permute-start.27 = (bf16[2,128,1024]{2,1,0:T(8,128)(2,1)S(1)}, bf16[2,128,1024]{2,1,0:T(8,128)(2,1)S(1)}, u32[]{:S(2)}, u32[]{:S(2)}) collective-permute-start(bf16[2,128,1024]{2,1,0:T(8,128)(2,1)S(1)} %add.91), channel_id=1, source_target_pairs={{0,1},{1,0},{2,3},{3,2},{4,5},{5,4},{6,7},{7,6},{8,9},{9,8},{10,11... | collective-permute-start | bytes 1572872 | tf_op jit(solution)/shard_map/ppermute | solution.py:22
  94.9 11.2 %collective-permute-start.29 = (bf16[576,256]{1,0:T(8,128)(2,1)S(1)}, bf16[576,256]{1,0:T(8,128)(2,1)S(1)}, u32[]{:S(2)}, u32[]{:S(2)}) collective-permute-start(bf16[576,256]{1,0:T(8,128)(2,1)S(1)} %get-tuple-element.90.refs_17_), channel_id=1, source_target_pairs={{0,16},{4,20},{8,24},{12,28},{16,0},{20,4},{24,8},{28,12},{1,17},{... | collective-permute-start | bytes 884744 | tf_op jit(solution)/shard_map/ppermute | solution.py:22
  96.5 8.1 %copy-start.18 = (bf16[128,4096]{1,0:T(8,128)(2,1)}, bf16[128,4096]{1,0:T(8,128)(2,1)S(1)}, u32[]{:S(2)}) copy-start(bf16[128,4096]{1,0:T(8,128)(2,1)S(1)} %collective-permute-done.23.refs_2_.refs_14_) | copy-start | bytes 3145732
  96.5 15.5 %collective-permute-start.25 = (bf16[128,1024]{1,0:T(8,128)(2,1)S(1)}, bf16[128,1024]{1,0:T(8,128)(2,1)S(1)}, u32[]{:S(2)}, u32[]{:S(2)}) collective-permute-start(bf16[128,1024]{1,0:T(8,128)(2,1)S(1)} %slice_bitcast_fusion.4), channel_id=1, source_target_pairs={{0,2},{1,3},{2,0},{3,1},{4,6},{5,7},{6,4},{7,5},{8,10},{9,11},{10,... | collective-permute-start | bytes 786440 | tf_op jit(solution)/shard_map/ppermute | solution.py:22
  99.8 15.8 %collective-permute-start.30 = (bf16[2,128,1024]{2,1,0:T(8,128)(2,1)S(1)}, bf16[2,128,1024]{2,1,0:T(8,128)(2,1)S(1)}, u32[]{:S(2)}, u32[]{:S(2)}) collective-permute-start(bf16[2,128,1024]{2,1,0:T(8,128)(2,1)S(1)} %get-tuple-element.93), channel_id=1, source_target_pairs={{0,4},{4,0},{8,12},{12,8},{16,20},{20,16},{24,28},{28,24},{1,5},{5... | collective-permute-start | bytes 1572872 | tf_op jit(solution)/shard_map/ppermute | solution.py:22
  104.6 16.7 %copy-start.22 = (bf16[2,128,1024]{2,1,0:T(8,128)(2,1)}, bf16[2,128,1024]{2,1,0:T(8,128)(2,1)S(1)}, u32[]{:S(2)}) copy-start(bf16[2,128,1024]{2,1,0:T(8,128)(2,1)S(1)} %get-tuple-element.101) | copy-start | bytes 1572868
  104.6 16.7 %copy-start.29 = (bf16[576,256]{1,0:T(8,128)(2,1)}, bf16[576,256]{1,0:T(8,128)(2,1)S(1)}, u32[]{:S(2)}) copy-start(bf16[576,256]{1,0:T(8,128)(2,1)S(1)} %get-tuple-element.106.refs_19_) | copy-start | bytes 884740
  104.6 16.7 %copy-start.25 = (bf16[576,256]{1,0:T(8,128)(2,1)}, bf16[576,256]{1,0:T(8,128)(2,1)S(1)}, u32[]{:S(2)}) copy-start(bf16[576,256]{1,0:T(8,128)(2,1)S(1)} %collective-permute-done.28.refs_20_) | copy-start | bytes 884740
  104.6 42.2 %collective-permute-start.40 = (bf16[576,256]{1,0:T(8,128)(2,1)}, bf16[576,256]{1,0:T(8,128)(2,1)}, u32[]{:S(2)}, u32[]{:S(2)}) collective-permute-start(bf16[576,256]{1,0:T(8,128)(2,1)} %get-tuple-element.105.refs_18_), channel_id=1, source_target_pairs={{0,16},{4,20},{8,24},{12,28},{16,0},{20,4},{24,8},{28,12},{1,17},{... | collective-permute-start | bytes 884744 | tf_op jit(solution)/shard_map/ppermute | solution.py:22
  106.1 15.2 %copy-start.27 = (bf16[576,256]{1,0:T(8,128)(2,1)}, bf16[576,256]{1,0:T(8,128)(2,1)S(1)}, u32[]{:S(2)}) copy-start(bf16[576,256]{1,0:T(8,128)(2,1)S(1)} %collective-permute-done.29.refs_21_) | copy-start | bytes 884740
  112.8 5.2 %collective-permute-start.31 = (bf16[2,128,1024]{2,1,0:T(8,128)(2,1)S(1)}, bf16[2,128,1024]{2,1,0:T(8,128)(2,1)S(1)}, u32[]{:S(2)}, u32[]{:S(2)}) collective-permute-start(bf16[2,128,1024]{2,1,0:T(8,128)(2,1)S(1)} %get-tuple-element.96), channel_id=1, source_target_pairs={{0,4},{4,0},{8,12},{12,8},{16,20},{20,16},{24,28},{28,24},{1,5},{5... | collective-permute-start | bytes 1572872 | tf_op jit(solution)/shard_map/ppermute | solution.py:22
  113.0 5.1 %collective-permute-start.32 = (f32[8,128]{1,0:T(8,128)S(1)}, f32[8,128]{1,0:T(8,128)S(1)}, u32[]{:S(2)}, u32[]{:S(2)}) collective-permute-start(f32[8,128]{1,0:T(8,128)S(1)} %maximum_maximum_fusion), channel_id=1, source_target_pairs={{0,1},{1,0},{2,3},{3,2},{4,5},{5,4},{6,7},{7,6},{8,9},{9,8},{10,11... | collective-permute-start | bytes 12296 | tf_op jit(solution)/shard_map/ppermute | solution.py:22
  116.5 24.4 %collective-permute-start.35 = (bf16[128,1024]{1,0:T(8,128)(2,1)}, bf16[128,1024]{1,0:T(8,128)(2,1)}, u32[]{:S(2)}, u32[]{:S(2)}) collective-permute-start(bf16[128,1024]{1,0:T(8,128)(2,1)} %slice_bitcast_fusion.2), channel_id=1, source_target_pairs={{0,2},{1,3},{2,0},{3,1},{4,6},{5,7},{6,4},{7,5},{8,10},{9,11},{10,... | collective-permute-start | bytes 786440 | tf_op jit(solution)/shard_map/ppermute | solution.py:22
  118.1 13.7 %collective-permute-start.33 = (f32[8,128]{1,0:T(8,128)S(1)}, f32[8,128]{1,0:T(8,128)S(1)}, u32[]{:S(2)}, u32[]{:S(2)}) collective-permute-start(f32[8,128]{1,0:T(8,128)S(1)} %add.96), channel_id=1, source_target_pairs={{0,2},{1,3},{2,0},{3,1},{4,6},{5,7},{6,4},{7,5},{8,10},{9,11},{10,... | collective-permute-start | bytes 12296 | tf_op jit(solution)/shard_map/ppermute | solution.py:22
  119.5 28.6 %copy-start.15 = (bf16[128,4096]{1,0:T(8,128)(2,1)S(1)}, bf16[128,4096]{1,0:T(8,128)(2,1)}, u32[]{:S(2)}) copy-start(bf16[128,4096]{1,0:T(8,128)(2,1)} %copy-done.14) | copy-start | bytes 3145732
  120.2 22.5 %collective-permute-start.38 = (bf16[2,128,1024]{2,1,0:T(8,128)(2,1)}, bf16[2,128,1024]{2,1,0:T(8,128)(2,1)}, u32[]{:S(2)}, u32[]{:S(2)}) collective-permute-start(bf16[2,128,1024]{2,1,0:T(8,128)(2,1)} %get-tuple-element.102), channel_id=1, source_target_pairs={{0,4},{4,0},{8,12},{12,8},{16,20},{20,16},{24,28},{28,24},{1,5},{5... | collective-permute-start | bytes 1572872 | tf_op jit(solution)/shard_map/ppermute | solution.py:22
  120.2 27.8 %copy-start.13 = (bf16[128,4096]{1,0:T(8,128)(2,1)S(1)}, bf16[128,4096]{1,0:T(8,128)(2,1)}, u32[]{:S(2)}) copy-start(bf16[128,4096]{1,0:T(8,128)(2,1)} %copy-done.12) | copy-start | bytes 3145732
  121.3 20.3 %collective-permute-start.34 = (bf16[2,128,1024]{2,1,0:T(8,128)(2,1)}, bf16[2,128,1024]{2,1,0:T(8,128)(2,1)}, u32[]{:S(2)}, u32[]{:S(2)}) collective-permute-start(bf16[2,128,1024]{2,1,0:T(8,128)(2,1)} %add.99), channel_id=1, source_target_pairs={{0,1},{1,0},{2,3},{3,2},{4,5},{5,4},{6,7},{7,6},{8,9},{9,8},{10,11... | collective-permute-start | bytes 1572872 | tf_op jit(solution)/shard_map/ppermute | solution.py:22
  133.0 7.9 %all-to-all-start = ((bf16[8,1,128]{2,1,0:T(2,128)(2,1)}), bf16[8,1,128]{2,1,0:T(2,128)(2,1)S(1)}, u32[]{:S(2)}, u32[]{:S(2)}) async-start(bf16[8,1,128]{2,1,0:T(2,128)(2,1)} %copy.24), calls=%async_computation | async-start | bytes 8192 | tf_op jit(solution)/shard_map/all_to_all | solution.py:251
  136.3 11.8 %copy-start.11 = (bf16[128,4096]{1,0:T(8,128)(2,1)S(1)}, bf16[128,4096]{1,0:T(8,128)(2,1)}, u32[]{:S(2)}) copy-start(bf16[128,4096]{1,0:T(8,128)(2,1)} %copy-done.10) | copy-start | bytes 3145732
  138.1 10.0 %collective-permute-start.41 = (bf16[576,256]{1,0:T(8,128)(2,1)}, bf16[576,256]{1,0:T(8,128)(2,1)}, u32[]{:S(2)}, u32[]{:S(2)}) collective-permute-start(bf16[576,256]{1,0:T(8,128)(2,1)} %copy-done.29), channel_id=1, source_target_pairs={{0,16},{4,20},{8,24},{12,28},{16,0},{20,4},{24,8},{28,12},{1,17},{... | collective-permute-start | bytes 884744 | tf_op jit(solution)/shard_map/ppermute | solution.py:22
  144.4 21.1 %collective-permute-start.39 = (bf16[128,1024]{1,0:T(8,128)(2,1)S(1)}, bf16[128,1024]{1,0:T(8,128)(2,1)S(1)}, u32[]{:S(2)}, u32[]{:S(2)}) collective-permute-start(bf16[128,1024]{1,0:T(8,128)(2,1)S(1)} %slice_bitcast_fusion), channel_id=1, source_target_pairs={{0,2},{1,3},{2,0},{3,1},{4,6},{5,7},{6,4},{7,5},{8,10},{9,11},{10,... | collective-permute-start | bytes 786440 | tf_op jit(solution)/shard_map/ppermute | solution.py:22
  144.5 24.4 %collective-permute-start.36 = (bf16[128,1024]{1,0:T(8,128)(2,1)S(1)}, bf16[128,1024]{1,0:T(8,128)(2,1)S(1)}, u32[]{:S(2)}, u32[]{:S(2)}) collective-permute-start(bf16[128,1024]{1,0:T(8,128)(2,1)S(1)} %pad_maximum_fusion.3), channel_id=1, source_target_pairs={{0,8},{4,12},{8,0},{12,4},{16,24},{20,28},{24,16},{28,20},{1,9},{5... | collective-permute-start | bytes 786440 | tf_op jit(solution)/shard_map/ppermute | solution.py:22
  145.2 23.8 %collective-permute-start.37 = (bf16[128,1024]{1,0:T(8,128)(2,1)S(1)}, bf16[128,1024]{1,0:T(8,128)(2,1)S(1)}, u32[]{:S(2)}, u32[]{:S(2)}) collective-permute-start(bf16[128,1024]{1,0:T(8,128)(2,1)S(1)} %pad_maximum_fusion.4), channel_id=1, source_target_pairs={{0,16},{4,20},{8,24},{12,28},{16,0},{20,4},{24,8},{28,12},{1,17},{... | collective-permute-start | bytes 786440 | tf_op jit(solution)/shard_map/ppermute | solution.py:22
  155.6 18.5 %copy-start.33 = (bf16[2,128,1024]{2,1,0:T(8,128)(2,1)S(1)}, bf16[2,128,1024]{2,1,0:T(8,128)(2,1)}, u32[]{:S(2)}) copy-start(bf16[2,128,1024]{2,1,0:T(8,128)(2,1)} %copy-done.32) | copy-start | bytes 1572868
  155.6 18.5 %copy-start.39 = (bf16[128,1024]{1,0:T(8,128)(2,1)S(1)}, bf16[128,1024]{1,0:T(8,128)(2,1)}, u32[]{:S(2)}) copy-start(bf16[128,1024]{1,0:T(8,128)(2,1)} %copy-done.38) | copy-start | bytes 786436
  165.6 8.5 %collective-permute-start.42 = (bf16[128,1024]{1,0:T(8,128)(2,1)S(1)}, bf16[128,1024]{1,0:T(8,128)(2,1)S(1)}, u32[]{:S(2)}, u32[]{:S(2)}) collective-permute-start(bf16[128,1024]{1,0:T(8,128)(2,1)S(1)} %fusion), channel_id=1, source_target_pairs={{0,24},{4,28},{8,16},{12,20},{16,8},{20,12},{24,0},{28,4},{1,25},{... | collective-permute-start | bytes 786440 | tf_op jit(solution)/shard_map/ppermute | solution.py:22
  (23 other events, 88.2 us)

commit v6 on v5

--- a/solution.py
+++ b/solution.py
@@ -10,7 +10,7 @@
 
 CONTRACT_LAST = (((1,), (1,)), ((), ()))
 CONTRACT_ROWS = (((0,), (0,)), ((), ()))
-VMEM = 20 * 1024 * 1024
+VMEM = 14 * 1024 * 1024
 
 
 def from_behind(value, axis, by):
@@ -31,15 +31,47 @@
     return [pltpu.with_memory_space_constraint(value, pltpu.VMEM) for value in values]
 
 
-def rows_of(messages, start, size, columns):
-    return jnp.concatenate([ref[pl.ds(start, size), columns] for ref in messages], axis=0)
-
-
-def activations_kernel(parts, where_ref, one_ref, two_ref, *refs):
-    messages = refs[:4]
-    in_ref, down_ref = refs[4:6]
-    acts_ref, score_ref, keep_near, keep_far, give_near, give_far, both = refs[7:]
-    rows, width = messages[0].shape
+def rows_of(pieces, columns):
+    return jnp.concatenate([ref[pl.ds(start, size), columns] for ref, start, size in pieces], axis=0)
+
+
+def pieces_of(places, refs):
+    return [(refs[i], start, size) for i, start, size in places]
+
+
+def pack_kernel(tokens, cotangent, first, second, sems):
+    half = tokens.shape[0] // 2
+    copies = []
+    for i, (ref, out) in enumerate(((tokens, first), (cotangent, first), (tokens, second), (cotangent, second))):
+        copies.append(
+            pltpu.make_async_copy(
+                ref.at[pl.ds(i // 2 * half, half), :], out.at[pl.ds(i % 2 * half, half), :], sems.at[i]
+            )
+        )
+    for copy in copies:
+        copy.start()
+    for copy in copies:
+        copy.wait()
+
+
+def pack(tokens, cotangent):
+    message = pltpu.VMEM(tokens.shape, tokens.dtype)
+    return pl.pallas_call(
+        pack_kernel,
+        out_shape=(message, message),
+        in_specs=[pl.BlockSpec(memory_space=pl.ANY)] * 2,
+        out_specs=[pl.BlockSpec(memory_space=pltpu.VMEM)] * 2,
+        scratch_shapes=[pltpu.SemaphoreType.DMA((4,))],
+        cost_estimate=pl.CostEstimate(flops=1, bytes_accessed=1, transcendentals=0),
+        name="pack",
+    )(tokens, cotangent)
+
+
+def activations_kernel(place, x_places, dy_places, count, parts, where_ref, one_ref, two_ref, *refs):
+    x_pieces, dy_pieces = pieces_of(x_places, refs), pieces_of(dy_places, refs)
+    in_ref, down_ref = refs[count : count + 2]
+    acts_ref, score_ref, keep_near, keep_far, give_near, give_far, both = refs[-7:]
+    rows, width = keep_near.shape[1], in_ref.shape[1]
     half = rows // 2
     units = down_ref.shape[0]
     chunk = width // parts
@@ -56,7 +88,7 @@
     pre, back = None, None
     for part in range(parts):
         columns = pl.ds(part * chunk, chunk)
-        x, dy = rows_of(messages, 0, half, columns), rows_of(messages, half, half, columns)
+        x, dy = rows_of(x_pieces, columns), rows_of(dy_pieces, columns)
         one = lax.dot_general(in_ref[:, columns], x, CONTRACT_LAST, preferred_element_type=jnp.float32)
         two = lax.dot_general(down_ref[:, columns], dy, CONTRACT_LAST, preferred_element_type=jnp.float32)
         pre = one if pre is None else pre + one
@@ -69,8 +101,8 @@
     grad_hidden = g * back
     slope = sigma * (1.0 + pre_gate * (1.0 - sigma))
     grads = jnp.concatenate([grad_hidden * pre_up * slope, grad_hidden * active], axis=0)
-    acts_ref[pl.ds(0, 2 * units), :] = grads.astype(jnp.bfloat16)
-    acts_ref[pl.ds(2 * units, units), :] = (g * hidden).astype(jnp.bfloat16)
+    acts_ref[place, pl.ds(0, 2 * units), :] = grads.astype(jnp.bfloat16)
+    acts_ref[place, pl.ds(2 * units, units), :] = (g * hidden).astype(jnp.bfloat16)
     both[...] = grads.T.astype(jnp.bfloat16)
     for part in range(parts):
         columns = pl.ds(pl.multiple_of((group ^ part) * chunk, chunk), chunk)
@@ -81,15 +113,17 @@
         give[part // 2] = share[rows:]
 
 
-def activations(parts, where, tables, messages, weights, before):
-    rows, width = messages[0].shape
+def activations(place, places, parts, where, tables, held, weights, before):
+    operands, x_places, dy_places = held
+    width = operands[0].shape[1]
+    rows = sum(size for _, _, size in x_places) // 2
     units = weights[1].shape[0]
     bf16 = jnp.bfloat16
     share = pltpu.VMEM((parts // 2, rows, width // parts), bf16)
     return pl.pallas_call(
-        functools.partial(activations_kernel, parts),
+        functools.partial(activations_kernel, place, x_places, dy_places, len(operands), parts),
         out_shape=(
-            pltpu.VMEM((3 * units, 2 * rows), bf16),
+            pltpu.VMEM((places, 3 * units, 2 * rows), bf16),
             pltpu.VMEM((1, 2 * rows), jnp.float32),
             share,
             share,
@@ -97,31 +131,47 @@
             share,
         ),
         in_specs=[pl.BlockSpec(memory_space=pltpu.SMEM)]
-        + [pl.BlockSpec(memory_space=pltpu.VMEM)] * 8
-        + [pl.BlockSpec(memory_space=pl.ANY)],
+        + [pl.BlockSpec(memory_space=pltpu.VMEM)] * (len(operands) + 4 + len(before)),
         out_specs=[pl.BlockSpec(memory_space=pltpu.VMEM)] * 6,
         scratch_shapes=[pltpu.VMEM((2 * rows, 2 * units), bf16)],
+        input_output_aliases={len(operands) + 5: 0} if before else {},
         compiler_params=pltpu.CompilerParams(vmem_limit_bytes=VMEM),
         cost_estimate=pl.CostEstimate(flops=1, bytes_accessed=1, transcendentals=0),
         name="activations",
-    )(where, *in_vmem(*tables, *messages, *weights), before)
-
-
-def weight_grads_kernel(sources, parts, flag_ref, *refs):
-    groups = len(sources)
-    messages, refs = refs[: 4 * groups], refs[4 * groups :]
-    own, other, refs = refs[:groups], refs[groups : 2 * groups], refs[2 * groups :]
+    )(where, *in_vmem(*tables, *operands, *weights, *before))
+
+
+def weight_grads_kernel(sources, x_places, dy_places, loaded, parts, flag_ref, *refs):
+    count = 1 + max(place[0] for place in x_places + dy_places)
+    operands, refs = list(refs[:count]), refs[count:]
+    own, other, refs = refs[:2], refs[2:4], refs[4:]
     outs = refs[:3]
-    acts, results, out_sems = refs[3:]
-    rows, width = messages[0].shape
+    held, acts, results, sems, out_sems = refs[3:]
+    units, width = outs[0].shape[1:]
+    rows = own[0].shape[2] // 2
     half = rows // 2
-    units = outs[0].shape[1]
     chunk = width // parts
+    copies = []
+    for part in range(parts):
+        columns = pl.ds(part * chunk, chunk)
+        copies.append([])
+        for i in range(loaded):
+            copies[-1].append(
+                pltpu.make_async_copy(
+                    operands[i].at[:, columns], held.at[i, pl.ds(0, operands[i].shape[0]), columns], sems.at[part, i]
+                )
+            )
+            copies[-1][-1].start()
+    for i in range(loaded):
+        operands[i] = held.at[i]
+    x_pieces, dy_pieces = pieces_of(x_places, operands), pieces_of(dy_places, operands)
     tiles = [(one ^ core, two ^ core) for one, two in sources for core in (0, CORE)]
     first = lax.broadcasted_iota(jnp.int32, (1, rows), 1) < half
 
     def tile_of(groups_of, place):
-        return groups_of[place // 2][:, pl.ds(place % 2 * rows, rows)]
+        group, early = place // 2, groups_of[0].shape[0]
+        ref, group = (groups_of[0], group) if group < early else (groups_of[1], group - early)
+        return ref[group, :, pl.ds(place % 2 * rows, rows)]
 
     for place, (one, two) in enumerate(tiles):
         from_one = [tile[0] for tile in tiles].index(one ^ ACROSS_Y)
@@ -130,8 +180,10 @@
         acts[:, pl.ds(place * rows, rows)] = jnp.where(flag_ref[0] == 1, arrived, tile_of(own, place))
     sent = []
     for part in range(parts):
+        for copy in copies[part]:
+            copy.wait()
         columns = pl.ds(part * chunk, chunk)
-        x, dy = rows_of(messages, 0, half, columns), rows_of(messages, half, half, columns)
+        x, dy = rows_of(x_pieces, columns), rows_of(dy_pieces, columns)
         both = jnp.dot(acts[pl.ds(0, 2 * units), :], x, preferred_element_type=jnp.float32)
         results[part, pl.ds(0, 2 * units), :] = both.astype(jnp.bfloat16)
         down = jnp.dot(acts[pl.ds(2 * units, units), :], dy, preferred_element_type=jnp.float32)
@@ -147,27 +199,36 @@
         copy.wait()
 
 
-def weight_grads(sources, flag, messages, own, other):
-    parts = 8
-    rows, width = messages[0].shape
-    units = own[0].shape[0] // 3
-    total = len(messages) * rows // 2
+def weight_grads(sources, flag, groups, own, other):
+    parts, loaded = 4, len(groups[0][0]) + len(groups[1][0])
+    operands, x_places, dy_places = [], [], []
+    for held, x_of, dy_of in groups:
+        x_places += [(i + len(operands), start, size) for i, start, size in x_of]
+        dy_places += [(i + len(operands), start, size) for i, start, size in dy_of]
+        operands += held
+    rows, width = operands[0].shape
+    units = own[0].shape[1] // 3
+    total = sum(size for _, _, size in x_places)
     bf16 = jnp.bfloat16
-    operands = in_vmem(*messages, *own, *other)
+    rest = in_vmem(*operands[loaded:], *own, *other)
     return pl.pallas_call(
-        functools.partial(weight_grads_kernel, sources, parts),
+        functools.partial(weight_grads_kernel, sources, x_places, dy_places, loaded, parts),
         out_shape=(jax.ShapeDtypeStruct((1, units, width), bf16),) * 3,
-        in_specs=[pl.BlockSpec(memory_space=pltpu.SMEM)] + [pl.BlockSpec(memory_space=pltpu.VMEM)] * len(operands),
+        in_specs=[pl.BlockSpec(memory_space=pltpu.SMEM)]
+        + [pl.BlockSpec(memory_space=pl.ANY)] * loaded
+        + [pl.BlockSpec(memory_space=pltpu.VMEM)] * len(rest),
         out_specs=[pl.BlockSpec(memory_space=pl.ANY)] * 3,
         scratch_shapes=[
+            pltpu.VMEM((loaded, rows, width), bf16),
             pltpu.VMEM((3 * units, total), bf16),
             pltpu.VMEM((parts, 3 * units, width // parts), bf16),
+            pltpu.SemaphoreType.DMA((parts, loaded)),
             pltpu.SemaphoreType.DMA((parts, 3)),
         ],
-        compiler_params=pltpu.CompilerParams(vmem_limit_bytes=VMEM),
+        compiler_params=pltpu.CompilerParams(vmem_limit_bytes=26 * 1024 * 1024),
         cost_estimate=pl.CostEstimate(flops=1, bytes_accessed=1, transcendentals=0),
         name="weight_grads",
-    )(flag, *operands)
+    )(flag, *operands[:loaded], *rest)
 
 
 CORE, ACROSS_X, ACROSS_Y = 1, 2, 4
@@ -187,72 +248,79 @@
     def expert_swap(value, by):
         return swap(value, "expert", by)
 
-    a = {0: jnp.concatenate([tokens[:half], cotangent[:half]])}
-    b = {0: jnp.concatenate([tokens[half:], cotangent[half:]])}
+    def core_swap(message):
+        return [expert_swap(message[:half], CORE), expert_swap(message[half:], CORE)]
+
+    rows = 2 * half
+    own_block = [tokens, cotangent, expert_swap(tokens, CORE), expert_swap(cotangent, CORE)]
+    own_block = (own_block, [(0, 0, rows), (2, 0, rows)], [(1, 0, rows), (3, 0, rows)])
+    a, b = {}, {}
+    a[0], b[0] = pack(tokens, cotangent)
     a[2], b[4] = expert_swap(a[0], ACROSS_X), expert_swap(b[0], ACROSS_Y)
     a[4], b[2] = expert_swap(a[0], ACROSS_Y), expert_swap(b[0], ACROSS_X)
-    a[1], b[1] = expert_swap(a[0], CORE), expert_swap(b[0], CORE)
 
     named = expert_ids[:, :, None] == jnp.arange(expert_count, dtype=jnp.int32)[None, None, :]
     table = jnp.sum(jnp.where(named, gates[:, :, None].astype(f32), 0), axis=1)
     tables = {0: jnp.concatenate([table.T, expert_swap(table.T, CORE)])}
     tables[2], tables[4] = expert_swap(tables[0], ACROSS_X), expert_swap(tables[0], ACROSS_Y)
 
-    acts, scores, messages = [], [], []
+    scores, groups = [], []
     barrier = lax.optimization_barrier
 
-    def work(one, two, before):
-        held = [a[one], b[two], a[one ^ CORE], b[two ^ CORE]]
-        act, score, keep_near, keep_far, give_near, give_far = activations(
-            parts, where, (tables[one], tables[two]), held, weights, before
+    def group_of(one, two):
+        mates = core_swap(one) + core_swap(two)
+        x_places = [(0, 0, half), (1, 0, half), (2, 0, half), (4, 0, half)]
+        dy_places = [(0, half, half), (1, half, half), (3, 0, half), (5, 0, half)]
+        return [one, two, *mates], x_places, dy_places
+
+    def work(one, two, held, *before, place=0, places=3):
+        acts, score, keep_near, keep_far, give_near, give_far = activations(
+            place, places, parts, where, (tables[one], tables[two]), held, weights, before
         )
-        acts.append(act)
         scores.append(score)
-        messages.extend(held)
-        return score, keep_near, keep_far, expert_swap(give_near, CORE), expert_swap(give_far, CORE)
-
-    def to_neighbour(keep_near, keep_far, near, far):
+        groups.append(held)
+        return acts, expert_swap(give_far, CORE), (keep_near, keep_far, expert_swap(give_near, CORE))
+
+    def to_neighbour(far, share):
+        keep_near, keep_far, near = share
         return keep_near + near, swap(keep_far + far, "dp", 1)
 
     def to_far(near, arrived):
         near = near + arrived
         return near[0].astype(f32), swap(near[1], "dp", 2)
 
-    done_a, *share_a = work(0, 0, where)
-    a[2], b[4], tables[2], tables[4], done_a = barrier((a[2], b[4], tables[2], tables[4], done_a))
+    acts, far_a, share_a = work(0, 0, own_block)
+    a[2], b[4], tables[2], tables[4], acts, far_a = barrier((a[2], b[4], tables[2], tables[4], acts, far_a))
     a[6], b[6] = expert_swap(a[2], ACROSS_Y), expert_swap(b[4], ACROSS_X)
     tables[6] = expert_swap(tables[2], ACROSS_Y)
-    a[3], b[5] = expert_swap(a[2], CORE), expert_swap(b[4], CORE)
-    done_b, *share_b = work(2, 4, done_a)
-    near_a, near_in_a = to_neighbour(*share_a)
-    a[4], b[2], done_b, near_in_a = barrier((a[4], b[2], done_b, near_in_a))
-    a[5], b[3] = expert_swap(a[4], CORE), expert_swap(b[2], CORE)
-    done_c, *share_c = work(4, 2, done_b)
+    near_a, near_in_a = to_neighbour(far_a, share_a)
+    acts, far_b, share_b = work(2, 4, group_of(a[2], b[4]), acts, place=1)
+    a[4], b[2], tables[6], acts, near_in_a, far_b = barrier((a[4], b[2], tables[6], acts, near_in_a, far_b))
+    near_b, near_in_b = to_neighbour(far_b, share_b)
     total_a, far_in_a = to_far(near_a, near_in_a)
-    near_b, near_in_b = to_neighbour(*share_b)
-    a[6], b[6], done_c, far_in_a, near_in_b = barrier((a[6], b[6], done_c, far_in_a, near_in_b))
-    a[7], b[7] = expert_swap(a[6], CORE), expert_swap(b[6], CORE)
-    other = [expert_swap(act, half_axis) for act in acts[:2]]
-    done_d, *share_d = work(6, 6, done_c)
+    acts, far_c, share_c = work(4, 2, group_of(a[4], b[2]), acts, place=2)
+    a[6], b[6], acts, far_in_a, near_in_b, far_c = barrier((a[6], b[6], acts, far_in_a, near_in_b, far_c))
+    near_c, near_in_c = to_neighbour(far_c, share_c)
+    other = expert_swap(acts, half_axis)
+    last_acts, far_d, share_d = work(6, 6, group_of(a[6], b[6]), places=1)
+    last_other = expert_swap(last_acts, half_axis)
     total_b, far_in_b = to_far(near_b, near_in_b)
-    near_c, near_in_c = to_neighbour(*share_c)
-    done_d, far_in_b, near_in_c, *other = barrier((done_d, far_in_b, near_in_c, *other))
-    other += [expert_swap(act, half_axis) for act in acts[2:]]
-    tiles = jnp.concatenate(scores[:3] + [done_d], axis=1).reshape(expert_count, 2 * half)
+    tiles = jnp.concatenate(scores, axis=1).reshape(expert_count, 2 * half)
     second = jnp.concatenate([tiles[:2, half:], tiles[4:6, half:], tiles[2:4, half:], tiles[6:, half:]])
     score_rows = jnp.concatenate([tiles[:, :half], second], axis=1)
     score_in = swap(score_rows, "dp", 1)
-    keep_near, keep_far, near, far = share_d
-    far, score_in = barrier((far, score_in))
-    near_d, near_in_d = to_neighbour(keep_near, keep_far, near, far)
+    far_d, score_in, far_in_b, near_in_c, other = barrier((far_d, score_in, far_in_b, near_in_c, other))
+    near_d, near_in_d = to_neighbour(far_d, share_d)
     score_rows = score_rows + score_in
     score_rows = score_rows + swap(score_rows, "dp", 2)
     score_rows = jnp.take(score_rows.astype(bf16), jnp.arange(expert_count, dtype=jnp.int32) ^ me, axis=0)
     score_rows = lax.all_to_all(score_rows, "expert", split_axis=0, concat_axis=0, tiled=True)
     total_c, far_in_c = to_far(near_c, near_in_c)
-    score_rows, near_in_d, far_in_c, own_flag = barrier((score_rows, near_in_d, far_in_c, own_flag))
+    score_rows, near_in_d, far_in_c, own_flag, last_other = barrier(
+        (score_rows, near_in_d, far_in_c, own_flag, last_other)
+    )
     total_d, far_in_d = to_far(near_d, near_in_d)
-    grads = weight_grads(((0, 0), (2, 4), (4, 2), (6, 6)), own_flag, messages, acts, other)
+    grads = weight_grads(((0, 0), (2, 4), (4, 2), (6, 6)), own_flag, groups, (acts, last_acts), (other, last_other))
     far_in_d, grads = barrier((far_in_d, grads))
 
     total_a, total_b = total_a + far_in_a.astype(f32), total_b + far_in_b.astype(f32)

time: 176 us -> 182 us (1.034)
  local copies, waits for them, and re-layouts: 14.6 us -> 18 us
  starting transfers between devices: 44.2 us -> 41.3 us
  other arithmetic: 10.2 us -> 12.8 us
    unnamed x87 -> x101, local copies, waits for them, and re-layouts: 9.08 us -> 14.3 us
    ppermute x43 -> x47, starting transfers between devices: 40.8 us -> 38 us  [swap(): lax.ppermute(value, axis, [(i, i ^ by) for i in range(lax.axis_size(axis))])]
    concatenate x1, other arithmetic: 0.2 us -> 2.37 us  [whole_shards(): weights = (jnp.concatenate([gate_weight[0], up_weight[0]]), down_weight[0])]
    concatenate x3 -> x1, other arithmetic: 2.09 us -> 0.01 us  [whole_shards(): tiles = jnp.concatenate(scores, axis=1).reshape(expert_count, 2 * half)]
    all_to_all x1, waiting for transfers between devices: 0.84 us -> 2.78 us  [whole_shards(): lax.all_to_all(score_rows, 'expert', split_axis=0, concat_axis=0, tiled=T...]
    pallas_call x5 -> x6, Pallas kernels: 30 us -> 31.8 us  [the longest x4 18.9 us: activations(): pl.pallas_call(functools.partial(activations_kernel, place, x_places, dy_...]
    ppermute x43 -> x47, waiting for transfers between devices: 74 us -> 73 us  [swap(): lax.ppermute(value, axis, [(i, i ^ by) for i in range(lax.axis_size(axis))])]
  transfers between devices with their start and end apart: 44 -> 48, of which waited for: 18 -> 14; matrix products, arithmetic and copies ran while one was open for 7% -> 8% of each run, Pallas kernels for 17% -> 18%
where the time goes in v6:
time: 182 us; the launch traced here: 181 us
  waiting for transfers between devices  75.8 us (42%)
  starting transfers between devices  41.3 us (23%)
  Pallas kernels  31.8 us (17%)
  local copies, waits for them, and re-layouts  18 us (10%)
  other arithmetic  12.8 us (7%)
    ppermute x47, waiting for transfers between devices, swap(): lax.ppermute(value, axis, [(i, i ^ by) for i in range(lax.axis_size(axis))])  73 us
    ppermute x47, starting transfers between devices, swap(): lax.ppermute(value, axis, [(i, i ^ by) for i in range(lax.axis_size(axis))])  38 us
    pallas_call x4, Pallas kernels, activations(): pl.pallas_call(functools.partial(activations_kernel, place, x_places, dy_...  18.9 us
    unnamed x101, local copies, waits for them, and re-layouts  14.3 us
    pallas_call x1, Pallas kernels, weight_grads(): pl.pallas_call(functools.partial(weight_grads_kernel, sources, x_places,...  9.97 us
  transfers between devices with their start and end apart: 48, of which 14 were waited for; matrix products, arithmetic and copies ran while one was open for 8% of the time, Pallas kernels for 18%

profile of v6, /device:TPU:0, one launch (start us, length us, event | category | flops | bytes accessed | tf_op | source)
XLA Modules:
  0.0 181.0 jit_solution(5293297323142016348)
XLA Ops:
  1.2 0.7 convert_element_type.74
  1.9 0.7 select_reduce_fusion.1
  3.0 2.9 %pack.1 = (bf16[128,4096]{1,0:T(8,128)(2,1)}, bf16[128,4096]{1,0:T(8,128)(2,1)}) custom-call(bf16[128,4096]{1,0:T(8,128)(2,1)} %refs_0_.3, bf16[128,4096]{1,0:T(8,128)(2,1)} %refs_1_.3), custom_call_target="tpu_custom_call" | custom-call | flops 1 | bytes 1 | tf_op jit(solution)/shard_map/pack/pallas_call | solution.py:59
  5.9 2.6 %collective-permute-start.6 = (bf16[128,4096]{1,0:T(8,128)(2,1)}, bf16[128,4096]{1,0:T(8,128)(2,1)S(1)}, u32[]{:S(2)}, u32[]{:S(2)}) collective-permute-start(bf16[128,4096]{1,0:T(8,128)(2,1)} %get-tuple-element.68), channel_id=1, source_target_pairs={{0,8},{4,12},{8,0},{12,4},{16,24},{20,28},{24,16},{28,20},{1,9},{5... | collective-permute-start | bytes 3145736 | tf_op jit(solution)/shard_map/ppermute | solution.py:22
  8.5 1.5 collective-permute-start.7
  10.1 2.4 %pad_maximum_fusion.refs_4_.refs_6_ = bf16[384,4096]{1,0:T(8,128)(2,1)S(1)} fusion(bf16[192,4096]{1,0:T(8,128)(2,1)} %bitcast.52, bf16[192,4096]{1,0:T(8,128)(2,1)} %bitcast.53), kind=kLoop, calls=%fused_computation.1 | loop fusion | flops 6291456 | bytes 6291456 | tf_op jit(solution)/shard_map/concatenate | solution.py:246
  13.0 5.0 %activations.4 = (bf16[3,576,256]{2,1,0:T(8,128)(2,1)S(1)}, f32[1,256]{1,0:T(1,128)S(1)}, bf16[2,128,1024]{2,1,0:T(8,128)(2,1)S(1)}, bf16[2,128,1024]{2,1,0:T(8,...) custom-call(s32[2]{0:T(128)S(1)} %pad_add_fusion.where_ref, ...), custom_call_target="tpu_custom_call" | custom-call | flops 1 | bytes 1 | tf_op jit(solution)/shard_map/activations/pallas_call | solution.py:123
  18.1 0.6 collective-permute-start.8
  18.9 13.8 %collective-permute-done.8.one_ref.two_ref = f32[16,128]{1,0:T(8,128)S(1)} collective-permute-done((f32[16,128]{1,0:T(8,128)S(1)}, f32[16,128]{1,0:T(8,128)S(1)}, u32[]{:S(2)}, u32[]{:S(2)}) %collective-permute-start.8) | collective-permute-done | bytes 8224 | tf_op jit(solution)/shard_map/ppermute | solution.py:22
  32.7 1.5 collective-permute-done.9.two_ref.one_ref
  34.8 1.3 fusion.13
  36.7 1.5 collective-permute-start.4
  39.0 1.6 collective-permute-start.16
  40.6 5.1 %activations.5 = (bf16[3,576,256]{2,1,0:T(8,128)(2,1)S(1)}, f32[1,256]{1,0:T(1,128)S(1)}, bf16[2,128,1024]{2,1,0:T(8,128)(2,1)S(1)}, bf16[2,128,1024]{2,1,0:T(8,...) custom-call(s32[2]{0:T(128)S(1)} %pad_add_fusion.where_ref, ...), custom_call_target="tpu_custom_call", output_to_operand_aliasing={{0}: (11, {})} | custom-call | flops 1 | bytes 1 | tf_op jit(solution)/shard_map/activations/pallas_call | solution.py:123
  45.9 0.6 collective-permute-start.11
  46.4 15.7 %collective-permute-done.4.refs_0_.refs_10_ = bf16[128,4096]{1,0:T(8,128)(2,1)S(1)} collective-permute-done((bf16[128,4096]{1,0:T(8,128)(2,1)}, bf16[128,4096]{1,0:T(8,128)(2,1)S(1)}, u32[]{:S(2)}, u32[]{:S(2)}) %collective-permute-start.4) | collective-permute-done | bytes 1048608 | tf_op jit(solution)/shard_map/ppermute | solution.py:22
  62.1 1.2 collective-permute-done.5.refs_1_.refs_11_
  64.7 0.7 collective-permute-done.20.refs_2_.refs_12_
  66.9 1.6 collective-permute-start.25
  68.5 4.0 %activations.6 = (bf16[3,576,256]{2,1,0:T(8,128)(2,1)S(1)}, f32[1,256]{1,0:T(1,128)S(1)}, bf16[2,128,1024]{2,1,0:T(8,128)(2,1)S(1)}, bf16[2,128,1024]{2,1,0:T(8,...) custom-call(s32[2]{0:T(128)S(1)} %pad_add_fusion.where_ref, ...), custom_call_target="tpu_custom_call", output_to_operand_aliasing={{0}: (11, {})} | custom-call | flops 1 | bytes 1 | tf_op jit(solution)/shard_map/activations/pallas_call | solution.py:123
  72.9 2.7 %collective-permute-start.24 = (bf16[128,1024]{1,0:T(8,128)(2,1)S(1)}, bf16[128,1024]{1,0:T(8,128)(2,1)S(1)}, u32[]{:S(2)}, u32[]{:S(2)}) collective-permute-start(bf16[128,1024]{1,0:T(8,128)(2,1)S(1)} %slice_bitcast_fusion.6), channel_id=1, source_target_pairs={{0,2},{1,3},{2,0},{3,1},{4,6},{5,7},{6,4},{7,5},{8,10},{9,11},{10,... | collective-permute-start | bytes 786440 | tf_op jit(solution)/shard_map/ppermute | solution.py:22
  75.5 0.7 fusion.7
  76.2 14.3 %collective-permute-done.18.refs_0_.refs_16_ = bf16[128,4096]{1,0:T(8,128)(2,1)S(1)} collective-permute-done((bf16[128,4096]{1,0:T(8,128)(2,1)S(1)}, bf16[128,4096]{1,0:T(8,128)(2,1)S(1)}, u32[]{:S(2)}, u32[]{:S(2)}) %collective-permute-start.18) | collective-permute-done | bytes 1048608 | tf_op jit(solution)/shard_map/ppermute | solution.py:22
  90.6 1.0 collective-permute-done.19.refs_1_.refs_17_
  92.9 1.1 collective-permute-start.36
  94.4 1.6 collective-permute-start.35
  96.1 2.6 %collective-permute-start.34 = (bf16[128,1024]{1,0:T(8,128)(2,1)S(1)}, bf16[128,1024]{1,0:T(8,128)(2,1)S(1)}, u32[]{:S(2)}, u32[]{:S(2)}) collective-permute-start(bf16[128,1024]{1,0:T(8,128)(2,1)S(1)} %slice_bitcast_fusion.4), channel_id=1, source_target_pairs={{0,2},{1,3},{2,0},{3,1},{4,6},{5,7},{6,4},{7,5},{8,10},{9,11},{10,... | collective-permute-start | bytes 786440 | tf_op jit(solution)/shard_map/ppermute | solution.py:22
  98.7 4.8 %activations.7 = (bf16[1,576,256]{2,1,0:T(8,128)(2,1)S(1)}, f32[1,256]{1,0:T(1,128)S(1)}, bf16[2,128,1024]{2,1,0:T(8,128)(2,1)S(1)}, bf16[2,128,1024]{2,1,0:T(8,...) custom-call(s32[2]{0:T(128)S(1)} %pad_add_fusion.where_ref, ...), custom_call_target="tpu_custom_call" | custom-call | flops 1 | bytes 1 | tf_op jit(solution)/shard_map/activations/pallas_call | solution.py:123
  103.7 9.7 %collective-permute-done.34 = bf16[128,1024]{1,0:T(8,128)(2,1)S(1)} collective-permute-done((bf16[128,1024]{1,0:T(8,128)(2,1)S(1)}, bf16[128,1024]{1,0:T(8,128)(2,1)S(1)}, u32[]{:S(2)}, u32[]{:S(2)}) %collective-permute-start.34) | collective-permute-done | bytes 262176 | tf_op jit(solution)/shard_map/ppermute | solution.py:22
  113.5 3.5 %collective-permute-start.33 = (f32[8,128]{1,0:T(8,128)S(1)}, f32[8,128]{1,0:T(8,128)S(1)}, u32[]{:S(2)}, u32[]{:S(2)}) collective-permute-start(f32[8,128]{1,0:T(8,128)S(1)} %maximum_maximum_fusion), channel_id=1, source_target_pairs={{0,1},{1,0},{2,3},{3,2},{4,5},{5,4},{6,7},{7,6},{8,9},{9,8},{10,11... | collective-permute-start | bytes 12296 | tf_op jit(solution)/shard_map/ppermute | solution.py:22
  117.0 1.1 collective-permute-start.41
  118.6 2.0 %collective-permute-start.38 = (f32[8,128]{1,0:T(8,128)S(1)}, f32[8,128]{1,0:T(8,128)S(1)}, u32[]{:S(2)}, u32[]{:S(2)}) collective-permute-start(f32[8,128]{1,0:T(8,128)S(1)} %add.96), channel_id=1, source_target_pairs={{0,2},{1,3},{2,0},{3,1},{4,6},{5,7},{6,4},{7,5},{8,10},{9,11},{10,... | collective-permute-start | bytes 12296 | tf_op jit(solution)/shard_map/ppermute | solution.py:22
  120.7 0.8 slice_bitcast_fusion.2
  121.4 1.0 collective-permute-start.40
  122.4 1.0 add.99
  123.4 2.0 %collective-permute-start.39 = (bf16[2,128,1024]{2,1,0:T(8,128)(2,1)}, bf16[2,128,1024]{2,1,0:T(8,128)(2,1)}, u32[]{:S(2)}, u32[]{:S(2)}) collective-permute-start(bf16[2,128,1024]{2,1,0:T(8,128)(2,1)} %add.99), channel_id=1, source_target_pairs={{0,1},{1,0},{2,3},{3,2},{4,5},{5,4},{6,7},{7,6},{8,9},{9,8},{10,11... | collective-permute-start | bytes 1572872 | tf_op jit(solution)/shard_map/ppermute | solution.py:22
  126.1 0.6 copy.26
  126.7 3.3 %all-to-all-start = ((bf16[8,1,128]{2,1,0:T(2,128)(2,1)}), bf16[8,1,128]{2,1,0:T(2,128)(2,1)S(1)}, u32[]{:S(2)}, u32[]{:S(2)}) async-start(bf16[8,1,128]{2,1,0:T(2,128)(2,1)} %copy.26), calls=%async_computation | async-start | bytes 8192 | tf_op jit(solution)/shard_map/all_to_all | solution.py:317
  130.0 1.8 fusion.2
  131.8 2.8 %all-to-all-done = bf16[8,1,128]{2,1,0:T(2,128)(2,1)S(1)} async-done(((bf16[8,1,128]{2,1,0:T(2,128)(2,1)}), bf16[8,1,128]{2,1,0:T(2,128)(2,1)S(1)}, u32[]{:S(2)}, u32[]{:S(2)}) %all-to-all-start) | async-done | bytes 2080 | tf_op jit(solution)/shard_map/all_to_all | solution.py:317
  134.6 2.1 %collective-permute-done.40 = bf16[128,1024]{1,0:T(8,128)(2,1)} collective-permute-done((bf16[128,1024]{1,0:T(8,128)(2,1)}, bf16[128,1024]{1,0:T(8,128)(2,1)}, u32[]{:S(2)}, u32[]{:S(2)}) %collective-permute-start.40) | collective-permute-done | bytes 262176 | tf_op jit(solution)/shard_map/ppermute | solution.py:22
  136.7 6.6 %collective-permute-done.39 = bf16[2,128,1024]{2,1,0:T(8,128)(2,1)} collective-permute-done((bf16[2,128,1024]{2,1,0:T(8,128)(2,1)}, bf16[2,128,1024]{2,1,0:T(8,128)(2,1)}, u32[]{:S(2)}, u32[]{:S(2)}) %collective-permute-start.39) | collective-permute-done | bytes 524320 | tf_op jit(solution)/shard_map/ppermute | solution.py:22
  143.3 1.2 fusion.1
  144.6 1.6 add_add_fusion
  146.3 0.6 collective-permute-start.42
  147.0 1.1 collective-permute-start.43
  148.1 1.0 copy-done.14
  149.1 1.0 copy-done.16
  150.2 1.0 copy-done.18
  151.2 1.0 copy-done.20
  152.3 1.0 copy-done.22
  153.3 1.0 copy-done.24
  154.3 1.0 copy-done.26
  155.4 1.0 copy-done.28
  156.4 1.0 copy-done.30
  157.5 1.0 copy-done.32
  158.5 1.0 copy-done.34
  159.5 1.0 copy-done.36
  160.6 1.2 copy-done.38
  161.8 10.0 %weight_grads.1 = (bf16[1,192,4096]{2,1,0:T(8,128)(2,1)}, bf16[1,192,4096]{2,1,0:T(8,128)(2,1)}, bf16[1,192,4096]{2,1,0:T(8,128)(2,1)}) custom-call(s32[1]{0:T(128)} %bitcast.17.flag_ref, bf16[128,4096]{1,0:T(8,128)(2,1)S(1)} %copy-done.1, bf16[128,4096]{1,0:T(8,128)(2,1)S(1)} %copy-done.2, bf16[128,4096]{1,0:T(8,128)(2,1)} %collective-permute-done.1.refs_2_, ...), custom_call_target="tpu_custom_call" | custom-call | flops 1 | bytes 1 | tf_op jit(solution)/shard_map/weight_grads/pallas_call | solution.py:214
  171.8 2.0 %collective-permute-start.46 = (bf16[128,1024]{1,0:T(8,128)(2,1)S(1)}, bf16[128,1024]{1,0:T(8,128)(2,1)S(1)}, u32[]{:S(2)}, u32[]{:S(2)}) collective-permute-start(bf16[128,1024]{1,0:T(8,128)(2,1)S(1)} %fusion), channel_id=1, source_target_pairs={{0,24},{4,28},{8,16},{12,20},{16,8},{20,12},{24,0},{28,4},{1,25},{... | collective-permute-start | bytes 786440 | tf_op jit(solution)/shard_map/ppermute | solution.py:22
  173.8 0.6 select_reduce_fusion
  174.4 5.7 %collective-permute-done.46 = bf16[128,1024]{1,0:T(8,128)(2,1)S(1)} collective-permute-done((bf16[128,1024]{1,0:T(8,128)(2,1)S(1)}, bf16[128,1024]{1,0:T(8,128)(2,1)S(1)}, u32[]{:S(2)}, u32[]{:S(2)}) %collective-permute-start.46) | collective-permute-done | bytes 262176 | tf_op jit(solution)/shard_map/ppermute | solution.py:22
  180.1 0.9 fusion.6
  (183 shorter events, 10.5 us)
Async XLA Ops:
  0.6 11.9 %collective-permute-start.1 = (bf16[128,4096]{1,0:T(8,128)(2,1)}, bf16[128,4096]{1,0:T(8,128)(2,1)}, u32[]{:S(2)}, u32[]{:S(2)}) collective-permute-start(bf16[128,4096]{1,0:T(8,128)(2,1)} %refs_0_.3), channel_id=1, source_target_pairs={{0,4},{4,0},{8,12},{12,8},{16,20},{20,16},{24,28},{28,24},{1,5},{5... | collective-permute-start | bytes 3145736 | tf_op jit(solution)/shard_map/ppermute | solution.py:22
  1.1 11.4 %collective-permute-start.2 = (bf16[128,4096]{1,0:T(8,128)(2,1)}, bf16[128,4096]{1,0:T(8,128)(2,1)}, u32[]{:S(2)}, u32[]{:S(2)}) collective-permute-start(bf16[128,4096]{1,0:T(8,128)(2,1)} %refs_1_.3), channel_id=1, source_target_pairs={{0,4},{4,0},{8,12},{12,8},{16,20},{20,16},{24,28},{28,24},{1,5},{5... | collective-permute-start | bytes 3145736 | tf_op jit(solution)/shard_map/ppermute | solution.py:22
  2.6 9.9 %collective-permute-start = (f32[8,128]{1,0:T(8,128)S(1)}, f32[8,128]{1,0:T(8,128)S(1)}, u32[]{:S(2)}, u32[]{:S(2)}) collective-permute-start(f32[8,128]{1,0:T(8,128)S(1)} %bitcast.56), channel_id=1, source_target_pairs={{0,4},{4,0},{8,12},{12,8},{16,20},{20,16},{24,28},{28,24},{1,5},{5... | collective-permute-start | bytes 12296 | tf_op jit(solution)/shard_map/ppermute | solution.py:22
  5.9 28.3 %collective-permute-start.6 = (bf16[128,4096]{1,0:T(8,128)(2,1)}, bf16[128,4096]{1,0:T(8,128)(2,1)S(1)}, u32[]{:S(2)}, u32[]{:S(2)}) collective-permute-start(bf16[128,4096]{1,0:T(8,128)(2,1)} %get-tuple-element.68), channel_id=1, source_target_pairs={{0,8},{4,12},{8,0},{12,4},{16,24},{20,28},{24,16},{28,20},{1,9},{5... | collective-permute-start | bytes 3145736 | tf_op jit(solution)/shard_map/ppermute | solution.py:22
  8.5 25.6 %collective-permute-start.7 = (bf16[128,4096]{1,0:T(8,128)(2,1)}, bf16[128,4096]{1,0:T(8,128)(2,1)}, u32[]{:S(2)}, u32[]{:S(2)}) collective-permute-start(bf16[128,4096]{1,0:T(8,128)(2,1)} %get-tuple-element.69), channel_id=1, source_target_pairs={{0,16},{4,20},{8,24},{12,28},{16,0},{20,4},{24,8},{28,12},{1,17},{... | collective-permute-start | bytes 3145736 | tf_op jit(solution)/shard_map/ppermute | solution.py:22
  18.1 16.1 %collective-permute-start.10 = (bf16[2,128,1024]{2,1,0:T(8,128)(2,1)S(1)}, bf16[2,128,1024]{2,1,0:T(8,128)(2,1)S(1)}, u32[]{:S(2)}, u32[]{:S(2)}) collective-permute-start(bf16[2,128,1024]{2,1,0:T(8,128)(2,1)S(1)} %get-tuple-element.71), channel_id=1, source_target_pairs={{0,4},{4,0},{8,12},{12,8},{16,20},{20,16},{24,28},{28,24},{1,5},{5... | collective-permute-start | bytes 1572872 | tf_op jit(solution)/shard_map/ppermute | solution.py:22
  18.1 14.5 %collective-permute-start.8 = (f32[16,128]{1,0:T(8,128)S(1)}, f32[16,128]{1,0:T(8,128)S(1)}, u32[]{:S(2)}, u32[]{:S(2)}) collective-permute-start(f32[16,128]{1,0:T(8,128)S(1)} %pad_maximum_fusion.3.one_ref.two_ref), channel_id=1, source_target_pairs={{0,8},{4,12},{8,0},{12,4},{16,24},{20,28},{24,16},{28,20},{1,9},{5... | collective-permute-start | bytes 24584 | tf_op jit(solution)/shard_map/ppermute | solution.py:22
  18.7 15.4 %collective-permute-start.9 = (f32[16,128]{1,0:T(8,128)S(1)}, f32[16,128]{1,0:T(8,128)S(1)}, u32[]{:S(2)}, u32[]{:S(2)}) collective-permute-start(f32[16,128]{1,0:T(8,128)S(1)} %pad_maximum_fusion.3.one_ref.two_ref), channel_id=1, source_target_pairs={{0,16},{4,20},{8,24},{12,28},{16,0},{20,4},{24,8},{28,12},{1,17},{... | collective-permute-start | bytes 24584 | tf_op jit(solution)/shard_map/ppermute | solution.py:22
  34.3 3.9 %collective-permute-start.12 = (bf16[64,4096]{1,0:T(8,128)(2,1)S(1)}, bf16[64,4096]{1,0:T(8,128)(2,1)S(1)}, u32[]{:S(2)}, u32[]{:S(2)}) collective-permute-start(bf16[64,4096]{1,0:T(8,128)(2,1)S(1)} %get-tuple-element.138), channel_id=1, source_target_pairs={{0,4},{4,0},{8,12},{12,8},{16,20},{20,16},{24,28},{28,24},{1,5},{5... | collective-permute-start | bytes 1572872 | tf_op jit(solution)/shard_map/ppermute | solution.py:22
  34.3 4.6 %collective-permute-start.13 = (bf16[64,4096]{1,0:T(8,128)(2,1)S(1)}, bf16[64,4096]{1,0:T(8,128)(2,1)S(1)}, u32[]{:S(2)}, u32[]{:S(2)}) collective-permute-start(bf16[64,4096]{1,0:T(8,128)(2,1)S(1)} %get-tuple-element.137), channel_id=1, source_target_pairs={{0,4},{4,0},{8,12},{12,8},{16,20},{20,16},{24,28},{28,24},{1,5},{5... | collective-permute-start | bytes 1572872 | tf_op jit(solution)/shard_map/ppermute | solution.py:22
  36.1 4.5 %collective-permute-start.14 = (bf16[64,4096]{1,0:T(8,128)(2,1)S(1)}, bf16[64,4096]{1,0:T(8,128)(2,1)S(1)}, u32[]{:S(2)}, u32[]{:S(2)}) collective-permute-start(bf16[64,4096]{1,0:T(8,128)(2,1)S(1)} %get-tuple-element.136), channel_id=1, source_target_pairs={{0,4},{4,0},{8,12},{12,8},{16,20},{20,16},{24,28},{28,24},{1,5},{5... | collective-permute-start | bytes 1572872 | tf_op jit(solution)/shard_map/ppermute | solution.py:22
  36.2 4.4 %collective-permute-start.15 = (bf16[64,4096]{1,0:T(8,128)(2,1)S(1)}, bf16[64,4096]{1,0:T(8,128)(2,1)S(1)}, u32[]{:S(2)}, u32[]{:S(2)}) collective-permute-start(bf16[64,4096]{1,0:T(8,128)(2,1)S(1)} %get-tuple-element.135), channel_id=1, source_target_pairs={{0,4},{4,0},{8,12},{12,8},{16,20},{20,16},{24,28},{28,24},{1,5},{5... | collective-permute-start | bytes 1572872 | tf_op jit(solution)/shard_map/ppermute | solution.py:22
  36.7 25.4 %collective-permute-start.4 = (bf16[128,4096]{1,0:T(8,128)(2,1)}, bf16[128,4096]{1,0:T(8,128)(2,1)S(1)}, u32[]{:S(2)}, u32[]{:S(2)}) collective-permute-start(bf16[128,4096]{1,0:T(8,128)(2,1)} %get-tuple-element.68), channel_id=1, source_target_pairs={{0,16},{4,20},{8,24},{12,28},{16,0},{20,4},{24,8},{28,12},{1,17},{... | collective-permute-start | bytes 3145736 | tf_op jit(solution)/shard_map/ppermute | solution.py:22
  38.2 7.5 %copy-start.13 = (bf16[64,4096]{1,0:T(8,128)(2,1)}, bf16[64,4096]{1,0:T(8,128)(2,1)S(1)}, u32[]{:S(2)}) copy-start(bf16[64,4096]{1,0:T(8,128)(2,1)S(1)} %collective-permute-done.12.refs_2_.refs_6_) | copy-start | bytes 1572868
  38.2 25.1 %collective-permute-start.5 = (bf16[128,4096]{1,0:T(8,128)(2,1)}, bf16[128,4096]{1,0:T(8,128)(2,1)S(1)}, u32[]{:S(2)}, u32[]{:S(2)}) collective-permute-start(bf16[128,4096]{1,0:T(8,128)(2,1)} %get-tuple-element.69), channel_id=1, source_target_pairs={{0,8},{4,12},{8,0},{12,4},{16,24},{20,28},{24,16},{28,20},{1,9},{5... | collective-permute-start | bytes 3145736 | tf_op jit(solution)/shard_map/ppermute | solution.py:22
  38.9 6.8 %copy-start.15 = (bf16[64,4096]{1,0:T(8,128)(2,1)}, bf16[64,4096]{1,0:T(8,128)(2,1)S(1)}, u32[]{:S(2)}) copy-start(bf16[64,4096]{1,0:T(8,128)(2,1)S(1)} %collective-permute-done.13.refs_3_.refs_7_) | copy-start | bytes 1572868
  39.0 24.3 %collective-permute-start.16 = (bf16[2,128,1024]{2,1,0:T(8,128)(2,1)S(1)}, bf16[2,128,1024]{2,1,0:T(8,128)(2,1)S(1)}, u32[]{:S(2)}, u32[]{:S(2)}) collective-permute-start(bf16[2,128,1024]{2,1,0:T(8,128)(2,1)S(1)} %add.85), channel_id=1, source_target_pairs={{0,1},{1,0},{2,3},{3,2},{4,5},{5,4},{6,7},{7,6},{8,9},{9,8},{10,11... | collective-permute-start | bytes 1572872 | tf_op jit(solution)/shard_map/ppermute | solution.py:22
  45.8 17.5 %collective-permute-start.17 = (bf16[2,128,1024]{2,1,0:T(8,128)(2,1)S(1)}, bf16[2,128,1024]{2,1,0:T(8,128)(2,1)S(1)}, u32[]{:S(2)}, u32[]{:S(2)}) collective-permute-start(bf16[2,128,1024]{2,1,0:T(8,128)(2,1)S(1)} %get-tuple-element.80), channel_id=1, source_target_pairs={{0,4},{4,0},{8,12},{12,8},{16,20},{20,16},{24,28},{28,24},{1,5},{5... | collective-permute-start | bytes 1572872 | tf_op jit(solution)/shard_map/ppermute | solution.py:22
  45.9 17.4 %collective-permute-start.11 = (f32[16,128]{1,0:T(8,128)S(1)}, f32[16,128]{1,0:T(8,128)S(1)}, u32[]{:S(2)}, u32[]{:S(2)}) collective-permute-start(f32[16,128]{1,0:T(8,128)S(1)} %collective-permute-done.8.one_ref.two_ref), channel_id=1, source_target_pairs={{0,16},{4,20},{8,24},{12,28},{16,0},{20,4},{24,8},{28,12},{1,17},{... | collective-permute-start | bytes 24584 | tf_op jit(solution)/shard_map/ppermute | solution.py:22
  63.4 2.0 %collective-permute-start.20 = (bf16[64,4096]{1,0:T(8,128)(2,1)S(1)}, bf16[64,4096]{1,0:T(8,128)(2,1)S(1)}, u32[]{:S(2)}, u32[]{:S(2)}) collective-permute-start(bf16[64,4096]{1,0:T(8,128)(2,1)S(1)} %get-tuple-element.134), channel_id=1, source_target_pairs={{0,4},{4,0},{8,12},{12,8},{16,20},{20,16},{24,28},{28,24},{1,5},{5... | collective-permute-start | bytes 1572872 | tf_op jit(solution)/shard_map/ppermute | solution.py:22
  63.5 2.6 %collective-permute-start.21 = (bf16[64,4096]{1,0:T(8,128)(2,1)S(1)}, bf16[64,4096]{1,0:T(8,128)(2,1)S(1)}, u32[]{:S(2)}, u32[]{:S(2)}) collective-permute-start(bf16[64,4096]{1,0:T(8,128)(2,1)S(1)} %get-tuple-element.133), channel_id=1, source_target_pairs={{0,4},{4,0},{8,12},{12,8},{16,20},{20,16},{24,28},{28,24},{1,5},{5... | collective-permute-start | bytes 1572872 | tf_op jit(solution)/shard_map/ppermute | solution.py:22
  64.0 2.8 %collective-permute-start.22 = (bf16[64,4096]{1,0:T(8,128)(2,1)S(1)}, bf16[64,4096]{1,0:T(8,128)(2,1)S(1)}, u32[]{:S(2)}, u32[]{:S(2)}) collective-permute-start(bf16[64,4096]{1,0:T(8,128)(2,1)S(1)} %get-tuple-element.132), channel_id=1, source_target_pairs={{0,4},{4,0},{8,12},{12,8},{16,20},{20,16},{24,28},{28,24},{1,5},{5... | collective-permute-start | bytes 1572872 | tf_op jit(solution)/shard_map/ppermute | solution.py:22
  64.2 4.3 %collective-permute-start.23 = (bf16[64,4096]{1,0:T(8,128)(2,1)S(1)}, bf16[64,4096]{1,0:T(8,128)(2,1)S(1)}, u32[]{:S(2)}, u32[]{:S(2)}) collective-permute-start(bf16[64,4096]{1,0:T(8,128)(2,1)S(1)} %get-tuple-element.131), channel_id=1, source_target_pairs={{0,4},{4,0},{8,12},{12,8},{16,20},{20,16},{24,28},{28,24},{1,5},{5... | collective-permute-start | bytes 1572872 | tf_op jit(solution)/shard_map/ppermute | solution.py:22
  64.6 8.1 %collective-permute-start.3 = (bf16[2,128,1024]{2,1,0:T(8,128)(2,1)S(1)}, bf16[2,128,1024]{2,1,0:T(8,128)(2,1)S(1)}, u32[]{:S(2)}, u32[]{:S(2)}) collective-permute-start(bf16[2,128,1024]{2,1,0:T(8,128)(2,1)S(1)} %get-tuple-element.67), channel_id=1, source_target_pairs={{0,4},{4,0},{8,12},{12,8},{16,20},{20,16},{24,28},{28,24},{1,5},{5... | collective-permute-start | bytes 1572872 | tf_op jit(solution)/shard_map/ppermute | solution.py:22
  65.4 7.2 %copy-start.21 = (bf16[64,4096]{1,0:T(8,128)(2,1)}, bf16[64,4096]{1,0:T(8,128)(2,1)S(1)}, u32[]{:S(2)}) copy-start(bf16[64,4096]{1,0:T(8,128)(2,1)S(1)} %collective-permute-done.20.refs_2_.refs_12_) | copy-start | bytes 1572868
  65.4 25.2 %collective-permute-start.18 = (bf16[128,4096]{1,0:T(8,128)(2,1)S(1)}, bf16[128,4096]{1,0:T(8,128)(2,1)S(1)}, u32[]{:S(2)}, u32[]{:S(2)}) collective-permute-start(bf16[128,4096]{1,0:T(8,128)(2,1)S(1)} %collective-permute-done.6.refs_0_.refs_4_), channel_id=1, source_target_pairs={{0,16},{4,20},{8,24},{12,28},{16,0},{20,4},{24,8},{28,12},{1,17},{... | collective-permute-start | bytes 3145736 | tf_op jit(solution)/shard_map/ppermute | solution.py:22
  66.1 6.5 %copy-start.23 = (bf16[64,4096]{1,0:T(8,128)(2,1)}, bf16[64,4096]{1,0:T(8,128)(2,1)S(1)}, u32[]{:S(2)}) copy-start(bf16[64,4096]{1,0:T(8,128)(2,1)S(1)} %collective-permute-done.21.refs_3_.refs_13_) | copy-start | bytes 1572868
  66.1 25.4 %collective-permute-start.19 = (bf16[128,4096]{1,0:T(8,128)(2,1)}, bf16[128,4096]{1,0:T(8,128)(2,1)S(1)}, u32[]{:S(2)}, u32[]{:S(2)}) collective-permute-start(bf16[128,4096]{1,0:T(8,128)(2,1)} %collective-permute-done.7.refs_1_.refs_5_), channel_id=1, source_target_pairs={{0,8},{4,12},{8,0},{12,4},{16,24},{20,28},{24,16},{28,20},{1,9},{5... | collective-permute-start | bytes 3145736 | tf_op jit(solution)/shard_map/ppermute | solution.py:22
  66.9 24.7 %collective-permute-start.25 = (bf16[2,128,1024]{2,1,0:T(8,128)(2,1)S(1)}, bf16[2,128,1024]{2,1,0:T(8,128)(2,1)S(1)}, u32[]{:S(2)}, u32[]{:S(2)}) collective-permute-start(bf16[2,128,1024]{2,1,0:T(8,128)(2,1)S(1)} %add.87), channel_id=1, source_target_pairs={{0,1},{1,0},{2,3},{3,2},{4,5},{5,4},{6,7},{7,6},{8,9},{9,8},{10,11... | collective-permute-start | bytes 1572872 | tf_op jit(solution)/shard_map/ppermute | solution.py:22
  72.6 20.3 %copy-start.11 = (bf16[3,576,256]{2,1,0:T(8,128)(2,1)}, bf16[3,576,256]{2,1,0:T(8,128)(2,1)S(1)}, u32[]{:S(2)}) copy-start(bf16[3,576,256]{2,1,0:T(8,128)(2,1)S(1)} %get-tuple-element.103.refs_22_) | copy-start | bytes 2654212
  72.6 18.9 %collective-permute-start.26 = (bf16[2,128,1024]{2,1,0:T(8,128)(2,1)S(1)}, bf16[2,128,1024]{2,1,0:T(8,128)(2,1)S(1)}, u32[]{:S(2)}, u32[]{:S(2)}) collective-permute-start(bf16[2,128,1024]{2,1,0:T(8,128)(2,1)S(1)} %get-tuple-element.88), channel_id=1, source_target_pairs={{0,4},{4,0},{8,12},{12,8},{16,20},{20,16},{24,28},{28,24},{1,5},{5... | collective-permute-start | bytes 1572872 | tf_op jit(solution)/shard_map/ppermute | solution.py:22
  72.8 19.5 %copy-start.42 = (bf16[2,128,1024]{2,1,0:T(8,128)(2,1)}, bf16[2,128,1024]{2,1,0:T(8,128)(2,1)S(1)}, u32[]{:S(2)}) copy-start(bf16[2,128,1024]{2,1,0:T(8,128)(2,1)S(1)} %add_add_fusion.3) | copy-start | bytes 1572868
  72.9 18.7 %collective-permute-start.24 = (bf16[128,1024]{1,0:T(8,128)(2,1)S(1)}, bf16[128,1024]{1,0:T(8,128)(2,1)S(1)}, u32[]{:S(2)}, u32[]{:S(2)}) collective-permute-start(bf16[128,1024]{1,0:T(8,128)(2,1)S(1)} %slice_bitcast_fusion.6), channel_id=1, source_target_pairs={{0,2},{1,3},{2,0},{3,1},{4,6},{5,7},{6,4},{7,5},{8,10},{9,11},{10,... | collective-permute-start | bytes 786440 | tf_op jit(solution)/shard_map/ppermute | solution.py:22
  90.6 8.1 %copy-start.7 = (bf16[128,4096]{1,0:T(8,128)(2,1)}, bf16[128,4096]{1,0:T(8,128)(2,1)S(1)}, u32[]{:S(2)}) copy-start(bf16[128,4096]{1,0:T(8,128)(2,1)S(1)} %collective-permute-done.18.refs_0_.refs_16_) | copy-start | bytes 3145732
  90.6 2.3 %collective-permute-start.27 = (bf16[2,128,1024]{2,1,0:T(8,128)(2,1)S(1)}, bf16[2,128,1024]{2,1,0:T(8,128)(2,1)S(1)}, u32[]{:S(2)}, u32[]{:S(2)}) collective-permute-start(bf16[2,128,1024]{2,1,0:T(8,128)(2,1)S(1)} %get-tuple-element.91), channel_id=1, source_target_pairs={{0,4},{4,0},{8,12},{12,8},{16,20},{20,16},{24,28},{28,24},{1,5},{5... | collective-permute-start | bytes 1572872 | tf_op jit(solution)/shard_map/ppermute | solution.py:22
  91.5 7.1 %copy-start.9 = (bf16[128,4096]{1,0:T(8,128)(2,1)}, bf16[128,4096]{1,0:T(8,128)(2,1)S(1)}, u32[]{:S(2)}) copy-start(bf16[128,4096]{1,0:T(8,128)(2,1)S(1)} %collective-permute-done.19.refs_1_.refs_17_) | copy-start | bytes 3145732
  91.6 2.7 %collective-permute-start.28 = (bf16[64,4096]{1,0:T(8,128)(2,1)S(1)}, bf16[64,4096]{1,0:T(8,128)(2,1)S(1)}, u32[]{:S(2)}, u32[]{:S(2)}) collective-permute-start(bf16[64,4096]{1,0:T(8,128)(2,1)S(1)} %get-tuple-element.130), channel_id=1, source_target_pairs={{0,4},{4,0},{8,12},{12,8},{16,20},{20,16},{24,28},{28,24},{1,5},{5... | collective-permute-start | bytes 1572872 | tf_op jit(solution)/shard_map/ppermute | solution.py:22
  91.7 2.7 %collective-permute-start.29 = (bf16[64,4096]{1,0:T(8,128)(2,1)S(1)}, bf16[64,4096]{1,0:T(8,128)(2,1)S(1)}, u32[]{:S(2)}, u32[]{:S(2)}) collective-permute-start(bf16[64,4096]{1,0:T(8,128)(2,1)S(1)} %get-tuple-element.129), channel_id=1, source_target_pairs={{0,4},{4,0},{8,12},{12,8},{16,20},{20,16},{24,28},{28,24},{1,5},{5... | collective-permute-start | bytes 1572872 | tf_op jit(solution)/shard_map/ppermute | solution.py:22
  92.3 3.8 %collective-permute-start.30 = (bf16[64,4096]{1,0:T(8,128)(2,1)S(1)}, bf16[64,4096]{1,0:T(8,128)(2,1)S(1)}, u32[]{:S(2)}, u32[]{:S(2)}) collective-permute-start(bf16[64,4096]{1,0:T(8,128)(2,1)S(1)} %get-tuple-element.128), channel_id=1, source_target_pairs={{0,4},{4,0},{8,12},{12,8},{16,20},{20,16},{24,28},{28,24},{1,5},{5... | collective-permute-start | bytes 1572872 | tf_op jit(solution)/shard_map/ppermute | solution.py:22
  92.4 6.2 %collective-permute-start.31 = (bf16[64,4096]{1,0:T(8,128)(2,1)S(1)}, bf16[64,4096]{1,0:T(8,128)(2,1)S(1)}, u32[]{:S(2)}, u32[]{:S(2)}) collective-permute-start(bf16[64,4096]{1,0:T(8,128)(2,1)S(1)} %get-tuple-element.127), channel_id=1, source_target_pairs={{0,4},{4,0},{8,12},{12,8},{16,20},{20,16},{24,28},{28,24},{1,5},{5... | collective-permute-start | bytes 1572872 | tf_op jit(solution)/shard_map/ppermute | solution.py:22
  92.9 25.6 %collective-permute-start.36 = (bf16[3,576,256]{2,1,0:T(8,128)(2,1)S(1)}, bf16[3,576,256]{2,1,0:T(8,128)(2,1)S(1)}, u32[]{:S(2)}, u32[]{:S(2)}) collective-permute-start(bf16[3,576,256]{2,1,0:T(8,128)(2,1)S(1)} %get-tuple-element.103.refs_22_), channel_id=1, source_target_pairs={{0,16},{4,20},{8,24},{12,28},{16,0},{20,4},{24,8},{28,12},{1,17},{... | collective-permute-start | bytes 2654216 | tf_op jit(solution)/shard_map/ppermute | solution.py:22
  94.3 9.1 %copy-start.29 = (bf16[64,4096]{1,0:T(8,128)(2,1)}, bf16[64,4096]{1,0:T(8,128)(2,1)S(1)}, u32[]{:S(2)}) copy-start(bf16[64,4096]{1,0:T(8,128)(2,1)S(1)} %collective-permute-done.28.refs_2_.refs_18_) | copy-start | bytes 1572868
  94.3 26.2 %collective-permute-start.37 = (bf16[2,128,1024]{2,1,0:T(8,128)(2,1)S(1)}, bf16[2,128,1024]{2,1,0:T(8,128)(2,1)S(1)}, u32[]{:S(2)}, u32[]{:S(2)}) collective-permute-start(bf16[2,128,1024]{2,1,0:T(8,128)(2,1)S(1)} %get-tuple-element.106), channel_id=1, source_target_pairs={{0,4},{4,0},{8,12},{12,8},{16,20},{20,16},{24,28},{28,24},{1,5},{5... | collective-permute-start | bytes 1572872 | tf_op jit(solution)/shard_map/ppermute | solution.py:22
  94.4 9.0 %copy-start.31 = (bf16[64,4096]{1,0:T(8,128)(2,1)}, bf16[64,4096]{1,0:T(8,128)(2,1)S(1)}, u32[]{:S(2)}) copy-start(bf16[64,4096]{1,0:T(8,128)(2,1)S(1)} %collective-permute-done.29.refs_3_.refs_19_) | copy-start | bytes 1572868
  94.4 22.5 %collective-permute-start.35 = (bf16[2,128,1024]{2,1,0:T(8,128)(2,1)S(1)}, bf16[2,128,1024]{2,1,0:T(8,128)(2,1)S(1)}, u32[]{:S(2)}, u32[]{:S(2)}) collective-permute-start(bf16[2,128,1024]{2,1,0:T(8,128)(2,1)S(1)} %add.91), channel_id=1, source_target_pairs={{0,1},{1,0},{2,3},{3,2},{4,5},{5,4},{6,7},{7,6},{8,9},{9,8},{10,11... | collective-permute-start | bytes 1572872 | tf_op jit(solution)/shard_map/ppermute | solution.py:22
  96.1 7.4 %copy-start.33 = (bf16[64,4096]{1,0:T(8,128)(2,1)}, bf16[64,4096]{1,0:T(8,128)(2,1)S(1)}, u32[]{:S(2)}) copy-start(bf16[64,4096]{1,0:T(8,128)(2,1)S(1)} %collective-permute-done.30.refs_4_.refs_20_) | copy-start | bytes 1572868
  96.1 17.4 %collective-permute-start.34 = (bf16[128,1024]{1,0:T(8,128)(2,1)S(1)}, bf16[128,1024]{1,0:T(8,128)(2,1)S(1)}, u32[]{:S(2)}, u32[]{:S(2)}) collective-permute-start(bf16[128,1024]{1,0:T(8,128)(2,1)S(1)} %slice_bitcast_fusion.4), channel_id=1, source_target_pairs={{0,2},{1,3},{2,0},{3,1},{4,6},{5,7},{6,4},{7,5},{8,10},{9,11},{10,... | collective-permute-start | bytes 786440 | tf_op jit(solution)/shard_map/ppermute | solution.py:22
  103.5 22.0 %copy-start.39 = (bf16[2,128,1024]{2,1,0:T(8,128)(2,1)}, bf16[2,128,1024]{2,1,0:T(8,128)(2,1)S(1)}, u32[]{:S(2)}) copy-start(bf16[2,128,1024]{2,1,0:T(8,128)(2,1)S(1)} %get-tuple-element.113) | copy-start | bytes 1572868
  103.5 15.1 %collective-permute-start.32 = (bf16[2,128,1024]{2,1,0:T(8,128)(2,1)S(1)}, bf16[2,128,1024]{2,1,0:T(8,128)(2,1)S(1)}, u32[]{:S(2)}, u32[]{:S(2)}) collective-permute-start(bf16[2,128,1024]{2,1,0:T(8,128)(2,1)S(1)} %get-tuple-element.96), channel_id=1, source_target_pairs={{0,4},{4,0},{8,12},{12,8},{16,20},{20,16},{24,28},{28,24},{1,5},{5... | collective-permute-start | bytes 1572872 | tf_op jit(solution)/shard_map/ppermute | solution.py:22
  113.5 10.0 %copy-start.45 = (bf16[128,1024]{1,0:T(8,128)(2,1)}, bf16[128,1024]{1,0:T(8,128)(2,1)S(1)}, u32[]{:S(2)}) copy-start(bf16[128,1024]{1,0:T(8,128)(2,1)S(1)} %collective-permute-done.34) | copy-start | bytes 786436
  113.5 5.1 %collective-permute-start.33 = (f32[8,128]{1,0:T(8,128)S(1)}, f32[8,128]{1,0:T(8,128)S(1)}, u32[]{:S(2)}, u32[]{:S(2)}) collective-permute-start(f32[8,128]{1,0:T(8,128)S(1)} %maximum_maximum_fusion), channel_id=1, source_target_pairs={{0,1},{1,0},{2,3},{3,2},{4,5},{5,4},{6,7},{7,6},{8,9},{9,8},{10,11... | collective-permute-start | bytes 12296 | tf_op jit(solution)/shard_map/ppermute | solution.py:22
  117.0 17.7 %collective-permute-start.41 = (bf16[1,576,256]{2,1,0:T(8,128)(2,1)S(1)}, bf16[1,576,256]{2,1,0:T(8,128)(2,1)}, u32[]{:S(2)}, u32[]{:S(2)}) collective-permute-start(bf16[1,576,256]{2,1,0:T(8,128)(2,1)S(1)} %get-tuple-element.111.refs_23_), channel_id=1, source_target_pairs={{0,16},{4,20},{8,24},{12,28},{16,0},{20,4},{24,8},{28,12},{1,17},{... | collective-permute-start | bytes 884744 | tf_op jit(solution)/shard_map/ppermute | solution.py:22
  118.5 26.0 %collective-permute-start.44 = (bf16[2,128,1024]{2,1,0:T(8,128)(2,1)}, bf16[2,128,1024]{2,1,0:T(8,128)(2,1)}, u32[]{:S(2)}, u32[]{:S(2)}) collective-permute-start(bf16[2,128,1024]{2,1,0:T(8,128)(2,1)} %get-tuple-element.114), channel_id=1, source_target_pairs={{0,4},{4,0},{8,12},{12,8},{16,20},{20,16},{24,28},{28,24},{1,5},{5... | collective-permute-start | bytes 1572872 | tf_op jit(solution)/shard_map/ppermute | solution.py:22
  118.6 6.9 %collective-permute-start.38 = (f32[8,128]{1,0:T(8,128)S(1)}, f32[8,128]{1,0:T(8,128)S(1)}, u32[]{:S(2)}, u32[]{:S(2)}) collective-permute-start(f32[8,128]{1,0:T(8,128)S(1)} %add.96), channel_id=1, source_target_pairs={{0,2},{1,3},{2,0},{3,1},{4,6},{5,7},{6,4},{7,5},{8,10},{9,11},{10,... | collective-permute-start | bytes 12296 | tf_op jit(solution)/shard_map/ppermute | solution.py:22
  121.4 15.3 %collective-permute-start.40 = (bf16[128,1024]{1,0:T(8,128)(2,1)}, bf16[128,1024]{1,0:T(8,128)(2,1)}, u32[]{:S(2)}, u32[]{:S(2)}) collective-permute-start(bf16[128,1024]{1,0:T(8,128)(2,1)} %slice_bitcast_fusion.2), channel_id=1, source_target_pairs={{0,2},{1,3},{2,0},{3,1},{4,6},{5,7},{6,4},{7,5},{8,10},{9,11},{10,... | collective-permute-start | bytes 786440 | tf_op jit(solution)/shard_map/ppermute | solution.py:22
  123.4 19.9 %collective-permute-start.39 = (bf16[2,128,1024]{2,1,0:T(8,128)(2,1)}, bf16[2,128,1024]{2,1,0:T(8,128)(2,1)}, u32[]{:S(2)}, u32[]{:S(2)}) collective-permute-start(bf16[2,128,1024]{2,1,0:T(8,128)(2,1)} %add.99), channel_id=1, source_target_pairs={{0,1},{1,0},{2,3},{3,2},{4,5},{5,4},{6,7},{7,6},{8,9},{9,8},{10,11... | collective-permute-start | bytes 1572872 | tf_op jit(solution)/shard_map/ppermute | solution.py:22
  126.7 7.9 %all-to-all-start = ((bf16[8,1,128]{2,1,0:T(2,128)(2,1)}), bf16[8,1,128]{2,1,0:T(2,128)(2,1)S(1)}, u32[]{:S(2)}, u32[]{:S(2)}) async-start(bf16[8,1,128]{2,1,0:T(2,128)(2,1)} %copy.26), calls=%async_computation | async-start | bytes 8192 | tf_op jit(solution)/shard_map/all_to_all | solution.py:317
  146.2 25.6 %collective-permute-start.45 = (bf16[128,1024]{1,0:T(8,128)(2,1)S(1)}, bf16[128,1024]{1,0:T(8,128)(2,1)S(1)}, u32[]{:S(2)}, u32[]{:S(2)}) collective-permute-start(bf16[128,1024]{1,0:T(8,128)(2,1)S(1)} %slice_bitcast_fusion), channel_id=1, source_target_pairs={{0,2},{1,3},{2,0},{3,1},{4,6},{5,7},{6,4},{7,5},{8,10},{9,11},{10,... | collective-permute-start | bytes 786440 | tf_op jit(solution)/shard_map/ppermute | solution.py:22
  146.3 28.1 %collective-permute-start.42 = (bf16[128,1024]{1,0:T(8,128)(2,1)S(1)}, bf16[128,1024]{1,0:T(8,128)(2,1)S(1)}, u32[]{:S(2)}, u32[]{:S(2)}) collective-permute-start(bf16[128,1024]{1,0:T(8,128)(2,1)S(1)} %pad_maximum_fusion.1), channel_id=1, source_target_pairs={{0,8},{4,12},{8,0},{12,4},{16,24},{20,28},{24,16},{28,20},{1,9},{5... | collective-permute-start | bytes 786440 | tf_op jit(solution)/shard_map/ppermute | solution.py:22
  147.0 27.4 %collective-permute-start.43 = (bf16[128,1024]{1,0:T(8,128)(2,1)S(1)}, bf16[128,1024]{1,0:T(8,128)(2,1)S(1)}, u32[]{:S(2)}, u32[]{:S(2)}) collective-permute-start(bf16[128,1024]{1,0:T(8,128)(2,1)S(1)} %pad_maximum_fusion.2), channel_id=1, source_target_pairs={{0,16},{4,20},{8,24},{12,28},{16,0},{20,4},{24,8},{28,12},{1,17},{... | collective-permute-start | bytes 786440 | tf_op jit(solution)/shard_map/ppermute | solution.py:22
  161.8 12.1 %copy-start.48 = (s32[128,4]{0,1:T(4,128)S(1)}, s32[128,4]{0,1:T(4,128)}, u32[]{:S(2)}) copy-start(s32[128,4]{0,1:T(4,128)} %param.13) | copy-start | bytes 6148
  161.8 18.4 %copy-start.43 = (bf16[2,128,1024]{2,1,0:T(8,128)(2,1)S(1)}, bf16[2,128,1024]{2,1,0:T(8,128)(2,1)}, u32[]{:S(2)}) copy-start(bf16[2,128,1024]{2,1,0:T(8,128)(2,1)} %copy-done.42) | copy-start | bytes 1572868
  161.8 18.4 %copy-start.47 = (bf16[128,1024]{1,0:T(8,128)(2,1)S(1)}, bf16[128,1024]{1,0:T(8,128)(2,1)}, u32[]{:S(2)}) copy-start(bf16[128,1024]{1,0:T(8,128)(2,1)} %copy-done.46) | copy-start | bytes 786436
  171.8 8.3 %collective-permute-start.46 = (bf16[128,1024]{1,0:T(8,128)(2,1)S(1)}, bf16[128,1024]{1,0:T(8,128)(2,1)S(1)}, u32[]{:S(2)}, u32[]{:S(2)}) collective-permute-start(bf16[128,1024]{1,0:T(8,128)(2,1)S(1)} %fusion), channel_id=1, source_target_pairs={{0,24},{4,28},{8,16},{12,20},{16,8},{20,12},{24,0},{28,4},{1,25},{... | collective-permute-start | bytes 786440 | tf_op jit(solution)/shard_map/ppermute | solution.py:22
  (34 other events, 94.9 us)

commit v7 on v6

--- a/solution.py
+++ b/solution.py
@@ -142,8 +142,7 @@
 
 
 def weight_grads_kernel(sources, x_places, dy_places, loaded, parts, flag_ref, *refs):
-    count = 1 + max(place[0] for place in x_places + dy_places)
-    operands, refs = list(refs[:count]), refs[count:]
+    operands, refs = list(refs[:loaded]), refs[loaded:]
     own, other, refs = refs[:2], refs[2:4], refs[4:]
     outs = refs[:3]
     held, acts, results, sems, out_sems = refs[3:]
@@ -157,9 +156,7 @@
         copies.append([])
         for i in range(loaded):
             copies[-1].append(
-                pltpu.make_async_copy(
-                    operands[i].at[:, columns], held.at[i, pl.ds(0, operands[i].shape[0]), columns], sems.at[part, i]
-                )
+                pltpu.make_async_copy(operands[i].at[:, columns], held.at[i, :, columns], sems.at[part, i])
             )
             copies[-1][-1].start()
     for i in range(loaded):
@@ -200,17 +197,18 @@
 
 
 def weight_grads(sources, flag, groups, own, other):
-    parts, loaded = 4, len(groups[0][0]) + len(groups[1][0])
+    parts = 4
     operands, x_places, dy_places = [], [], []
     for held, x_of, dy_of in groups:
         x_places += [(i + len(operands), start, size) for i, start, size in x_of]
         dy_places += [(i + len(operands), start, size) for i, start, size in dy_of]
         operands += held
     rows, width = operands[0].shape
+    loaded = len(operands)
     units = own[0].shape[1] // 3
     total = sum(size for _, _, size in x_places)
     bf16 = jnp.bfloat16
-    rest = in_vmem(*operands[loaded:], *own, *other)
+    rest = in_vmem(*own, *other)
     return pl.pallas_call(
         functools.partial(weight_grads_kernel, sources, x_places, dy_places, loaded, parts),
         out_shape=(jax.ShapeDtypeStruct((1, units, width), bf16),) * 3,
@@ -225,10 +223,10 @@
             pltpu.SemaphoreType.DMA((parts, loaded)),
             pltpu.SemaphoreType.DMA((parts, 3)),
         ],
-        compiler_params=pltpu.CompilerParams(vmem_limit_bytes=26 * 1024 * 1024),
+        compiler_params=pltpu.CompilerParams(vmem_limit_bytes=32 * 1024 * 1024),
         cost_estimate=pl.CostEstimate(flops=1, bytes_accessed=1, transcendentals=0),
         name="weight_grads",
-    )(flag, *operands[:loaded], *rest)
+    )(flag, *operands, *rest)
 
 
 CORE, ACROSS_X, ACROSS_Y = 1, 2, 4
@@ -248,9 +246,6 @@
     def expert_swap(value, by):
         return swap(value, "expert", by)
 
-    def core_swap(message):
-        return [expert_swap(message[:half], CORE), expert_swap(message[half:], CORE)]
-
     rows = 2 * half
     own_block = [tokens, cotangent, expert_swap(tokens, CORE), expert_swap(cotangent, CORE)]
     own_block = (own_block, [(0, 0, rows), (2, 0, rows)], [(1, 0, rows), (3, 0, rows)])
@@ -268,10 +263,8 @@
     barrier = lax.optimization_barrier
 
     def group_of(one, two):
-        mates = core_swap(one) + core_swap(two)
-        x_places = [(0, 0, half), (1, 0, half), (2, 0, half), (4, 0, half)]
-        dy_places = [(0, half, half), (1, half, half), (3, 0, half), (5, 0, half)]
-        return [one, two, *mates], x_places, dy_places
+        messages = [one, two, expert_swap(one, CORE), expert_swap(two, CORE)]
+        return messages, [(i, 0, half) for i in range(4)], [(i, half, half) for i in range(4)]
 
     def work(one, two, held, *before, place=0, places=3):
         acts, score, keep_near, keep_far, give_near, give_far = activations(
@@ -309,19 +302,18 @@
     second = jnp.concatenate([tiles[:2, half:], tiles[4:6, half:], tiles[2:4, half:], tiles[6:, half:]])
     score_rows = jnp.concatenate([tiles[:, :half], second], axis=1)
     score_in = swap(score_rows, "dp", 1)
-    far_d, score_in, far_in_b, near_in_c, other = barrier((far_d, score_in, far_in_b, near_in_c, other))
+    far_d, score_in, near_in_c, other = barrier((far_d, score_in, near_in_c, other))
     near_d, near_in_d = to_neighbour(far_d, share_d)
     score_rows = score_rows + score_in
     score_rows = score_rows + swap(score_rows, "dp", 2)
     score_rows = jnp.take(score_rows.astype(bf16), jnp.arange(expert_count, dtype=jnp.int32) ^ me, axis=0)
     score_rows = lax.all_to_all(score_rows, "expert", split_axis=0, concat_axis=0, tiled=True)
     total_c, far_in_c = to_far(near_c, near_in_c)
-    score_rows, near_in_d, far_in_c, own_flag, last_other = barrier(
-        (score_rows, near_in_d, far_in_c, own_flag, last_other)
-    )
+    grads = weight_grads(
+        ((0, 0), (2, 4), (4, 2), (6, 6)), own_flag, groups, (acts, last_acts), (other, last_other)
+    )
+    score_rows, near_in_d, far_in_b, far_in_c, grads = barrier((score_rows, near_in_d, far_in_b, far_in_c, grads))
     total_d, far_in_d = to_far(near_d, near_in_d)
-    grads = weight_grads(((0, 0), (2, 4), (4, 2), (6, 6)), own_flag, groups, (acts, last_acts), (other, last_other))
-    far_in_d, grads = barrier((far_in_d, grads))
 
     total_a, total_b = total_a + far_in_a.astype(f32), total_b + far_in_b.astype(f32)
     total_c, total_d = total_c + far_in_c.astype(f32), (total_d + far_in_d.astype(f32)).astype(bf16)

time: 182 us -> 179 us (0.984)
  waiting for transfers between devices: 75.8 us -> 70.9 us
  other arithmetic: 12.8 us -> 9.33 us
  starting transfers between devices: 41.3 us -> 44.5 us
  local copies, waits for them, and re-layouts: 18 us -> 19.9 us
    ppermute x47 -> x41, starting transfers between devices: 38 us -> 41.2 us  [swap(): lax.ppermute(value, axis, [(i, i ^ by) for i in range(lax.axis_size(axis))])]
    unnamed x101 -> x79, local copies, waits for them, and re-layouts: 14.3 us -> 17.1 us
    all_to_all x1, waiting for transfers between devices: 2.78 us -> 0.01 us  [whole_shards(): lax.all_to_all(score_rows, 'expert', split_axis=0, concat_axis=0, tiled=T...]
    ppermute x47 -> x41, waiting for transfers between devices: 73 us -> 70.9 us  [swap(): lax.ppermute(value, axis, [(i, i ^ by) for i in range(lax.axis_size(axis))])]
  transfers between devices with their start and end apart: 48 -> 42, of which waited for: 14 -> 12; matrix products, arithmetic and copies ran while one was open for 8% -> 6% of each run, Pallas kernels for 18% -> 18%
where the time goes in v7:
time: 179 us; the launch traced here: 178 us
  waiting for transfers between devices  70.9 us (40%)
  starting transfers between devices  44.5 us (25%)
  Pallas kernels  32.6 us (18%)
  local copies, waits for them, and re-layouts  19.9 us (11%)
  other arithmetic  9.33 us (5%)
    ppermute x41, waiting for transfers between devices, swap(): lax.ppermute(value, axis, [(i, i ^ by) for i in range(lax.axis_size(axis))])  70.9 us
    ppermute x41, starting transfers between devices, swap(): lax.ppermute(value, axis, [(i, i ^ by) for i in range(lax.axis_size(axis))])  41.2 us
    pallas_call x4, Pallas kernels, activations(): pl.pallas_call(functools.partial(activations_kernel, place, x_places, dy_...  19.3 us
    unnamed x79, local copies, waits for them, and re-layouts  17.1 us
    pallas_call x1, Pallas kernels, weight_grads(): pl.pallas_call(functools.partial(weight_grads_kernel, sources, x_places,...  10.4 us
  transfers between devices with their start and end apart: 42, of which 12 were waited for; matrix products, arithmetic and copies ran while one was open for 6% of the time, Pallas kernels for 18%

profile of v7, /device:TPU:0, one launch (start us, length us, event | category | flops | bytes accessed | tf_op | source)
XLA Modules:
  0.0 178.4 jit_solution(9229097684299670188)
XLA Ops:
  1.3 2.9 %pack.1 = (bf16[128,4096]{1,0:T(8,128)(2,1)}, bf16[128,4096]{1,0:T(8,128)(2,1)}) custom-call(bf16[128,4096]{1,0:T(8,128)(2,1)} %refs_0_.3, bf16[128,4096]{1,0:T(8,128)(2,1)} %refs_1_.3), custom_call_target="tpu_custom_call" | custom-call | flops 1 | bytes 1 | tf_op jit(solution)/shard_map/pack/pallas_call | solution.py:59
  4.1 3.0 %collective-permute-start.6 = (bf16[128,4096]{1,0:T(8,128)(2,1)}, bf16[128,4096]{1,0:T(8,128)(2,1)}, u32[]{:S(2)}, u32[]{:S(2)}) collective-permute-start(bf16[128,4096]{1,0:T(8,128)(2,1)} %get-tuple-element.65), channel_id=1, source_target_pairs={{0,8},{4,12},{8,0},{12,4},{16,24},{20,28},{24,16},{28,20},{1,9},{5... | collective-permute-start | bytes 3145736 | tf_op jit(solution)/shard_map/ppermute | solution.py:22
  7.1 1.5 collective-permute-start.7
  8.8 2.4 %pad_maximum_fusion.refs_4_ = bf16[384,4096]{1,0:T(8,128)(2,1)S(1)} fusion(bf16[192,4096]{1,0:T(8,128)(2,1)} %bitcast.52, bf16[192,4096]{1,0:T(8,128)(2,1)} %bitcast.53), kind=kLoop, calls=%fused_computation.1 | loop fusion | flops 6291456 | bytes 6291456 | tf_op jit(solution)/shard_map/concatenate | solution.py:244
  11.2 1.0 copy-done.3
  12.2 1.2 copy-done.4
  13.5 4.7 %activations.4 = (bf16[3,576,256]{2,1,0:T(8,128)(2,1)S(1)}, f32[1,256]{1,0:T(1,128)S(1)}, bf16[2,128,1024]{2,1,0:T(8,128)(2,1)S(1)}, bf16[2,128,1024]{2,1,0:T(8,...) custom-call(s32[2]{0:T(128)S(1)} %pad_add_fusion.where_ref, ...), custom_call_target="tpu_custom_call" | custom-call | flops 1 | bytes 1 | tf_op jit(solution)/shard_map/activations/pallas_call | solution.py:123
  18.7 0.5 collective-permute-start.8
  19.3 11.6 %collective-permute-done.8.one_ref.two_ref = f32[16,128]{1,0:T(8,128)S(1)} collective-permute-done((f32[16,128]{1,0:T(8,128)S(1)}, f32[16,128]{1,0:T(8,128)S(1)}, u32[]{:S(2)}, u32[]{:S(2)}) %collective-permute-start.8) | collective-permute-done | bytes 8224 | tf_op jit(solution)/shard_map/ppermute | solution.py:22
  30.9 1.5 collective-permute-done.9.two_ref.one_ref
  33.0 1.5 collective-permute-start.4
  34.5 0.5 collective-permute-start.5
  35.2 1.6 collective-permute-start.14
  36.9 5.8 %activations.5 = (bf16[3,576,256]{2,1,0:T(8,128)(2,1)S(1)}, f32[1,256]{1,0:T(1,128)S(1)}, bf16[2,128,1024]{2,1,0:T(8,128)(2,1)S(1)}, bf16[2,128,1024]{2,1,0:T(8,...) custom-call(s32[2]{0:T(128)S(1)} %pad_add_fusion.where_ref, ...), custom_call_target="tpu_custom_call", output_to_operand_aliasing={{0}: (9, {})} | custom-call | flops 1 | bytes 1 | tf_op jit(solution)/shard_map/activations/pallas_call | solution.py:123
  42.8 1.2 collective-permute-start.11
  44.0 14.4 %collective-permute-done.4.refs_0_.refs_8_ = bf16[128,4096]{1,0:T(8,128)(2,1)S(1)} collective-permute-done((bf16[128,4096]{1,0:T(8,128)(2,1)}, bf16[128,4096]{1,0:T(8,128)(2,1)S(1)}, u32[]{:S(2)}, u32[]{:S(2)}) %collective-permute-start.4) | collective-permute-done | bytes 1048608 | tf_op jit(solution)/shard_map/ppermute | solution.py:22
  58.4 1.1 collective-permute-done.5.refs_1_.refs_9_
  61.4 0.9 collective-permute-done.18.refs_2_.refs_10_
  62.3 1.6 collective-permute-start.21
  63.9 4.0 %activations.6 = (bf16[3,576,256]{2,1,0:T(8,128)(2,1)S(1)}, f32[1,256]{1,0:T(1,128)S(1)}, bf16[2,128,1024]{2,1,0:T(8,128)(2,1)S(1)}, bf16[2,128,1024]{2,1,0:T(8,...) custom-call(s32[2]{0:T(128)S(1)} %pad_add_fusion.where_ref, ...), custom_call_target="tpu_custom_call", output_to_operand_aliasing={{0}: (9, {})} | custom-call | flops 1 | bytes 1 | tf_op jit(solution)/shard_map/activations/pallas_call | solution.py:123
  68.2 2.7 %collective-permute-start.20 = (bf16[128,1024]{1,0:T(8,128)(2,1)S(1)}, bf16[128,1024]{1,0:T(8,128)(2,1)S(1)}, u32[]{:S(2)}, u32[]{:S(2)}) collective-permute-start(bf16[128,1024]{1,0:T(8,128)(2,1)S(1)} %slice_bitcast_fusion.6), channel_id=1, source_target_pairs={{0,2},{1,3},{2,0},{3,1},{4,6},{5,7},{6,4},{7,5},{8,10},{9,11},{10,... | collective-permute-start | bytes 786440 | tf_op jit(solution)/shard_map/ppermute | solution.py:22
  70.9 15.1 %collective-permute-done.16.refs_0_.refs_12_ = bf16[128,4096]{1,0:T(8,128)(2,1)S(1)} collective-permute-done((bf16[128,4096]{1,0:T(8,128)(2,1)}, bf16[128,4096]{1,0:T(8,128)(2,1)S(1)}, u32[]{:S(2)}, u32[]{:S(2)}) %collective-permute-start.16) | collective-permute-done | bytes 1048608 | tf_op jit(solution)/shard_map/ppermute | solution.py:22
  87.6 1.6 collective-permute-start.28
  89.2 2.0 %collective-permute-done.23 = bf16[2,128,1024]{2,1,0:T(8,128)(2,1)S(1)} collective-permute-done((bf16[2,128,1024]{2,1,0:T(8,128)(2,1)S(1)}, bf16[2,128,1024]{2,1,0:T(8,128)(2,1)S(1)}, u32[]{:S(2)}, u32[]{:S(2)}) %collective-permute-start.23) | collective-permute-done | bytes 524320 | tf_op jit(solution)/shard_map/ppermute | solution.py:22
  91.2 1.5 collective-permute-start.29
  92.9 4.7 %activations.7 = (bf16[1,576,256]{2,1,0:T(8,128)(2,1)}, f32[1,256]{1,0:T(1,128)S(1)}, bf16[2,128,1024]{2,1,0:T(8,128)(2,1)S(1)}, bf16[2,128,1024]{2,1,0:T(8,128)...) custom-call(s32[2]{0:T(128)S(1)} %pad_add_fusion.where_ref, ...), custom_call_target="tpu_custom_call" | custom-call | flops 1 | bytes 1 | tf_op jit(solution)/shard_map/activations/pallas_call | solution.py:123
  97.8 1.6 collective-permute-start.27
  99.4 0.7 slice_bitcast_fusion.4
  100.1 1.5 collective-permute-done.28
  101.6 2.6 %collective-permute-start.32 = (bf16[128,1024]{1,0:T(8,128)(2,1)}, bf16[128,1024]{1,0:T(8,128)(2,1)}, u32[]{:S(2)}, u32[]{:S(2)}) collective-permute-start(bf16[128,1024]{1,0:T(8,128)(2,1)} %slice_bitcast_fusion.4), channel_id=1, source_target_pairs={{0,2},{1,3},{2,0},{3,1},{4,6},{5,7},{6,4},{7,5},{8,10},{9,11},{10,... | collective-permute-start | bytes 786440 | tf_op jit(solution)/shard_map/ppermute | solution.py:22
  104.2 8.7 %collective-permute-done.29.refs_18_ = bf16[3,576,256]{2,1,0:T(8,128)(2,1)S(1)} collective-permute-done((bf16[3,576,256]{2,1,0:T(8,128)(2,1)S(1)}, bf16[3,576,256]{2,1,0:T(8,128)(2,1)S(1)}, u32[]{:S(2)}, u32[]{:S(2)}) %collective-permute-start.29) | collective-permute-done | bytes 884768 | tf_op jit(solution)/shard_map/ppermute | solution.py:22
  112.9 1.5 collective-permute-start.35
  114.4 2.7 %collective-permute-start.30 = (f32[8,128]{1,0:T(8,128)S(1)}, f32[8,128]{1,0:T(8,128)S(1)}, u32[]{:S(2)}, u32[]{:S(2)}) collective-permute-start(f32[8,128]{1,0:T(8,128)S(1)} %add.93), channel_id=1, source_target_pairs={{0,2},{1,3},{2,0},{3,1},{4,6},{5,7},{6,4},{7,5},{8,10},{9,11},{10,... | collective-permute-start | bytes 12296 | tf_op jit(solution)/shard_map/ppermute | solution.py:22
  117.1 1.0 add.96
  118.1 1.6 collective-permute-start.31
  119.8 0.8 slice_bitcast_fusion.3
  120.7 0.9 collective-permute-start.34
  121.6 0.6 gather_fusion
  122.2 0.6 copy.26
  122.8 3.3 %all-to-all-start = ((bf16[8,1,128]{2,1,0:T(2,128)(2,1)}), bf16[8,1,128]{2,1,0:T(2,128)(2,1)S(1)}, u32[]{:S(2)}, u32[]{:S(2)}) async-start(bf16[8,1,128]{2,1,0:T(2,128)(2,1)} %copy.26), calls=%async_computation | async-start | bytes 8192 | tf_op jit(solution)/shard_map/all_to_all | solution.py:310
  126.2 0.6 fusion.7
  126.8 1.2 copy-done.5
  128.0 1.2 copy-done.7
  129.3 1.2 copy-done.9
  130.5 1.2 copy-done.11
  131.7 1.2 copy-done.13
  132.9 1.2 copy-done.15
  134.2 1.2 copy-done.17
  135.4 1.2 copy-done.19
  136.6 1.2 copy-done.21
  137.8 1.2 copy-done.23
  139.1 1.2 copy-done.25
  140.3 1.2 copy-done.27
  141.4 10.4 %weight_grads.1 = (bf16[1,192,4096]{2,1,0:T(8,128)(2,1)}, bf16[1,192,4096]{2,1,0:T(8,128)(2,1)}, bf16[1,192,4096]{2,1,0:T(8,128)(2,1)}) custom-call(s32[1]{0:T(128)} %bitcast.16.flag_ref, bf16[128,4096]{1,0:T(8,128)(2,1)S(1)} %copy-done.1, bf16[128,4096]{1,0:T(8,128)(2,1)S(1)} %copy-done.2, bf16[128,4096]{1,0:T(8,128)(2,1)S(1)} %copy-done.5, ...), custom_call_target="tpu_custom_call" | custom-call | flops 1 | bytes 1 | tf_op jit(solution)/shard_map/weight_grads/pallas_call | solution.py:212
  152.0 1.4 add_add_fusion
  153.4 2.1 %collective-permute-start.39 = (bf16[128,1024]{1,0:T(8,128)(2,1)S(1)}, bf16[128,1024]{1,0:T(8,128)(2,1)S(1)}, u32[]{:S(2)}, u32[]{:S(2)}) collective-permute-start(bf16[128,1024]{1,0:T(8,128)(2,1)S(1)} %slice_bitcast_fusion), channel_id=1, source_target_pairs={{0,2},{1,3},{2,0},{3,1},{4,6},{5,7},{6,4},{7,5},{8,10},{9,11},{10,... | collective-permute-start | bytes 786440 | tf_op jit(solution)/shard_map/ppermute | solution.py:22
  155.5 1.2 fusion.1
  156.8 2.0 %collective-permute-start.37 = (bf16[128,1024]{1,0:T(8,128)(2,1)S(1)}, bf16[128,1024]{1,0:T(8,128)(2,1)S(1)}, u32[]{:S(2)}, u32[]{:S(2)}) collective-permute-start(bf16[128,1024]{1,0:T(8,128)(2,1)S(1)} %pad_maximum_fusion.2), channel_id=1, source_target_pairs={{0,16},{4,20},{8,24},{12,28},{16,0},{20,4},{24,8},{28,12},{1,17},{... | collective-permute-start | bytes 786440 | tf_op jit(solution)/shard_map/ppermute | solution.py:22
  158.8 1.5 collective-permute-start.36
  160.3 8.2 %collective-permute-done.39 = bf16[128,1024]{1,0:T(8,128)(2,1)S(1)} collective-permute-done((bf16[128,1024]{1,0:T(8,128)(2,1)S(1)}, bf16[128,1024]{1,0:T(8,128)(2,1)S(1)}, u32[]{:S(2)}, u32[]{:S(2)}) %collective-permute-start.39) | collective-permute-done | bytes 262176 | tf_op jit(solution)/shard_map/ppermute | solution.py:22
  168.6 2.6 %collective-permute-start.40 = (bf16[128,1024]{1,0:T(8,128)(2,1)S(1)}, bf16[128,1024]{1,0:T(8,128)(2,1)S(1)}, u32[]{:S(2)}, u32[]{:S(2)}) collective-permute-start(bf16[128,1024]{1,0:T(8,128)(2,1)S(1)} %fusion), channel_id=1, source_target_pairs={{0,24},{4,28},{8,16},{12,20},{16,8},{20,12},{24,0},{28,4},{1,25},{... | collective-permute-start | bytes 786440 | tf_op jit(solution)/shard_map/ppermute | solution.py:22
  171.3 0.6 select_reduce_fusion
  171.9 5.6 %collective-permute-done.40 = bf16[128,1024]{1,0:T(8,128)(2,1)S(1)} collective-permute-done((bf16[128,1024]{1,0:T(8,128)(2,1)S(1)}, bf16[128,1024]{1,0:T(8,128)(2,1)S(1)}, u32[]{:S(2)}, u32[]{:S(2)}) %collective-permute-start.40) | collective-permute-done | bytes 262176 | tf_op jit(solution)/shard_map/ppermute | solution.py:22
  177.5 0.9 fusion.6
  (143 shorter events, 6.7 us)
Async XLA Ops:
  0.6 8.0 %copy-start.37 = (bf16[128,4]{0,1:T(4,128)(2,1)S(1)}, bf16[128,4]{0,1:T(4,128)(2,1)}, u32[]{:S(2)}) copy-start(bf16[128,4]{0,1:T(4,128)(2,1)} %param.14) | copy-start | bytes 3076
  0.6 8.0 %copy-start.36 = (s32[128,4]{0,1:T(4,128)S(1)}, s32[128,4]{0,1:T(4,128)}, u32[]{:S(2)}) copy-start(s32[128,4]{0,1:T(4,128)} %param.13) | copy-start | bytes 6148
  0.7 10.6 %collective-permute-start.1 = (bf16[128,4096]{1,0:T(8,128)(2,1)}, bf16[128,4096]{1,0:T(8,128)(2,1)S(1)}, u32[]{:S(2)}, u32[]{:S(2)}) collective-permute-start(bf16[128,4096]{1,0:T(8,128)(2,1)} %refs_0_.3), channel_id=1, source_target_pairs={{0,4},{4,0},{8,12},{12,8},{16,20},{20,16},{24,28},{28,24},{1,5},{5... | collective-permute-start | bytes 3145736 | tf_op jit(solution)/shard_map/ppermute | solution.py:22
  1.2 11.0 %collective-permute-start.2 = (bf16[128,4096]{1,0:T(8,128)(2,1)}, bf16[128,4096]{1,0:T(8,128)(2,1)}, u32[]{:S(2)}, u32[]{:S(2)}) collective-permute-start(bf16[128,4096]{1,0:T(8,128)(2,1)} %refs_1_.3), channel_id=1, source_target_pairs={{0,4},{4,0},{8,12},{12,8},{16,20},{20,16},{24,28},{28,24},{1,5},{5... | collective-permute-start | bytes 3145736 | tf_op jit(solution)/shard_map/ppermute | solution.py:22
  4.1 28.3 %collective-permute-start.6 = (bf16[128,4096]{1,0:T(8,128)(2,1)}, bf16[128,4096]{1,0:T(8,128)(2,1)}, u32[]{:S(2)}, u32[]{:S(2)}) collective-permute-start(bf16[128,4096]{1,0:T(8,128)(2,1)} %get-tuple-element.65), channel_id=1, source_target_pairs={{0,8},{4,12},{8,0},{12,4},{16,24},{20,28},{24,16},{28,20},{1,9},{5... | collective-permute-start | bytes 3145736 | tf_op jit(solution)/shard_map/ppermute | solution.py:22
  7.1 25.3 %collective-permute-start.7 = (bf16[128,4096]{1,0:T(8,128)(2,1)}, bf16[128,4096]{1,0:T(8,128)(2,1)}, u32[]{:S(2)}, u32[]{:S(2)}) collective-permute-start(bf16[128,4096]{1,0:T(8,128)(2,1)} %get-tuple-element.66), channel_id=1, source_target_pairs={{0,16},{4,20},{8,24},{12,28},{16,0},{20,4},{24,8},{28,12},{1,17},{... | collective-permute-start | bytes 3145736 | tf_op jit(solution)/shard_map/ppermute | solution.py:22
  8.6 2.6 %collective-permute-start = (f32[8,128]{1,0:T(8,128)S(1)}, f32[8,128]{1,0:T(8,128)S(1)}, u32[]{:S(2)}, u32[]{:S(2)}) collective-permute-start(f32[8,128]{1,0:T(8,128)S(1)} %bitcast.56), channel_id=1, source_target_pairs={{0,4},{4,0},{8,12},{12,8},{16,20},{20,16},{24,28},{28,24},{1,5},{5... | collective-permute-start | bytes 12296 | tf_op jit(solution)/shard_map/ppermute | solution.py:22
  8.7 3.5 %copy-start = (bf16[1,192,4096]{2,1,0:T(8,128)(2,1)S(1)}, bf16[1,192,4096]{2,1,0:T(8,128)(2,1)}, u32[]{:S(2)}) copy-start(bf16[1,192,4096]{2,1,0:T(8,128)(2,1)} %param.12) | copy-start | bytes 4718596
  8.7 3.5 %copy-start.1 = (bf16[128,4096]{1,0:T(8,128)(2,1)S(1)}, bf16[128,4096]{1,0:T(8,128)(2,1)}, u32[]{:S(2)}) copy-start(bf16[128,4096]{1,0:T(8,128)(2,1)} %refs_0_.3) | copy-start | bytes 3145732
  18.2 14.2 %collective-permute-start.10 = (bf16[2,128,1024]{2,1,0:T(8,128)(2,1)S(1)}, bf16[2,128,1024]{2,1,0:T(8,128)(2,1)S(1)}, u32[]{:S(2)}, u32[]{:S(2)}) collective-permute-start(bf16[2,128,1024]{2,1,0:T(8,128)(2,1)S(1)} %get-tuple-element.68), channel_id=1, source_target_pairs={{0,4},{4,0},{8,12},{12,8},{16,20},{20,16},{24,28},{28,24},{1,5},{5... | collective-permute-start | bytes 1572872 | tf_op jit(solution)/shard_map/ppermute | solution.py:22
  18.7 12.2 %collective-permute-start.8 = (f32[16,128]{1,0:T(8,128)S(1)}, f32[16,128]{1,0:T(8,128)S(1)}, u32[]{:S(2)}, u32[]{:S(2)}) collective-permute-start(f32[16,128]{1,0:T(8,128)S(1)} %pad_maximum_fusion.3.one_ref.two_ref), channel_id=1, source_target_pairs={{0,8},{4,12},{8,0},{12,4},{16,24},{20,28},{24,16},{28,20},{1,9},{5... | collective-permute-start | bytes 24584 | tf_op jit(solution)/shard_map/ppermute | solution.py:22
  19.2 13.1 %collective-permute-start.9 = (f32[16,128]{1,0:T(8,128)S(1)}, f32[16,128]{1,0:T(8,128)S(1)}, u32[]{:S(2)}, u32[]{:S(2)}) collective-permute-start(f32[16,128]{1,0:T(8,128)S(1)} %pad_maximum_fusion.3.one_ref.two_ref), channel_id=1, source_target_pairs={{0,16},{4,20},{8,24},{12,28},{16,0},{20,4},{24,8},{28,12},{1,17},{... | collective-permute-start | bytes 24584 | tf_op jit(solution)/shard_map/ppermute | solution.py:22
  32.4 4.5 %collective-permute-start.12 = (bf16[128,4096]{1,0:T(8,128)(2,1)}, bf16[128,4096]{1,0:T(8,128)(2,1)S(1)}, u32[]{:S(2)}, u32[]{:S(2)}) collective-permute-start(bf16[128,4096]{1,0:T(8,128)(2,1)} %collective-permute-done.6.refs_0_.refs_4_), channel_id=1, source_target_pairs={{0,4},{4,0},{8,12},{12,8},{16,20},{20,16},{24,28},{28,24},{1,5},{5... | collective-permute-start | bytes 3145736 | tf_op jit(solution)/shard_map/ppermute | solution.py:22
  32.5 4.4 %collective-permute-start.13 = (bf16[128,4096]{1,0:T(8,128)(2,1)}, bf16[128,4096]{1,0:T(8,128)(2,1)S(1)}, u32[]{:S(2)}, u32[]{:S(2)}) collective-permute-start(bf16[128,4096]{1,0:T(8,128)(2,1)} %collective-permute-done.7.refs_1_.refs_5_), channel_id=1, source_target_pairs={{0,4},{4,0},{8,12},{12,8},{16,20},{20,16},{24,28},{28,24},{1,5},{5... | collective-permute-start | bytes 3145736 | tf_op jit(solution)/shard_map/ppermute | solution.py:22
  33.0 25.4 %collective-permute-start.4 = (bf16[128,4096]{1,0:T(8,128)(2,1)}, bf16[128,4096]{1,0:T(8,128)(2,1)S(1)}, u32[]{:S(2)}, u32[]{:S(2)}) collective-permute-start(bf16[128,4096]{1,0:T(8,128)(2,1)} %get-tuple-element.65), channel_id=1, source_target_pairs={{0,16},{4,20},{8,24},{12,28},{16,0},{20,4},{24,8},{28,12},{1,17},{... | collective-permute-start | bytes 3145736 | tf_op jit(solution)/shard_map/ppermute | solution.py:22
  34.5 25.1 %collective-permute-start.5 = (bf16[128,4096]{1,0:T(8,128)(2,1)}, bf16[128,4096]{1,0:T(8,128)(2,1)S(1)}, u32[]{:S(2)}, u32[]{:S(2)}) collective-permute-start(bf16[128,4096]{1,0:T(8,128)(2,1)} %get-tuple-element.66), channel_id=1, source_target_pairs={{0,8},{4,12},{8,0},{12,4},{16,24},{20,28},{24,16},{28,20},{1,9},{5... | collective-permute-start | bytes 3145736 | tf_op jit(solution)/shard_map/ppermute | solution.py:22
  35.2 24.3 %collective-permute-start.14 = (bf16[2,128,1024]{2,1,0:T(8,128)(2,1)S(1)}, bf16[2,128,1024]{2,1,0:T(8,128)(2,1)S(1)}, u32[]{:S(2)}, u32[]{:S(2)}) collective-permute-start(bf16[2,128,1024]{2,1,0:T(8,128)(2,1)S(1)} %add.85), channel_id=1, source_target_pairs={{0,1},{1,0},{2,3},{3,2},{4,5},{5,4},{6,7},{7,6},{8,9},{9,8},{10,11... | collective-permute-start | bytes 1572872 | tf_op jit(solution)/shard_map/ppermute | solution.py:22
  36.9 5.8 %copy-start.6 = (bf16[128,4096]{1,0:T(8,128)(2,1)}, bf16[128,4096]{1,0:T(8,128)(2,1)S(1)}, u32[]{:S(2)}) copy-start(bf16[128,4096]{1,0:T(8,128)(2,1)S(1)} %collective-permute-done.12.refs_2_.refs_6_) | copy-start | bytes 3145732
  36.9 5.8 %copy-start.8 = (bf16[128,4096]{1,0:T(8,128)(2,1)}, bf16[128,4096]{1,0:T(8,128)(2,1)S(1)}, u32[]{:S(2)}) copy-start(bf16[128,4096]{1,0:T(8,128)(2,1)S(1)} %collective-permute-done.13.refs_3_.refs_7_) | copy-start | bytes 3145732
  42.7 16.9 %collective-permute-start.15 = (bf16[2,128,1024]{2,1,0:T(8,128)(2,1)S(1)}, bf16[2,128,1024]{2,1,0:T(8,128)(2,1)S(1)}, u32[]{:S(2)}, u32[]{:S(2)}) collective-permute-start(bf16[2,128,1024]{2,1,0:T(8,128)(2,1)S(1)} %get-tuple-element.77), channel_id=1, source_target_pairs={{0,4},{4,0},{8,12},{12,8},{16,20},{20,16},{24,28},{28,24},{1,5},{5... | collective-permute-start | bytes 1572872 | tf_op jit(solution)/shard_map/ppermute | solution.py:22
  42.8 16.8 %collective-permute-start.11 = (f32[16,128]{1,0:T(8,128)S(1)}, f32[16,128]{1,0:T(8,128)S(1)}, u32[]{:S(2)}, u32[]{:S(2)}) collective-permute-start(f32[16,128]{1,0:T(8,128)S(1)} %collective-permute-done.8.one_ref.two_ref), channel_id=1, source_target_pairs={{0,16},{4,20},{8,24},{12,28},{16,0},{20,4},{24,8},{28,12},{1,17},{... | collective-permute-start | bytes 24584 | tf_op jit(solution)/shard_map/ppermute | solution.py:22
  58.4 9.5 %copy-start.10 = (bf16[128,4096]{1,0:T(8,128)(2,1)}, bf16[128,4096]{1,0:T(8,128)(2,1)S(1)}, u32[]{:S(2)}) copy-start(bf16[128,4096]{1,0:T(8,128)(2,1)S(1)} %collective-permute-done.4.refs_0_.refs_8_) | copy-start | bytes 3145732
  59.6 8.4 %copy-start.12 = (bf16[128,4096]{1,0:T(8,128)(2,1)}, bf16[128,4096]{1,0:T(8,128)(2,1)S(1)}, u32[]{:S(2)}) copy-start(bf16[128,4096]{1,0:T(8,128)(2,1)S(1)} %collective-permute-done.5.refs_1_.refs_9_) | copy-start | bytes 3145732
  59.6 2.7 %collective-permute-start.18 = (bf16[128,4096]{1,0:T(8,128)(2,1)S(1)}, bf16[128,4096]{1,0:T(8,128)(2,1)S(1)}, u32[]{:S(2)}, u32[]{:S(2)}) collective-permute-start(bf16[128,4096]{1,0:T(8,128)(2,1)S(1)} %collective-permute-done.4.refs_0_.refs_8_), channel_id=1, source_target_pairs={{0,4},{4,0},{8,12},{12,8},{16,20},{20,16},{24,28},{28,24},{1,5},{5... | collective-permute-start | bytes 3145736 | tf_op jit(solution)/shard_map/ppermute | solution.py:22
  59.7 4.2 %collective-permute-start.19 = (bf16[128,4096]{1,0:T(8,128)(2,1)S(1)}, bf16[128,4096]{1,0:T(8,128)(2,1)S(1)}, u32[]{:S(2)}, u32[]{:S(2)}) collective-permute-start(bf16[128,4096]{1,0:T(8,128)(2,1)S(1)} %collective-permute-done.5.refs_1_.refs_9_), channel_id=1, source_target_pairs={{0,4},{4,0},{8,12},{12,8},{16,20},{20,16},{24,28},{28,24},{1,5},{5... | collective-permute-start | bytes 3145736 | tf_op jit(solution)/shard_map/ppermute | solution.py:22
  60.2 7.9 %collective-permute-start.3 = (bf16[2,128,1024]{2,1,0:T(8,128)(2,1)S(1)}, bf16[2,128,1024]{2,1,0:T(8,128)(2,1)S(1)}, u32[]{:S(2)}, u32[]{:S(2)}) collective-permute-start(bf16[2,128,1024]{2,1,0:T(8,128)(2,1)S(1)} %get-tuple-element.64), channel_id=1, source_target_pairs={{0,4},{4,0},{8,12},{12,8},{16,20},{20,16},{24,28},{28,24},{1,5},{5... | collective-permute-start | bytes 1572872 | tf_op jit(solution)/shard_map/ppermute | solution.py:22
  60.2 25.7 %collective-permute-start.16 = (bf16[128,4096]{1,0:T(8,128)(2,1)}, bf16[128,4096]{1,0:T(8,128)(2,1)S(1)}, u32[]{:S(2)}, u32[]{:S(2)}) collective-permute-start(bf16[128,4096]{1,0:T(8,128)(2,1)} %collective-permute-done.6.refs_0_.refs_4_), channel_id=1, source_target_pairs={{0,16},{4,20},{8,24},{12,28},{16,0},{20,4},{24,8},{28,12},{1,17},{... | collective-permute-start | bytes 3145736 | tf_op jit(solution)/shard_map/ppermute | solution.py:22
  60.7 25.4 %collective-permute-start.17 = (bf16[128,4096]{1,0:T(8,128)(2,1)}, bf16[128,4096]{1,0:T(8,128)(2,1)S(1)}, u32[]{:S(2)}, u32[]{:S(2)}) collective-permute-start(bf16[128,4096]{1,0:T(8,128)(2,1)} %collective-permute-done.7.refs_1_.refs_5_), channel_id=1, source_target_pairs={{0,8},{4,12},{8,0},{12,4},{16,24},{20,28},{24,16},{28,20},{1,9},{5... | collective-permute-start | bytes 3145736 | tf_op jit(solution)/shard_map/ppermute | solution.py:22
  62.3 5.6 %copy-start.14 = (bf16[128,4096]{1,0:T(8,128)(2,1)}, bf16[128,4096]{1,0:T(8,128)(2,1)S(1)}, u32[]{:S(2)}) copy-start(bf16[128,4096]{1,0:T(8,128)(2,1)S(1)} %collective-permute-done.18.refs_2_.refs_10_) | copy-start | bytes 3145732
  62.3 23.9 %collective-permute-start.21 = (bf16[2,128,1024]{2,1,0:T(8,128)(2,1)S(1)}, bf16[2,128,1024]{2,1,0:T(8,128)(2,1)S(1)}, u32[]{:S(2)}, u32[]{:S(2)}) collective-permute-start(bf16[2,128,1024]{2,1,0:T(8,128)(2,1)S(1)} %add.87), channel_id=1, source_target_pairs={{0,1},{1,0},{2,3},{3,2},{4,5},{5,4},{6,7},{7,6},{8,9},{9,8},{10,11... | collective-permute-start | bytes 1572872 | tf_op jit(solution)/shard_map/ppermute | solution.py:22
  63.9 4.1 %copy-start.16 = (bf16[128,4096]{1,0:T(8,128)(2,1)}, bf16[128,4096]{1,0:T(8,128)(2,1)S(1)}, u32[]{:S(2)}) copy-start(bf16[128,4096]{1,0:T(8,128)(2,1)S(1)} %collective-permute-done.19.refs_3_.refs_11_) | copy-start | bytes 3145732
  68.0 18.2 %collective-permute-start.22 = (bf16[2,128,1024]{2,1,0:T(8,128)(2,1)S(1)}, bf16[2,128,1024]{2,1,0:T(8,128)(2,1)S(1)}, u32[]{:S(2)}, u32[]{:S(2)}) collective-permute-start(bf16[2,128,1024]{2,1,0:T(8,128)(2,1)S(1)} %get-tuple-element.85), channel_id=1, source_target_pairs={{0,4},{4,0},{8,12},{12,8},{16,20},{20,16},{24,28},{28,24},{1,5},{5... | collective-permute-start | bytes 1572872 | tf_op jit(solution)/shard_map/ppermute | solution.py:22
  68.2 21.0 %copy-start.28 = (bf16[2,128,1024]{2,1,0:T(8,128)(2,1)}, bf16[2,128,1024]{2,1,0:T(8,128)(2,1)S(1)}, u32[]{:S(2)}) copy-start(bf16[2,128,1024]{2,1,0:T(8,128)(2,1)S(1)} %add_add_fusion.3) | copy-start | bytes 1572868
  68.2 17.9 %collective-permute-start.20 = (bf16[128,1024]{1,0:T(8,128)(2,1)S(1)}, bf16[128,1024]{1,0:T(8,128)(2,1)S(1)}, u32[]{:S(2)}, u32[]{:S(2)}) collective-permute-start(bf16[128,1024]{1,0:T(8,128)(2,1)S(1)} %slice_bitcast_fusion.6), channel_id=1, source_target_pairs={{0,2},{1,3},{2,0},{3,1},{4,6},{5,7},{6,4},{7,5},{8,10},{9,11},{10,... | collective-permute-start | bytes 786440 | tf_op jit(solution)/shard_map/ppermute | solution.py:22
  86.0 6.9 %copy-start.18 = (bf16[128,4096]{1,0:T(8,128)(2,1)}, bf16[128,4096]{1,0:T(8,128)(2,1)S(1)}, u32[]{:S(2)}) copy-start(bf16[128,4096]{1,0:T(8,128)(2,1)S(1)} %collective-permute-done.16.refs_0_.refs_12_) | copy-start | bytes 3145732
  86.2 6.7 %copy-start.20 = (bf16[128,4096]{1,0:T(8,128)(2,1)}, bf16[128,4096]{1,0:T(8,128)(2,1)S(1)}, u32[]{:S(2)}) copy-start(bf16[128,4096]{1,0:T(8,128)(2,1)S(1)} %collective-permute-done.17.refs_1_.refs_13_) | copy-start | bytes 3145732
  86.2 6.6 %collective-permute-start.24 = (bf16[128,4096]{1,0:T(8,128)(2,1)S(1)}, bf16[128,4096]{1,0:T(8,128)(2,1)S(1)}, u32[]{:S(2)}, u32[]{:S(2)}) collective-permute-start(bf16[128,4096]{1,0:T(8,128)(2,1)S(1)} %collective-permute-done.16.refs_0_.refs_12_), channel_id=1, source_target_pairs={{0,4},{4,0},{8,12},{12,8},{16,20},{20,16},{24,28},{28,24},{1,5},{5... | collective-permute-start | bytes 3145736 | tf_op jit(solution)/shard_map/ppermute | solution.py:22
  86.3 6.6 %collective-permute-start.25 = (bf16[128,4096]{1,0:T(8,128)(2,1)S(1)}, bf16[128,4096]{1,0:T(8,128)(2,1)S(1)}, u32[]{:S(2)}, u32[]{:S(2)}) collective-permute-start(bf16[128,4096]{1,0:T(8,128)(2,1)S(1)} %collective-permute-done.17.refs_1_.refs_13_), channel_id=1, source_target_pairs={{0,4},{4,0},{8,12},{12,8},{16,20},{20,16},{24,28},{28,24},{1,5},{5... | collective-permute-start | bytes 3145736 | tf_op jit(solution)/shard_map/ppermute | solution.py:22
  86.8 4.4 %collective-permute-start.23 = (bf16[2,128,1024]{2,1,0:T(8,128)(2,1)S(1)}, bf16[2,128,1024]{2,1,0:T(8,128)(2,1)S(1)}, u32[]{:S(2)}, u32[]{:S(2)}) collective-permute-start(bf16[2,128,1024]{2,1,0:T(8,128)(2,1)S(1)} %get-tuple-element.88), channel_id=1, source_target_pairs={{0,4},{4,0},{8,12},{12,8},{16,20},{20,16},{24,28},{28,24},{1,5},{5... | collective-permute-start | bytes 1572872 | tf_op jit(solution)/shard_map/ppermute | solution.py:22
  86.9 31.2 %collective-permute-start.33 = (bf16[2,128,1024]{2,1,0:T(8,128)(2,1)S(1)}, bf16[2,128,1024]{2,1,0:T(8,128)(2,1)S(1)}, u32[]{:S(2)}, u32[]{:S(2)}) collective-permute-start(bf16[2,128,1024]{2,1,0:T(8,128)(2,1)S(1)} %get-tuple-element.105), channel_id=1, source_target_pairs={{0,4},{4,0},{8,12},{12,8},{16,20},{20,16},{24,28},{28,24},{1,5},{5... | collective-permute-start | bytes 1572872 | tf_op jit(solution)/shard_map/ppermute | solution.py:22
  87.6 14.0 %collective-permute-start.28 = (bf16[2,128,1024]{2,1,0:T(8,128)(2,1)S(1)}, bf16[2,128,1024]{2,1,0:T(8,128)(2,1)S(1)}, u32[]{:S(2)}, u32[]{:S(2)}) collective-permute-start(bf16[2,128,1024]{2,1,0:T(8,128)(2,1)S(1)} %add.92), channel_id=1, source_target_pairs={{0,1},{1,0},{2,3},{3,2},{4,5},{5,4},{6,7},{7,6},{8,9},{9,8},{10,11... | collective-permute-start | bytes 1572872 | tf_op jit(solution)/shard_map/ppermute | solution.py:22
  91.2 21.7 %collective-permute-start.29 = (bf16[3,576,256]{2,1,0:T(8,128)(2,1)S(1)}, bf16[3,576,256]{2,1,0:T(8,128)(2,1)S(1)}, u32[]{:S(2)}, u32[]{:S(2)}) collective-permute-start(bf16[3,576,256]{2,1,0:T(8,128)(2,1)S(1)} %get-tuple-element.100.refs_16_), channel_id=1, source_target_pairs={{0,16},{4,20},{8,24},{12,28},{16,0},{20,4},{24,8},{28,12},{1,17},{... | collective-permute-start | bytes 2654216 | tf_op jit(solution)/shard_map/ppermute | solution.py:22
  92.8 6.6 %copy-start.30 = (bf16[2,128,1024]{2,1,0:T(8,128)(2,1)}, bf16[2,128,1024]{2,1,0:T(8,128)(2,1)S(1)}, u32[]{:S(2)}) copy-start(bf16[2,128,1024]{2,1,0:T(8,128)(2,1)S(1)} %add_add_fusion.2) | copy-start | bytes 1572868
  92.8 4.8 %copy-start.22 = (bf16[128,4096]{1,0:T(8,128)(2,1)}, bf16[128,4096]{1,0:T(8,128)(2,1)S(1)}, u32[]{:S(2)}) copy-start(bf16[128,4096]{1,0:T(8,128)(2,1)S(1)} %collective-permute-done.24.refs_2_.refs_14_) | copy-start | bytes 3145732
  92.9 4.7 %copy-start.24 = (bf16[128,4096]{1,0:T(8,128)(2,1)}, bf16[128,4096]{1,0:T(8,128)(2,1)S(1)}, u32[]{:S(2)}) copy-start(bf16[128,4096]{1,0:T(8,128)(2,1)S(1)} %collective-permute-done.25.refs_3_.refs_15_) | copy-start | bytes 3145732
  97.6 16.8 %collective-permute-start.26 = (bf16[2,128,1024]{2,1,0:T(8,128)(2,1)S(1)}, bf16[2,128,1024]{2,1,0:T(8,128)(2,1)S(1)}, u32[]{:S(2)}, u32[]{:S(2)}) collective-permute-start(bf16[2,128,1024]{2,1,0:T(8,128)(2,1)S(1)} %get-tuple-element.97), channel_id=1, source_target_pairs={{0,4},{4,0},{8,12},{12,8},{16,20},{20,16},{24,28},{28,24},{1,5},{5... | collective-permute-start | bytes 1572872 | tf_op jit(solution)/shard_map/ppermute | solution.py:22
  97.8 16.6 %collective-permute-start.27 = (f32[8,128]{1,0:T(8,128)S(1)}, f32[8,128]{1,0:T(8,128)S(1)}, u32[]{:S(2)}, u32[]{:S(2)}) collective-permute-start(f32[8,128]{1,0:T(8,128)S(1)} %maximum_maximum_fusion), channel_id=1, source_target_pairs={{0,1},{1,0},{2,3},{3,2},{4,5},{5,4},{6,7},{7,6},{8,9},{9,8},{10,11... | collective-permute-start | bytes 12296 | tf_op jit(solution)/shard_map/ppermute | solution.py:22
  101.6 50.3 %collective-permute-start.32 = (bf16[128,1024]{1,0:T(8,128)(2,1)}, bf16[128,1024]{1,0:T(8,128)(2,1)}, u32[]{:S(2)}, u32[]{:S(2)}) collective-permute-start(bf16[128,1024]{1,0:T(8,128)(2,1)} %slice_bitcast_fusion.4), channel_id=1, source_target_pairs={{0,2},{1,3},{2,0},{3,1},{4,6},{5,7},{6,4},{7,5},{8,10},{9,11},{10,... | collective-permute-start | bytes 786440 | tf_op jit(solution)/shard_map/ppermute | solution.py:22
  112.9 6.9 %copy-start.26 = (bf16[3,576,256]{2,1,0:T(8,128)(2,1)}, bf16[3,576,256]{2,1,0:T(8,128)(2,1)S(1)}, u32[]{:S(2)}) copy-start(bf16[3,576,256]{2,1,0:T(8,128)(2,1)S(1)} %collective-permute-done.29.refs_18_) | copy-start | bytes 2654212
  112.9 13.9 %collective-permute-start.35 = (bf16[1,576,256]{2,1,0:T(8,128)(2,1)}, bf16[1,576,256]{2,1,0:T(8,128)(2,1)}, u32[]{:S(2)}, u32[]{:S(2)}) collective-permute-start(bf16[1,576,256]{2,1,0:T(8,128)(2,1)} %get-tuple-element.107.refs_17_), channel_id=1, source_target_pairs={{0,16},{4,20},{8,24},{12,28},{16,0},{20,4},{24,8},{28,12},{1,17},{... | collective-permute-start | bytes 884744 | tf_op jit(solution)/shard_map/ppermute | solution.py:22
  114.4 37.6 %collective-permute-start.38 = (bf16[2,128,1024]{2,1,0:T(8,128)(2,1)}, bf16[2,128,1024]{2,1,0:T(8,128)(2,1)}, u32[]{:S(2)}, u32[]{:S(2)}) collective-permute-start(bf16[2,128,1024]{2,1,0:T(8,128)(2,1)} %get-tuple-element.115), channel_id=1, source_target_pairs={{0,4},{4,0},{8,12},{12,8},{16,20},{20,16},{24,28},{28,24},{1,5},{5... | collective-permute-start | bytes 1572872 | tf_op jit(solution)/shard_map/ppermute | solution.py:22
  114.4 6.3 %collective-permute-start.30 = (f32[8,128]{1,0:T(8,128)S(1)}, f32[8,128]{1,0:T(8,128)S(1)}, u32[]{:S(2)}, u32[]{:S(2)}) collective-permute-start(f32[8,128]{1,0:T(8,128)S(1)} %add.93), channel_id=1, source_target_pairs={{0,2},{1,3},{2,0},{3,1},{4,6},{5,7},{6,4},{7,5},{8,10},{9,11},{10,... | collective-permute-start | bytes 12296 | tf_op jit(solution)/shard_map/ppermute | solution.py:22
  118.1 8.1 %copy-start.38 = (s32[4]{0:T(128)S(1)}, s32[4]{0:T(128)}, u32[]{:S(2)}) copy-start(s32[4]{0:T(128)} %param.15) | copy-start | bytes 52
  118.1 33.9 %collective-permute-start.31 = (bf16[2,128,1024]{2,1,0:T(8,128)(2,1)}, bf16[2,128,1024]{2,1,0:T(8,128)(2,1)}, u32[]{:S(2)}, u32[]{:S(2)}) collective-permute-start(bf16[2,128,1024]{2,1,0:T(8,128)(2,1)} %add.96), channel_id=1, source_target_pairs={{0,1},{1,0},{2,3},{3,2},{4,5},{5,4},{6,7},{7,6},{8,9},{9,8},{10,11... | collective-permute-start | bytes 1572872 | tf_op jit(solution)/shard_map/ppermute | solution.py:22
  120.7 31.3 %collective-permute-start.34 = (bf16[128,1024]{1,0:T(8,128)(2,1)}, bf16[128,1024]{1,0:T(8,128)(2,1)}, u32[]{:S(2)}, u32[]{:S(2)}) collective-permute-start(bf16[128,1024]{1,0:T(8,128)(2,1)} %slice_bitcast_fusion.3), channel_id=1, source_target_pairs={{0,2},{1,3},{2,0},{3,1},{4,6},{5,7},{6,4},{7,5},{8,10},{9,11},{10,... | collective-permute-start | bytes 786440 | tf_op jit(solution)/shard_map/ppermute | solution.py:22
  122.8 29.1 %all-to-all-start = ((bf16[8,1,128]{2,1,0:T(2,128)(2,1)}), bf16[8,1,128]{2,1,0:T(2,128)(2,1)S(1)}, u32[]{:S(2)}, u32[]{:S(2)}) async-start(bf16[8,1,128]{2,1,0:T(2,128)(2,1)} %copy.26), calls=%async_computation | async-start | bytes 8192 | tf_op jit(solution)/shard_map/all_to_all | solution.py:310
  151.9 3.6 %copy-start.31 = (bf16[2,128,1024]{2,1,0:T(8,128)(2,1)S(1)}, bf16[2,128,1024]{2,1,0:T(8,128)(2,1)}, u32[]{:S(2)}) copy-start(bf16[2,128,1024]{2,1,0:T(8,128)(2,1)} %copy-done.30) | copy-start | bytes 1572868
  151.9 3.6 %copy-start.33 = (bf16[2,128,1024]{2,1,0:T(8,128)(2,1)S(1)}, bf16[2,128,1024]{2,1,0:T(8,128)(2,1)}, u32[]{:S(2)}) copy-start(bf16[2,128,1024]{2,1,0:T(8,128)(2,1)} %copy-done.32) | copy-start | bytes 1572868
  153.4 15.2 %collective-permute-start.39 = (bf16[128,1024]{1,0:T(8,128)(2,1)S(1)}, bf16[128,1024]{1,0:T(8,128)(2,1)S(1)}, u32[]{:S(2)}, u32[]{:S(2)}) collective-permute-start(bf16[128,1024]{1,0:T(8,128)(2,1)S(1)} %slice_bitcast_fusion), channel_id=1, source_target_pairs={{0,2},{1,3},{2,0},{3,1},{4,6},{5,7},{6,4},{7,5},{8,10},{9,11},{10,... | collective-permute-start | bytes 786440 | tf_op jit(solution)/shard_map/ppermute | solution.py:22
  156.7 20.8 %copy-start.29 = (bf16[2,128,1024]{2,1,0:T(8,128)(2,1)S(1)}, bf16[2,128,1024]{2,1,0:T(8,128)(2,1)}, u32[]{:S(2)}) copy-start(bf16[2,128,1024]{2,1,0:T(8,128)(2,1)} %copy-done.28) | copy-start | bytes 1572868
  156.7 20.8 %copy-start.35 = (bf16[128,1024]{1,0:T(8,128)(2,1)S(1)}, bf16[128,1024]{1,0:T(8,128)(2,1)}, u32[]{:S(2)}) copy-start(bf16[128,1024]{1,0:T(8,128)(2,1)} %copy-done.34) | copy-start | bytes 786436
  156.8 15.1 %collective-permute-start.37 = (bf16[128,1024]{1,0:T(8,128)(2,1)S(1)}, bf16[128,1024]{1,0:T(8,128)(2,1)S(1)}, u32[]{:S(2)}, u32[]{:S(2)}) collective-permute-start(bf16[128,1024]{1,0:T(8,128)(2,1)S(1)} %pad_maximum_fusion.2), channel_id=1, source_target_pairs={{0,16},{4,20},{8,24},{12,28},{16,0},{20,4},{24,8},{28,12},{1,17},{... | collective-permute-start | bytes 786440 | tf_op jit(solution)/shard_map/ppermute | solution.py:22
  158.8 13.1 %collective-permute-start.36 = (bf16[128,1024]{1,0:T(8,128)(2,1)S(1)}, bf16[128,1024]{1,0:T(8,128)(2,1)S(1)}, u32[]{:S(2)}, u32[]{:S(2)}) collective-permute-start(bf16[128,1024]{1,0:T(8,128)(2,1)S(1)} %pad_maximum_fusion.1), channel_id=1, source_target_pairs={{0,8},{4,12},{8,0},{12,4},{16,24},{20,28},{24,16},{28,20},{1,9},{5... | collective-permute-start | bytes 786440 | tf_op jit(solution)/shard_map/ppermute | solution.py:22
  168.6 8.8 %collective-permute-start.40 = (bf16[128,1024]{1,0:T(8,128)(2,1)S(1)}, bf16[128,1024]{1,0:T(8,128)(2,1)S(1)}, u32[]{:S(2)}, u32[]{:S(2)}) collective-permute-start(bf16[128,1024]{1,0:T(8,128)(2,1)S(1)} %fusion), channel_id=1, source_target_pairs={{0,24},{4,28},{8,16},{12,20},{16,8},{20,12},{24,0},{28,4},{1,25},{... | collective-permute-start | bytes 786440 | tf_op jit(solution)/shard_map/ppermute | solution.py:22
  (17 other events, 24.3 us)

commit v8 on v7

--- a/solution.py
+++ b/solution.py
@@ -62,12 +62,13 @@
         in_specs=[pl.BlockSpec(memory_space=pl.ANY)] * 2,
         out_specs=[pl.BlockSpec(memory_space=pltpu.VMEM)] * 2,
         scratch_shapes=[pltpu.SemaphoreType.DMA((4,))],
+        compiler_params=pltpu.CompilerParams(vmem_limit_bytes=4 * 1024 * 1024),
         cost_estimate=pl.CostEstimate(flops=1, bytes_accessed=1, transcendentals=0),
         name="pack",
     )(tokens, cotangent)
 
 
-def activations_kernel(place, x_places, dy_places, count, parts, where_ref, one_ref, two_ref, *refs):
+def activations_kernel(x_places, dy_places, count, parts, where_ref, one_ref, two_ref, *refs):
     x_pieces, dy_pieces = pieces_of(x_places, refs), pieces_of(dy_places, refs)
     in_ref, down_ref = refs[count : count + 2]
     acts_ref, score_ref, keep_near, keep_far, give_near, give_far, both = refs[-7:]
@@ -101,8 +102,8 @@
     grad_hidden = g * back
     slope = sigma * (1.0 + pre_gate * (1.0 - sigma))
     grads = jnp.concatenate([grad_hidden * pre_up * slope, grad_hidden * active], axis=0)
-    acts_ref[place, pl.ds(0, 2 * units), :] = grads.astype(jnp.bfloat16)
-    acts_ref[place, pl.ds(2 * units, units), :] = (g * hidden).astype(jnp.bfloat16)
+    acts_ref[pl.ds(0, 2 * units), :] = grads.astype(jnp.bfloat16)
+    acts_ref[pl.ds(2 * units, units), :] = (g * hidden).astype(jnp.bfloat16)
     both[...] = grads.T.astype(jnp.bfloat16)
     for part in range(parts):
         columns = pl.ds(pl.multiple_of((group ^ part) * chunk, chunk), chunk)
@@ -113,7 +114,7 @@
         give[part // 2] = share[rows:]
 
 
-def activations(place, places, parts, where, tables, held, weights, before):
+def activations(parts, where, tables, held, weights):
     operands, x_places, dy_places = held
     width = operands[0].shape[1]
     rows = sum(size for _, _, size in x_places) // 2
@@ -121,9 +122,9 @@
     bf16 = jnp.bfloat16
     share = pltpu.VMEM((parts // 2, rows, width // parts), bf16)
     return pl.pallas_call(
-        functools.partial(activations_kernel, place, x_places, dy_places, len(operands), parts),
+        functools.partial(activations_kernel, x_places, dy_places, len(operands), parts),
         out_shape=(
-            pltpu.VMEM((places, 3 * units, 2 * rows), bf16),
+            pltpu.VMEM((3 * units, 2 * rows), bf16),
             pltpu.VMEM((1, 2 * rows), jnp.float32),
             share,
             share,
@@ -131,23 +132,23 @@
             share,
         ),
         in_specs=[pl.BlockSpec(memory_space=pltpu.SMEM)]
-        + [pl.BlockSpec(memory_space=pltpu.VMEM)] * (len(operands) + 4 + len(before)),
+        + [pl.BlockSpec(memory_space=pltpu.VMEM)] * (len(operands) + 4),
         out_specs=[pl.BlockSpec(memory_space=pltpu.VMEM)] * 6,
         scratch_shapes=[pltpu.VMEM((2 * rows, 2 * units), bf16)],
-        input_output_aliases={len(operands) + 5: 0} if before else {},
         compiler_params=pltpu.CompilerParams(vmem_limit_bytes=VMEM),
         cost_estimate=pl.CostEstimate(flops=1, bytes_accessed=1, transcendentals=0),
         name="activations",
-    )(where, *in_vmem(*tables, *operands, *weights, *before))
+    )(where, *in_vmem(*tables, *operands, *weights))
 
 
 def weight_grads_kernel(sources, x_places, dy_places, loaded, parts, flag_ref, *refs):
     operands, refs = list(refs[:loaded]), refs[loaded:]
-    own, other, refs = refs[:2], refs[2:4], refs[4:]
+    count = len(sources)
+    own, other, refs = refs[:count], refs[count : 2 * count], refs[2 * count :]
     outs = refs[:3]
     held, acts, results, sems, out_sems = refs[3:]
     units, width = outs[0].shape[1:]
-    rows = own[0].shape[2] // 2
+    rows = own[0].shape[1] // 2
     half = rows // 2
     chunk = width // parts
     copies = []
@@ -166,9 +167,7 @@
     first = lax.broadcasted_iota(jnp.int32, (1, rows), 1) < half
 
     def tile_of(groups_of, place):
-        group, early = place // 2, groups_of[0].shape[0]
-        ref, group = (groups_of[0], group) if group < early else (groups_of[1], group - early)
-        return ref[group, :, pl.ds(place % 2 * rows, rows)]
+        return groups_of[place // 2][:, pl.ds(place % 2 * rows, rows)]
 
     for place, (one, two) in enumerate(tiles):
         from_one = [tile[0] for tile in tiles].index(one ^ ACROSS_Y)
@@ -205,7 +204,7 @@
         operands += held
     rows, width = operands[0].shape
     loaded = len(operands)
-    units = own[0].shape[1] // 3
+    units = own[0].shape[0] // 3
     total = sum(size for _, _, size in x_places)
     bf16 = jnp.bfloat16
     rest = in_vmem(*own, *other)
@@ -223,10 +222,10 @@
             pltpu.SemaphoreType.DMA((parts, loaded)),
             pltpu.SemaphoreType.DMA((parts, 3)),
         ],
-        compiler_params=pltpu.CompilerParams(vmem_limit_bytes=32 * 1024 * 1024),
+        compiler_params=pltpu.CompilerParams(vmem_limit_bytes=28 * 1024 * 1024),
         cost_estimate=pl.CostEstimate(flops=1, bytes_accessed=1, transcendentals=0),
         name="weight_grads",
-    )(flag, *operands, *rest)
+    )(flag, *[pltpu.with_memory_space_constraint(value, pltpu.HBM) for value in operands], *rest)
 
 
 CORE, ACROSS_X, ACROSS_Y = 1, 2, 4
@@ -266,9 +265,9 @@
         messages = [one, two, expert_swap(one, CORE), expert_swap(two, CORE)]
         return messages, [(i, 0, half) for i in range(4)], [(i, half, half) for i in range(4)]
 
-    def work(one, two, held, *before, place=0, places=3):
+    def work(one, two, held):
         acts, score, keep_near, keep_far, give_near, give_far = activations(
-            place, places, parts, where, (tables[one], tables[two]), held, weights, before
+            parts, where, (tables[one], tables[two]), held, weights
         )
         scores.append(score)
         groups.append(held)
@@ -282,38 +281,40 @@
         near = near + arrived
         return near[0].astype(f32), swap(near[1], "dp", 2)
 
-    acts, far_a, share_a = work(0, 0, own_block)
-    a[2], b[4], tables[2], tables[4], acts, far_a = barrier((a[2], b[4], tables[2], tables[4], acts, far_a))
+    acts_a, far_a, share_a = work(0, 0, own_block)
+    a[2], b[4], tables[2], tables[4], acts_a, far_a = barrier((a[2], b[4], tables[2], tables[4], acts_a, far_a))
     a[6], b[6] = expert_swap(a[2], ACROSS_Y), expert_swap(b[4], ACROSS_X)
     tables[6] = expert_swap(tables[2], ACROSS_Y)
     near_a, near_in_a = to_neighbour(far_a, share_a)
-    acts, far_b, share_b = work(2, 4, group_of(a[2], b[4]), acts, place=1)
-    a[4], b[2], tables[6], acts, near_in_a, far_b = barrier((a[4], b[2], tables[6], acts, near_in_a, far_b))
+    acts_b, far_b, share_b = work(2, 4, group_of(a[2], b[4]))
+    a[4], b[2], tables[6], acts_b, near_in_a, far_b = barrier((a[4], b[2], tables[6], acts_b, near_in_a, far_b))
     near_b, near_in_b = to_neighbour(far_b, share_b)
     total_a, far_in_a = to_far(near_a, near_in_a)
-    acts, far_c, share_c = work(4, 2, group_of(a[4], b[2]), acts, place=2)
-    a[6], b[6], acts, far_in_a, near_in_b, far_c = barrier((a[6], b[6], acts, far_in_a, near_in_b, far_c))
+    acts_c, far_c, share_c = work(4, 2, group_of(a[4], b[2]))
+    a[6], b[6], acts_c, far_in_a, near_in_b, far_c = barrier((a[6], b[6], acts_c, far_in_a, near_in_b, far_c))
     near_c, near_in_c = to_neighbour(far_c, share_c)
-    other = expert_swap(acts, half_axis)
-    last_acts, far_d, share_d = work(6, 6, group_of(a[6], b[6]), places=1)
-    last_other = expert_swap(last_acts, half_axis)
+    other_a, other_b = expert_swap(acts_a, half_axis), expert_swap(acts_b, half_axis)
+    acts_d, far_d, share_d = work(6, 6, group_of(a[6], b[6]))
+    other_c, other_d = expert_swap(acts_c, half_axis), expert_swap(acts_d, half_axis)
     total_b, far_in_b = to_far(near_b, near_in_b)
     tiles = jnp.concatenate(scores, axis=1).reshape(expert_count, 2 * half)
     second = jnp.concatenate([tiles[:2, half:], tiles[4:6, half:], tiles[2:4, half:], tiles[6:, half:]])
     score_rows = jnp.concatenate([tiles[:, :half], second], axis=1)
     score_in = swap(score_rows, "dp", 1)
-    far_d, score_in, near_in_c, other = barrier((far_d, score_in, near_in_c, other))
+    far_d, score_in, near_in_c, other_a, other_b = barrier((far_d, score_in, near_in_c, other_a, other_b))
     near_d, near_in_d = to_neighbour(far_d, share_d)
     score_rows = score_rows + score_in
     score_rows = score_rows + swap(score_rows, "dp", 2)
     score_rows = jnp.take(score_rows.astype(bf16), jnp.arange(expert_count, dtype=jnp.int32) ^ me, axis=0)
     score_rows = lax.all_to_all(score_rows, "expert", split_axis=0, concat_axis=0, tiled=True)
     total_c, far_in_c = to_far(near_c, near_in_c)
-    grads = weight_grads(
-        ((0, 0), (2, 4), (4, 2), (6, 6)), own_flag, groups, (acts, last_acts), (other, last_other)
-    )
-    score_rows, near_in_d, far_in_b, far_in_c, grads = barrier((score_rows, near_in_d, far_in_b, far_in_c, grads))
+    score_rows, near_in_d, far_in_b, far_in_c, other_c, other_d, own_flag = barrier(
+        (score_rows, near_in_d, far_in_b, far_in_c, other_c, other_d, own_flag)
+    )
     total_d, far_in_d = to_far(near_d, near_in_d)
+    own, other = (acts_a, acts_b, acts_c, acts_d), (other_a, other_b, other_c, other_d)
+    grads = weight_grads(((0, 0), (2, 4), (4, 2), (6, 6)), own_flag, groups, own, other)
+    far_in_d, grads = barrier((far_in_d, grads))
 
     total_a, total_b = total_a + far_in_a.astype(f32), total_b + far_in_b.astype(f32)
     total_c, total_d = total_c + far_in_c.astype(f32), (total_d + far_in_d.astype(f32)).astype(bf16)

time: 179 us -> 170 us (0.950)
  local copies, waits for them, and re-layouts: 19.9 us -> 5.3 us
  waiting for transfers between devices: 70.9 us -> 81.3 us
  starting transfers between devices: 44.5 us -> 39.8 us
    unnamed x79 -> x61, local copies, waits for them, and re-layouts: 17.1 us -> 3.26 us
    ppermute x41 -> x43, waiting for transfers between devices: 70.9 us -> 78.6 us  [swap(): lax.ppermute(value, axis, [(i, i ^ by) for i in range(lax.axis_size(axis))])]
    ppermute x41 -> x43, starting transfers between devices: 41.2 us -> 36.4 us  [swap(): lax.ppermute(value, axis, [(i, i ^ by) for i in range(lax.axis_size(axis))])]
    all_to_all x1, waiting for transfers between devices: 0.01 us -> 2.73 us  [whole_shards(): lax.all_to_all(score_rows, 'expert', split_axis=0, concat_axis=0, tiled=T...]
  transfers between devices with their start and end apart: 42 -> 44, of which waited for: 12 -> 15; matrix products, arithmetic and copies ran while one was open for 6% -> 6% of each run, Pallas kernels for 18% -> 19%
where the time goes in v8:
time: 170 us
  waiting for transfers between devices  81.3 us (48%)
  starting transfers between devices  39.8 us (23%)
  Pallas kernels  31.7 us (19%)
  other arithmetic  10.7 us (6%)
  local copies, waits for them, and re-layouts  5.3 us (3%)
    ppermute x43, waiting for transfers between devices, swap(): lax.ppermute(value, axis, [(i, i ^ by) for i in range(lax.axis_size(axis))])  78.6 us
    ppermute x43, starting transfers between devices, swap(): lax.ppermute(value, axis, [(i, i ^ by) for i in range(lax.axis_size(axis))])  36.4 us
    pallas_call x4, Pallas kernels, activations(): pl.pallas_call(functools.partial(activations_kernel, x_places, dy_places,...  18.8 us
    pallas_call x1, Pallas kernels, weight_grads(): pl.pallas_call(functools.partial(weight_grads_kernel, sources, x_places,...  11.5 us
  transfers between devices with their start and end apart: 44, of which 15 were waited for; matrix products, arithmetic and copies ran while one was open for 6% of the time, Pallas kernels for 19%

profile of v8, /device:TPU:0, one launch (start us, length us, event | category | flops | bytes accessed | tf_op | source)
XLA Modules:
  0.0 170.0 jit_solution(9229362487128213783)
XLA Ops:
  0.6 0.5 collective-permute-start.1
  1.2 0.7 convert_element_type.74
  1.9 0.7 select_reduce_fusion.1
  2.6 0.4 collective-permute-start
  3.0 1.2 copy-done.1
  4.3 1.2 copy-done.3
  5.5 1.5 pack.1
  7.0 2.6 %collective-permute-start.6 = (bf16[128,4096]{1,0:T(8,128)(2,1)}, bf16[128,4096]{1,0:T(8,128)(2,1)}, u32[]{:S(2)}, u32[]{:S(2)}) collective-permute-start(bf16[128,4096]{1,0:T(8,128)(2,1)} %get-tuple-element.70), channel_id=1, source_target_pairs={{0,8},{4,12},{8,0},{12,4},{16,24},{20,28},{24,16},{28,20},{1,9},{5... | collective-permute-start | bytes 3145736 | tf_op jit(solution)/shard_map/ppermute | solution.py:22
  9.6 1.5 collective-permute-start.7
  11.2 1.8 %pad_maximum_fusion.refs_4_ = bf16[384,4096]{1,0:T(8,128)(2,1)S(1)} fusion(bf16[192,4096]{1,0:T(8,128)(2,1)S(1)} %bitcast.52, bf16[192,4096]{1,0:T(8,128)(2,1)} %bitcast.53), kind=kLoop, calls=%fused_computation.1 | loop fusion | flops 6291456 | bytes 6291456 | tf_op jit(solution)/shard_map/concatenate | solution.py:243
  13.6 4.7 %activations.4 = (bf16[576,256]{1,0:T(8,128)(2,1)S(1)}, f32[1,256]{1,0:T(1,128)S(1)}, bf16[2,128,1024]{2,1,0:T(8,128)(2,1)S(1)}, bf16[2,128,1024]{2,1,0:T(8,128)...) custom-call(s32[2]{0:T(128)S(1)} %pad_add_fusion.where_ref, ...), custom_call_target="tpu_custom_call" | custom-call | flops 1 | bytes 1 | tf_op jit(solution)/shard_map/activations/pallas_call | solution.py:124
  18.5 0.6 collective-permute-start.8
  19.1 0.4 collective-permute-start.9
  19.5 14.3 %collective-permute-done.8.one_ref.two_ref = f32[16,128]{1,0:T(8,128)S(1)} collective-permute-done((f32[16,128]{1,0:T(8,128)S(1)}, f32[16,128]{1,0:T(8,128)S(1)}, u32[]{:S(2)}, u32[]{:S(2)}) %collective-permute-start.8) | collective-permute-done | bytes 8224 | tf_op jit(solution)/shard_map/ppermute | solution.py:22
  33.8 1.5 collective-permute-done.9.two_ref.one_ref
  35.3 0.5 collective-permute-start.13
  35.8 1.5 collective-permute-start.4
  37.4 0.5 collective-permute-start.5
  38.1 1.6 collective-permute-start.14
  39.8 5.8 %activations.5 = (bf16[576,256]{1,0:T(8,128)(2,1)S(1)}, f32[1,256]{1,0:T(1,128)S(1)}, bf16[2,128,1024]{2,1,0:T(8,128)(2,1)S(1)}, bf16[2,128,1024]{2,1,0:T(8,128)...) custom-call(s32[2]{0:T(128)S(1)} %pad_add_fusion.where_ref, ...), custom_call_target="tpu_custom_call" | custom-call | flops 1 | bytes 1 | tf_op jit(solution)/shard_map/activations/pallas_call | solution.py:124
  45.7 1.2 collective-permute-start.11
  46.9 14.4 %collective-permute-done.4.refs_0_.refs_8_ = bf16[128,4096]{1,0:T(8,128)(2,1)S(1)} collective-permute-done((bf16[128,4096]{1,0:T(8,128)(2,1)}, bf16[128,4096]{1,0:T(8,128)(2,1)S(1)}, u32[]{:S(2)}, u32[]{:S(2)}) %collective-permute-start.4) | collective-permute-done | bytes 1048608 | tf_op jit(solution)/shard_map/ppermute | solution.py:22
  61.3 1.1 collective-permute-done.5.refs_1_.refs_9_
  62.5 0.5 collective-permute-start.19
  63.1 0.5 collective-permute-start.16
  63.6 0.4 collective-permute-start.17
  64.3 0.9 collective-permute-done.18.refs_2_.refs_10_
  65.2 1.6 collective-permute-start.21
  66.8 4.0 %activations.6 = (bf16[576,256]{1,0:T(8,128)(2,1)}, f32[1,256]{1,0:T(1,128)S(1)}, bf16[2,128,1024]{2,1,0:T(8,128)(2,1)S(1)}, bf16[2,128,1024]{2,1,0:T(8,128)(2,1...) custom-call(s32[2]{0:T(128)S(1)} %pad_add_fusion.where_ref, ...), custom_call_target="tpu_custom_call" | custom-call | flops 1 | bytes 1 | tf_op jit(solution)/shard_map/activations/pallas_call | solution.py:124
  71.1 2.7 %collective-permute-start.20 = (bf16[128,1024]{1,0:T(8,128)(2,1)S(1)}, bf16[128,1024]{1,0:T(8,128)(2,1)S(1)}, u32[]{:S(2)}, u32[]{:S(2)}) collective-permute-start(bf16[128,1024]{1,0:T(8,128)(2,1)S(1)} %slice_bitcast_fusion.6), channel_id=1, source_target_pairs={{0,2},{1,3},{2,0},{3,1},{4,6},{5,7},{6,4},{7,5},{8,10},{9,11},{10,... | collective-permute-start | bytes 786440 | tf_op jit(solution)/shard_map/ppermute | solution.py:22
  73.7 15.1 %collective-permute-done.16.refs_0_.refs_12_ = bf16[128,4096]{1,0:T(8,128)(2,1)S(1)} collective-permute-done((bf16[128,4096]{1,0:T(8,128)(2,1)}, bf16[128,4096]{1,0:T(8,128)(2,1)S(1)}, u32[]{:S(2)}, u32[]{:S(2)}) %collective-permute-start.16) | collective-permute-done | bytes 1048608 | tf_op jit(solution)/shard_map/ppermute | solution.py:22
  89.2 0.5 collective-permute-start.25
  89.9 1.4 collective-permute-start.29
  91.4 0.6 collective-permute-start.30
  92.2 1.9 %collective-permute-done.23 = bf16[2,128,1024]{2,1,0:T(8,128)(2,1)S(1)} collective-permute-done((bf16[2,128,1024]{2,1,0:T(8,128)(2,1)S(1)}, bf16[2,128,1024]{2,1,0:T(8,128)(2,1)S(1)}, u32[]{:S(2)}, u32[]{:S(2)}) %collective-permute-start.23) | collective-permute-done | bytes 524320 | tf_op jit(solution)/shard_map/ppermute | solution.py:22
  94.3 1.7 collective-permute-start.28
  96.0 4.2 %activations.7 = (bf16[576,256]{1,0:T(8,128)(2,1)}, f32[1,256]{1,0:T(1,128)S(1)}, bf16[2,128,1024]{2,1,0:T(8,128)(2,1)S(1)}, bf16[2,128,1024]{2,1,0:T(8,128)(2,1...) custom-call(s32[2]{0:T(128)S(1)} %pad_add_fusion.where_ref, ...), custom_call_target="tpu_custom_call" | custom-call | flops 1 | bytes 1 | tf_op jit(solution)/shard_map/activations/pallas_call | solution.py:124
  100.6 0.8 collective-permute-start.27
  101.4 4.2 %collective-permute-done.30.refs_21_ = bf16[576,256]{1,0:T(8,128)(2,1)S(1)} collective-permute-done((bf16[576,256]{1,0:T(8,128)(2,1)S(1)}, bf16[576,256]{1,0:T(8,128)(2,1)S(1)}, u32[]{:S(2)}, u32[]{:S(2)}) %collective-permute-start.30) | collective-permute-done | bytes 294944 | tf_op jit(solution)/shard_map/ppermute | solution.py:22
  105.5 2.6 %collective-permute-start.33 = (bf16[128,1024]{1,0:T(8,128)(2,1)S(1)}, bf16[128,1024]{1,0:T(8,128)(2,1)}, u32[]{:S(2)}, u32[]{:S(2)}) collective-permute-start(bf16[128,1024]{1,0:T(8,128)(2,1)S(1)} %slice_bitcast_fusion.4), channel_id=1, source_target_pairs={{0,2},{1,3},{2,0},{3,1},{4,6},{5,7},{6,4},{7,5},{8,10},{9,11},{10,... | collective-permute-start | bytes 786440 | tf_op jit(solution)/shard_map/ppermute | solution.py:22
  108.1 0.5 collective-permute-done.28
  108.6 1.5 collective-permute-start.36
  110.3 0.4 collective-permute-start.37
  110.7 3.1 %collective-permute-start.31 = (f32[8,128]{1,0:T(8,128)S(1)}, f32[8,128]{1,0:T(8,128)S(1)}, u32[]{:S(2)}, u32[]{:S(2)}) collective-permute-start(f32[8,128]{1,0:T(8,128)S(1)} %add.93), channel_id=1, source_target_pairs={{0,2},{1,3},{2,0},{3,1},{4,6},{5,7},{6,4},{7,5},{8,10},{9,11},{10,... | collective-permute-start | bytes 12296 | tf_op jit(solution)/shard_map/ppermute | solution.py:22
  113.9 0.7 slice_bitcast_fusion.3
  114.6 1.0 add.96
  115.6 11.5 %collective-permute-done.31 = f32[8,128]{1,0:T(8,128)S(1)} collective-permute-done((f32[8,128]{1,0:T(8,128)S(1)}, f32[8,128]{1,0:T(8,128)S(1)}, u32[]{:S(2)}, u32[]{:S(2)}) %collective-permute-start.31) | collective-permute-done | bytes 4128 | tf_op jit(solution)/shard_map/ppermute | solution.py:22
  127.1 0.6 gather_fusion
  127.7 0.6 copy.24
  128.3 3.3 %all-to-all-start = ((bf16[8,1,128]{2,1,0:T(2,128)(2,1)}), bf16[8,1,128]{2,1,0:T(2,128)(2,1)S(1)}, u32[]{:S(2)}, u32[]{:S(2)}) async-start(bf16[8,1,128]{2,1,0:T(2,128)(2,1)} %copy.24), calls=%async_computation | async-start | bytes 8192 | tf_op jit(solution)/shard_map/all_to_all | solution.py:309
  131.7 0.5 collective-permute-start.40
  132.1 1.4 fusion.7
  133.5 2.7 %all-to-all-done = bf16[8,1,128]{2,1,0:T(2,128)(2,1)S(1)} async-done(((bf16[8,1,128]{2,1,0:T(2,128)(2,1)}), bf16[8,1,128]{2,1,0:T(2,128)(2,1)S(1)}, u32[]{:S(2)}, u32[]{:S(2)}) %all-to-all-start) | async-done | bytes 2080 | tf_op jit(solution)/shard_map/all_to_all | solution.py:309
  136.3 6.3 %collective-permute-done.32 = bf16[2,128,1024]{2,1,0:T(8,128)(2,1)} collective-permute-done((bf16[2,128,1024]{2,1,0:T(8,128)(2,1)}, bf16[2,128,1024]{2,1,0:T(8,128)(2,1)}, u32[]{:S(2)}, u32[]{:S(2)}) %collective-permute-start.32) | collective-permute-done | bytes 524320 | tf_op jit(solution)/shard_map/ppermute | solution.py:22
  142.6 1.2 fusion.1
  143.8 1.3 add_add_fusion
  145.2 1.6 collective-permute-start.41
  146.8 0.6 collective-permute-start.38
  147.5 1.7 collective-permute-start.39
  149.2 11.5 %weight_grads.1 = (bf16[1,192,4096]{2,1,0:T(8,128)(2,1)}, bf16[1,192,4096]{2,1,0:T(8,128)(2,1)}, bf16[1,192,4096]{2,1,0:T(8,128)(2,1)}) custom-call(s32[1]{0:T(128)} %bitcast.16.flag_ref, bf16[128,4096]{1,0:T(8,128)(2,1)} %refs_0_.3, bf16[128,4096]{1,0:T(8,128)(2,1)} %refs_1_.3, bf16[128,4096]{1,0:T(8,128)(2,1)} %copy-done.5, ...), custom_call_target="tpu_custom_call" | custom-call | flops 1 | bytes 1 | tf_op jit(solution)/shard_map/weight_grads/pallas_call | solution.py:211
  160.7 1.4 collective-permute-start.42
  162.1 0.6 select_reduce_fusion
  162.7 6.4 %collective-permute-done.42 = bf16[128,1024]{1,0:T(8,128)(2,1)S(1)} collective-permute-done((bf16[128,1024]{1,0:T(8,128)(2,1)S(1)}, bf16[128,1024]{1,0:T(8,128)(2,1)S(1)}, u32[]{:S(2)}, u32[]{:S(2)}) %collective-permute-start.42) | collective-permute-done | bytes 262176 | tf_op jit(solution)/shard_map/ppermute | solution.py:22
  169.1 0.9 fusion.6
  (129 shorter events, 3.6 us)
Async XLA Ops:
  0.6 12.4 %collective-permute-start.1 = (bf16[128,4096]{1,0:T(8,128)(2,1)}, bf16[128,4096]{1,0:T(8,128)(2,1)S(1)}, u32[]{:S(2)}, u32[]{:S(2)}) collective-permute-start(bf16[128,4096]{1,0:T(8,128)(2,1)} %refs_0_.3), channel_id=1, source_target_pairs={{0,4},{4,0},{8,12},{12,8},{16,20},{20,16},{24,28},{28,24},{1,5},{5... | collective-permute-start | bytes 3145736 | tf_op jit(solution)/shard_map/ppermute | solution.py:22
  1.1 11.9 %collective-permute-start.2 = (bf16[128,4096]{1,0:T(8,128)(2,1)}, bf16[128,4096]{1,0:T(8,128)(2,1)}, u32[]{:S(2)}, u32[]{:S(2)}) collective-permute-start(bf16[128,4096]{1,0:T(8,128)(2,1)} %refs_1_.3), channel_id=1, source_target_pairs={{0,4},{4,0},{8,12},{12,8},{16,20},{20,16},{24,28},{28,24},{1,5},{5... | collective-permute-start | bytes 3145736 | tf_op jit(solution)/shard_map/ppermute | solution.py:22
  2.6 10.4 %collective-permute-start = (f32[8,128]{1,0:T(8,128)S(1)}, f32[8,128]{1,0:T(8,128)S(1)}, u32[]{:S(2)}, u32[]{:S(2)}) collective-permute-start(f32[8,128]{1,0:T(8,128)S(1)} %bitcast.56), channel_id=1, source_target_pairs={{0,4},{4,0},{8,12},{12,8},{16,20},{20,16},{24,28},{28,24},{1,5},{5... | collective-permute-start | bytes 12296 | tf_op jit(solution)/shard_map/ppermute | solution.py:22
  5.5 5.7 %copy-start.26 = (bf16[1,192,4096]{2,1,0:T(8,128)(2,1)S(1)}, bf16[1,192,4096]{2,1,0:T(8,128)(2,1)}, u32[]{:S(2)}) copy-start(bf16[1,192,4096]{2,1,0:T(8,128)(2,1)} %param.11) | copy-start | bytes 4718596
  7.0 28.3 %collective-permute-start.6 = (bf16[128,4096]{1,0:T(8,128)(2,1)}, bf16[128,4096]{1,0:T(8,128)(2,1)}, u32[]{:S(2)}, u32[]{:S(2)}) collective-permute-start(bf16[128,4096]{1,0:T(8,128)(2,1)} %get-tuple-element.70), channel_id=1, source_target_pairs={{0,8},{4,12},{8,0},{12,4},{16,24},{20,28},{24,16},{28,20},{1,9},{5... | collective-permute-start | bytes 3145736 | tf_op jit(solution)/shard_map/ppermute | solution.py:22
  9.6 25.6 %collective-permute-start.7 = (bf16[128,4096]{1,0:T(8,128)(2,1)}, bf16[128,4096]{1,0:T(8,128)(2,1)}, u32[]{:S(2)}, u32[]{:S(2)}) collective-permute-start(bf16[128,4096]{1,0:T(8,128)(2,1)} %get-tuple-element.71), channel_id=1, source_target_pairs={{0,16},{4,20},{8,24},{12,28},{16,0},{20,4},{24,8},{28,12},{1,17},{... | collective-permute-start | bytes 3145736 | tf_op jit(solution)/shard_map/ppermute | solution.py:22
  13.1 5.3 %copy-start.5 = (bf16[128,4096]{1,0:T(8,128)(2,1)}, bf16[128,4096]{1,0:T(8,128)(2,1)S(1)}, u32[]{:S(2)}) copy-start(bf16[128,4096]{1,0:T(8,128)(2,1)S(1)} %collective-permute-done.1.refs_2_) | copy-start | bytes 3145732
  18.4 16.9 %collective-permute-start.10 = (bf16[2,128,1024]{2,1,0:T(8,128)(2,1)S(1)}, bf16[2,128,1024]{2,1,0:T(8,128)(2,1)S(1)}, u32[]{:S(2)}, u32[]{:S(2)}) collective-permute-start(bf16[2,128,1024]{2,1,0:T(8,128)(2,1)S(1)} %get-tuple-element.73), channel_id=1, source_target_pairs={{0,4},{4,0},{8,12},{12,8},{16,20},{20,16},{24,28},{28,24},{1,5},{5... | collective-permute-start | bytes 1572872 | tf_op jit(solution)/shard_map/ppermute | solution.py:22
  18.5 15.3 %collective-permute-start.8 = (f32[16,128]{1,0:T(8,128)S(1)}, f32[16,128]{1,0:T(8,128)S(1)}, u32[]{:S(2)}, u32[]{:S(2)}) collective-permute-start(f32[16,128]{1,0:T(8,128)S(1)} %pad_maximum_fusion.3.one_ref.two_ref), channel_id=1, source_target_pairs={{0,8},{4,12},{8,0},{12,4},{16,24},{20,28},{24,16},{28,20},{1,9},{5... | collective-permute-start | bytes 24584 | tf_op jit(solution)/shard_map/ppermute | solution.py:22
  19.1 16.2 %collective-permute-start.9 = (f32[16,128]{1,0:T(8,128)S(1)}, f32[16,128]{1,0:T(8,128)S(1)}, u32[]{:S(2)}, u32[]{:S(2)}) collective-permute-start(f32[16,128]{1,0:T(8,128)S(1)} %pad_maximum_fusion.3.one_ref.two_ref), channel_id=1, source_target_pairs={{0,16},{4,20},{8,24},{12,28},{16,0},{20,4},{24,8},{28,12},{1,17},{... | collective-permute-start | bytes 24584 | tf_op jit(solution)/shard_map/ppermute | solution.py:22
  35.3 4.5 %collective-permute-start.12 = (bf16[128,4096]{1,0:T(8,128)(2,1)}, bf16[128,4096]{1,0:T(8,128)(2,1)S(1)}, u32[]{:S(2)}, u32[]{:S(2)}) collective-permute-start(bf16[128,4096]{1,0:T(8,128)(2,1)} %collective-permute-done.6.refs_0_.refs_4_), channel_id=1, source_target_pairs={{0,4},{4,0},{8,12},{12,8},{16,20},{20,16},{24,28},{28,24},{1,5},{5... | collective-permute-start | bytes 3145736 | tf_op jit(solution)/shard_map/ppermute | solution.py:22
  35.3 4.4 %collective-permute-start.13 = (bf16[128,4096]{1,0:T(8,128)(2,1)}, bf16[128,4096]{1,0:T(8,128)(2,1)S(1)}, u32[]{:S(2)}, u32[]{:S(2)}) collective-permute-start(bf16[128,4096]{1,0:T(8,128)(2,1)} %collective-permute-done.7.refs_1_.refs_5_), channel_id=1, source_target_pairs={{0,4},{4,0},{8,12},{12,8},{16,20},{20,16},{24,28},{28,24},{1,5},{5... | collective-permute-start | bytes 3145736 | tf_op jit(solution)/shard_map/ppermute | solution.py:22
  35.8 25.4 %collective-permute-start.4 = (bf16[128,4096]{1,0:T(8,128)(2,1)}, bf16[128,4096]{1,0:T(8,128)(2,1)S(1)}, u32[]{:S(2)}, u32[]{:S(2)}) collective-permute-start(bf16[128,4096]{1,0:T(8,128)(2,1)} %get-tuple-element.70), channel_id=1, source_target_pairs={{0,16},{4,20},{8,24},{12,28},{16,0},{20,4},{24,8},{28,12},{1,17},{... | collective-permute-start | bytes 3145736 | tf_op jit(solution)/shard_map/ppermute | solution.py:22
  37.4 25.1 %collective-permute-start.5 = (bf16[128,4096]{1,0:T(8,128)(2,1)}, bf16[128,4096]{1,0:T(8,128)(2,1)S(1)}, u32[]{:S(2)}, u32[]{:S(2)}) collective-permute-start(bf16[128,4096]{1,0:T(8,128)(2,1)} %get-tuple-element.71), channel_id=1, source_target_pairs={{0,8},{4,12},{8,0},{12,4},{16,24},{20,28},{24,16},{28,20},{1,9},{5... | collective-permute-start | bytes 3145736 | tf_op jit(solution)/shard_map/ppermute | solution.py:22
  38.1 24.3 %collective-permute-start.14 = (bf16[2,128,1024]{2,1,0:T(8,128)(2,1)S(1)}, bf16[2,128,1024]{2,1,0:T(8,128)(2,1)S(1)}, u32[]{:S(2)}, u32[]{:S(2)}) collective-permute-start(bf16[2,128,1024]{2,1,0:T(8,128)(2,1)S(1)} %add.85), channel_id=1, source_target_pairs={{0,1},{1,0},{2,3},{3,2},{4,5},{5,4},{6,7},{7,6},{8,9},{9,8},{10,11... | collective-permute-start | bytes 1572872 | tf_op jit(solution)/shard_map/ppermute | solution.py:22
  39.7 5.8 %copy-start.6 = (bf16[128,4096]{1,0:T(8,128)(2,1)}, bf16[128,4096]{1,0:T(8,128)(2,1)S(1)}, u32[]{:S(2)}) copy-start(bf16[128,4096]{1,0:T(8,128)(2,1)S(1)} %collective-permute-done.12.refs_2_.refs_6_) | copy-start | bytes 3145732
  39.7 5.8 %copy-start.7 = (bf16[128,4096]{1,0:T(8,128)(2,1)}, bf16[128,4096]{1,0:T(8,128)(2,1)S(1)}, u32[]{:S(2)}) copy-start(bf16[128,4096]{1,0:T(8,128)(2,1)S(1)} %collective-permute-done.13.refs_3_.refs_7_) | copy-start | bytes 3145732
  45.6 45.8 %copy-start.16 = (bf16[576,256]{1,0:T(8,128)(2,1)}, bf16[576,256]{1,0:T(8,128)(2,1)S(1)}, u32[]{:S(2)}) copy-start(bf16[576,256]{1,0:T(8,128)(2,1)S(1)} %get-tuple-element.104.refs_17_) | copy-start | bytes 884740
  45.6 16.8 %collective-permute-start.15 = (bf16[2,128,1024]{2,1,0:T(8,128)(2,1)S(1)}, bf16[2,128,1024]{2,1,0:T(8,128)(2,1)S(1)}, u32[]{:S(2)}, u32[]{:S(2)}) collective-permute-start(bf16[2,128,1024]{2,1,0:T(8,128)(2,1)S(1)} %get-tuple-element.81), channel_id=1, source_target_pairs={{0,4},{4,0},{8,12},{12,8},{16,20},{20,16},{24,28},{28,24},{1,5},{5... | collective-permute-start | bytes 1572872 | tf_op jit(solution)/shard_map/ppermute | solution.py:22
  45.7 16.8 %collective-permute-start.11 = (f32[16,128]{1,0:T(8,128)S(1)}, f32[16,128]{1,0:T(8,128)S(1)}, u32[]{:S(2)}, u32[]{:S(2)}) collective-permute-start(f32[16,128]{1,0:T(8,128)S(1)} %collective-permute-done.8.one_ref.two_ref), channel_id=1, source_target_pairs={{0,16},{4,20},{8,24},{12,28},{16,0},{20,4},{24,8},{28,12},{1,17},{... | collective-permute-start | bytes 24584 | tf_op jit(solution)/shard_map/ppermute | solution.py:22
  61.3 9.5 %copy-start.8 = (bf16[128,4096]{1,0:T(8,128)(2,1)}, bf16[128,4096]{1,0:T(8,128)(2,1)S(1)}, u32[]{:S(2)}) copy-start(bf16[128,4096]{1,0:T(8,128)(2,1)S(1)} %collective-permute-done.4.refs_0_.refs_8_) | copy-start | bytes 3145732
  62.4 8.4 %copy-start.9 = (bf16[128,4096]{1,0:T(8,128)(2,1)}, bf16[128,4096]{1,0:T(8,128)(2,1)S(1)}, u32[]{:S(2)}) copy-start(bf16[128,4096]{1,0:T(8,128)(2,1)S(1)} %collective-permute-done.5.refs_1_.refs_9_) | copy-start | bytes 3145732
  62.5 2.7 %collective-permute-start.18 = (bf16[128,4096]{1,0:T(8,128)(2,1)S(1)}, bf16[128,4096]{1,0:T(8,128)(2,1)S(1)}, u32[]{:S(2)}, u32[]{:S(2)}) collective-permute-start(bf16[128,4096]{1,0:T(8,128)(2,1)S(1)} %collective-permute-done.4.refs_0_.refs_8_), channel_id=1, source_target_pairs={{0,4},{4,0},{8,12},{12,8},{16,20},{20,16},{24,28},{28,24},{1,5},{5... | collective-permute-start | bytes 3145736 | tf_op jit(solution)/shard_map/ppermute | solution.py:22
  62.5 4.2 %collective-permute-start.19 = (bf16[128,4096]{1,0:T(8,128)(2,1)S(1)}, bf16[128,4096]{1,0:T(8,128)(2,1)S(1)}, u32[]{:S(2)}, u32[]{:S(2)}) collective-permute-start(bf16[128,4096]{1,0:T(8,128)(2,1)S(1)} %collective-permute-done.5.refs_1_.refs_9_), channel_id=1, source_target_pairs={{0,4},{4,0},{8,12},{12,8},{16,20},{20,16},{24,28},{28,24},{1,5},{5... | collective-permute-start | bytes 3145736 | tf_op jit(solution)/shard_map/ppermute | solution.py:22
  63.0 7.9 %collective-permute-start.3 = (bf16[2,128,1024]{2,1,0:T(8,128)(2,1)S(1)}, bf16[2,128,1024]{2,1,0:T(8,128)(2,1)S(1)}, u32[]{:S(2)}, u32[]{:S(2)}) collective-permute-start(bf16[2,128,1024]{2,1,0:T(8,128)(2,1)S(1)} %get-tuple-element.69), channel_id=1, source_target_pairs={{0,4},{4,0},{8,12},{12,8},{16,20},{20,16},{24,28},{28,24},{1,5},{5... | collective-permute-start | bytes 1572872 | tf_op jit(solution)/shard_map/ppermute | solution.py:22
  63.1 25.7 %collective-permute-start.16 = (bf16[128,4096]{1,0:T(8,128)(2,1)}, bf16[128,4096]{1,0:T(8,128)(2,1)S(1)}, u32[]{:S(2)}, u32[]{:S(2)}) collective-permute-start(bf16[128,4096]{1,0:T(8,128)(2,1)} %collective-permute-done.6.refs_0_.refs_4_), channel_id=1, source_target_pairs={{0,16},{4,20},{8,24},{12,28},{16,0},{20,4},{24,8},{28,12},{1,17},{... | collective-permute-start | bytes 3145736 | tf_op jit(solution)/shard_map/ppermute | solution.py:22
  63.6 25.4 %collective-permute-start.17 = (bf16[128,4096]{1,0:T(8,128)(2,1)}, bf16[128,4096]{1,0:T(8,128)(2,1)S(1)}, u32[]{:S(2)}, u32[]{:S(2)}) collective-permute-start(bf16[128,4096]{1,0:T(8,128)(2,1)} %collective-permute-done.7.refs_1_.refs_5_), channel_id=1, source_target_pairs={{0,8},{4,12},{8,0},{12,4},{16,24},{20,28},{24,16},{28,20},{1,9},{5... | collective-permute-start | bytes 3145736 | tf_op jit(solution)/shard_map/ppermute | solution.py:22
  65.2 5.6 %copy-start.10 = (bf16[128,4096]{1,0:T(8,128)(2,1)}, bf16[128,4096]{1,0:T(8,128)(2,1)S(1)}, u32[]{:S(2)}) copy-start(bf16[128,4096]{1,0:T(8,128)(2,1)S(1)} %collective-permute-done.18.refs_2_.refs_10_) | copy-start | bytes 3145732
  65.2 23.9 %collective-permute-start.21 = (bf16[2,128,1024]{2,1,0:T(8,128)(2,1)S(1)}, bf16[2,128,1024]{2,1,0:T(8,128)(2,1)S(1)}, u32[]{:S(2)}, u32[]{:S(2)}) collective-permute-start(bf16[2,128,1024]{2,1,0:T(8,128)(2,1)S(1)} %add.87), channel_id=1, source_target_pairs={{0,1},{1,0},{2,3},{3,2},{4,5},{5,4},{6,7},{7,6},{8,9},{9,8},{10,11... | collective-permute-start | bytes 1572872 | tf_op jit(solution)/shard_map/ppermute | solution.py:22
  70.8 18.2 %collective-permute-start.22 = (bf16[2,128,1024]{2,1,0:T(8,128)(2,1)S(1)}, bf16[2,128,1024]{2,1,0:T(8,128)(2,1)S(1)}, u32[]{:S(2)}, u32[]{:S(2)}) collective-permute-start(bf16[2,128,1024]{2,1,0:T(8,128)(2,1)S(1)} %get-tuple-element.88), channel_id=1, source_target_pairs={{0,4},{4,0},{8,12},{12,8},{16,20},{20,16},{24,28},{28,24},{1,5},{5... | collective-permute-start | bytes 1572872 | tf_op jit(solution)/shard_map/ppermute | solution.py:22
  71.0 23.2 %copy-start.22 = (bf16[2,128,1024]{2,1,0:T(8,128)(2,1)}, bf16[2,128,1024]{2,1,0:T(8,128)(2,1)S(1)}, u32[]{:S(2)}) copy-start(bf16[2,128,1024]{2,1,0:T(8,128)(2,1)S(1)} %add_add_fusion.3) | copy-start | bytes 1572868
  71.1 18.0 %collective-permute-start.20 = (bf16[128,1024]{1,0:T(8,128)(2,1)S(1)}, bf16[128,1024]{1,0:T(8,128)(2,1)S(1)}, u32[]{:S(2)}, u32[]{:S(2)}) collective-permute-start(bf16[128,1024]{1,0:T(8,128)(2,1)S(1)} %slice_bitcast_fusion.6), channel_id=1, source_target_pairs={{0,2},{1,3},{2,0},{3,1},{4,6},{5,7},{6,4},{7,5},{8,10},{9,11},{10,... | collective-permute-start | bytes 786440 | tf_op jit(solution)/shard_map/ppermute | solution.py:22
  88.8 7.1 %copy-start.12 = (bf16[128,4096]{1,0:T(8,128)(2,1)}, bf16[128,4096]{1,0:T(8,128)(2,1)S(1)}, u32[]{:S(2)}) copy-start(bf16[128,4096]{1,0:T(8,128)(2,1)S(1)} %collective-permute-done.16.refs_0_.refs_12_) | copy-start | bytes 3145732
  89.1 6.9 %copy-start.13 = (bf16[128,4096]{1,0:T(8,128)(2,1)}, bf16[128,4096]{1,0:T(8,128)(2,1)S(1)}, u32[]{:S(2)}) copy-start(bf16[128,4096]{1,0:T(8,128)(2,1)S(1)} %collective-permute-done.17.refs_1_.refs_13_) | copy-start | bytes 3145732
  89.1 5.2 %collective-permute-start.24 = (bf16[128,4096]{1,0:T(8,128)(2,1)S(1)}, bf16[128,4096]{1,0:T(8,128)(2,1)S(1)}, u32[]{:S(2)}, u32[]{:S(2)}) collective-permute-start(bf16[128,4096]{1,0:T(8,128)(2,1)S(1)} %collective-permute-done.16.refs_0_.refs_12_), channel_id=1, source_target_pairs={{0,4},{4,0},{8,12},{12,8},{16,20},{20,16},{24,28},{28,24},{1,5},{5... | collective-permute-start | bytes 3145736 | tf_op jit(solution)/shard_map/ppermute | solution.py:22
  89.2 6.8 %collective-permute-start.25 = (bf16[128,4096]{1,0:T(8,128)(2,1)S(1)}, bf16[128,4096]{1,0:T(8,128)(2,1)S(1)}, u32[]{:S(2)}, u32[]{:S(2)}) collective-permute-start(bf16[128,4096]{1,0:T(8,128)(2,1)S(1)} %collective-permute-done.17.refs_1_.refs_13_), channel_id=1, source_target_pairs={{0,4},{4,0},{8,12},{12,8},{16,20},{20,16},{24,28},{28,24},{1,5},{5... | collective-permute-start | bytes 3145736 | tf_op jit(solution)/shard_map/ppermute | solution.py:22
  89.7 4.4 %collective-permute-start.23 = (bf16[2,128,1024]{2,1,0:T(8,128)(2,1)S(1)}, bf16[2,128,1024]{2,1,0:T(8,128)(2,1)S(1)}, u32[]{:S(2)}, u32[]{:S(2)}) collective-permute-start(bf16[2,128,1024]{2,1,0:T(8,128)(2,1)S(1)} %get-tuple-element.91), channel_id=1, source_target_pairs={{0,4},{4,0},{8,12},{12,8},{16,20},{20,16},{24,28},{28,24},{1,5},{5... | collective-permute-start | bytes 1572872 | tf_op jit(solution)/shard_map/ppermute | solution.py:22
  89.9 10.6 %collective-permute-start.29 = (bf16[576,256]{1,0:T(8,128)(2,1)S(1)}, bf16[576,256]{1,0:T(8,128)(2,1)S(1)}, u32[]{:S(2)}, u32[]{:S(2)}) collective-permute-start(bf16[576,256]{1,0:T(8,128)(2,1)S(1)} %get-tuple-element.103.refs_16_), channel_id=1, source_target_pairs={{0,16},{4,20},{8,24},{12,28},{16,0},{20,4},{24,8},{28,12},{1,17},{... | collective-permute-start | bytes 884744 | tf_op jit(solution)/shard_map/ppermute | solution.py:22
  91.4 14.1 %collective-permute-start.30 = (bf16[576,256]{1,0:T(8,128)(2,1)S(1)}, bf16[576,256]{1,0:T(8,128)(2,1)S(1)}, u32[]{:S(2)}, u32[]{:S(2)}) collective-permute-start(bf16[576,256]{1,0:T(8,128)(2,1)S(1)} %get-tuple-element.104.refs_17_), channel_id=1, source_target_pairs={{0,16},{4,20},{8,24},{12,28},{16,0},{20,4},{24,8},{28,12},{1,17},{... | collective-permute-start | bytes 884744 | tf_op jit(solution)/shard_map/ppermute | solution.py:22
  94.1 19.7 %collective-permute-start.34 = (bf16[2,128,1024]{2,1,0:T(8,128)(2,1)S(1)}, bf16[2,128,1024]{2,1,0:T(8,128)(2,1)S(1)}, u32[]{:S(2)}, u32[]{:S(2)}) collective-permute-start(bf16[2,128,1024]{2,1,0:T(8,128)(2,1)S(1)} %get-tuple-element.109), channel_id=1, source_target_pairs={{0,4},{4,0},{8,12},{12,8},{16,20},{20,16},{24,28},{28,24},{1,5},{5... | collective-permute-start | bytes 1572872 | tf_op jit(solution)/shard_map/ppermute | solution.py:22
  94.3 7.0 %copy-start.24 = (bf16[2,128,1024]{2,1,0:T(8,128)(2,1)}, bf16[2,128,1024]{2,1,0:T(8,128)(2,1)S(1)}, u32[]{:S(2)}) copy-start(bf16[2,128,1024]{2,1,0:T(8,128)(2,1)S(1)} %add_add_fusion.2) | copy-start | bytes 1572868
  94.3 5.9 %copy-start.14 = (bf16[128,4096]{1,0:T(8,128)(2,1)}, bf16[128,4096]{1,0:T(8,128)(2,1)S(1)}, u32[]{:S(2)}) copy-start(bf16[128,4096]{1,0:T(8,128)(2,1)S(1)} %collective-permute-done.24.refs_2_.refs_14_) | copy-start | bytes 3145732
  94.3 14.3 %collective-permute-start.28 = (bf16[2,128,1024]{2,1,0:T(8,128)(2,1)S(1)}, bf16[2,128,1024]{2,1,0:T(8,128)(2,1)S(1)}, u32[]{:S(2)}, u32[]{:S(2)}) collective-permute-start(bf16[2,128,1024]{2,1,0:T(8,128)(2,1)S(1)} %add.92), channel_id=1, source_target_pairs={{0,1},{1,0},{2,3},{3,2},{4,5},{5,4},{6,7},{7,6},{8,9},{9,8},{10,11... | collective-permute-start | bytes 1572872 | tf_op jit(solution)/shard_map/ppermute | solution.py:22
  100.2 14.3 %copy-start.20 = (bf16[2,128,1024]{2,1,0:T(8,128)(2,1)}, bf16[2,128,1024]{2,1,0:T(8,128)(2,1)S(1)}, u32[]{:S(2)}) copy-start(bf16[2,128,1024]{2,1,0:T(8,128)(2,1)S(1)} %get-tuple-element.116) | copy-start | bytes 1572868
  100.3 10.4 %collective-permute-start.26 = (bf16[2,128,1024]{2,1,0:T(8,128)(2,1)S(1)}, bf16[2,128,1024]{2,1,0:T(8,128)(2,1)S(1)}, u32[]{:S(2)}, u32[]{:S(2)}) collective-permute-start(bf16[2,128,1024]{2,1,0:T(8,128)(2,1)S(1)} %get-tuple-element.100), channel_id=1, source_target_pairs={{0,4},{4,0},{8,12},{12,8},{16,20},{20,16},{24,28},{28,24},{1,5},{5... | collective-permute-start | bytes 1572872 | tf_op jit(solution)/shard_map/ppermute | solution.py:22
  100.6 9.7 %collective-permute-start.27 = (f32[8,128]{1,0:T(8,128)S(1)}, f32[8,128]{1,0:T(8,128)S(1)}, u32[]{:S(2)}, u32[]{:S(2)}) collective-permute-start(f32[8,128]{1,0:T(8,128)S(1)} %maximum_maximum_fusion), channel_id=1, source_target_pairs={{0,1},{1,0},{2,3},{3,2},{4,5},{5,4},{6,7},{7,6},{8,9},{9,8},{10,11... | collective-permute-start | bytes 12296 | tf_op jit(solution)/shard_map/ppermute | solution.py:22
  105.5 10.1 %copy-start.18 = (bf16[576,256]{1,0:T(8,128)(2,1)}, bf16[576,256]{1,0:T(8,128)(2,1)S(1)}, u32[]{:S(2)}) copy-start(bf16[576,256]{1,0:T(8,128)(2,1)S(1)} %collective-permute-done.30.refs_21_) | copy-start | bytes 884740
  105.5 26.1 %collective-permute-start.33 = (bf16[128,1024]{1,0:T(8,128)(2,1)S(1)}, bf16[128,1024]{1,0:T(8,128)(2,1)}, u32[]{:S(2)}, u32[]{:S(2)}) collective-permute-start(bf16[128,1024]{1,0:T(8,128)(2,1)S(1)} %slice_bitcast_fusion.4), channel_id=1, source_target_pairs={{0,2},{1,3},{2,0},{3,1},{4,6},{5,7},{6,4},{7,5},{8,10},{9,11},{10,... | collective-permute-start | bytes 786440 | tf_op jit(solution)/shard_map/ppermute | solution.py:22
  108.6 27.6 %collective-permute-start.36 = (bf16[576,256]{1,0:T(8,128)(2,1)}, bf16[576,256]{1,0:T(8,128)(2,1)S(1)}, u32[]{:S(2)}, u32[]{:S(2)}) collective-permute-start(bf16[576,256]{1,0:T(8,128)(2,1)} %get-tuple-element.111.refs_18_), channel_id=1, source_target_pairs={{0,16},{4,20},{8,24},{12,28},{16,0},{20,4},{24,8},{28,12},{1,17},{... | collective-permute-start | bytes 884744 | tf_op jit(solution)/shard_map/ppermute | solution.py:22
  110.3 25.9 %collective-permute-start.37 = (bf16[576,256]{1,0:T(8,128)(2,1)}, bf16[576,256]{1,0:T(8,128)(2,1)S(1)}, u32[]{:S(2)}, u32[]{:S(2)}) collective-permute-start(bf16[576,256]{1,0:T(8,128)(2,1)} %get-tuple-element.112.refs_19_), channel_id=1, source_target_pairs={{0,16},{4,20},{8,24},{12,28},{16,0},{20,4},{24,8},{28,12},{1,17},{... | collective-permute-start | bytes 884744 | tf_op jit(solution)/shard_map/ppermute | solution.py:22
  110.7 16.4 %collective-permute-start.31 = (f32[8,128]{1,0:T(8,128)S(1)}, f32[8,128]{1,0:T(8,128)S(1)}, u32[]{:S(2)}, u32[]{:S(2)}) collective-permute-start(f32[8,128]{1,0:T(8,128)S(1)} %add.93), channel_id=1, source_target_pairs={{0,2},{1,3},{2,0},{3,1},{4,6},{5,7},{6,4},{7,5},{8,10},{9,11},{10,... | collective-permute-start | bytes 12296 | tf_op jit(solution)/shard_map/ppermute | solution.py:22
  113.9 28.7 %copy-start.25 = (bf16[2,128,1024]{2,1,0:T(8,128)(2,1)S(1)}, bf16[2,128,1024]{2,1,0:T(8,128)(2,1)}, u32[]{:S(2)}) copy-start(bf16[2,128,1024]{2,1,0:T(8,128)(2,1)} %copy-done.24) | copy-start | bytes 1572868
  114.6 21.6 %collective-permute-start.35 = (bf16[128,1024]{1,0:T(8,128)(2,1)}, bf16[128,1024]{1,0:T(8,128)(2,1)}, u32[]{:S(2)}, u32[]{:S(2)}) collective-permute-start(bf16[128,1024]{1,0:T(8,128)(2,1)} %slice_bitcast_fusion.3), channel_id=1, source_target_pairs={{0,2},{1,3},{2,0},{3,1},{4,6},{5,7},{6,4},{7,5},{8,10},{9,11},{10,... | collective-permute-start | bytes 786440 | tf_op jit(solution)/shard_map/ppermute | solution.py:22
  114.6 17.0 %copy-start.21 = (bf16[2,128,1024]{2,1,0:T(8,128)(2,1)S(1)}, bf16[2,128,1024]{2,1,0:T(8,128)(2,1)}, u32[]{:S(2)}) copy-start(bf16[2,128,1024]{2,1,0:T(8,128)(2,1)} %copy-done.20) | copy-start | bytes 1572868
  127.1 15.5 %collective-permute-start.32 = (bf16[2,128,1024]{2,1,0:T(8,128)(2,1)}, bf16[2,128,1024]{2,1,0:T(8,128)(2,1)}, u32[]{:S(2)}, u32[]{:S(2)}) collective-permute-start(bf16[2,128,1024]{2,1,0:T(8,128)(2,1)} %add.96), channel_id=1, source_target_pairs={{0,1},{1,0},{2,3},{3,2},{4,5},{5,4},{6,7},{7,6},{8,9},{9,8},{10,11... | collective-permute-start | bytes 1572872 | tf_op jit(solution)/shard_map/ppermute | solution.py:22
  128.3 7.9 %all-to-all-start = ((bf16[8,1,128]{2,1,0:T(2,128)(2,1)}), bf16[8,1,128]{2,1,0:T(2,128)(2,1)S(1)}, u32[]{:S(2)}, u32[]{:S(2)}) async-start(bf16[8,1,128]{2,1,0:T(2,128)(2,1)} %copy.24), calls=%async_computation | async-start | bytes 8192 | tf_op jit(solution)/shard_map/all_to_all | solution.py:309
  131.7 12.2 %collective-permute-start.40 = (bf16[2,128,1024]{2,1,0:T(8,128)(2,1)S(1)}, bf16[2,128,1024]{2,1,0:T(8,128)(2,1)}, u32[]{:S(2)}, u32[]{:S(2)}) collective-permute-start(bf16[2,128,1024]{2,1,0:T(8,128)(2,1)S(1)} %copy-done.21), channel_id=1, source_target_pairs={{0,4},{4,0},{8,12},{12,8},{16,20},{20,16},{24,28},{28,24},{1,5},{5... | collective-permute-start | bytes 1572872 | tf_op jit(solution)/shard_map/ppermute | solution.py:22
  145.2 15.5 %collective-permute-start.41 = (bf16[128,1024]{1,0:T(8,128)(2,1)S(1)}, bf16[128,1024]{1,0:T(8,128)(2,1)S(1)}, u32[]{:S(2)}, u32[]{:S(2)}) collective-permute-start(bf16[128,1024]{1,0:T(8,128)(2,1)S(1)} %slice_bitcast_fusion), channel_id=1, source_target_pairs={{0,2},{1,3},{2,0},{3,1},{4,6},{5,7},{6,4},{7,5},{8,10},{9,11},{10,... | collective-permute-start | bytes 786440 | tf_op jit(solution)/shard_map/ppermute | solution.py:22
  146.8 15.9 %collective-permute-start.38 = (bf16[128,1024]{1,0:T(8,128)(2,1)S(1)}, bf16[128,1024]{1,0:T(8,128)(2,1)S(1)}, u32[]{:S(2)}, u32[]{:S(2)}) collective-permute-start(bf16[128,1024]{1,0:T(8,128)(2,1)S(1)} %pad_maximum_fusion.1), channel_id=1, source_target_pairs={{0,8},{4,12},{8,0},{12,4},{16,24},{20,28},{24,16},{28,20},{1,9},{5... | collective-permute-start | bytes 786440 | tf_op jit(solution)/shard_map/ppermute | solution.py:22
  147.4 14.7 %copy-start.29 = (s32[128,4]{0,1:T(4,128)S(1)}, s32[128,4]{0,1:T(4,128)}, u32[]{:S(2)}) copy-start(s32[128,4]{0,1:T(4,128)} %param.13) | copy-start | bytes 6148
  147.4 21.7 %copy-start.23 = (bf16[2,128,1024]{2,1,0:T(8,128)(2,1)S(1)}, bf16[2,128,1024]{2,1,0:T(8,128)(2,1)}, u32[]{:S(2)}) copy-start(bf16[2,128,1024]{2,1,0:T(8,128)(2,1)} %copy-done.22) | copy-start | bytes 1572868
  147.5 21.7 %copy-start.28 = (bf16[128,1024]{1,0:T(8,128)(2,1)S(1)}, bf16[128,1024]{1,0:T(8,128)(2,1)}, u32[]{:S(2)}) copy-start(bf16[128,1024]{1,0:T(8,128)(2,1)} %copy-done.27) | copy-start | bytes 786436
  147.5 15.3 %collective-permute-start.39 = (bf16[128,1024]{1,0:T(8,128)(2,1)S(1)}, bf16[128,1024]{1,0:T(8,128)(2,1)S(1)}, u32[]{:S(2)}, u32[]{:S(2)}) collective-permute-start(bf16[128,1024]{1,0:T(8,128)(2,1)S(1)} %pad_maximum_fusion.2), channel_id=1, source_target_pairs={{0,16},{4,20},{8,24},{12,28},{16,0},{20,4},{24,8},{28,12},{1,17},{... | collective-permute-start | bytes 786440 | tf_op jit(solution)/shard_map/ppermute | solution.py:22
  160.7 8.4 %collective-permute-start.42 = (bf16[128,1024]{1,0:T(8,128)(2,1)S(1)}, bf16[128,1024]{1,0:T(8,128)(2,1)S(1)}, u32[]{:S(2)}, u32[]{:S(2)}) collective-permute-start(bf16[128,1024]{1,0:T(8,128)(2,1)S(1)} %fusion), channel_id=1, source_target_pairs={{0,24},{4,28},{8,16},{12,20},{16,8},{20,12},{24,0},{28,4},{1,25},{... | collective-permute-start | bytes 786440 | tf_op jit(solution)/shard_map/ppermute | solution.py:22
  (10 other events, 26.3 us)

commit v9 on v8

--- a/solution.py
+++ b/solution.py
@@ -65,7 +65,7 @@
         compiler_params=pltpu.CompilerParams(vmem_limit_bytes=4 * 1024 * 1024),
         cost_estimate=pl.CostEstimate(flops=1, bytes_accessed=1, transcendentals=0),
         name="pack",
-    )(tokens, cotangent)
+    )(*[pltpu.with_memory_space_constraint(value, pltpu.HBM) for value in (tokens, cotangent)])
 
 
 def activations_kernel(x_places, dy_places, count, parts, where_ref, one_ref, two_ref, *refs):
@@ -304,14 +304,14 @@
     far_d, score_in, near_in_c, other_a, other_b = barrier((far_d, score_in, near_in_c, other_a, other_b))
     near_d, near_in_d = to_neighbour(far_d, share_d)
     score_rows = score_rows + score_in
+    total_c, far_in_c = to_far(near_c, near_in_c)
+    score_rows, near_in_d, far_in_b, far_in_c, other_c, other_d, own_flag = barrier(
+        (score_rows, near_in_d, far_in_b, far_in_c, other_c, other_d, own_flag)
+    )
+    total_d, far_in_d = to_far(near_d, near_in_d)
     score_rows = score_rows + swap(score_rows, "dp", 2)
     score_rows = jnp.take(score_rows.astype(bf16), jnp.arange(expert_count, dtype=jnp.int32) ^ me, axis=0)
     score_rows = lax.all_to_all(score_rows, "expert", split_axis=0, concat_axis=0, tiled=True)
-    total_c, far_in_c = to_far(near_c, near_in_c)
-    score_rows, near_in_d, far_in_b, far_in_c, other_c, other_d, own_flag = barrier(
-        (score_rows, near_in_d, far_in_b, far_in_c, other_c, other_d, own_flag)
-    )
-    total_d, far_in_d = to_far(near_d, near_in_d)
     own, other = (acts_a, acts_b, acts_c, acts_d), (other_a, other_b, other_c, other_d)
     grads = weight_grads(((0, 0), (2, 4), (4, 2), (6, 6)), own_flag, groups, own, other)
     far_in_d, grads = barrier((far_in_d, grads))

time: 170 us -> 161 us (0.947)
  waiting for transfers between devices: 81.3 us -> 72.7 us
  blocking collectives: 0 us -> 7.01 us
  local copies, waits for them, and re-layouts: 5.3 us -> 1.27 us
  other arithmetic: 10.7 us -> 7.56 us
    all_to_all x0 -> x1, blocking collectives: none -> 7.01 us  [whole_shards(): lax.all_to_all(score_rows, 'expert', split_axis=0, concat_axis=0, tiled=T...]
    ppermute x43, waiting for transfers between devices: 78.6 us -> 72.7 us  [swap(): lax.ppermute(value, axis, [(i, i ^ by) for i in range(lax.axis_size(axis))])]
    ppermute x43, starting transfers between devices: 36.4 us -> 40.1 us  [swap(): lax.ppermute(value, axis, [(i, i ^ by) for i in range(lax.axis_size(axis))])]
    all_to_all x1 -> x0, starting transfers between devices: 3.33 us -> none  [whole_shards(): lax.all_to_all(score_rows, 'expert', split_axis=0, concat_axis=0, tiled=T...]
    unnamed x61 -> x36, local copies, waits for them, and re-layouts: 3.26 us -> 0.51 us
    all_to_all x1 -> x0, waiting for transfers between devices: 2.73 us -> none  [whole_shards(): lax.all_to_all(score_rows, 'expert', split_axis=0, concat_axis=0, tiled=T...]
  transfers between devices with their start and end apart: 44 -> 43, of which waited for: 15 -> 15; matrix products, arithmetic and copies ran while one was open for 6% -> 5% of each run, Pallas kernels for 19% -> 19%
where the time goes in v9:
time: 161 us
  waiting for transfers between devices  72.7 us (45%)
  starting transfers between devices  40.1 us (25%)
  Pallas kernels  31 us (19%)
  other arithmetic  7.56 us (5%)
  blocking collectives  7.01 us (4%)
    ppermute x43, waiting for transfers between devices, swap(): lax.ppermute(value, axis, [(i, i ^ by) for i in range(lax.axis_size(axis))])  72.7 us
    ppermute x43, starting transfers between devices, swap(): lax.ppermute(value, axis, [(i, i ^ by) for i in range(lax.axis_size(axis))])  40.1 us
    pallas_call x4, Pallas kernels, activations(): pl.pallas_call(functools.partial(activations_kernel, x_places, dy_places,...  17.7 us
    pallas_call x1, Pallas kernels, weight_grads(): pl.pallas_call(functools.partial(weight_grads_kernel, sources, x_places,...  10.4 us
    all_to_all x1, blocking collectives, whole_shards(): lax.all_to_all(score_rows, 'expert', split_axis=0, concat_axis=0, tiled=T...  7.01 us
  transfers between devices with their start and end apart: 43, of which 15 were waited for; matrix products, arithmetic and copies ran while one was open for 5% of the time, Pallas kernels for 19%

profile of v9, /device:TPU:0, one launch (start us, length us, event | category | flops | bytes accessed | tf_op | source)
XLA Modules:
  0.0 160.7 jit_solution(13203933138172606988)
XLA Ops:
  0.6 0.5 collective-permute-start.1
  1.2 0.7 convert_element_type.77
  1.9 0.7 select_reduce_fusion.1
  2.6 0.4 collective-permute-start
  3.0 2.9 %pack.1 = (bf16[128,4096]{1,0:T(8,128)(2,1)}, bf16[128,4096]{1,0:T(8,128)(2,1)}) custom-call(bf16[128,4096]{1,0:T(8,128)(2,1)} %refs_0_.3, bf16[128,4096]{1,0:T(8,128)(2,1)} %refs_1_.3), custom_call_target="tpu_custom_call" | custom-call | flops 1 | bytes 1 | tf_op jit(solution)/shard_map/pack/pallas_call | solution.py:59
  5.9 2.6 %collective-permute-start.6 = (bf16[128,4096]{1,0:T(8,128)(2,1)}, bf16[128,4096]{1,0:T(8,128)(2,1)S(1)}, u32[]{:S(2)}, u32[]{:S(2)}) collective-permute-start(bf16[128,4096]{1,0:T(8,128)(2,1)} %get-tuple-element.70), channel_id=1, source_target_pairs={{0,8},{4,12},{8,0},{12,4},{16,24},{20,28},{24,16},{28,20},{1,9},{5... | collective-permute-start | bytes 3145736 | tf_op jit(solution)/shard_map/ppermute | solution.py:22
  8.5 1.5 collective-permute-start.7
  10.1 2.4 %pad_maximum_fusion.refs_4_ = bf16[384,4096]{1,0:T(8,128)(2,1)S(1)} fusion(bf16[192,4096]{1,0:T(8,128)(2,1)} %bitcast.50, bf16[192,4096]{1,0:T(8,128)(2,1)} %bitcast.51), kind=kLoop, calls=%fused_computation.1 | loop fusion | flops 6291456 | bytes 6291456 | tf_op jit(solution)/shard_map/concatenate | solution.py:243
  12.7 0.3 copy-done.2
  13.0 4.0 %activations.4 = (bf16[576,256]{1,0:T(8,128)(2,1)S(1)}, f32[1,256]{1,0:T(1,128)S(1)}, bf16[2,128,1024]{2,1,0:T(8,128)(2,1)S(1)}, bf16[2,128,1024]{2,1,0:T(8,128)...) custom-call(s32[2]{0:T(128)S(1)} %pad_add_fusion.where_ref, ...), custom_call_target="tpu_custom_call" | custom-call | flops 1 | bytes 1 | tf_op jit(solution)/shard_map/activations/pallas_call | solution.py:124
  17.2 0.6 collective-permute-start.8
  17.9 14.8 %collective-permute-done.8.one_ref.two_ref = f32[16,128]{1,0:T(8,128)S(1)} collective-permute-done((f32[16,128]{1,0:T(8,128)S(1)}, f32[16,128]{1,0:T(8,128)S(1)}, u32[]{:S(2)}, u32[]{:S(2)}) %collective-permute-start.8) | collective-permute-done | bytes 8224 | tf_op jit(solution)/shard_map/ppermute | solution.py:22
  32.7 1.5 collective-permute-done.9.two_ref.one_ref
  34.3 0.5 collective-permute-start.13
  34.8 1.5 collective-permute-start.4
  36.3 0.5 collective-permute-start.5
  36.8 0.2 add.85
  37.0 1.6 %collective-permute-start.14 = (bf16[2,128,1024]{2,1,0:T(8,128)(2,1)S(1)}, bf16[2,128,1024]{2,1,0:T(8,128)(2,1)S(1)}, u32[]{:S(2)}, u32[]{:S(2)}) collective-permute-start(bf16[2,128,1024]{2,1,0:T(8,128)(2,1)S(1)} %add.85), channel_id=1, source_target_pairs={{0,1},{1,0},{2,3},{3,2},{4,5},{5,4},{6,7},{7,6},{8,9},{9,8},{10,11... | collective-permute-start | bytes 1572872 | tf_op jit(solution)/shard_map/ppermute | solution.py:22
  38.7 5.5 %activations.5 = (bf16[576,256]{1,0:T(8,128)(2,1)S(1)}, f32[1,256]{1,0:T(1,128)S(1)}, bf16[2,128,1024]{2,1,0:T(8,128)(2,1)S(1)}, bf16[2,128,1024]{2,1,0:T(8,128)...) custom-call(s32[2]{0:T(128)S(1)} %pad_add_fusion.where_ref, ...), custom_call_target="tpu_custom_call" | custom-call | flops 1 | bytes 1 | tf_op jit(solution)/shard_map/activations/pallas_call | solution.py:124
  44.3 1.2 collective-permute-start.11
  45.5 14.7 %collective-permute-done.4.refs_0_.refs_8_ = bf16[128,4096]{1,0:T(8,128)(2,1)S(1)} collective-permute-done((bf16[128,4096]{1,0:T(8,128)(2,1)}, bf16[128,4096]{1,0:T(8,128)(2,1)S(1)}, u32[]{:S(2)}, u32[]{:S(2)}) %collective-permute-start.4) | collective-permute-done | bytes 1048608 | tf_op jit(solution)/shard_map/ppermute | solution.py:22
  60.2 1.1 collective-permute-done.5.refs_1_.refs_9_
  61.5 0.5 collective-permute-start.19
  62.0 0.5 collective-permute-start.16
  62.5 0.4 collective-permute-start.17
  63.0 0.2 add.87
  63.2 0.9 collective-permute-done.18.refs_2_.refs_10_
  64.1 1.6 collective-permute-start.21
  65.7 4.0 %activations.6 = (bf16[576,256]{1,0:T(8,128)(2,1)S(1)}, f32[1,256]{1,0:T(1,128)S(1)}, bf16[2,128,1024]{2,1,0:T(8,128)(2,1)S(1)}, bf16[2,128,1024]{2,1,0:T(8,128)...) custom-call(s32[2]{0:T(128)S(1)} %pad_add_fusion.where_ref, ...), custom_call_target="tpu_custom_call" | custom-call | flops 1 | bytes 1 | tf_op jit(solution)/shard_map/activations/pallas_call | solution.py:124
  70.0 2.7 %collective-permute-start.20 = (bf16[128,1024]{1,0:T(8,128)(2,1)S(1)}, bf16[128,1024]{1,0:T(8,128)(2,1)S(1)}, u32[]{:S(2)}, u32[]{:S(2)}) collective-permute-start(bf16[128,1024]{1,0:T(8,128)(2,1)S(1)} %slice_bitcast_fusion.6), channel_id=1, source_target_pairs={{0,2},{1,3},{2,0},{3,1},{4,6},{5,7},{6,4},{7,5},{8,10},{9,11},{10,... | collective-permute-start | bytes 786440 | tf_op jit(solution)/shard_map/ppermute | solution.py:22
  72.6 14.9 %collective-permute-done.16.refs_0_.refs_12_ = bf16[128,4096]{1,0:T(8,128)(2,1)S(1)} collective-permute-done((bf16[128,4096]{1,0:T(8,128)(2,1)S(1)}, bf16[128,4096]{1,0:T(8,128)(2,1)S(1)}, u32[]{:S(2)}, u32[]{:S(2)}) %collective-permute-start.16) | collective-permute-done | bytes 1048608 | tf_op jit(solution)/shard_map/ppermute | solution.py:22
  87.5 0.4 collective-permute-done.17.refs_1_.refs_13_
  88.1 0.5 collective-permute-start.25
  88.7 1.5 collective-permute-start.29
  90.2 0.5 collective-permute-start.30
  90.7 0.2 add.91
  90.9 2.1 %collective-permute-done.23 = bf16[2,128,1024]{2,1,0:T(8,128)(2,1)S(1)} collective-permute-done((bf16[2,128,1024]{2,1,0:T(8,128)(2,1)S(1)}, bf16[2,128,1024]{2,1,0:T(8,128)(2,1)S(1)}, u32[]{:S(2)}, u32[]{:S(2)}) %collective-permute-start.23) | collective-permute-done | bytes 524320 | tf_op jit(solution)/shard_map/ppermute | solution.py:22
  93.2 1.7 %collective-permute-start.28 = (bf16[2,128,1024]{2,1,0:T(8,128)(2,1)S(1)}, bf16[2,128,1024]{2,1,0:T(8,128)(2,1)S(1)}, u32[]{:S(2)}, u32[]{:S(2)}) collective-permute-start(bf16[2,128,1024]{2,1,0:T(8,128)(2,1)S(1)} %add.91), channel_id=1, source_target_pairs={{0,1},{1,0},{2,3},{3,2},{4,5},{5,4},{6,7},{7,6},{8,9},{9,8},{10,11... | collective-permute-start | bytes 1572872 | tf_op jit(solution)/shard_map/ppermute | solution.py:22
  94.9 4.2 %activations.7 = (bf16[576,256]{1,0:T(8,128)(2,1)S(1)}, f32[1,256]{1,0:T(1,128)S(1)}, bf16[2,128,1024]{2,1,0:T(8,128)(2,1)S(1)}, bf16[2,128,1024]{2,1,0:T(8,128)...) custom-call(s32[2]{0:T(128)S(1)} %pad_add_fusion.where_ref, ...), custom_call_target="tpu_custom_call" | custom-call | flops 1 | bytes 1 | tf_op jit(solution)/shard_map/activations/pallas_call | solution.py:124
  99.5 0.6 collective-permute-start.27
  100.1 4.3 %collective-permute-done.30.refs_21_ = bf16[576,256]{1,0:T(8,128)(2,1)S(1)} collective-permute-done((bf16[576,256]{1,0:T(8,128)(2,1)S(1)}, bf16[576,256]{1,0:T(8,128)(2,1)S(1)}, u32[]{:S(2)}, u32[]{:S(2)}) %collective-permute-start.30) | collective-permute-done | bytes 294944 | tf_op jit(solution)/shard_map/ppermute | solution.py:22
  104.3 2.6 %collective-permute-start.32 = (bf16[128,1024]{1,0:T(8,128)(2,1)S(1)}, bf16[128,1024]{1,0:T(8,128)(2,1)S(1)}, u32[]{:S(2)}, u32[]{:S(2)}) collective-permute-start(bf16[128,1024]{1,0:T(8,128)(2,1)S(1)} %slice_bitcast_fusion.4), channel_id=1, source_target_pairs={{0,2},{1,3},{2,0},{3,1},{4,6},{5,7},{6,4},{7,5},{8,10},{9,11},{10,... | collective-permute-start | bytes 786440 | tf_op jit(solution)/shard_map/ppermute | solution.py:22
  106.9 0.6 collective-permute-done.28
  107.6 1.5 collective-permute-start.35
  109.1 0.5 collective-permute-start.36
  109.6 0.2 add.93
  109.8 1.6 %collective-permute-start.31 = (bf16[2,128,1024]{2,1,0:T(8,128)(2,1)S(1)}, bf16[2,128,1024]{2,1,0:T(8,128)(2,1)S(1)}, u32[]{:S(2)}, u32[]{:S(2)}) collective-permute-start(bf16[2,128,1024]{2,1,0:T(8,128)(2,1)S(1)} %add.93), channel_id=1, source_target_pairs={{0,1},{1,0},{2,3},{3,2},{4,5},{5,4},{6,7},{7,6},{8,9},{9,8},{10,11... | collective-permute-start | bytes 1572872 | tf_op jit(solution)/shard_map/ppermute | solution.py:22
  111.6 2.7 %collective-permute-start.34 = (bf16[128,1024]{1,0:T(8,128)(2,1)S(1)}, bf16[128,1024]{1,0:T(8,128)(2,1)S(1)}, u32[]{:S(2)}, u32[]{:S(2)}) collective-permute-start(bf16[128,1024]{1,0:T(8,128)(2,1)S(1)} %slice_bitcast_fusion.3), channel_id=1, source_target_pairs={{0,2},{1,3},{2,0},{3,1},{4,6},{5,7},{6,4},{7,5},{8,10},{9,11},{10,... | collective-permute-start | bytes 786440 | tf_op jit(solution)/shard_map/ppermute | solution.py:22
  114.3 0.6 fusion.7
  114.9 5.3 %collective-permute-done.32 = bf16[128,1024]{1,0:T(8,128)(2,1)S(1)} collective-permute-done((bf16[128,1024]{1,0:T(8,128)(2,1)S(1)}, bf16[128,1024]{1,0:T(8,128)(2,1)S(1)}, u32[]{:S(2)}, u32[]{:S(2)}) %collective-permute-start.32) | collective-permute-done | bytes 262176 | tf_op jit(solution)/shard_map/ppermute | solution.py:22
  120.2 2.1 %collective-permute-done.36.refs_23_ = bf16[576,256]{1,0:T(8,128)(2,1)S(1)} collective-permute-done((bf16[576,256]{1,0:T(8,128)(2,1)S(1)}, bf16[576,256]{1,0:T(8,128)(2,1)S(1)}, u32[]{:S(2)}, u32[]{:S(2)}) %collective-permute-start.36) | collective-permute-done | bytes 294944 | tf_op jit(solution)/shard_map/ppermute | solution.py:22
  122.3 6.9 %collective-permute-done.34 = bf16[128,1024]{1,0:T(8,128)(2,1)S(1)} collective-permute-done((bf16[128,1024]{1,0:T(8,128)(2,1)S(1)}, bf16[128,1024]{1,0:T(8,128)(2,1)S(1)}, u32[]{:S(2)}, u32[]{:S(2)}) %collective-permute-start.34) | collective-permute-done | bytes 262176 | tf_op jit(solution)/shard_map/ppermute | solution.py:22
  129.2 2.5 %collective-permute-done.31 = bf16[2,128,1024]{2,1,0:T(8,128)(2,1)S(1)} collective-permute-done((bf16[2,128,1024]{2,1,0:T(8,128)(2,1)S(1)}, bf16[2,128,1024]{2,1,0:T(8,128)(2,1)S(1)}, u32[]{:S(2)}, u32[]{:S(2)}) %collective-permute-start.31) | collective-permute-done | bytes 524320 | tf_op jit(solution)/shard_map/ppermute | solution.py:22
  131.7 3.8 %collective-permute-start.42 = (f32[8,128]{1,0:T(8,128)S(1)}, f32[8,128]{1,0:T(8,128)S(1)}, u32[]{:S(2)}, u32[]{:S(2)}) collective-permute-start(f32[8,128]{1,0:T(8,128)S(1)} %add.92), channel_id=1, source_target_pairs={{0,2},{1,3},{2,0},{3,1},{4,6},{5,7},{6,4},{7,5},{8,10},{9,11},{10,... | collective-permute-start | bytes 12296 | tf_op jit(solution)/shard_map/ppermute | solution.py:22
  135.5 0.2 fusion.1
  135.7 0.6 collective-permute-start.37
  136.6 1.6 collective-permute-start.38
  138.2 10.4 %weight_grads.1 = (bf16[1,192,4096]{2,1,0:T(8,128)(2,1)}, bf16[1,192,4096]{2,1,0:T(8,128)(2,1)}, bf16[1,192,4096]{2,1,0:T(8,128)(2,1)}) custom-call(s32[1]{0:T(128)} %bitcast.14.flag_ref, bf16[128,4096]{1,0:T(8,128)(2,1)} %refs_0_.3, bf16[128,4096]{1,0:T(8,128)(2,1)} %refs_1_.3, bf16[128,4096]{1,0:T(8,128)(2,1)} %copy-done.3, bf16[128,4096]{1,0:T(8,128)(2,1)} %copy-done.4, ...), custom_call_target="tpu_custom_call" | custom-call | flops 1 | bytes 1 | tf_op jit(solution)/shard_map/weight_grads/pallas_call | solution.py:211
  148.6 0.6 gather_fusion
  149.1 0.4 collective-permute-done.40
  149.7 2.5 %collective-permute-start.41 = (bf16[128,1024]{1,0:T(8,128)(2,1)S(1)}, bf16[128,1024]{1,0:T(8,128)(2,1)S(1)}, u32[]{:S(2)}, u32[]{:S(2)}) collective-permute-start(bf16[128,1024]{1,0:T(8,128)(2,1)S(1)} %fusion), channel_id=1, source_target_pairs={{0,24},{4,28},{8,16},{12,20},{16,8},{20,12},{24,0},{28,4},{1,25},{... | collective-permute-start | bytes 786440 | tf_op jit(solution)/shard_map/ppermute | solution.py:22
  152.2 7.0 %all_to_all.6 = bf16[8,1,128]{2,1,0:T(2,128)(2,1)S(1)} all-to-all(bf16[8,1,128]{2,1,0:T(2,128)(2,1)S(1)} %copy.20), channel_id=1, replica_groups=mesh['expert'=8,'dp'=4] {'expert'}, dimensions={0} | all-to-all | bytes 4096 | tf_op jit(solution)/shard_map/all_to_all | solution.py:314
  159.2 0.6 select_reduce_fusion
  159.8 0.9 fusion.6
  (103 shorter events, 2.4 us)
Async XLA Ops:
  0.6 11.9 %collective-permute-start.1 = (bf16[128,4096]{1,0:T(8,128)(2,1)}, bf16[128,4096]{1,0:T(8,128)(2,1)S(1)}, u32[]{:S(2)}, u32[]{:S(2)}) collective-permute-start(bf16[128,4096]{1,0:T(8,128)(2,1)} %refs_0_.3), channel_id=1, source_target_pairs={{0,4},{4,0},{8,12},{12,8},{16,20},{20,16},{24,28},{28,24},{1,5},{5... | collective-permute-start | bytes 3145736 | tf_op jit(solution)/shard_map/ppermute | solution.py:22
  1.1 11.4 %collective-permute-start.2 = (bf16[128,4096]{1,0:T(8,128)(2,1)}, bf16[128,4096]{1,0:T(8,128)(2,1)S(1)}, u32[]{:S(2)}, u32[]{:S(2)}) collective-permute-start(bf16[128,4096]{1,0:T(8,128)(2,1)} %refs_1_.3), channel_id=1, source_target_pairs={{0,4},{4,0},{8,12},{12,8},{16,20},{20,16},{24,28},{28,24},{1,5},{5... | collective-permute-start | bytes 3145736 | tf_op jit(solution)/shard_map/ppermute | solution.py:22
  2.6 9.9 %collective-permute-start = (f32[8,128]{1,0:T(8,128)S(1)}, f32[8,128]{1,0:T(8,128)S(1)}, u32[]{:S(2)}, u32[]{:S(2)}) collective-permute-start(f32[8,128]{1,0:T(8,128)S(1)} %bitcast.55), channel_id=1, source_target_pairs={{0,4},{4,0},{8,12},{12,8},{16,20},{20,16},{24,28},{28,24},{1,5},{5... | collective-permute-start | bytes 12296 | tf_op jit(solution)/shard_map/ppermute | solution.py:22
  5.9 28.3 %collective-permute-start.6 = (bf16[128,4096]{1,0:T(8,128)(2,1)}, bf16[128,4096]{1,0:T(8,128)(2,1)S(1)}, u32[]{:S(2)}, u32[]{:S(2)}) collective-permute-start(bf16[128,4096]{1,0:T(8,128)(2,1)} %get-tuple-element.70), channel_id=1, source_target_pairs={{0,8},{4,12},{8,0},{12,4},{16,24},{20,28},{24,16},{28,20},{1,9},{5... | collective-permute-start | bytes 3145736 | tf_op jit(solution)/shard_map/ppermute | solution.py:22
  8.5 25.6 %collective-permute-start.7 = (bf16[128,4096]{1,0:T(8,128)(2,1)}, bf16[128,4096]{1,0:T(8,128)(2,1)}, u32[]{:S(2)}, u32[]{:S(2)}) collective-permute-start(bf16[128,4096]{1,0:T(8,128)(2,1)} %get-tuple-element.71), channel_id=1, source_target_pairs={{0,16},{4,20},{8,24},{12,28},{16,0},{20,4},{24,8},{28,12},{1,17},{... | collective-permute-start | bytes 3145736 | tf_op jit(solution)/shard_map/ppermute | solution.py:22
  10.1 2.5 %copy-start = (bf16[1,192,4096]{2,1,0:T(8,128)(2,1)S(1)}, bf16[1,192,4096]{2,1,0:T(8,128)(2,1)}, u32[]{:S(2)}) copy-start(bf16[1,192,4096]{2,1,0:T(8,128)(2,1)} %param.12) | copy-start | bytes 4718596
  10.1 2.6 %copy-start.1 = (bf16[128,4096]{1,0:T(8,128)(2,1)S(1)}, bf16[128,4096]{1,0:T(8,128)(2,1)}, u32[]{:S(2)}) copy-start(bf16[128,4096]{1,0:T(8,128)(2,1)} %refs_0_.3) | copy-start | bytes 3145732
  10.1 3.0 %copy-start.2 = (bf16[128,4096]{1,0:T(8,128)(2,1)S(1)}, bf16[128,4096]{1,0:T(8,128)(2,1)}, u32[]{:S(2)}) copy-start(bf16[128,4096]{1,0:T(8,128)(2,1)} %refs_1_.3) | copy-start | bytes 3145732
  12.5 4.5 %copy-start.3 = (bf16[128,4096]{1,0:T(8,128)(2,1)}, bf16[128,4096]{1,0:T(8,128)(2,1)S(1)}, u32[]{:S(2)}) copy-start(bf16[128,4096]{1,0:T(8,128)(2,1)S(1)} %collective-permute-done.1.refs_2_) | copy-start | bytes 3145732
  12.6 4.5 %copy-start.4 = (bf16[128,4096]{1,0:T(8,128)(2,1)}, bf16[128,4096]{1,0:T(8,128)(2,1)S(1)}, u32[]{:S(2)}) copy-start(bf16[128,4096]{1,0:T(8,128)(2,1)S(1)} %collective-permute-done.2.refs_3_) | copy-start | bytes 3145732
  17.1 17.1 %collective-permute-start.10 = (bf16[2,128,1024]{2,1,0:T(8,128)(2,1)S(1)}, bf16[2,128,1024]{2,1,0:T(8,128)(2,1)S(1)}, u32[]{:S(2)}, u32[]{:S(2)}) collective-permute-start(bf16[2,128,1024]{2,1,0:T(8,128)(2,1)S(1)} %get-tuple-element.73), channel_id=1, source_target_pairs={{0,4},{4,0},{8,12},{12,8},{16,20},{20,16},{24,28},{28,24},{1,5},{5... | collective-permute-start | bytes 1572872 | tf_op jit(solution)/shard_map/ppermute | solution.py:22
  17.2 15.5 %collective-permute-start.8 = (f32[16,128]{1,0:T(8,128)S(1)}, f32[16,128]{1,0:T(8,128)S(1)}, u32[]{:S(2)}, u32[]{:S(2)}) collective-permute-start(f32[16,128]{1,0:T(8,128)S(1)} %pad_maximum_fusion.3.one_ref.two_ref), channel_id=1, source_target_pairs={{0,8},{4,12},{8,0},{12,4},{16,24},{20,28},{24,16},{28,20},{1,9},{5... | collective-permute-start | bytes 24584 | tf_op jit(solution)/shard_map/ppermute | solution.py:22
  17.8 16.4 %collective-permute-start.9 = (f32[16,128]{1,0:T(8,128)S(1)}, f32[16,128]{1,0:T(8,128)S(1)}, u32[]{:S(2)}, u32[]{:S(2)}) collective-permute-start(f32[16,128]{1,0:T(8,128)S(1)} %pad_maximum_fusion.3.one_ref.two_ref), channel_id=1, source_target_pairs={{0,16},{4,20},{8,24},{12,28},{16,0},{20,4},{24,8},{28,12},{1,17},{... | collective-permute-start | bytes 24584 | tf_op jit(solution)/shard_map/ppermute | solution.py:22
  34.2 27.9 %copy-start.5 = (bf16[128,4096]{1,0:T(8,128)(2,1)}, bf16[128,4096]{1,0:T(8,128)(2,1)S(1)}, u32[]{:S(2)}) copy-start(bf16[128,4096]{1,0:T(8,128)(2,1)S(1)} %collective-permute-done.6.refs_0_.refs_4_) | copy-start | bytes 3145732
  34.2 4.5 %collective-permute-start.12 = (bf16[128,4096]{1,0:T(8,128)(2,1)S(1)}, bf16[128,4096]{1,0:T(8,128)(2,1)S(1)}, u32[]{:S(2)}, u32[]{:S(2)}) collective-permute-start(bf16[128,4096]{1,0:T(8,128)(2,1)S(1)} %collective-permute-done.6.refs_0_.refs_4_), channel_id=1, source_target_pairs={{0,4},{4,0},{8,12},{12,8},{16,20},{20,16},{24,28},{28,24},{1,5},{5... | collective-permute-start | bytes 3145736 | tf_op jit(solution)/shard_map/ppermute | solution.py:22
  34.3 4.4 %collective-permute-start.13 = (bf16[128,4096]{1,0:T(8,128)(2,1)}, bf16[128,4096]{1,0:T(8,128)(2,1)S(1)}, u32[]{:S(2)}, u32[]{:S(2)}) collective-permute-start(bf16[128,4096]{1,0:T(8,128)(2,1)} %collective-permute-done.7.refs_1_.refs_5_), channel_id=1, source_target_pairs={{0,4},{4,0},{8,12},{12,8},{16,20},{20,16},{24,28},{28,24},{1,5},{5... | collective-permute-start | bytes 3145736 | tf_op jit(solution)/shard_map/ppermute | solution.py:22
  34.8 25.4 %collective-permute-start.4 = (bf16[128,4096]{1,0:T(8,128)(2,1)}, bf16[128,4096]{1,0:T(8,128)(2,1)S(1)}, u32[]{:S(2)}, u32[]{:S(2)}) collective-permute-start(bf16[128,4096]{1,0:T(8,128)(2,1)} %get-tuple-element.70), channel_id=1, source_target_pairs={{0,16},{4,20},{8,24},{12,28},{16,0},{20,4},{24,8},{28,12},{1,17},{... | collective-permute-start | bytes 3145736 | tf_op jit(solution)/shard_map/ppermute | solution.py:22
  36.3 25.1 %collective-permute-start.5 = (bf16[128,4096]{1,0:T(8,128)(2,1)}, bf16[128,4096]{1,0:T(8,128)(2,1)S(1)}, u32[]{:S(2)}, u32[]{:S(2)}) collective-permute-start(bf16[128,4096]{1,0:T(8,128)(2,1)} %get-tuple-element.71), channel_id=1, source_target_pairs={{0,8},{4,12},{8,0},{12,4},{16,24},{20,28},{24,16},{28,20},{1,9},{5... | collective-permute-start | bytes 3145736 | tf_op jit(solution)/shard_map/ppermute | solution.py:22
  37.0 24.3 %collective-permute-start.14 = (bf16[2,128,1024]{2,1,0:T(8,128)(2,1)S(1)}, bf16[2,128,1024]{2,1,0:T(8,128)(2,1)S(1)}, u32[]{:S(2)}, u32[]{:S(2)}) collective-permute-start(bf16[2,128,1024]{2,1,0:T(8,128)(2,1)S(1)} %add.85), channel_id=1, source_target_pairs={{0,1},{1,0},{2,3},{3,2},{4,5},{5,4},{6,7},{7,6},{8,9},{9,8},{10,11... | collective-permute-start | bytes 1572872 | tf_op jit(solution)/shard_map/ppermute | solution.py:22
  38.7 5.5 %copy-start.6 = (bf16[128,4096]{1,0:T(8,128)(2,1)}, bf16[128,4096]{1,0:T(8,128)(2,1)S(1)}, u32[]{:S(2)}) copy-start(bf16[128,4096]{1,0:T(8,128)(2,1)S(1)} %collective-permute-done.12.refs_2_.refs_6_) | copy-start | bytes 3145732
  38.7 5.5 %copy-start.7 = (bf16[128,4096]{1,0:T(8,128)(2,1)}, bf16[128,4096]{1,0:T(8,128)(2,1)S(1)}, u32[]{:S(2)}) copy-start(bf16[128,4096]{1,0:T(8,128)(2,1)S(1)} %collective-permute-done.13.refs_3_.refs_7_) | copy-start | bytes 3145732
  44.2 17.2 %collective-permute-start.15 = (bf16[2,128,1024]{2,1,0:T(8,128)(2,1)S(1)}, bf16[2,128,1024]{2,1,0:T(8,128)(2,1)S(1)}, u32[]{:S(2)}, u32[]{:S(2)}) collective-permute-start(bf16[2,128,1024]{2,1,0:T(8,128)(2,1)S(1)} %get-tuple-element.81), channel_id=1, source_target_pairs={{0,4},{4,0},{8,12},{12,8},{16,20},{20,16},{24,28},{28,24},{1,5},{5... | collective-permute-start | bytes 1572872 | tf_op jit(solution)/shard_map/ppermute | solution.py:22
  44.3 17.1 %collective-permute-start.11 = (f32[16,128]{1,0:T(8,128)S(1)}, f32[16,128]{1,0:T(8,128)S(1)}, u32[]{:S(2)}, u32[]{:S(2)}) collective-permute-start(f32[16,128]{1,0:T(8,128)S(1)} %collective-permute-done.8.one_ref.two_ref), channel_id=1, source_target_pairs={{0,16},{4,20},{8,24},{12,28},{16,0},{20,4},{24,8},{28,12},{1,17},{... | collective-permute-start | bytes 24584 | tf_op jit(solution)/shard_map/ppermute | solution.py:22
  60.2 9.5 %copy-start.8 = (bf16[128,4096]{1,0:T(8,128)(2,1)}, bf16[128,4096]{1,0:T(8,128)(2,1)S(1)}, u32[]{:S(2)}) copy-start(bf16[128,4096]{1,0:T(8,128)(2,1)S(1)} %collective-permute-done.4.refs_0_.refs_8_) | copy-start | bytes 3145732
  61.4 8.4 %copy-start.9 = (bf16[128,4096]{1,0:T(8,128)(2,1)}, bf16[128,4096]{1,0:T(8,128)(2,1)S(1)}, u32[]{:S(2)}) copy-start(bf16[128,4096]{1,0:T(8,128)(2,1)S(1)} %collective-permute-done.5.refs_1_.refs_9_) | copy-start | bytes 3145732
  61.4 2.7 %collective-permute-start.18 = (bf16[128,4096]{1,0:T(8,128)(2,1)S(1)}, bf16[128,4096]{1,0:T(8,128)(2,1)S(1)}, u32[]{:S(2)}, u32[]{:S(2)}) collective-permute-start(bf16[128,4096]{1,0:T(8,128)(2,1)S(1)} %collective-permute-done.4.refs_0_.refs_8_), channel_id=1, source_target_pairs={{0,4},{4,0},{8,12},{12,8},{16,20},{20,16},{24,28},{28,24},{1,5},{5... | collective-permute-start | bytes 3145736 | tf_op jit(solution)/shard_map/ppermute | solution.py:22
  61.5 4.2 %collective-permute-start.19 = (bf16[128,4096]{1,0:T(8,128)(2,1)S(1)}, bf16[128,4096]{1,0:T(8,128)(2,1)S(1)}, u32[]{:S(2)}, u32[]{:S(2)}) collective-permute-start(bf16[128,4096]{1,0:T(8,128)(2,1)S(1)} %collective-permute-done.5.refs_1_.refs_9_), channel_id=1, source_target_pairs={{0,4},{4,0},{8,12},{12,8},{16,20},{20,16},{24,28},{28,24},{1,5},{5... | collective-permute-start | bytes 3145736 | tf_op jit(solution)/shard_map/ppermute | solution.py:22
  62.0 7.9 %collective-permute-start.3 = (bf16[2,128,1024]{2,1,0:T(8,128)(2,1)S(1)}, bf16[2,128,1024]{2,1,0:T(8,128)(2,1)S(1)}, u32[]{:S(2)}, u32[]{:S(2)}) collective-permute-start(bf16[2,128,1024]{2,1,0:T(8,128)(2,1)S(1)} %get-tuple-element.69), channel_id=1, source_target_pairs={{0,4},{4,0},{8,12},{12,8},{16,20},{20,16},{24,28},{28,24},{1,5},{5... | collective-permute-start | bytes 1572872 | tf_op jit(solution)/shard_map/ppermute | solution.py:22
  62.0 25.5 %collective-permute-start.16 = (bf16[128,4096]{1,0:T(8,128)(2,1)S(1)}, bf16[128,4096]{1,0:T(8,128)(2,1)S(1)}, u32[]{:S(2)}, u32[]{:S(2)}) collective-permute-start(bf16[128,4096]{1,0:T(8,128)(2,1)S(1)} %collective-permute-done.6.refs_0_.refs_4_), channel_id=1, source_target_pairs={{0,16},{4,20},{8,24},{12,28},{16,0},{20,4},{24,8},{28,12},{1,17},{... | collective-permute-start | bytes 3145736 | tf_op jit(solution)/shard_map/ppermute | solution.py:22
  62.5 25.4 %collective-permute-start.17 = (bf16[128,4096]{1,0:T(8,128)(2,1)}, bf16[128,4096]{1,0:T(8,128)(2,1)S(1)}, u32[]{:S(2)}, u32[]{:S(2)}) collective-permute-start(bf16[128,4096]{1,0:T(8,128)(2,1)} %collective-permute-done.7.refs_1_.refs_5_), channel_id=1, source_target_pairs={{0,8},{4,12},{8,0},{12,4},{16,24},{20,28},{24,16},{28,20},{1,9},{5... | collective-permute-start | bytes 3145736 | tf_op jit(solution)/shard_map/ppermute | solution.py:22
  64.1 5.6 %copy-start.10 = (bf16[128,4096]{1,0:T(8,128)(2,1)}, bf16[128,4096]{1,0:T(8,128)(2,1)S(1)}, u32[]{:S(2)}) copy-start(bf16[128,4096]{1,0:T(8,128)(2,1)S(1)} %collective-permute-done.18.refs_2_.refs_10_) | copy-start | bytes 3145732
  64.1 23.9 %collective-permute-start.21 = (bf16[2,128,1024]{2,1,0:T(8,128)(2,1)S(1)}, bf16[2,128,1024]{2,1,0:T(8,128)(2,1)S(1)}, u32[]{:S(2)}, u32[]{:S(2)}) collective-permute-start(bf16[2,128,1024]{2,1,0:T(8,128)(2,1)S(1)} %add.87), channel_id=1, source_target_pairs={{0,1},{1,0},{2,3},{3,2},{4,5},{5,4},{6,7},{7,6},{8,9},{9,8},{10,11... | collective-permute-start | bytes 1572872 | tf_op jit(solution)/shard_map/ppermute | solution.py:22
  65.7 4.1 %copy-start.11 = (bf16[128,4096]{1,0:T(8,128)(2,1)}, bf16[128,4096]{1,0:T(8,128)(2,1)S(1)}, u32[]{:S(2)}) copy-start(bf16[128,4096]{1,0:T(8,128)(2,1)S(1)} %collective-permute-done.19.refs_3_.refs_11_) | copy-start | bytes 3145732
  69.8 18.2 %collective-permute-start.22 = (bf16[2,128,1024]{2,1,0:T(8,128)(2,1)S(1)}, bf16[2,128,1024]{2,1,0:T(8,128)(2,1)S(1)}, u32[]{:S(2)}, u32[]{:S(2)}) collective-permute-start(bf16[2,128,1024]{2,1,0:T(8,128)(2,1)S(1)} %get-tuple-element.88), channel_id=1, source_target_pairs={{0,4},{4,0},{8,12},{12,8},{16,20},{20,16},{24,28},{28,24},{1,5},{5... | collective-permute-start | bytes 1572872 | tf_op jit(solution)/shard_map/ppermute | solution.py:22
  70.0 18.0 %collective-permute-start.20 = (bf16[128,1024]{1,0:T(8,128)(2,1)S(1)}, bf16[128,1024]{1,0:T(8,128)(2,1)S(1)}, u32[]{:S(2)}, u32[]{:S(2)}) collective-permute-start(bf16[128,1024]{1,0:T(8,128)(2,1)S(1)} %slice_bitcast_fusion.6), channel_id=1, source_target_pairs={{0,2},{1,3},{2,0},{3,1},{4,6},{5,7},{6,4},{7,5},{8,10},{9,11},{10,... | collective-permute-start | bytes 786440 | tf_op jit(solution)/shard_map/ppermute | solution.py:22
  87.5 7.4 %copy-start.12 = (bf16[128,4096]{1,0:T(8,128)(2,1)}, bf16[128,4096]{1,0:T(8,128)(2,1)S(1)}, u32[]{:S(2)}) copy-start(bf16[128,4096]{1,0:T(8,128)(2,1)S(1)} %collective-permute-done.16.refs_0_.refs_12_) | copy-start | bytes 3145732
  88.0 6.9 %copy-start.13 = (bf16[128,4096]{1,0:T(8,128)(2,1)}, bf16[128,4096]{1,0:T(8,128)(2,1)S(1)}, u32[]{:S(2)}) copy-start(bf16[128,4096]{1,0:T(8,128)(2,1)S(1)} %collective-permute-done.17.refs_1_.refs_13_) | copy-start | bytes 3145732
  88.0 5.2 %collective-permute-start.24 = (bf16[128,4096]{1,0:T(8,128)(2,1)S(1)}, bf16[128,4096]{1,0:T(8,128)(2,1)S(1)}, u32[]{:S(2)}, u32[]{:S(2)}) collective-permute-start(bf16[128,4096]{1,0:T(8,128)(2,1)S(1)} %collective-permute-done.16.refs_0_.refs_12_), channel_id=1, source_target_pairs={{0,4},{4,0},{8,12},{12,8},{16,20},{20,16},{24,28},{28,24},{1,5},{5... | collective-permute-start | bytes 3145736 | tf_op jit(solution)/shard_map/ppermute | solution.py:22
  88.1 6.8 %collective-permute-start.25 = (bf16[128,4096]{1,0:T(8,128)(2,1)S(1)}, bf16[128,4096]{1,0:T(8,128)(2,1)S(1)}, u32[]{:S(2)}, u32[]{:S(2)}) collective-permute-start(bf16[128,4096]{1,0:T(8,128)(2,1)S(1)} %collective-permute-done.17.refs_1_.refs_13_), channel_id=1, source_target_pairs={{0,4},{4,0},{8,12},{12,8},{16,20},{20,16},{24,28},{28,24},{1,5},{5... | collective-permute-start | bytes 3145736 | tf_op jit(solution)/shard_map/ppermute | solution.py:22
  88.6 4.4 %collective-permute-start.23 = (bf16[2,128,1024]{2,1,0:T(8,128)(2,1)S(1)}, bf16[2,128,1024]{2,1,0:T(8,128)(2,1)S(1)}, u32[]{:S(2)}, u32[]{:S(2)}) collective-permute-start(bf16[2,128,1024]{2,1,0:T(8,128)(2,1)S(1)} %get-tuple-element.91), channel_id=1, source_target_pairs={{0,4},{4,0},{8,12},{12,8},{16,20},{20,16},{24,28},{28,24},{1,5},{5... | collective-permute-start | bytes 1572872 | tf_op jit(solution)/shard_map/ppermute | solution.py:22
  88.7 10.8 %collective-permute-start.29 = (bf16[576,256]{1,0:T(8,128)(2,1)S(1)}, bf16[576,256]{1,0:T(8,128)(2,1)S(1)}, u32[]{:S(2)}, u32[]{:S(2)}) collective-permute-start(bf16[576,256]{1,0:T(8,128)(2,1)S(1)} %get-tuple-element.103.refs_16_), channel_id=1, source_target_pairs={{0,16},{4,20},{8,24},{12,28},{16,0},{20,4},{24,8},{28,12},{1,17},{... | collective-permute-start | bytes 884744 | tf_op jit(solution)/shard_map/ppermute | solution.py:22
  90.2 14.2 %collective-permute-start.30 = (bf16[576,256]{1,0:T(8,128)(2,1)S(1)}, bf16[576,256]{1,0:T(8,128)(2,1)S(1)}, u32[]{:S(2)}, u32[]{:S(2)}) collective-permute-start(bf16[576,256]{1,0:T(8,128)(2,1)S(1)} %get-tuple-element.104.refs_17_), channel_id=1, source_target_pairs={{0,16},{4,20},{8,24},{12,28},{16,0},{20,4},{24,8},{28,12},{1,17},{... | collective-permute-start | bytes 884744 | tf_op jit(solution)/shard_map/ppermute | solution.py:22
  93.0 18.5 %collective-permute-start.33 = (bf16[2,128,1024]{2,1,0:T(8,128)(2,1)S(1)}, bf16[2,128,1024]{2,1,0:T(8,128)(2,1)S(1)}, u32[]{:S(2)}, u32[]{:S(2)}) collective-permute-start(bf16[2,128,1024]{2,1,0:T(8,128)(2,1)S(1)} %get-tuple-element.109), channel_id=1, source_target_pairs={{0,4},{4,0},{8,12},{12,8},{16,20},{20,16},{24,28},{28,24},{1,5},{5... | collective-permute-start | bytes 1572872 | tf_op jit(solution)/shard_map/ppermute | solution.py:22
  93.2 5.9 %copy-start.14 = (bf16[128,4096]{1,0:T(8,128)(2,1)}, bf16[128,4096]{1,0:T(8,128)(2,1)S(1)}, u32[]{:S(2)}) copy-start(bf16[128,4096]{1,0:T(8,128)(2,1)S(1)} %collective-permute-done.24.refs_2_.refs_14_) | copy-start | bytes 3145732
  93.2 14.3 %collective-permute-start.28 = (bf16[2,128,1024]{2,1,0:T(8,128)(2,1)S(1)}, bf16[2,128,1024]{2,1,0:T(8,128)(2,1)S(1)}, u32[]{:S(2)}, u32[]{:S(2)}) collective-permute-start(bf16[2,128,1024]{2,1,0:T(8,128)(2,1)S(1)} %add.91), channel_id=1, source_target_pairs={{0,1},{1,0},{2,3},{3,2},{4,5},{5,4},{6,7},{7,6},{8,9},{9,8},{10,11... | collective-permute-start | bytes 1572872 | tf_op jit(solution)/shard_map/ppermute | solution.py:22
  94.9 4.2 %copy-start.15 = (bf16[128,4096]{1,0:T(8,128)(2,1)}, bf16[128,4096]{1,0:T(8,128)(2,1)S(1)}, u32[]{:S(2)}) copy-start(bf16[128,4096]{1,0:T(8,128)(2,1)S(1)} %collective-permute-done.25.refs_3_.refs_15_) | copy-start | bytes 3145732
  99.2 10.5 %collective-permute-start.26 = (bf16[2,128,1024]{2,1,0:T(8,128)(2,1)S(1)}, bf16[2,128,1024]{2,1,0:T(8,128)(2,1)S(1)}, u32[]{:S(2)}, u32[]{:S(2)}) collective-permute-start(bf16[2,128,1024]{2,1,0:T(8,128)(2,1)S(1)} %get-tuple-element.100), channel_id=1, source_target_pairs={{0,4},{4,0},{8,12},{12,8},{16,20},{20,16},{24,28},{28,24},{1,5},{5... | collective-permute-start | bytes 1572872 | tf_op jit(solution)/shard_map/ppermute | solution.py:22
  99.5 9.6 %collective-permute-start.27 = (f32[8,128]{1,0:T(8,128)S(1)}, f32[8,128]{1,0:T(8,128)S(1)}, u32[]{:S(2)}, u32[]{:S(2)}) collective-permute-start(f32[8,128]{1,0:T(8,128)S(1)} %maximum_maximum_fusion), channel_id=1, source_target_pairs={{0,1},{1,0},{2,3},{3,2},{4,5},{5,4},{6,7},{7,6},{8,9},{9,8},{10,11... | collective-permute-start | bytes 12296 | tf_op jit(solution)/shard_map/ppermute | solution.py:22
  104.3 15.8 %collective-permute-start.32 = (bf16[128,1024]{1,0:T(8,128)(2,1)S(1)}, bf16[128,1024]{1,0:T(8,128)(2,1)S(1)}, u32[]{:S(2)}, u32[]{:S(2)}) collective-permute-start(bf16[128,1024]{1,0:T(8,128)(2,1)S(1)} %slice_bitcast_fusion.4), channel_id=1, source_target_pairs={{0,2},{1,3},{2,0},{3,1},{4,6},{5,7},{6,4},{7,5},{8,10},{9,11},{10,... | collective-permute-start | bytes 786440 | tf_op jit(solution)/shard_map/ppermute | solution.py:22
  107.6 12.6 %collective-permute-start.35 = (bf16[576,256]{1,0:T(8,128)(2,1)S(1)}, bf16[576,256]{1,0:T(8,128)(2,1)S(1)}, u32[]{:S(2)}, u32[]{:S(2)}) collective-permute-start(bf16[576,256]{1,0:T(8,128)(2,1)S(1)} %get-tuple-element.111.refs_18_), channel_id=1, source_target_pairs={{0,16},{4,20},{8,24},{12,28},{16,0},{20,4},{24,8},{28,12},{1,17},{... | collective-permute-start | bytes 884744 | tf_op jit(solution)/shard_map/ppermute | solution.py:22
  109.1 13.2 %collective-permute-start.36 = (bf16[576,256]{1,0:T(8,128)(2,1)S(1)}, bf16[576,256]{1,0:T(8,128)(2,1)S(1)}, u32[]{:S(2)}, u32[]{:S(2)}) collective-permute-start(bf16[576,256]{1,0:T(8,128)(2,1)S(1)} %get-tuple-element.112.refs_19_), channel_id=1, source_target_pairs={{0,16},{4,20},{8,24},{12,28},{16,0},{20,4},{24,8},{28,12},{1,17},{... | collective-permute-start | bytes 884744 | tf_op jit(solution)/shard_map/ppermute | solution.py:22
  109.8 4.4 %copy-start.17 = (s32[4]{0:T(128)S(1)}, s32[4]{0:T(128)}, u32[]{:S(2)}) copy-start(s32[4]{0:T(128)} %param.15) | copy-start | bytes 52
  109.8 21.9 %collective-permute-start.31 = (bf16[2,128,1024]{2,1,0:T(8,128)(2,1)S(1)}, bf16[2,128,1024]{2,1,0:T(8,128)(2,1)S(1)}, u32[]{:S(2)}, u32[]{:S(2)}) collective-permute-start(bf16[2,128,1024]{2,1,0:T(8,128)(2,1)S(1)} %add.93), channel_id=1, source_target_pairs={{0,1},{1,0},{2,3},{3,2},{4,5},{5,4},{6,7},{7,6},{8,9},{9,8},{10,11... | collective-permute-start | bytes 1572872 | tf_op jit(solution)/shard_map/ppermute | solution.py:22
  111.6 17.7 %collective-permute-start.34 = (bf16[128,1024]{1,0:T(8,128)(2,1)S(1)}, bf16[128,1024]{1,0:T(8,128)(2,1)S(1)}, u32[]{:S(2)}, u32[]{:S(2)}) collective-permute-start(bf16[128,1024]{1,0:T(8,128)(2,1)S(1)} %slice_bitcast_fusion.3), channel_id=1, source_target_pairs={{0,2},{1,3},{2,0},{3,1},{4,6},{5,7},{6,4},{7,5},{8,10},{9,11},{10,... | collective-permute-start | bytes 786440 | tf_op jit(solution)/shard_map/ppermute | solution.py:22
  120.2 16.2 %collective-permute-start.39 = (bf16[2,128,1024]{2,1,0:T(8,128)(2,1)S(1)}, bf16[2,128,1024]{2,1,0:T(8,128)(2,1)S(1)}, u32[]{:S(2)}, u32[]{:S(2)}) collective-permute-start(bf16[2,128,1024]{2,1,0:T(8,128)(2,1)S(1)} %get-tuple-element.116), channel_id=1, source_target_pairs={{0,4},{4,0},{8,12},{12,8},{16,20},{20,16},{24,28},{28,24},{1,5},{5... | collective-permute-start | bytes 1572872 | tf_op jit(solution)/shard_map/ppermute | solution.py:22
  131.7 16.9 %collective-permute-start.42 = (f32[8,128]{1,0:T(8,128)S(1)}, f32[8,128]{1,0:T(8,128)S(1)}, u32[]{:S(2)}, u32[]{:S(2)}) collective-permute-start(f32[8,128]{1,0:T(8,128)S(1)} %add.92), channel_id=1, source_target_pairs={{0,2},{1,3},{2,0},{3,1},{4,6},{5,7},{6,4},{7,5},{8,10},{9,11},{10,... | collective-permute-start | bytes 12296 | tf_op jit(solution)/shard_map/ppermute | solution.py:22
  135.7 24.1 %collective-permute-start.37 = (bf16[128,1024]{1,0:T(8,128)(2,1)S(1)}, bf16[128,1024]{1,0:T(8,128)(2,1)S(1)}, u32[]{:S(2)}, u32[]{:S(2)}) collective-permute-start(bf16[128,1024]{1,0:T(8,128)(2,1)S(1)} %pad_maximum_fusion.1), channel_id=1, source_target_pairs={{0,8},{4,12},{8,0},{12,4},{16,24},{20,28},{24,16},{28,20},{1,9},{5... | collective-permute-start | bytes 786440 | tf_op jit(solution)/shard_map/ppermute | solution.py:22
  136.5 13.1 %collective-permute-start.40 = (bf16[128,1024]{1,0:T(8,128)(2,1)S(1)}, bf16[128,1024]{1,0:T(8,128)(2,1)S(1)}, u32[]{:S(2)}, u32[]{:S(2)}) collective-permute-start(bf16[128,1024]{1,0:T(8,128)(2,1)S(1)} %slice_bitcast_fusion), channel_id=1, source_target_pairs={{0,2},{1,3},{2,0},{3,1},{4,6},{5,7},{6,4},{7,5},{8,10},{9,11},{10,... | collective-permute-start | bytes 786440 | tf_op jit(solution)/shard_map/ppermute | solution.py:22
  136.6 22.7 %copy-start.16 = (s32[128,4]{0,1:T(4,128)S(1)}, s32[128,4]{0,1:T(4,128)}, u32[]{:S(2)}) copy-start(s32[128,4]{0,1:T(4,128)} %param.13) | copy-start | bytes 6148
  136.6 23.2 %collective-permute-start.38 = (bf16[128,1024]{1,0:T(8,128)(2,1)S(1)}, bf16[128,1024]{1,0:T(8,128)(2,1)S(1)}, u32[]{:S(2)}, u32[]{:S(2)}) collective-permute-start(bf16[128,1024]{1,0:T(8,128)(2,1)S(1)} %pad_maximum_fusion.2), channel_id=1, source_target_pairs={{0,16},{4,20},{8,24},{12,28},{16,0},{20,4},{24,8},{28,12},{1,17},{... | collective-permute-start | bytes 786440 | tf_op jit(solution)/shard_map/ppermute | solution.py:22
  149.7 10.2 %collective-permute-start.41 = (bf16[128,1024]{1,0:T(8,128)(2,1)S(1)}, bf16[128,1024]{1,0:T(8,128)(2,1)S(1)}, u32[]{:S(2)}, u32[]{:S(2)}) collective-permute-start(bf16[128,1024]{1,0:T(8,128)(2,1)S(1)} %fusion), channel_id=1, source_target_pairs={{0,24},{4,28},{8,16},{12,20},{16,8},{20,12},{24,0},{28,4},{1,25},{... | collective-permute-start | bytes 786440 | tf_op jit(solution)/shard_map/ppermute | solution.py:22
